TPU v7x, 32 devices: a whole 2x2x4 slice. The times are simulated.
32 devices in a mesh: rows: 8 (over z, y), cols: 4 (over x, core).
Axes of the slice: x: 2, y: 2, z: 4, core: 2. Of those that a mesh axis runs over, the one named last changes fastest.
Arguments:
- crawl: bfloat16 [8192, 128], P('rows'), may hold values from -16 to 16
- bench: bfloat16 [16384, 128], P('cols'), may hold values from -2 to 2
- start_duals: float32 [16384], P('cols'), may hold values from -0.15 to 0.15
- row_cotangent: float32 [8192], P('rows'), may hold values from -24 to 24
- col_cotangent: float32 [16384], P('cols'), may hold values from -24 to 24
Outputs:
- crawl_grad: float32 [8192, 128], P('rows')
- bench_grad: float32 [16384, 128], P('cols')
All inputs are finite; a program needn't handle non-finite values.
Results may differ from a plain program's by a relative error of at most 0.0039.
Values sent between devices are 32-bit elements; how exact they have to be, the bound alone decides.
No kernel may reach another device: no remote copies, remote signals or barrier semaphores. Data moves between devices by JAX's collectives and lax.ppermute only.
A program may use at most 64 MiB of HBM per device.

v0:
```python
import math

import jax
import jax.numpy as jnp
from jax import lax
from jax.sharding import PartitionSpec as P

EPSILON = 0.05


def row_lse(logits):
    highest = jnp.max(logits, 1)
    highest = lax.pmax(highest, "cols")
    summed = lax.psum(jnp.sum(jnp.exp(logits - highest[:, None]), 1), "cols")
    return highest + jnp.log(summed)


def col_lse(logits):
    highest = jnp.max(logits, 0)
    highest = lax.pmax(highest, "rows")
    summed = lax.psum(jnp.sum(jnp.exp(logits - highest[None, :]), 0), "rows")
    return highest + jnp.log(summed)


def row_reduce(values):
    return lax.psum(jnp.sum(values, 1), "cols")


def per_device(crawl, bench, start_duals, row_cotangent, col_cotangent):
    log_bench = math.log(bench.shape[0] * lax.axis_size("cols"))
    log_crawl = math.log(crawl.shape[0] * lax.axis_size("rows"))
    tile = lax.dot_general(
        crawl, bench, (((1,), (1,)), ((), ())), preferred_element_type=jnp.float32
    )
    row_level1 = row_lse((start_duals[None, :] + tile) / EPSILON)
    row_dual1 = -EPSILON * (row_level1 - log_bench)
    col_level1 = col_lse((row_dual1[:, None] + tile) / EPSILON)
    col_dual1 = -EPSILON * (col_level1 - log_crawl)
    row_level2 = row_lse((col_dual1[None, :] + tile) / EPSILON)
    row_dual2 = -EPSILON * (row_level2 - log_bench)
    col_level2 = col_lse((row_dual2[:, None] + tile) / EPSILON)
    col_soft2 = jnp.exp((row_dual2[:, None] + tile) / EPSILON - col_level2[None, :])
    row_back2 = row_cotangent - row_reduce(col_soft2 * col_cotangent[None, :])
    row_soft2 = jnp.exp((col_dual1[None, :] + tile) / EPSILON - row_level2[:, None])
    col_back1 = -lax.psum(jnp.sum(row_soft2 * row_back2[:, None], 0), "rows")
    col_soft1 = jnp.exp((row_dual1[:, None] + tile) / EPSILON - col_level1[None, :])
    row_back1 = -row_reduce(col_soft1 * col_back1[None, :])
    row_soft1 = jnp.exp((start_duals[None, :] + tile) / EPSILON - row_level1[:, None])
    score_grad = -(
        col_soft2 * col_cotangent[None, :]
        + row_soft2 * row_back2[:, None]
        + col_soft1 * col_back1[None, :]
        + row_soft1 * row_back1[:, None]
    )
    score_grad = score_grad.astype(jnp.bfloat16)
    crawl_part = jnp.dot(score_grad, bench, preferred_element_type=jnp.float32)
    crawl_grad = lax.psum(crawl_part, "cols")
    bench_part = lax.dot_general(
        score_grad, crawl, (((0,), (0,)), ((), ())), preferred_element_type=jnp.float32
    )
    bench_grad = lax.psum(bench_part, "rows")
    return (crawl_grad, bench_grad)


def solution(mesh):
    placed = (P("rows", None), P("cols", None), P("cols"), P("rows"), P("cols"))
    return jax.shard_map(
        per_device,
        mesh=mesh,
        in_specs=placed,
        out_specs=(P("rows", None), P("cols", None)),
        check_vma=False,
    )
```

profile of v0, /device:TPU:0, one launch (start us, length us, event | category | flops | bytes accessed | tf_op | source)
XLA Modules:
  0.0 476.2 jit_solution(9827906639839641422)
XLA Ops:
  7.2 1.2 copy-done
  8.4 7.9 %fusion.3 = (f32[1024]{0:T(1024)S(1)}, f32[1024,4096]{1,0:T(8,128)}) fusion(f32[4096]{0:T(1024)} %param.7, bf16[1024,128]{1,0:T(8,128)(2,1)} %param.5, bf16[4096,128]{1,0:T(8,128)(2,1)S(1)} %copy-done), kind=kOutput, calls=%fused_computation.15 | convolution fusion | flops 1086323712 | bytes 18108416 | tf_op jit(solution)/shard_map/dot_general | solution.py:32
  16.3 8.3 %pmax.28 = f32[1024]{0:T(1024)S(1)} all-reduce(f32[1024]{0:T(1024)S(1)} %get-tuple-element.8), channel_id=1, replica_groups=mesh['rows'=8,'cols'=4] {'cols'}, use_global_device_ids=true, to_apply=%region_1.0 | all-reduce | flops 1024 | bytes 8192 | tf_op jit(solution)/shard_map/pmax | solution.py:13
  24.7 7.8 %exponential_reduce_fusion.3 = f32[1024]{0:T(1024)S(1)} fusion(f32[1024,4096]{1,0:T(8,128)} %get-tuple-element.9, f32[1024]{0:T(1024)S(1)} %pmax.28, f32[4096]{0:T(1024)S(1)} %copy-done.3), kind=kLoop, calls=%fused_computation.10 | loop fusion | flops 16776192 | bytes 16801792 | tf_op jit(solution)/shard_map/reduce_sum | solution.py:14
  32.5 5.8 %psum.63 = f32[1024]{0:T(1024)S(1)} all-reduce(f32[1024]{0:T(1024)S(1)} %exponential_reduce_fusion.3), channel_id=1, replica_groups=mesh['rows'=8,'cols'=4] {'cols'}, use_global_device_ids=true, to_apply=%region_3.0 | all-reduce | flops 1024 | bytes 8192 | tf_op jit(solution)/shard_map/psum | solution.py:14
  38.3 7.7 %fusion.4 = f32[4096]{0:T(1024)S(1)} fusion(f32[1024,4096]{1,0:T(8,128)} %get-tuple-element.9, f32[1024]{0:T(1024)S(1)} %get-tuple-element.6), kind=kLoop, calls=%fused_computation.16 | loop fusion | flops 12578816 | bytes 16797696 | tf_op jit(solution)/shard_map/reduce_max | solution.py:19
  46.0 37.5 %pmax.29 = f32[4096]{0:T(1024)S(1)} all-reduce(f32[4096]{0:T(1024)S(1)} %fusion.4), channel_id=1, replica_groups=mesh['rows'=8,'cols'=4] {'rows'}, use_global_device_ids=true, to_apply=%region_5.0 | all-reduce | flops 4096 | bytes 32768 | tf_op jit(solution)/shard_map/pmax | solution.py:20
  83.5 7.7 %exponential_reduce_fusion.2 = f32[4096]{0:T(1024)S(1)} fusion(f32[1024,4096]{1,0:T(8,128)} %get-tuple-element.9, f32[4096]{0:T(1024)S(1)} %pmax.29, f32[1024]{0:T(1024)S(1)} %get-tuple-element.6), kind=kLoop, calls=%fused_computation.8 | loop fusion | flops 16773120 | bytes 16814080 | tf_op jit(solution)/shard_map/reduce_sum | solution.py:21
  91.2 33.0 %psum.64 = f32[4096]{0:T(1024)S(1)} all-reduce(f32[4096]{0:T(1024)S(1)} %exponential_reduce_fusion.2), channel_id=1, replica_groups=mesh['rows'=8,'cols'=4] {'rows'}, use_global_device_ids=true, to_apply=%region_7.0 | all-reduce | flops 4096 | bytes 32768 | tf_op jit(solution)/shard_map/psum | solution.py:21
  124.2 7.5 %fusion.5 = f32[1024]{0:T(1024)S(1)} fusion(f32[1024,4096]{1,0:T(8,128)} %get-tuple-element.9, f32[4096]{0:T(1024)S(1)} %get-tuple-element.4), kind=kLoop, calls=%fused_computation.17 | loop fusion | flops 12581888 | bytes 16797696 | tf_op jit(solution)/shard_map/reduce_max | solution.py:12
  131.7 5.8 %pmax.30 = f32[1024]{0:T(1024)S(1)} all-reduce(f32[1024]{0:T(1024)S(1)} %fusion.5), channel_id=1, replica_groups=mesh['rows'=8,'cols'=4] {'cols'}, use_global_device_ids=true, to_apply=%region_9.0 | all-reduce | flops 1024 | bytes 8192 | tf_op jit(solution)/shard_map/pmax | solution.py:13
  137.5 7.8 %exponential_reduce_fusion.1 = f32[1024]{0:T(1024)S(1)} fusion(f32[1024,4096]{1,0:T(8,128)} %get-tuple-element.9, f32[1024]{0:T(1024)S(1)} %pmax.30, f32[4096]{0:T(1024)S(1)} %get-tuple-element.4), kind=kLoop, calls=%fused_computation.6 | loop fusion | flops 16776192 | bytes 16801792 | tf_op jit(solution)/shard_map/reduce_sum | solution.py:14
  145.3 5.8 %psum.65 = f32[1024]{0:T(1024)S(1)} all-reduce(f32[1024]{0:T(1024)S(1)} %exponential_reduce_fusion.1), channel_id=1, replica_groups=mesh['rows'=8,'cols'=4] {'cols'}, use_global_device_ids=true, to_apply=%region_11.0 | all-reduce | flops 1024 | bytes 8192 | tf_op jit(solution)/shard_map/psum | solution.py:14
  151.1 7.7 %fusion.6 = f32[4096]{0:T(1024)S(1)} fusion(f32[1024,4096]{1,0:T(8,128)} %get-tuple-element.9, f32[1024]{0:T(1024)S(1)} %get-tuple-element.2), kind=kLoop, calls=%fused_computation.18 | loop fusion | flops 12578816 | bytes 16797696 | tf_op jit(solution)/shard_map/reduce_max | solution.py:19
  158.9 33.2 %pmax.31 = f32[4096]{0:T(1024)S(1)} all-reduce(f32[4096]{0:T(1024)S(1)} %fusion.6), channel_id=1, replica_groups=mesh['rows'=8,'cols'=4] {'rows'}, use_global_device_ids=true, to_apply=%region_13.0 | all-reduce | flops 4096 | bytes 32768 | tf_op jit(solution)/shard_map/pmax | solution.py:20
  192.0 7.7 %exponential_reduce_fusion = f32[4096]{0:T(1024)S(1)} fusion(f32[1024,4096]{1,0:T(8,128)} %get-tuple-element.9, f32[4096]{0:T(1024)S(1)} %pmax.31, f32[1024]{0:T(1024)S(1)} %get-tuple-element.2), kind=kLoop, calls=%fused_computation.4 | loop fusion | flops 16773120 | bytes 16814080 | tf_op jit(solution)/shard_map/reduce_sum | solution.py:21
  199.8 33.0 %psum.66 = f32[4096]{0:T(1024)S(1)} all-reduce(f32[4096]{0:T(1024)S(1)} %exponential_reduce_fusion), channel_id=1, replica_groups=mesh['rows'=8,'cols'=4] {'rows'}, use_global_device_ids=true, to_apply=%region_15.0 | all-reduce | flops 4096 | bytes 32768 | tf_op jit(solution)/shard_map/psum | solution.py:21
  232.8 8.2 %fusion = f32[1024]{0:T(1024)S(1)} fusion(f32[1024,4096]{1,0:T(8,128)} %get-tuple-element.9, f32[4096]{0:T(1024)S(1)} %copy-done.4, f32[4096]{0:T(1024)S(1)} %log_add_fusion, f32[1024]{0:T(1024)S(1)} %get-tuple-element.2), kind=kLoop, calls=%fused_computation.12 | loop fusion | flops 20970496 | bytes 16818176 | tf_op jit(solution)/shard_map/reduce_sum | solution.py:26
  241.0 5.7 %psum.67 = f32[1024]{0:T(1024)S(1)} all-reduce(f32[1024]{0:T(1024)S(1)} %fusion), channel_id=1, replica_groups=mesh['rows'=8,'cols'=4] {'cols'}, use_global_device_ids=true, to_apply=%region_17.0 | all-reduce | flops 1024 | bytes 8192 | tf_op jit(solution)/shard_map/psum | solution.py:26
  246.7 8.1 %fusion.1 = f32[4096]{0:T(1024)S(1)} fusion(f32[1024,4096]{1,0:T(8,128)} %get-tuple-element.9, f32[1024]{0:T(1024)S(1)} %sub.92, f32[1024]{0:T(1024)S(1)} %get-tuple-element.3, f32[4096]{0:T(1024)S(1)} %get-tuple-element.4), kind=kLoop, calls=%fused_computation.13 | loop fusion | flops 20967424 | bytes 16818176 | tf_op jit(solution)/shard_map/reduce_sum | solution.py:45
  254.8 33.0 %psum.68 = f32[4096]{0:T(1024)S(1)} all-reduce(f32[4096]{0:T(1024)S(1)} %fusion.1), channel_id=1, replica_groups=mesh['rows'=8,'cols'=4] {'rows'}, use_global_device_ids=true, to_apply=%region_19.0 | all-reduce | flops 4096 | bytes 32768 | tf_op jit(solution)/shard_map/psum | solution.py:45
  287.8 8.1 %fusion.2 = f32[1024]{0:T(1024)S(1)} fusion(f32[1024,4096]{1,0:T(8,128)} %get-tuple-element.9, f32[4096]{0:T(1024)S(1)} %neg.9, f32[4096]{0:T(1024)S(1)} %get-tuple-element.5, f32[1024]{0:T(1024)S(1)} %get-tuple-element.6), kind=kLoop, calls=%fused_computation.14 | loop fusion | flops 20970496 | bytes 16818176 | tf_op jit(solution)/shard_map/reduce_sum | solution.py:26
  295.9 5.7 %psum.69 = f32[1024]{0:T(1024)S(1)} all-reduce(f32[1024]{0:T(1024)S(1)} %fusion.2), channel_id=1, replica_groups=mesh['rows'=8,'cols'=4] {'cols'}, use_global_device_ids=true, to_apply=%region_21.0 | all-reduce | flops 1024 | bytes 8192 | tf_op jit(solution)/shard_map/psum | solution.py:26
  301.6 20.0 %negate_convert_fusion = bf16[1024,4096]{1,0:T(8,128)(2,1)S(1)} fusion(f32[1024,4096]{1,0:T(8,128)} %get-tuple-element.9, f32[1024]{0:T(1024)S(1)} %neg.10, f32[1024]{0:T(1024)S(1)} %get-tuple-element.7, f32[4096]{0:T(1024)S(1)} %neg.9, f32[4096]{0:T(1024)S(1)} %get-tuple-element.5, f32[1024]{0:T(1024)S(1)} %sub.92, f32[1024]{0:T(1024)S(1)} %get-tuple-element.3, ...), kind=kLoop, calls=%fused_computation | loop fusion | flops 88080384 | bytes 25288704 | tf_op jit(solution)/shard_map/convert_element_type | solution.py:55
  321.6 3.2 copy-done.1
  324.8 3.1 fusion.7
  328.0 0.3 all-reduce.5.cloned.1.call-start
  328.2 7.2 %fusion.8 = f32[4096,128]{1,0:T(8,128)} fusion(bf16[1024,4096]{1,0:T(8,128)(2,1)} %copy-done.1, bf16[1024,128]{1,0:T(8,128)(2,1)S(1)} %copy-done.2), kind=kOutput, calls=%fused_computation.27 | convolution fusion | flops 1073741824 | bytes 10747904 | tf_op jit(solution)/shard_map/dot_general | solution.py:58
  335.5 23.0 %all-reduce.3.cloned.1.call-done = f32[1024,128]{1,0:T(8,128)} async-done(((f32[1024,128]{1,0:T(8,128)}), f32[1024,128]{1,0:T(8,128)}) %all-reduce.3.cloned.1.call-update) | async-done | bytes 524304 | tf_op jit(solution)/shard_map/psum | solution.py:57
  358.4 106.1 %all-reduce.5.cloned.1.call-done = f32[4096,128]{1,0:T(8,128)} async-done(((f32[4096,128]{1,0:T(8,128)}), f32[4096,128]{1,0:T(8,128)}) %all-reduce.5.cloned.1.call-update) | async-done | bytes 2097168 | tf_op jit(solution)/shard_map/psum | solution.py:61
  464.5 1.9 copy.9
  466.4 3.0 copy.10
  (20 shorter events, 0.2 us)
Async XLA Ops:
  7.2 1.2 copy-start
  7.2 17.5 %copy-start.3 = (f32[4096]{0:T(1024)S(1)}, f32[4096]{0:T(1024)}, u32[]{:S(2)}) copy-start(f32[4096]{0:T(1024)} %param.7) | copy-start | bytes 49156
  7.2 351.2 %all-reduce.3.cloned.1.call-start = ((), (), s32[]{:S(2)}) async-start(), calls=%async_computation | async-start | bytes 1048576 | tf_op jit(solution)/shard_map/psum | solution.py:57
  151.1 81.7 %copy-start.4 = (f32[4096]{0:T(1024)S(1)}, f32[4096]{0:T(1024)}, u32[]{:S(2)}) copy-start(f32[4096]{0:T(1024)} %param.9) | copy-start | bytes 49156
  192.0 54.6 %copy-start.5 = (f32[1024]{0:T(1024)S(1)}, f32[1024]{0:T(1024)}, u32[]{:S(2)}) copy-start(f32[1024]{0:T(1024)} %param.8) | copy-start | bytes 12292
  301.6 26.7 %copy-start.2 = (bf16[1024,128]{1,0:T(8,128)(2,1)S(1)}, bf16[1024,128]{1,0:T(8,128)(2,1)}, u32[]{:S(2)}) copy-start(bf16[1024,128]{1,0:T(8,128)(2,1)} %param.5) | copy-start | bytes 786436
  321.6 3.2 copy-start.1
  328.0 136.5 %all-reduce.5.cloned.1.call-start = ((), (), s32[]{:S(2)}) async-start(), calls=%async_computation.1 | async-start | bytes 4194304 | tf_op jit(solution)/shard_map/psum | solution.py:61
Sparse Core Ops, SparseCore 0:
  328.1 30.2 all-reduce.2
  362.6 101.8 all-reduce.4
where the time goes:
time: 477 us; the launch traced here: 476 us
  blocking collectives  207 us (43%)
  waiting for transfers between devices  129 us (27%)
  other arithmetic  98.6 us (21%)
  matrix products  18.3 us (4%)
  between operations  14.1 us (3%)
  local copies, waits for them, and re-layouts  9.31 us (2%)
    psum x1, waiting for transfers between devices, per_device(): bench_grad = lax.psum(bench_part, 'rows')  106 us
    pmax x2, blocking collectives, col_lse(): highest = lax.pmax(highest, 'rows')  70.7 us
    psum x2, blocking collectives, col_lse(): summed = lax.psum(jnp.sum(jnp.exp(logits - highest[None, :]), 0), 'rows')  66 us
    psum x1, blocking collectives, per_device(): col_back1 = -lax.psum(jnp.sum(row_soft2 * row_back2[:, None], 0), 'rows')  33 us
    psum x1, waiting for transfers between devices, per_device(): crawl_grad = lax.psum(crawl_part, 'cols')  23 us
    convert_element_type x1, other arithmetic, per_device(): score_grad = score_grad.astype(jnp.bfloat16)  20 us
    reduce_sum x2, other arithmetic, row_reduce(): return lax.psum(jnp.sum(values, 1), 'cols')  16.3 us
    reduce_sum x2, other arithmetic, row_lse(): summed = lax.psum(jnp.sum(jnp.exp(logits - highest[:, None]), 1), 'cols')  15.7 us
  transfers between devices with their start and end apart: 2, of which 2 were waited for; matrix products, arithmetic and copies ran while one was open for 2% of the time, Pallas kernels for 0%

commit v1 on v0

v1 whole, which is shorter than its diff:
```python
import functools
import math

import jax
import jax.numpy as jnp
from jax import lax
from jax.experimental import pallas as pl
from jax.experimental.pallas import tpu as pltpu
from jax.sharding import PartitionSpec as P

EPSILON = 0.05
KAPPA = math.log2(math.e) / EPSILON
LOWEST = -90.0
LANES = 128
WIDE = 512
TALL = 256
F32 = jnp.float32


def transposed_dot(a, b):
    return lax.dot_general(a, b, (((1,), (1,)), ((), ())), preferred_element_type=F32)


def column_form(row):
    return jnp.transpose(jnp.broadcast_to(row, (LANES, row.shape[1])))


def row_form(partial):
    return jnp.sum(jnp.transpose(partial), axis=0, keepdims=True)


def log_sum(parts):
    top = functools.reduce(jnp.maximum, parts)
    return top + jnp.log2(sum(jnp.exp2(p - top) for p in parts))


def row_sums(tile_ref, weights_ref, partial_ref):
    height = 64

    def body(block, _):
        rows = pl.ds(pl.multiple_of(block * height, height), height)
        acc = jnp.zeros((height, LANES), F32)
        for at in range(0, tile_ref.shape[1], LANES):
            acc += tile_ref[rows, at:at + LANES] * weights_ref[:, at:at + LANES]
        partial_ref[rows, :] = acc
        return _

    lax.fori_loop(0, tile_ref.shape[0] // height, body, 0)
    return row_form(partial_ref[...])


def column_sums(tile_ref, weights_ref, out_ref):
    starts = range(0, tile_ref.shape[1], LANES)

    def body(block, accs):
        for half in range(2):
            rows = pl.ds(pl.multiple_of(block * 16 + half * 8, 8), 8)
            weights = weights_ref[rows, :]
            accs = tuple(acc + tile_ref[rows, at:at + LANES] * weights for acc, at in zip(accs, starts))
        return accs

    accs = lax.fori_loop(0, tile_ref.shape[0] // 16, body, tuple(jnp.zeros((8, LANES), F32) for _ in starts))
    for acc, at in zip(accs, starts):
        out_ref[:, at:at + LANES] = jnp.sum(acc, axis=0, keepdims=True)


def exponent_block(crawl_ref, bench_ref, shift_ref, rows, columns):
    scores = transposed_dot(crawl_ref[rows, :], bench_ref[columns, :])
    return scores * KAPPA + shift_ref[:, columns]


def row_level_kernel(crawl_ref, bench_ref, shift_ref, tile_ref, top_ref, level_ref, top_scratch, sum_scratch):
    height = 64

    def fill(block, _):
        rows = pl.ds(pl.multiple_of(block * TALL, TALL), TALL)
        top = jnp.full((TALL, LANES), -jnp.inf, F32)
        for at in range(0, tile_ref.shape[1], WIDE):
            exponent = exponent_block(crawl_ref, bench_ref, shift_ref, rows, pl.ds(at, WIDE))
            tile_ref[rows, at:at + WIDE] = exponent
            for lane in range(0, WIDE, LANES):
                top = jnp.maximum(top, exponent[:, lane:lane + LANES])
        top_scratch[rows, :] = top
        return _

    lax.fori_loop(0, tile_ref.shape[0] // TALL, fill, 0)

    def power(block, _):
        rows = pl.ds(pl.multiple_of(block * height, height), height)
        top = jnp.broadcast_to(jnp.max(top_scratch[rows, :], axis=1, keepdims=True), (height, LANES))
        acc = jnp.zeros((height, LANES), F32)
        for at in range(0, tile_ref.shape[1], LANES):
            value = jnp.exp2(tile_ref[rows, at:at + LANES] - top)
            tile_ref[rows, at:at + LANES] = value
            acc += value
        top_scratch[rows, :] = top
        sum_scratch[rows, :] = acc
        return _

    lax.fori_loop(0, tile_ref.shape[0] // height, power, 0)
    top = jnp.transpose(top_scratch[...])[0:1, :]
    top_ref[...] = top
    level_ref[...] = top + jnp.log2(row_form(sum_scratch[...]))


def column_level_kernel(parts, tile_ref, top_ref, *refs):
    part_refs, (crawl_ref, bench_ref, shift_ref, level_ref, out_ref, weights) = refs[:parts], refs[parts:]
    level = log_sum([p[...] for p in part_refs])
    level_ref[...] = level
    weights[...] = column_form(jnp.exp2(top_ref[...] - level))
    column_sums(tile_ref, weights, out_ref)
    out_ref[...] = jnp.log2(out_ref[...])

    @pl.when(jnp.min(out_ref[...]) < LOWEST)
    def _():
        weights[...] = column_form(level)
        blocks = tile_ref.shape[0] // TALL

        def column_block(column, _):
            columns = pl.ds(pl.multiple_of(column * WIDE, WIDE), WIDE)

            def logs(block):
                rows = pl.ds(pl.multiple_of(block * TALL, TALL), TALL)
                return exponent_block(crawl_ref, bench_ref, shift_ref, rows, columns) - weights[rows, 0:1]

            top = lax.fori_loop(
                0, blocks, lambda b, t: jnp.maximum(t, jnp.max(logs(b), axis=0, keepdims=True)),
                jnp.full((1, WIDE), -jnp.inf, F32))
            total = lax.fori_loop(
                0, blocks, lambda b, t: t + jnp.sum(jnp.exp2(logs(b) - top), axis=0, keepdims=True),
                jnp.zeros((1, WIDE), F32))
            out_ref[:, columns] = top + jnp.log2(total)
            return _

        lax.fori_loop(0, tile_ref.shape[1] // WIDE, column_block, 0)


def soft_kernel(parts, tile_ref, top_ref, level_ref, *refs):
    part_refs = refs[:parts]
    crawl_ref, bench_ref, shift_ref, soft_ref, mass_ref, sums_ref, partial, weights, scale = refs[parts:]
    logs = log_sum([p[...] for p in part_refs])
    mass_ref[...] = jnp.exp2(logs)
    lowest = jnp.min(logs)
    height = 64

    @pl.when(lowest >= LOWEST)
    def _():
        weights[...] = column_form(jnp.exp2(top_ref[...] - level_ref[...]))
        scale[...] = jnp.exp2(-logs)

        def body(block, _):
            rows = pl.ds(pl.multiple_of(block * height, height), height)
            weight = weights[rows, :]
            acc = jnp.zeros((height, LANES), F32)
            for at in range(0, tile_ref.shape[1], LANES):
                value = tile_ref[rows, at:at + LANES] * weight * scale[:, at:at + LANES]
                soft_ref[rows, at:at + LANES] = value
                acc += value
            partial[rows, :] = acc
            return _

        lax.fori_loop(0, tile_ref.shape[0] // height, body, 0)

    @pl.when(lowest < LOWEST)
    def _():
        weights[...] = column_form(level_ref[...])
        scale[...] = logs
        partial[...] = jnp.zeros_like(partial)

        def body(block, _):
            rows = pl.ds(pl.multiple_of(block * TALL, TALL), TALL)
            level = weights[rows, 0:1]

            def column_block(column, _):
                columns = pl.ds(pl.multiple_of(column * WIDE, WIDE), WIDE)
                exponent = exponent_block(crawl_ref, bench_ref, shift_ref, rows, columns)
                value = jnp.exp2(exponent - level - scale[:, columns])
                soft_ref[rows, columns] = value
                partial[rows, :] += sum(value[:, lane:lane + LANES] for lane in range(0, WIDE, LANES))
                return _

            return lax.fori_loop(0, tile_ref.shape[1] // WIDE, column_block, _)

        lax.fori_loop(0, tile_ref.shape[0] // TALL, body, 0)

    sums_ref[...] = row_form(partial[...])


def second_column_kernel(parts, soft_ref, *refs):
    part_refs, (inverse_ref, out_ref, weights) = refs[:parts], refs[parts:]
    inverse = 1.0 / sum(p[...] for p in part_refs)
    inverse_ref[...] = inverse
    weights[...] = column_form(inverse)
    column_sums(soft_ref, weights, out_ref)


def second_row_kernel(parts, soft_ref, inverse_ref, cotangent_ref, *refs):
    part_refs, (scaled_ref, out_ref, partial) = refs[:parts], refs[parts:]
    scaled_ref[...] = cotangent_ref[...] / sum(p[...] for p in part_refs)
    out_ref[...] = row_sums(soft_ref, scaled_ref, partial) * inverse_ref[...]


def first_column_kernel(parts, soft_ref, inverse_ref, cotangent_ref, *refs):
    part_refs, (scaled_ref, out_ref, weights) = refs[:parts], refs[parts:]
    scaled = (cotangent_ref[...] - sum(p[...] for p in part_refs)) * inverse_ref[...]
    scaled_ref[...] = scaled
    weights[...] = column_form(-scaled)
    column_sums(soft_ref, weights, out_ref)


def first_row_kernel(parts, soft_ref, *refs):
    part_refs, (back_ref, out_ref, partial) = refs[:parts], refs[parts:]
    back_ref[...] = sum(p[...] for p in part_refs)
    out_ref[...] = -row_sums(soft_ref, back_ref, partial)


def ring_order(n):
    return [*range(0, n, 2), *range(n - 1, 0, -2)]


def ring_share(n, at):
    me = lax.axis_index("rows")
    place = lax.rem(lax.select(lax.rem(me, 2) == 0, me // 2, n - 1 - me // 2) + at, n)
    return lax.select(place < n // 2, 2 * place, 2 * (n - 1 - place) + 1)


def far_kernel(parts, n, soft_ref, inverse_ref, scaled2_ref, back_ref, mass_ref, scaled_ref, crawl_ref, *refs):
    part_refs, (first, second, third, *piece_refs, flat) = refs[:parts], refs[parts:]
    first[...] = column_form(-inverse_ref[...])
    second[...] = column_form(-scaled_ref[...])
    third[...] = column_form(-sum(p[...] for p in part_refs))
    if not piece_refs:
        return
    width = flat.shape[1]
    start = ring_share(n, n // 2) * width
    flat[...] = jnp.zeros_like(flat)

    def body(block, _):
        rows = pl.ds(pl.multiple_of(block * TALL, TALL), TALL)
        a, b, c = first[rows, :], second[rows, :], third[rows, :]
        pieces = []
        for lane in range(0, width, LANES):
            span = pl.ds(pl.multiple_of(start + lane, LANES), LANES)
            factor = a * scaled2_ref[:, span] + b + (c * mass_ref[:, span] - back_ref[:, span])
            pieces.append((soft_ref[rows, span] * factor).astype(jnp.bfloat16))
        grad = jnp.concatenate(pieces, axis=1)
        flat[...] += lax.dot_general(crawl_ref[rows, :], grad, (((0,), (0,)), ((), ())), preferred_element_type=F32)
        return _

    lax.fori_loop(0, soft_ref.shape[0] // TALL, body, 0)
    half = width // 2
    for k, piece in enumerate(piece_refs):
        piece[...] = jnp.transpose(flat[:, k * half:(k + 1) * half])


def gradient_kernel(n, places, soft_ref, first, second, third, scaled2_ref, back_ref, mass_ref, crawl_ref, bench_ref, *refs):
    keep_ref, send_ref, *piece_refs, flat, whole, total = refs
    flat[...] = jnp.zeros_like(flat)

    def body(block, _):
        rows = pl.ds(pl.multiple_of(block * TALL, TALL), TALL)
        a, b, c = first[rows, :], second[rows, :], third[rows, :]
        x = crawl_ref[rows, :]
        acc = jnp.zeros((TALL, LANES), F32)
        for at in range(0, soft_ref.shape[1], WIDE):
            pieces = []
            for lane in range(at, at + WIDE, LANES):
                span = slice(lane, lane + LANES)
                factor = a * scaled2_ref[:, span] + b + (c * mass_ref[:, span] - back_ref[:, span])
                pieces.append((soft_ref[rows, span] * factor).astype(jnp.bfloat16))
            grad = jnp.concatenate(pieces, axis=1)
            acc += jnp.dot(grad, bench_ref[at:at + WIDE, :], preferred_element_type=F32)
            flat[:, at:at + WIDE] += lax.dot_general(x, grad, (((0,), (0,)), ((), ())), preferred_element_type=F32)
        total[rows, :] = acc
        return _

    lax.fori_loop(0, soft_ref.shape[0] // TALL, body, 0)
    me = lax.axis_index("cols")
    quarter = total.shape[0] // 4
    for k, (ref, low) in enumerate(((keep_ref, 0), (send_ref, 0), (keep_ref, quarter), (send_ref, quarter))):
        start = pl.multiple_of(lax.bitwise_xor(me, k) * quarter, quarter)
        ref[low:low + quarter, :] = total[pl.ds(start, quarter), :]
    whole[...] = jnp.transpose(flat[...])
    height = piece_refs[0].shape[0]
    for k, piece in enumerate(piece_refs):
        start = ring_share(n, places[k // 2]) * 2 * height + k % 2 * height
        piece[...] = whole[pl.ds(pl.multiple_of(start, height), height), :]


def placing_kernel(n, *refs):
    (own_ref, beside_ref, pair_ref, *pieces), (crawl_out, bench_out, sems) = refs[:-3], refs[-3:]
    me = lax.axis_index("cols")
    quarter = own_ref.shape[0]
    moves = []
    for k, piece in ((0, own_ref), (2, beside_ref), (1, pair_ref.at[:quarter]), (3, pair_ref.at[quarter:])):
        start = pl.multiple_of(lax.bitwise_xor(me, k) * quarter, quarter)
        moves.append((piece, crawl_out.at[pl.ds(start, quarter)]))
    height = pieces[0].shape[0]
    for at, piece in enumerate(pieces):
        start = pl.multiple_of(ring_share(n, at // 2) * 2 * height + at % 2 * height, height)
        moves.append((piece, bench_out.at[pl.ds(start, height)]))
    copies = [pltpu.make_async_copy(source, target, sems.at[k]) for k, (source, target) in enumerate(moves)]
    for copy in copies:
        copy.start()
    for copy in copies:
        copy.wait()


def call(kernel, args, outs, scratch, aliases=None, held=()):
    ins = len(args)

    def body(*refs):
        kernel(*refs[:ins], *refs[ins + len(held):])

    return pl.pallas_call(
        body,
        in_specs=[pl.BlockSpec(memory_space=pltpu.VMEM)] * (ins + len(held)),
        out_specs=[pl.BlockSpec(memory_space=pltpu.VMEM)] * len(outs),
        out_shape=outs,
        scratch_shapes=[pltpu.VMEM(shape, F32) for shape in scratch],
        input_output_aliases=aliases or {},
        compiler_params=pltpu.CompilerParams(vmem_limit_bytes=20 * 2**20),
    )(*args, *held)


def shaped(*shape):
    return jax.ShapeDtypeStruct(shape, F32)


def resident(*shape):
    return pltpu.VMEM(shape, F32)


def kept(x):
    return pltpu.with_memory_space_constraint(x, pltpu.VMEM)


def exchange(x, axis, stride, size):
    n = lax.axis_size(axis)
    return [x] + [lax.ppermute(x, axis, [(i, i ^ (k * stride)) for i in range(n)]) for k in range(1, size)]


def spread(x, axis, first, join):
    n = lax.axis_size(axis)
    stride, size = 1, min(first, n)
    while True:
        parts = exchange(x, axis, stride, size)
        stride *= size
        if stride == n:
            return parts
        x = join(parts)
        size = min(4, n // stride)


def ring_all_reduce(pieces, n):
    order = ring_order(n)
    up = [(order[p], order[(p + 1) % n]) for p in range(n)]
    down = [(b, a) for a, b in up]
    far = n // 2
    mine = [[pieces[2 * at], pieces[2 * at + 1]] for at in range(n)]

    def ahead(x):
        return lax.ppermute(x, "rows", up)

    def behind(x):
        return lax.ppermute(x, "rows", down)

    rise, fall = [ahead(mine[far][0]), None], [None, behind(mine[far][1])]
    for step in range(far - 1, 0, -1):
        rise = [ahead(m if r is None else m + r) for m, r in zip(mine[step], rise)]
        fall = [behind(m if f is None else m + f) for m, f in zip(mine[-step], fall)]
    own = [m + r + f for m, r, f in zip(mine[0], rise, fall)]
    found = {0: own}
    rise = fall = own
    for step in range(1, far):
        rise, fall = [ahead(r) for r in rise], [behind(f) for f in fall]
        found[n - step], found[step] = rise, fall
    found[far] = [ahead(rise[0]), behind(fall[1])]
    return [half for at in range(n) for half in found[at]]


def quarter_all_reduce(keep, send):
    quarter = keep.shape[0] // 2
    keep = keep + exchange(send, "cols", 1, 2)[1]
    own = keep[:quarter] + exchange(keep[quarter:], "cols", 2, 2)[1]
    beside = exchange(own, "cols", 2, 2)[1]
    return own, beside, exchange(jnp.concatenate([own, beside]), "cols", 1, 2)[1]


def per_device(crawl, bench, start_duals, row_cotangent, col_cotangent):
    rows, columns = crawl.shape[0], bench.shape[0]
    shift = (start_duals * KAPPA).reshape(1, columns)
    row_cotangent = row_cotangent.reshape(1, rows)
    col_cotangent = col_cotangent.reshape(1, columns)
    row, column, tall = shaped(1, rows), shaped(1, columns), (rows, LANES)
    tile_shape = resident(rows, columns)

    def over_cols(x, join=sum):
        return spread(x, "cols", 4, join)

    def over_rows(x, join=sum):
        return spread(x, "rows", 2, join)

    tile, top, local = call(row_level_kernel, [crawl, bench, shift], [tile_shape, row, row], [tall, tall])
    parts = over_cols(local, log_sum)
    level, local = call(
        functools.partial(column_level_kernel, len(parts)),
        [kept(tile), top, *parts, crawl, bench, shift], [row, column], [tall])
    parts = over_rows(local, log_sum)
    soft, mass, local = call(
        functools.partial(soft_kernel, len(parts)),
        [kept(tile), top, level, *parts, crawl, bench, shift], [tile_shape, column, row],
        [tall, tall, (1, columns)], aliases={0: 0})
    parts = over_cols(local)
    inverse, local = call(functools.partial(second_column_kernel, len(parts)), [kept(soft), *parts], [row, column], [tall], held=[bench, crawl])
    parts = over_rows(local)
    scaled2, local = call(
        functools.partial(second_row_kernel, len(parts)),
        [kept(soft), inverse, col_cotangent, *parts], [column, row], [tall], held=[bench, crawl])
    parts = over_cols(local)
    scaled, local = call(
        functools.partial(first_column_kernel, len(parts)),
        [kept(soft), inverse, row_cotangent, *parts], [row, column], [tall], held=[bench, crawl])
    parts = over_rows(local)
    back, local = call(functools.partial(first_row_kernel, len(parts)), [kept(soft), *parts], [column, row], [tall], held=[bench, crawl])
    parts = over_cols(local)
    n = lax.axis_size("rows")
    width = bench.shape[1]
    share = columns // n
    piece = shaped(share // 2, width)
    ahead = share % (2 * LANES) == 0
    *factors, = call(
        functools.partial(far_kernel, len(parts), n),
        [kept(soft), inverse, scaled2, back, mass, scaled, crawl, *parts],
        [shaped(*tall)] * 3 + [piece] * (2 * ahead), [(LANES, share)], held=[bench])
    factors, far = factors[:3], factors[3:]
    places = [at for at in range(n) if at != n // 2 or not ahead]
    keep, send, *pieces = call(
        functools.partial(gradient_kernel, n, places),
        [kept(soft), *factors, scaled2, back, mass, crawl, bench],
        [shaped(rows // 2, width)] * 2 + [piece] * (2 * len(places)), [(LANES, columns), (columns, LANES), tall])
    if ahead:
        pieces[n:n] = far
    pieces = ring_all_reduce(pieces, n)
    quarters = quarter_all_reduce(keep, send)
    crawl_grad, bench_grad = pl.pallas_call(
        functools.partial(placing_kernel, n),
        in_specs=[pl.BlockSpec(memory_space=pltpu.VMEM)] * (3 + len(pieces)),
        out_specs=[pl.BlockSpec(memory_space=pl.ANY)] * 2,
        out_shape=[shaped(rows, width), shaped(columns, width)],
        scratch_shapes=[pltpu.SemaphoreType.DMA((4 + len(pieces),))],
    )(*quarters, *pieces)
    return (crawl_grad, bench_grad)


def solution(mesh):
    placed = (P("rows", None), P("cols", None), P("cols"), P("rows"), P("cols"))
    return jax.shard_map(
        per_device,
        mesh=mesh,
        in_specs=placed,
        out_specs=(P("rows", None), P("cols", None)),
        check_vma=False,
    )
```

time: 477 us -> 159 us (0.33)
  blocking collectives: 207 us -> 0 us
  other arithmetic: 98.6 us -> 1.12 us
  waiting for transfers between devices: 129 us -> 36.4 us
  starting transfers between devices: 0.3 us -> 61.7 us
  Pallas kernels: 0 us -> 55.3 us
  matrix products: 18.3 us -> 0 us
  between operations: 14.1 us -> 1 us
  local copies, waits for them, and re-layouts: 9.31 us -> 2.9 us
    psum x2 -> x0, waiting for transfers between devices: 129 us -> none  [the longest x1 106 us: per_device(): bench_grad = lax.psum(bench_part, 'rows')]
    psum x7 -> x0, blocking collectives: 122 us -> none  [the longest x2 66 us: col_lse(): summed = lax.psum(jnp.sum(jnp.exp(logits - highest[None, :]), 0), 'rows')]
    pmax x4 -> x0, blocking collectives: 84.7 us -> none  [the longest x2 70.7 us: col_lse(): highest = lax.pmax(highest, 'rows')]
    ppermute x0 -> x56, starting transfers between devices: none -> 61.7 us  [the longest x28 28.6 us: exchange(): lax.ppermute(x, axis, [(i, i ^ k * stride) for i in range(n)])]
    reduce_sum x7 -> x0, other arithmetic: 55.6 us -> none  [the longest x2 16.3 us: row_reduce(): return lax.psum(jnp.sum(values, 1), 'cols')]
    pallas_call x0 -> x10, Pallas kernels: none -> 55.3 us  [the longest x9 51.9 us: call(): pl.pallas_call(body, in_specs=[pl.BlockSpec(memory_space=pltpu.VMEM)] * (...]
    ppermute x0 -> x56, waiting for transfers between devices: none -> 36.4 us  [the longest x28 23.6 us: exchange(): lax.ppermute(x, axis, [(i, i ^ k * stride) for i in range(n)])]
    reduce_max x3 -> x0, other arithmetic: 23 us -> none  [the longest x2 15.5 us: col_lse(): highest = jnp.max(logits, 0)]
  transfers between devices with their start and end apart: 2 -> 56, of which waited for: 2 -> 35; matrix products, arithmetic and copies ran while one was open for 2% -> 0% of each run, Pallas kernels for 0% -> 4%
where the time goes in v1:
time: 159 us; the launch traced here: 158 us
  starting transfers between devices  61.7 us (39%)
  Pallas kernels  55.3 us (35%)
  waiting for transfers between devices  36.4 us (23%)
  local copies, waits for them, and re-layouts  2.9 us (2%)
    pallas_call x9, Pallas kernels, call(): pl.pallas_call(body, in_specs=[pl.BlockSpec(memory_space=pltpu.VMEM)] * (...  51.9 us
    ppermute x28, starting transfers between devices, exchange(): lax.ppermute(x, axis, [(i, i ^ k * stride) for i in range(n)])  28.6 us
    ppermute x28, waiting for transfers between devices, exchange(): lax.ppermute(x, axis, [(i, i ^ k * stride) for i in range(n)])  23.6 us
    ppermute x14, starting transfers between devices, behind(): return lax.ppermute(x, 'rows', down)  20.3 us
    ppermute x14, starting transfers between devices, ahead(): return lax.ppermute(x, 'rows', up)  12.7 us
    ppermute x14, waiting for transfers between devices, ahead(): return lax.ppermute(x, 'rows', up)  8.08 us
    ppermute x14, waiting for transfers between devices, behind(): return lax.ppermute(x, 'rows', down)  4.68 us
    pallas_call x1, Pallas kernels, per_device(): pl.pallas_call(functools.partial(placing_kernel, n), in_specs=[pl.BlockSp...  3.4 us
  transfers between devices with their start and end apart: 56, of which 35 were waited for; matrix products, arithmetic and copies ran while one was open for 0% of the time, Pallas kernels for 4%

profile of v1, /device:TPU:0, one launch (start us, length us, event | category | flops | bytes accessed | tf_op | source)
XLA Modules:
  0.0 158.5 jit_solution(3108246995233714300)
XLA Ops:
  3.5 6.7 %shard_map.68 = (f32[1024,4096]{1,0:T(8,128)S(1)}, f32[1,1024]{1,0:T(1,128)S(1)}, f32[1,1024]{1,0:T(1,128)S(1)}) custom-call(bf16[1024,128]{1,0:T(8,128)(2,1)S(1)} %copy-done.1, bf16[4096,128]{1,0:T(8,128)(2,1)S(1)} %copy-done, f32[1,4096]{1,0:T(1,128)S(1)} %bitcast.3), custom_call_target="tpu_custom_call" | custom-call | tf_op jit(solution)/shard_map/pallas_call | solution.py:315
  10.3 2.4 %collective-permute-start.2 = (f32[1,1024]{1,0:T(1,128)S(1)}, f32[1,1024]{1,0:T(1,128)S(1)}, u32[]{:S(2)}, u32[]{:S(2)}) collective-permute-start(f32[1,1024]{1,0:T(1,128)S(1)} %get-tuple-element.41.refs_2_), channel_id=1, source_target_pairs={{0,3},{1,2},{2,1},{3,0},{4,7},{5,6},{6,5},{7,4},{8,11},{9,10},{10,... | collective-permute-start | bytes 12296 | tf_op jit(solution)/shard_map/ppermute | solution.py:340
  14.0 2.3 %collective-permute-done.1.refs_4_ = f32[1,1024]{1,0:T(1,128)S(1)} collective-permute-done((f32[1,1024]{1,0:T(1,128)S(1)}, f32[1,1024]{1,0:T(1,128)S(1)}, u32[]{:S(2)}, u32[]{:S(2)}) %collective-permute-start.1) | collective-permute-done | bytes 4128 | tf_op jit(solution)/shard_map/ppermute | solution.py:340
  16.3 19.2 %shard_map.69 = (f32[1,1024]{1,0:T(1,128)S(1)}, f32[1,4096]{1,0:T(1,128)S(1)}) custom-call(f32[1024,4096]{1,0:T(8,128)S(1)} %get-tuple-element.39.refs_0_, f32[1,1024]{1,0:T(1,128)S(1)} %get-tuple-element.40.refs_1_, f32[1,1024]{1,0:T(1,128)S(1)} %get-tuple-element.41.refs_2_, f32[1,1024]{1,0:T(1,128)S(1)} %collective-permute-done.refs_3_, ...), custom_call_target="tpu_custom_call" | custom-call | tf_op jit(solution)/shard_map/pallas_call | solution.py:315
  35.5 1.6 collective-permute-start.3
  37.1 2.2 %collective-permute-done.3 = f32[1,4096]{1,0:T(1,128)S(1)} collective-permute-done((f32[1,4096]{1,0:T(1,128)S(1)}, f32[1,4096]{1,0:T(1,128)S(1)}, u32[]{:S(2)}, u32[]{:S(2)}) %collective-permute-start.3) | collective-permute-done | bytes 16416 | tf_op jit(solution)/shard_map/ppermute | solution.py:340
  39.4 3.7 %collective-permute-start.6 = (f32[1,4096]{1,0:T(1,128)S(1)}, f32[1,4096]{1,0:T(1,128)S(1)}, u32[]{:S(2)}, u32[]{:S(2)}) collective-permute-start(f32[1,4096]{1,0:T(1,128)S(1)} %multiply_add_fusion.refs_3_), channel_id=1, source_target_pairs={{0,24},{4,28},{8,16},{12,20},{16,8},{20,12},{24,0},{28,4},{1,25},{... | collective-permute-start | bytes 49160 | tf_op jit(solution)/shard_map/ppermute | solution.py:340
  45.0 2.7 %collective-permute-done.5.refs_5_ = f32[1,4096]{1,0:T(1,128)S(1)} collective-permute-done((f32[1,4096]{1,0:T(1,128)S(1)}, f32[1,4096]{1,0:T(1,128)S(1)}, u32[]{:S(2)}, u32[]{:S(2)}) %collective-permute-start.5) | collective-permute-done | bytes 16416 | tf_op jit(solution)/shard_map/ppermute | solution.py:340
  47.7 9.5 %shard_map.70 = (f32[1024,4096]{1,0:T(8,128)S(1)}, f32[1,4096]{1,0:T(1,128)S(1)}, f32[1,1024]{1,0:T(1,128)S(1)}) custom-call(f32[1024,4096]{1,0:T(8,128)S(1)} %get-tuple-element.39.refs_0_, f32[1,1024]{1,0:T(1,128)S(1)} %get-tuple-element.40.refs_1_, f32[1,1024]{1,0:T(1,128)S(1)} %get-tuple-element.42.refs_2_, ...), custom_call_target="tpu_custom_call", output_to_operand_aliasing={{0}: (0, {})} | custom-call | tf_op jit(solution)/shard_map/pallas_call | solution.py:315
  61.0 2.0 %shard_map.71 = (f32[1,1024]{1,0:T(1,128)S(1)}, f32[1,4096]{1,0:T(1,128)S(1)}) custom-call(f32[1024,4096]{1,0:T(8,128)S(1)} %get-tuple-element.44.refs_0_, f32[1,1024]{1,0:T(1,128)S(1)} %get-tuple-element.45.refs_1_, f32[1,1024]{1,0:T(1,128)S(1)} %collective-permute-done.7.refs_2_, f32[1,1024]{1,0:T(1,128)S(1)} %collective-permute-done.8.refs_3_, ...), custom_call_target="tpu_custom_call" | custom-call | tf_op jit(solution)/shard_map/pallas_call | solution.py:315
  63.0 1.6 collective-permute-start.10
  64.5 2.2 %collective-permute-done.10 = f32[1,4096]{1,0:T(1,128)S(1)} collective-permute-done((f32[1,4096]{1,0:T(1,128)S(1)}, f32[1,4096]{1,0:T(1,128)S(1)}, u32[]{:S(2)}, u32[]{:S(2)}) %collective-permute-start.10) | collective-permute-done | bytes 16416 | tf_op jit(solution)/shard_map/ppermute | solution.py:340
  68.9 2.3 %collective-permute-start.11 = (f32[1,4096]{1,0:T(1,128)S(1)}, f32[1,4096]{1,0:T(1,128)S(1)}, u32[]{:S(2)}, u32[]{:S(2)}) collective-permute-start(f32[1,4096]{1,0:T(1,128)S(1)} %add.62.refs_3_), channel_id=1, source_target_pairs={{0,8},{4,12},{8,0},{12,4},{16,24},{20,28},{24,16},{28,20},{1,9},{5... | collective-permute-start | bytes 49160 | tf_op jit(solution)/shard_map/ppermute | solution.py:340
  73.1 1.9 %shard_map.72 = (f32[1,4096]{1,0:T(1,128)S(1)}, f32[1,1024]{1,0:T(1,128)S(1)}) custom-call(f32[1024,4096]{1,0:T(8,128)S(1)} %get-tuple-element.44.refs_0_, f32[1,1024]{1,0:T(1,128)S(1)} %get-tuple-element.46.refs_1_, f32[1,4096]{1,0:T(1,128)S(1)} %bitcast.6, f32[1,4096]{1,0:T(1,128)S(1)} %add.62.refs_3_, f32[1,4096]{1,0:T(1,128)S(1)} %collective-permute-done.11.refs_4_, ...), custom_call_target="tpu_custom_call" | custom-call | tf_op jit(solution)/shard_map/pallas_call | solution.py:315
  78.8 2.0 %shard_map.73 = (f32[1,1024]{1,0:T(1,128)S(1)}, f32[1,4096]{1,0:T(1,128)S(1)}) custom-call(f32[1024,4096]{1,0:T(8,128)S(1)} %get-tuple-element.44.refs_0_, f32[1,1024]{1,0:T(1,128)S(1)} %get-tuple-element.46.refs_1_, f32[1,1024]{1,0:T(1,128)S(1)} %bitcast.7, f32[1,1024]{1,0:T(1,128)S(1)} %get-tuple-element.49.refs_3_, ...), custom_call_target="tpu_custom_call" | custom-call | tf_op jit(solution)/shard_map/pallas_call | solution.py:315
  80.8 1.6 collective-permute-start.17
  82.4 2.2 %collective-permute-done.17 = f32[1,4096]{1,0:T(1,128)S(1)} collective-permute-done((f32[1,4096]{1,0:T(1,128)S(1)}, f32[1,4096]{1,0:T(1,128)S(1)}, u32[]{:S(2)}, u32[]{:S(2)}) %collective-permute-start.17) | collective-permute-done | bytes 16416 | tf_op jit(solution)/shard_map/ppermute | solution.py:340
  84.7 2.5 %collective-permute-start.20 = (f32[1,4096]{1,0:T(1,128)S(1)}, f32[1,4096]{1,0:T(1,128)S(1)}, u32[]{:S(2)}, u32[]{:S(2)}) collective-permute-start(f32[1,4096]{1,0:T(1,128)S(1)} %add.63.refs_1_), channel_id=1, source_target_pairs={{0,24},{4,28},{8,16},{12,20},{16,8},{20,12},{24,0},{28,4},{1,25},{... | collective-permute-start | bytes 49160 | tf_op jit(solution)/shard_map/ppermute | solution.py:340
  91.9 1.9 %shard_map.74 = (f32[1,4096]{1,0:T(1,128)S(1)}, f32[1,1024]{1,0:T(1,128)S(1)}) custom-call(f32[1024,4096]{1,0:T(8,128)S(1)} %get-tuple-element.44.refs_0_, f32[1,4096]{1,0:T(1,128)S(1)} %add.63.refs_1_, f32[1,4096]{1,0:T(1,128)S(1)} %collective-permute-done.18.refs_2_, f32[1,4096]{1,0:T(1,128)S(1)} %collective-permute-done.19.refs_3_, ...), custom_call_target="tpu_custom_call" | custom-call | tf_op jit(solution)/shard_map/pallas_call | solution.py:315
  97.6 1.7 %shard_map.75 = (f32[1024,128]{1,0:T(8,128)S(1)}, f32[1024,128]{1,0:T(8,128)S(1)}, f32[1024,128]{1,0:T(8,128)S(1)}, f32[256,128]{1,0:T(8,128)S(1)}, f32[256,128]{1,0:T(8,128)S(1)}) custom-call(f32[1024,4096]{1,0:T(8,128)S(1)} %get-tuple-element.44.refs_0_, f32[1,1024]{1,0:T(1,128)S(1)} %get-tuple-element.46.refs_1_, ...), custom_call_target="tpu_custom_call" | custom-call | tf_op jit(solution)/shard_map/pallas_call | solution.py:315
  101.5 6.9 %shard_map.76 = (f32[512,128]{1,0:T(8,128)S(1)}, f32[512,128]{1,0:T(8,128)S(1)}, f32[256,128]{1,0:T(8,128)S(1)}, f32[256,128]{1,0:T(8,128)S(1)}, f32[256,128]{1,...) custom-call(f32[1024,4096]{1,0:T(8,128)S(1)} %get-tuple-element.44.r, ...), custom_call_target="tpu_custom_call" | custom-call | tf_op jit(solution)/shard_map/pallas_call | solution.py:315
  108.4 1.6 collective-permute-start.32
  113.4 1.6 collective-permute-start.33
  123.6 1.6 %collective-permute-start.37 = (f32[256,128]{1,0:T(8,128)S(1)}, f32[256,128]{1,0:T(8,128)S(1)}, u32[]{:S(2)}, u32[]{:S(2)}) collective-permute-start(f32[256,128]{1,0:T(8,128)S(1)} %add.74), channel_id=1, source_target_pairs={{0,8},{8,16},{16,24},{24,28},{28,20},{20,12},{12,4},{4,0},{1,9},{9... | collective-permute-start | bytes 393224 | tf_op jit(solution)/shard_map/ppermute | solution.py:363
  125.9 1.9 %collective-permute-done.31 = f32[256,128]{1,0:T(8,128)S(1)} collective-permute-done((f32[256,128]{1,0:T(8,128)S(1)}, f32[256,128]{1,0:T(8,128)S(1)}, u32[]{:S(2)}, u32[]{:S(2)}) %collective-permute-start.31) | collective-permute-done | bytes 131104 | tf_op jit(solution)/shard_map/ppermute | solution.py:363
  130.6 1.6 collective-permute-start.43
  136.7 1.7 %collective-permute-start.45 = (f32[256,128]{1,0:T(8,128)S(1)}, f32[256,128]{1,0:T(8,128)S(1)}, u32[]{:S(2)}, u32[]{:S(2)}) collective-permute-start(f32[256,128]{1,0:T(8,128)S(1)} %collective-permute-done.43.refs_6_), channel_id=1, source_target_pairs={{8,0},{16,8},{24,16},{28,24},{20,28},{12,20},{4,12},{0,4},{9,1},{1... | collective-permute-start | bytes 393224 | tf_op jit(solution)/shard_map/ppermute | solution.py:366
  142.0 2.5 %collective-permute-start.47 = (f32[256,128]{1,0:T(8,128)S(1)}, f32[256,128]{1,0:T(8,128)S(1)}, u32[]{:S(2)}, u32[]{:S(2)}) collective-permute-start(f32[256,128]{1,0:T(8,128)S(1)} %collective-permute-done.45.refs_8_), channel_id=1, source_target_pairs={{8,0},{16,8},{24,16},{28,24},{20,28},{12,20},{4,12},{0,4},{9,1},{1... | collective-permute-start | bytes 393224 | tf_op jit(solution)/shard_map/ppermute | solution.py:366
  144.9 2.4 %collective-permute-start.46 = (f32[256,128]{1,0:T(8,128)S(1)}, f32[256,128]{1,0:T(8,128)S(1)}, u32[]{:S(2)}, u32[]{:S(2)}) collective-permute-start(f32[256,128]{1,0:T(8,128)S(1)} %collective-permute-done.44.refs_7_), channel_id=1, source_target_pairs={{8,0},{16,8},{24,16},{28,24},{20,28},{12,20},{4,12},{0,4},{9,1},{1... | collective-permute-start | bytes 393224 | tf_op jit(solution)/shard_map/ppermute | solution.py:366
  147.7 1.6 %collective-permute-start.51 = (f32[256,128]{1,0:T(8,128)S(1)}, f32[256,128]{1,0:T(8,128)S(1)}, u32[]{:S(2)}, u32[]{:S(2)}) collective-permute-start(f32[256,128]{1,0:T(8,128)S(1)} %collective-permute-done.50.refs_13_), channel_id=1, source_target_pairs={{0,8},{8,16},{16,24},{24,28},{28,20},{20,12},{12,4},{4,0},{1,9},{9... | collective-permute-start | bytes 393224 | tf_op jit(solution)/shard_map/ppermute | solution.py:363
  150.7 1.7 %collective-permute-done.55.refs_14_ = f32[256,128]{1,0:T(8,128)S(1)} collective-permute-done((f32[256,128]{1,0:T(8,128)S(1)}, f32[256,128]{1,0:T(8,128)S(1)}, u32[]{:S(2)}, u32[]{:S(2)}) %collective-permute-start.55) | collective-permute-done | bytes 131104 | tf_op jit(solution)/shard_map/ppermute | solution.py:363
  155.1 3.4 %shard_map.77 = (f32[1024,128]{1,0:T(8,128)}, f32[4096,128]{1,0:T(8,128)}) custom-call(f32[256,128]{1,0:T(8,128)} %copy-done.4, f32[256,128]{1,0:T(8,128)} %copy-done.7, f32[512,128]{1,0:T(8,128)} %copy-done.8, f32[256,128]{1,0:T(8,128)} %copy-done.5, f32[256,128]{1,0:T(8,128)} %copy-done.6, f32[256,128]{1,0:T(8,128)} %copy-done.11, f32[256,128]{1,0:T(8,128)} %copy-done.10, ...), custom_call_target="tpu_custom_call" | custom-call | tf_op jit(solution)/shard_map/pallas_call | solution.py:446
  (156 shorter events, 56.8 us)
Async XLA Ops:
  39.4 5.6 %collective-permute-start.6 = (f32[1,4096]{1,0:T(1,128)S(1)}, f32[1,4096]{1,0:T(1,128)S(1)}, u32[]{:S(2)}, u32[]{:S(2)}) collective-permute-start(f32[1,4096]{1,0:T(1,128)S(1)} %multiply_add_fusion.refs_3_), channel_id=1, source_target_pairs={{0,24},{4,28},{8,16},{12,20},{16,8},{20,12},{24,0},{28,4},{1,25},{... | collective-permute-start | bytes 49160 | tf_op jit(solution)/shard_map/ppermute | solution.py:340
  66.8 5.6 %collective-permute-start.13 = (f32[1,4096]{1,0:T(1,128)S(1)}, f32[1,4096]{1,0:T(1,128)S(1)}, u32[]{:S(2)}, u32[]{:S(2)}) collective-permute-start(f32[1,4096]{1,0:T(1,128)S(1)} %add.62.refs_3_), channel_id=1, source_target_pairs={{0,24},{4,28},{8,16},{12,20},{16,8},{20,12},{24,0},{28,4},{1,25},{... | collective-permute-start | bytes 49160 | tf_op jit(solution)/shard_map/ppermute | solution.py:340
  84.7 5.6 %collective-permute-start.20 = (f32[1,4096]{1,0:T(1,128)S(1)}, f32[1,4096]{1,0:T(1,128)S(1)}, u32[]{:S(2)}, u32[]{:S(2)}) collective-permute-start(f32[1,4096]{1,0:T(1,128)S(1)} %add.63.refs_1_), channel_id=1, source_target_pairs={{0,24},{4,28},{8,16},{12,20},{16,8},{20,12},{24,0},{28,4},{1,25},{... | collective-permute-start | bytes 49160 | tf_op jit(solution)/shard_map/ppermute | solution.py:340
  99.4 10.6 %collective-permute-start.28 = (f32[256,128]{1,0:T(8,128)S(1)}, f32[256,128]{1,0:T(8,128)S(1)}, u32[]{:S(2)}, u32[]{:S(2)}) collective-permute-start(f32[256,128]{1,0:T(8,128)S(1)} %get-tuple-element.64), channel_id=1, source_target_pairs={{0,8},{8,16},{16,24},{24,28},{28,20},{20,12},{12,4},{4,0},{1,9},{9... | collective-permute-start | bytes 393224 | tf_op jit(solution)/shard_map/ppermute | solution.py:363
  100.3 11.1 %collective-permute-start.38 = (f32[256,128]{1,0:T(8,128)S(1)}, f32[256,128]{1,0:T(8,128)S(1)}, u32[]{:S(2)}, u32[]{:S(2)}) collective-permute-start(f32[256,128]{1,0:T(8,128)S(1)} %get-tuple-element.75), channel_id=1, source_target_pairs={{8,0},{16,8},{24,16},{28,24},{20,28},{12,20},{4,12},{0,4},{9,1},{1... | collective-permute-start | bytes 393224 | tf_op jit(solution)/shard_map/ppermute | solution.py:366
  110.0 5.5 %collective-permute-start.29 = (f32[256,128]{1,0:T(8,128)S(1)}, f32[256,128]{1,0:T(8,128)S(1)}, u32[]{:S(2)}, u32[]{:S(2)}) collective-permute-start(f32[256,128]{1,0:T(8,128)S(1)} %add.66), channel_id=1, source_target_pairs={{0,8},{8,16},{16,24},{24,28},{28,20},{20,12},{12,4},{4,0},{1,9},{9... | collective-permute-start | bytes 393224 | tf_op jit(solution)/shard_map/ppermute | solution.py:363
  110.5 6.4 %collective-permute-start.35 = (f32[256,128]{1,0:T(8,128)S(1)}, f32[256,128]{1,0:T(8,128)S(1)}, u32[]{:S(2)}, u32[]{:S(2)}) collective-permute-start(f32[256,128]{1,0:T(8,128)S(1)} %get-tuple-element.71), channel_id=1, source_target_pairs={{0,8},{8,16},{16,24},{24,28},{28,20},{20,12},{12,4},{4,0},{1,9},{9... | collective-permute-start | bytes 393224 | tf_op jit(solution)/shard_map/ppermute | solution.py:363
  111.4 11.4 %collective-permute-start.24 = (f32[512,128]{1,0:T(8,128)S(1)}, f32[512,128]{1,0:T(8,128)S(1)}, u32[]{:S(2)}, u32[]{:S(2)}) collective-permute-start(f32[512,128]{1,0:T(8,128)S(1)} %get-tuple-element.59), channel_id=1, source_target_pairs={{0,1},{1,0},{2,3},{3,2},{4,5},{5,4},{6,7},{7,6},{8,9},{9,8},{10,11... | collective-permute-start | bytes 786440 | tf_op jit(solution)/shard_map/ppermute | solution.py:340
  111.5 6.3 %collective-permute-start.39 = (f32[256,128]{1,0:T(8,128)S(1)}, f32[256,128]{1,0:T(8,128)S(1)}, u32[]{:S(2)}, u32[]{:S(2)}) collective-permute-start(f32[256,128]{1,0:T(8,128)S(1)} %add.76), channel_id=1, source_target_pairs={{8,0},{16,8},{24,16},{28,24},{20,28},{12,20},{4,12},{0,4},{9,1},{1... | collective-permute-start | bytes 393224 | tf_op jit(solution)/shard_map/ppermute | solution.py:366
  113.4 7.2 %collective-permute-start.33 = (f32[256,128]{1,0:T(8,128)S(1)}, f32[256,128]{1,0:T(8,128)S(1)}, u32[]{:S(2)}, u32[]{:S(2)}) collective-permute-start(f32[256,128]{1,0:T(8,128)S(1)} %add.70), channel_id=1, source_target_pairs={{8,0},{16,8},{24,16},{28,24},{20,28},{12,20},{4,12},{0,4},{9,1},{1... | collective-permute-start | bytes 393224 | tf_op jit(solution)/shard_map/ppermute | solution.py:366
  115.6 6.3 %collective-permute-start.30 = (f32[256,128]{1,0:T(8,128)S(1)}, f32[256,128]{1,0:T(8,128)S(1)}, u32[]{:S(2)}, u32[]{:S(2)}) collective-permute-start(f32[256,128]{1,0:T(8,128)S(1)} %add.67), channel_id=1, source_target_pairs={{0,8},{8,16},{16,24},{24,28},{28,20},{20,12},{12,4},{4,0},{1,9},{9... | collective-permute-start | bytes 393224 | tf_op jit(solution)/shard_map/ppermute | solution.py:363
  117.0 6.6 %collective-permute-start.36 = (f32[256,128]{1,0:T(8,128)S(1)}, f32[256,128]{1,0:T(8,128)S(1)}, u32[]{:S(2)}, u32[]{:S(2)}) collective-permute-start(f32[256,128]{1,0:T(8,128)S(1)} %add.73), channel_id=1, source_target_pairs={{0,8},{8,16},{16,24},{24,28},{28,20},{20,12},{12,4},{4,0},{1,9},{9... | collective-permute-start | bytes 393224 | tf_op jit(solution)/shard_map/ppermute | solution.py:363
  117.8 7.3 %collective-permute-start.40 = (f32[256,128]{1,0:T(8,128)S(1)}, f32[256,128]{1,0:T(8,128)S(1)}, u32[]{:S(2)}, u32[]{:S(2)}) collective-permute-start(f32[256,128]{1,0:T(8,128)S(1)} %add.77), channel_id=1, source_target_pairs={{8,0},{16,8},{24,16},{28,24},{20,28},{12,20},{4,12},{0,4},{9,1},{1... | collective-permute-start | bytes 393224 | tf_op jit(solution)/shard_map/ppermute | solution.py:366
  120.6 5.2 %collective-permute-start.34 = (f32[256,128]{1,0:T(8,128)S(1)}, f32[256,128]{1,0:T(8,128)S(1)}, u32[]{:S(2)}, u32[]{:S(2)}) collective-permute-start(f32[256,128]{1,0:T(8,128)S(1)} %add.71), channel_id=1, source_target_pairs={{8,0},{16,8},{24,16},{28,24},{20,28},{12,20},{4,12},{0,4},{9,1},{1... | collective-permute-start | bytes 393224 | tf_op jit(solution)/shard_map/ppermute | solution.py:366
  121.8 5.9 %collective-permute-start.31 = (f32[256,128]{1,0:T(8,128)S(1)}, f32[256,128]{1,0:T(8,128)S(1)}, u32[]{:S(2)}, u32[]{:S(2)}) collective-permute-start(f32[256,128]{1,0:T(8,128)S(1)} %add.68), channel_id=1, source_target_pairs={{0,8},{8,16},{16,24},{24,28},{28,20},{20,12},{12,4},{4,0},{1,9},{9... | collective-permute-start | bytes 393224 | tf_op jit(solution)/shard_map/ppermute | solution.py:363
  122.9 9.3 %collective-permute-start.25 = (f32[256,128]{1,0:T(8,128)S(1)}, f32[256,128]{1,0:T(8,128)S(1)}, u32[]{:S(2)}, u32[]{:S(2)}) collective-permute-start(f32[256,128]{1,0:T(8,128)S(1)} %slice.9), channel_id=1, source_target_pairs={{0,2},{1,3},{2,0},{3,1},{4,6},{5,7},{6,4},{7,5},{8,10},{9,11},{10,... | collective-permute-start | bytes 393224 | tf_op jit(solution)/shard_map/ppermute | solution.py:340
  123.6 6.9 %collective-permute-start.37 = (f32[256,128]{1,0:T(8,128)S(1)}, f32[256,128]{1,0:T(8,128)S(1)}, u32[]{:S(2)}, u32[]{:S(2)}) collective-permute-start(f32[256,128]{1,0:T(8,128)S(1)} %add.74), channel_id=1, source_target_pairs={{0,8},{8,16},{16,24},{24,28},{28,20},{20,12},{12,4},{4,0},{1,9},{9... | collective-permute-start | bytes 393224 | tf_op jit(solution)/shard_map/ppermute | solution.py:363
  125.2 5.3 %collective-permute-start.41 = (f32[256,128]{1,0:T(8,128)S(1)}, f32[256,128]{1,0:T(8,128)S(1)}, u32[]{:S(2)}, u32[]{:S(2)}) collective-permute-start(f32[256,128]{1,0:T(8,128)S(1)} %add.78), channel_id=1, source_target_pairs={{8,0},{16,8},{24,16},{28,24},{20,28},{12,20},{4,12},{0,4},{9,1},{1... | collective-permute-start | bytes 393224 | tf_op jit(solution)/shard_map/ppermute | solution.py:366
  127.8 7.3 %collective-permute-start.48 = (f32[256,128]{1,0:T(8,128)S(1)}, f32[256,128]{1,0:T(8,128)S(1)}, u32[]{:S(2)}, u32[]{:S(2)}) collective-permute-start(f32[256,128]{1,0:T(8,128)S(1)} %add_add_fusion.1.refs_3_), channel_id=1, source_target_pairs={{0,8},{8,16},{16,24},{24,28},{28,20},{20,12},{12,4},{4,0},{1,9},{9... | collective-permute-start | bytes 393224 | tf_op jit(solution)/shard_map/ppermute | solution.py:363
  130.6 6.2 %collective-permute-start.43 = (f32[256,128]{1,0:T(8,128)S(1)}, f32[256,128]{1,0:T(8,128)S(1)}, u32[]{:S(2)}, u32[]{:S(2)}) collective-permute-start(f32[256,128]{1,0:T(8,128)S(1)} %add_add_fusion.refs_4_), channel_id=1, source_target_pairs={{8,0},{16,8},{24,16},{28,24},{20,28},{12,20},{4,12},{0,4},{9,1},{1... | collective-permute-start | bytes 393224 | tf_op jit(solution)/shard_map/ppermute | solution.py:366
  132.2 6.2 %collective-permute-start.26 = (f32[256,128]{1,0:T(8,128)S(1)}, f32[256,128]{1,0:T(8,128)S(1)}, u32[]{:S(2)}, u32[]{:S(2)}) collective-permute-start(f32[256,128]{1,0:T(8,128)S(1)} %slice_add_fusion.refs_0_), channel_id=1, source_target_pairs={{0,2},{1,3},{2,0},{3,1},{4,6},{5,7},{6,4},{7,5},{8,10},{9,11},{10,... | collective-permute-start | bytes 393224 | tf_op jit(solution)/shard_map/ppermute | solution.py:340
  133.1 5.4 %collective-permute-start.42 = (f32[256,128]{1,0:T(8,128)S(1)}, f32[256,128]{1,0:T(8,128)S(1)}, u32[]{:S(2)}, u32[]{:S(2)}) collective-permute-start(f32[256,128]{1,0:T(8,128)S(1)} %add_add_fusion.1.refs_3_), channel_id=1, source_target_pairs={{8,0},{16,8},{24,16},{28,24},{20,28},{12,20},{4,12},{0,4},{9,1},{1... | collective-permute-start | bytes 393224 | tf_op jit(solution)/shard_map/ppermute | solution.py:366
  134.3 5.5 %collective-permute-start.53 = (f32[256,128]{1,0:T(8,128)S(1)}, f32[256,128]{1,0:T(8,128)S(1)}, u32[]{:S(2)}, u32[]{:S(2)}) collective-permute-start(f32[256,128]{1,0:T(8,128)S(1)} %add_add_fusion.refs_4_), channel_id=1, source_target_pairs={{0,8},{8,16},{16,24},{24,28},{28,20},{20,12},{12,4},{4,0},{1,9},{9... | collective-permute-start | bytes 393224 | tf_op jit(solution)/shard_map/ppermute | solution.py:363
  135.1 5.6 %collective-permute-start.49 = (f32[256,128]{1,0:T(8,128)S(1)}, f32[256,128]{1,0:T(8,128)S(1)}, u32[]{:S(2)}, u32[]{:S(2)}) collective-permute-start(f32[256,128]{1,0:T(8,128)S(1)} %collective-permute-done.48.refs_17_), channel_id=1, source_target_pairs={{0,8},{8,16},{16,24},{24,28},{28,20},{20,12},{12,4},{4,0},{1,9},{9... | collective-permute-start | bytes 393224 | tf_op jit(solution)/shard_map/ppermute | solution.py:363
  136.7 5.3 %collective-permute-start.45 = (f32[256,128]{1,0:T(8,128)S(1)}, f32[256,128]{1,0:T(8,128)S(1)}, u32[]{:S(2)}, u32[]{:S(2)}) collective-permute-start(f32[256,128]{1,0:T(8,128)S(1)} %collective-permute-done.43.refs_6_), channel_id=1, source_target_pairs={{8,0},{16,8},{24,16},{28,24},{20,28},{12,20},{4,12},{0,4},{9,1},{1... | collective-permute-start | bytes 393224 | tf_op jit(solution)/shard_map/ppermute | solution.py:366
  138.4 12.2 %collective-permute-start.27 = (f32[512,128]{1,0:T(8,128)S(1)}, f32[512,128]{1,0:T(8,128)S(1)}, u32[]{:S(2)}, u32[]{:S(2)}) collective-permute-start(f32[512,128]{1,0:T(8,128)S(1)} %pad_maximum_fusion), channel_id=1, source_target_pairs={{0,1},{1,0},{2,3},{3,2},{4,5},{5,4},{6,7},{7,6},{8,9},{9,8},{10,11... | collective-permute-start | bytes 786440 | tf_op jit(solution)/shard_map/ppermute | solution.py:340
  138.5 6.4 %collective-permute-start.44 = (f32[256,128]{1,0:T(8,128)S(1)}, f32[256,128]{1,0:T(8,128)S(1)}, u32[]{:S(2)}, u32[]{:S(2)}) collective-permute-start(f32[256,128]{1,0:T(8,128)S(1)} %collective-permute-done.42.refs_5_), channel_id=1, source_target_pairs={{8,0},{16,8},{24,16},{28,24},{20,28},{12,20},{4,12},{0,4},{9,1},{1... | collective-permute-start | bytes 393224 | tf_op jit(solution)/shard_map/ppermute | solution.py:366
  139.8 7.5 %collective-permute-start.54 = (f32[256,128]{1,0:T(8,128)S(1)}, f32[256,128]{1,0:T(8,128)S(1)}, u32[]{:S(2)}, u32[]{:S(2)}) collective-permute-start(f32[256,128]{1,0:T(8,128)S(1)} %collective-permute-done.53.refs_18_), channel_id=1, source_target_pairs={{0,8},{8,16},{16,24},{24,28},{28,20},{20,12},{12,4},{4,0},{1,9},{9... | collective-permute-start | bytes 393224 | tf_op jit(solution)/shard_map/ppermute | solution.py:363
  140.6 7.1 %collective-permute-start.50 = (f32[256,128]{1,0:T(8,128)S(1)}, f32[256,128]{1,0:T(8,128)S(1)}, u32[]{:S(2)}, u32[]{:S(2)}) collective-permute-start(f32[256,128]{1,0:T(8,128)S(1)} %collective-permute-done.49.refs_15_), channel_id=1, source_target_pairs={{0,8},{8,16},{16,24},{24,28},{28,20},{20,12},{12,4},{4,0},{1,9},{9... | collective-permute-start | bytes 393224 | tf_op jit(solution)/shard_map/ppermute | solution.py:363
  142.0 7.3 %collective-permute-start.47 = (f32[256,128]{1,0:T(8,128)S(1)}, f32[256,128]{1,0:T(8,128)S(1)}, u32[]{:S(2)}, u32[]{:S(2)}) collective-permute-start(f32[256,128]{1,0:T(8,128)S(1)} %collective-permute-done.45.refs_8_), channel_id=1, source_target_pairs={{8,0},{16,8},{24,16},{28,24},{20,28},{12,20},{4,12},{0,4},{9,1},{1... | collective-permute-start | bytes 393224 | tf_op jit(solution)/shard_map/ppermute | solution.py:366
  144.9 5.8 %collective-permute-start.46 = (f32[256,128]{1,0:T(8,128)S(1)}, f32[256,128]{1,0:T(8,128)S(1)}, u32[]{:S(2)}, u32[]{:S(2)}) collective-permute-start(f32[256,128]{1,0:T(8,128)S(1)} %collective-permute-done.44.refs_7_), channel_id=1, source_target_pairs={{8,0},{16,8},{24,16},{28,24},{20,28},{12,20},{4,12},{0,4},{9,1},{1... | collective-permute-start | bytes 393224 | tf_op jit(solution)/shard_map/ppermute | solution.py:366
  147.7 6.1 %collective-permute-start.51 = (f32[256,128]{1,0:T(8,128)S(1)}, f32[256,128]{1,0:T(8,128)S(1)}, u32[]{:S(2)}, u32[]{:S(2)}) collective-permute-start(f32[256,128]{1,0:T(8,128)S(1)} %collective-permute-done.50.refs_13_), channel_id=1, source_target_pairs={{0,8},{8,16},{16,24},{24,28},{28,20},{20,12},{12,4},{4,0},{1,9},{9... | collective-permute-start | bytes 393224 | tf_op jit(solution)/shard_map/ppermute | solution.py:363
  (47 other events, 358.8 us)

commit v2 on v1

--- a/solution.py
+++ b/solution.py
@@ -14,6 +14,7 @@
 LANES = 128
 WIDE = 512
 TALL = 256
+LIMIT = 20 * 2**20
 F32 = jnp.float32
 
 
@@ -69,13 +70,29 @@
     return scores * KAPPA + shift_ref[:, columns]
 
 
-def row_level_kernel(crawl_ref, bench_ref, shift_ref, tile_ref, top_ref, level_ref, top_scratch, sum_scratch):
+def row_level_kernel(crawl_hbm, bench_hbm, duals_hbm, tile_ref, top_ref, level_ref, crawl_ref, bench_ref, shift_ref,
+                     top_scratch, sum_scratch, sems):
     height = 64
-
-    def fill(block, _):
+    chunks = 4
+    part = bench_ref.shape[0] // chunks
+    copies = [pltpu.make_async_copy(crawl_hbm, crawl_ref, sems.at[chunks]),
+              pltpu.make_async_copy(duals_hbm, shift_ref, sems.at[chunks + 1])]
+    fetches = [
+        pltpu.make_async_copy(bench_hbm.at[k * part:(k + 1) * part], bench_ref.at[k * part:(k + 1) * part], sems.at[k])
+        for k in range(chunks)]
+    for copy in (*copies, *fetches):
+        copy.start()
+    for copy in copies:
+        copy.wait()
+    shift_ref[...] = shift_ref[...] * KAPPA
+
+    def fill(block, _, fetches=()):
         rows = pl.ds(pl.multiple_of(block * TALL, TALL), TALL)
         top = jnp.full((TALL, LANES), -jnp.inf, F32)
         for at in range(0, tile_ref.shape[1], WIDE):
+            for k, fetch in enumerate(fetches):
+                if at <= k * part < at + WIDE:
+                    fetch.wait()
             exponent = exponent_block(crawl_ref, bench_ref, shift_ref, rows, pl.ds(at, WIDE))
             tile_ref[rows, at:at + WIDE] = exponent
             for lane in range(0, WIDE, LANES):
@@ -83,7 +100,8 @@
         top_scratch[rows, :] = top
         return _
 
-    lax.fori_loop(0, tile_ref.shape[0] // TALL, fill, 0)
+    fill(0, 0, fetches)
+    lax.fori_loop(1, tile_ref.shape[0] // TALL, fill, 0)
 
     def power(block, _):
         rows = pl.ds(pl.multiple_of(block * height, height), height)
@@ -306,29 +324,24 @@
         copy.wait()
 
 
-def call(kernel, args, outs, scratch, aliases=None, held=()):
-    ins = len(args)
-
-    def body(*refs):
-        kernel(*refs[:ins], *refs[ins + len(held):])
-
+def call(kernel, args, outs, scratch, aliases=None):
     return pl.pallas_call(
-        body,
-        in_specs=[pl.BlockSpec(memory_space=pltpu.VMEM)] * (ins + len(held)),
+        kernel,
+        in_specs=[pl.BlockSpec(memory_space=pltpu.VMEM)] * len(args),
         out_specs=[pl.BlockSpec(memory_space=pltpu.VMEM)] * len(outs),
         out_shape=outs,
         scratch_shapes=[pltpu.VMEM(shape, F32) for shape in scratch],
         input_output_aliases=aliases or {},
-        compiler_params=pltpu.CompilerParams(vmem_limit_bytes=20 * 2**20),
-    )(*args, *held)
-
-
-def shaped(*shape):
-    return jax.ShapeDtypeStruct(shape, F32)
-
-
-def resident(*shape):
-    return pltpu.VMEM(shape, F32)
+        compiler_params=pltpu.CompilerParams(vmem_limit_bytes=LIMIT),
+    )(*args)
+
+
+def shaped(*shape, kind=F32):
+    return jax.ShapeDtypeStruct(shape, kind)
+
+
+def resident(*shape, kind=F32):
+    return pltpu.VMEM(shape, kind)
 
 
 def kept(x):
@@ -389,7 +402,6 @@
 
 def per_device(crawl, bench, start_duals, row_cotangent, col_cotangent):
     rows, columns = crawl.shape[0], bench.shape[0]
-    shift = (start_duals * KAPPA).reshape(1, columns)
     row_cotangent = row_cotangent.reshape(1, rows)
     col_cotangent = col_cotangent.reshape(1, columns)
     row, column, tall = shaped(1, rows), shaped(1, columns), (rows, LANES)
@@ -399,9 +411,18 @@
         return spread(x, "cols", 4, join)
 
     def over_rows(x, join=sum):
-        return spread(x, "rows", 2, join)
-
-    tile, top, local = call(row_level_kernel, [crawl, bench, shift], [tile_shape, row, row], [tall, tall])
+        return spread(x, "rows", 4, join)
+
+    tile, top, local, crawl, bench, shift = pl.pallas_call(
+        row_level_kernel,
+        in_specs=[pl.BlockSpec(memory_space=pltpu.HBM)] * 3,
+        out_specs=[pl.BlockSpec(memory_space=pltpu.VMEM)] * 6,
+        out_shape=[tile_shape, row, row, resident(*crawl.shape, kind=crawl.dtype), resident(*bench.shape, kind=bench.dtype),
+                   resident(1, columns)],
+        scratch_shapes=[pltpu.VMEM(tall, F32)] * 2 + [pltpu.SemaphoreType.DMA((6,))],
+        compiler_params=pltpu.CompilerParams(vmem_limit_bytes=LIMIT),
+    )(*(pltpu.with_memory_space_constraint(x, pltpu.HBM) for x in (crawl, bench, start_duals.reshape(1, columns))))
+    crawl, bench, shift = kept(crawl), kept(bench), kept(shift)
     parts = over_cols(local, log_sum)
     level, local = call(
         functools.partial(column_level_kernel, len(parts)),
@@ -412,17 +433,17 @@
         [kept(tile), top, level, *parts, crawl, bench, shift], [tile_shape, column, row],
         [tall, tall, (1, columns)], aliases={0: 0})
     parts = over_cols(local)
-    inverse, local = call(functools.partial(second_column_kernel, len(parts)), [kept(soft), *parts], [row, column], [tall], held=[bench, crawl])
+    inverse, local = call(functools.partial(second_column_kernel, len(parts)), [kept(soft), *parts], [row, column], [tall])
     parts = over_rows(local)
     scaled2, local = call(
         functools.partial(second_row_kernel, len(parts)),
-        [kept(soft), inverse, col_cotangent, *parts], [column, row], [tall], held=[bench, crawl])
+        [kept(soft), inverse, col_cotangent, *parts], [column, row], [tall])
     parts = over_cols(local)
     scaled, local = call(
         functools.partial(first_column_kernel, len(parts)),
-        [kept(soft), inverse, row_cotangent, *parts], [row, column], [tall], held=[bench, crawl])
+        [kept(soft), inverse, row_cotangent, *parts], [row, column], [tall])
     parts = over_rows(local)
-    back, local = call(functools.partial(first_row_kernel, len(parts)), [kept(soft), *parts], [column, row], [tall], held=[bench, crawl])
+    back, local = call(functools.partial(first_row_kernel, len(parts)), [kept(soft), *parts], [column, row], [tall])
     parts = over_cols(local)
     n = lax.axis_size("rows")
     width = bench.shape[1]
@@ -432,7 +453,7 @@
     *factors, = call(
         functools.partial(far_kernel, len(parts), n),
         [kept(soft), inverse, scaled2, back, mass, scaled, crawl, *parts],
-        [shaped(*tall)] * 3 + [piece] * (2 * ahead), [(LANES, share)], held=[bench])
+        [shaped(*tall)] * 3 + [piece] * (2 * ahead), [(LANES, share)])
     factors, far = factors[:3], factors[3:]
     places = [at for at in range(n) if at != n // 2 or not ahead]
     keep, send, *pieces = call(
@@ -449,7 +470,8 @@
         out_specs=[pl.BlockSpec(memory_space=pl.ANY)] * 2,
         out_shape=[shaped(rows, width), shaped(columns, width)],
         scratch_shapes=[pltpu.SemaphoreType.DMA((4 + len(pieces),))],
-    )(*quarters, *pieces)
+        compiler_params=pltpu.CompilerParams(vmem_limit_bytes=LIMIT),
+    )(*map(kept, (*quarters, *pieces)))
     return (crawl_grad, bench_grad)
 
 

time: 159 us -> 155 us (0.975)
  waiting for transfers between devices: 36.4 us -> 40.4 us
  starting transfers between devices: 61.7 us -> 58.3 us
  local copies, waits for them, and re-layouts: 2.9 us -> 0.02 us
    ppermute x14, starting transfers between devices: 20.3 us -> 6.07 us  [behind(): return lax.ppermute(x, 'rows', down)]
    ppermute x14, starting transfers between devices: 12.7 us -> 22.5 us  [ahead(): return lax.ppermute(x, 'rows', up)]
    ppermute x14, waiting for transfers between devices: 4.68 us -> 12.4 us  [behind(): return lax.ppermute(x, 'rows', down)]
    ppermute x14, waiting for transfers between devices: 8.08 us -> 4.83 us  [ahead(): return lax.ppermute(x, 'rows', up)]
    unnamed x46 -> x4, local copies, waits for them, and re-layouts: 2.89 us -> 0.01 us
    pallas_call x1, Pallas kernels: 3.4 us -> 1.64 us  [per_device(): pl.pallas_call(functools.partial(placing_kernel, n), in_specs=[pl.BlockSp...]
where the time goes in v2:
time: 155 us
  starting transfers between devices  58.3 us (38%)
  Pallas kernels  54.8 us (35%)
  waiting for transfers between devices  40.4 us (26%)
    pallas_call x8, Pallas kernels, call(): pl.pallas_call(kernel, in_specs=[pl.BlockSpec(memory_space=pltpu.VMEM)] *...  44.8 us
    ppermute x28, starting transfers between devices, exchange(): lax.ppermute(x, axis, [(i, i ^ k * stride) for i in range(n)])  29.6 us
    ppermute x28, waiting for transfers between devices, exchange(): lax.ppermute(x, axis, [(i, i ^ k * stride) for i in range(n)])  23.2 us
    ppermute x14, starting transfers between devices, ahead(): return lax.ppermute(x, 'rows', up)  22.5 us
    ppermute x14, waiting for transfers between devices, behind(): return lax.ppermute(x, 'rows', down)  12.4 us
    pallas_call x1, Pallas kernels, per_device(): pl.pallas_call(row_level_kernel, in_specs=[pl.BlockSpec(memory_space=pltp...  8.37 us
    ppermute x14, starting transfers between devices, behind(): return lax.ppermute(x, 'rows', down)  6.07 us
    ppermute x14, waiting for transfers between devices, ahead(): return lax.ppermute(x, 'rows', up)  4.83 us
  transfers between devices with their start and end apart: 56, of which 35 were waited for; matrix products, arithmetic and copies ran while one was open for 0% of the time, Pallas kernels for 4%

profile of v2, /device:TPU:0, one launch (start us, length us, event | category | flops | bytes accessed | tf_op | source)
XLA Modules:
  0.0 154.8 jit_solution(2237072902593391658)
XLA Ops:
  0.6 8.4 %shard_map.68 = (f32[1024,4096]{1,0:T(8,128)S(1)}, f32[1,1024]{1,0:T(1,128)S(1)}, f32[1,1024]{1,0:T(1,128)S(1)}, bf16[1024,128]{1,0:T(8,128)(2,1)S(1)}, bf16[409...) custom-call(bf16[1024,128]{1,0:T(8,128)(2,1)} %crawl_hbm.1, bf16[4096,128]{1,0:T(8,128)(2,1)} %bench_hbm.1, f32[1,4096]{1,0:T(1,128)} %bitcast.5), custom_call_target="tpu_custom_call" | custom-call | tf_op jit(solution)/shard_map/pallas_call | solution.py:416
  9.0 2.4 %collective-permute-start.2 = (f32[1,1024]{1,0:T(1,128)S(1)}, f32[1,1024]{1,0:T(1,128)S(1)}, u32[]{:S(2)}, u32[]{:S(2)}) collective-permute-start(f32[1,1024]{1,0:T(1,128)S(1)} %get-tuple-element.44.refs_0_), channel_id=1, source_target_pairs={{0,3},{1,2},{2,1},{3,0},{4,7},{5,6},{6,5},{7,4},{8,11},{9,10},{10,... | collective-permute-start | bytes 12296 | tf_op jit(solution)/shard_map/ppermute | solution.py:353
  12.8 2.3 %collective-permute-done.1.refs_2_ = f32[1,1024]{1,0:T(1,128)S(1)} collective-permute-done((f32[1,1024]{1,0:T(1,128)S(1)}, f32[1,1024]{1,0:T(1,128)S(1)}, u32[]{:S(2)}, u32[]{:S(2)}) %collective-permute-start.1) | collective-permute-done | bytes 4128 | tf_op jit(solution)/shard_map/ppermute | solution.py:353
  15.1 19.2 %shard_map.69 = (f32[1,1024]{1,0:T(1,128)S(1)}, f32[1,4096]{1,0:T(1,128)S(1)}) custom-call(f32[1024,4096]{1,0:T(8,128)S(1)} %get-tuple-element.42.tile_ref, f32[1,1024]{1,0:T(1,128)S(1)} %get-tuple-element.43.top_ref, f32[1,1024]{1,0:T(1,128)S(1)} %get-tuple-element.44.refs_0_, f32[1,1024]{1,0:T(1,128)S(1)} %collective-permute-done.refs_1_, ...), custom_call_target="tpu_custom_call" | custom-call | tf_op jit(solution)/shard_map/pallas_call | solution.py:328
  34.2 2.6 %collective-permute-start.5 = (f32[1,4096]{1,0:T(1,128)S(1)}, f32[1,4096]{1,0:T(1,128)S(1)}, u32[]{:S(2)}, u32[]{:S(2)}) collective-permute-start(f32[1,4096]{1,0:T(1,128)S(1)} %get-tuple-element.49), channel_id=1, source_target_pairs={{0,12},{4,8},{8,4},{12,0},{16,28},{20,24},{24,20},{28,16},{1,13},{... | collective-permute-start | bytes 49160 | tf_op jit(solution)/shard_map/ppermute | solution.py:353
  39.0 1.6 %collective-permute-done.4 = f32[1,4096]{1,0:T(1,128)S(1)} collective-permute-done((f32[1,4096]{1,0:T(1,128)S(1)}, f32[1,4096]{1,0:T(1,128)S(1)}, u32[]{:S(2)}, u32[]{:S(2)}) %collective-permute-start.4) | collective-permute-done | bytes 16416 | tf_op jit(solution)/shard_map/ppermute | solution.py:353
  41.2 2.7 %collective-permute-start.6 = (f32[1,4096]{1,0:T(1,128)S(1)}, f32[1,4096]{1,0:T(1,128)S(1)}, u32[]{:S(2)}, u32[]{:S(2)}) collective-permute-start(f32[1,4096]{1,0:T(1,128)S(1)} %multiply_add_fusion.refs_0_), channel_id=1, source_target_pairs={{0,16},{4,20},{8,24},{12,28},{16,0},{20,4},{24,8},{28,12},{1,17},{... | collective-permute-start | bytes 49160 | tf_op jit(solution)/shard_map/ppermute | solution.py:353
  43.8 2.0 %collective-permute-done.6.refs_1_ = f32[1,4096]{1,0:T(1,128)S(1)} collective-permute-done((f32[1,4096]{1,0:T(1,128)S(1)}, f32[1,4096]{1,0:T(1,128)S(1)}, u32[]{:S(2)}, u32[]{:S(2)}) %collective-permute-start.6) | collective-permute-done | bytes 16416 | tf_op jit(solution)/shard_map/ppermute | solution.py:353
  45.9 9.5 %shard_map.70 = (f32[1024,4096]{1,0:T(8,128)S(1)}, f32[1,4096]{1,0:T(1,128)S(1)}, f32[1,1024]{1,0:T(1,128)S(1)}) custom-call(f32[1024,4096]{1,0:T(8,128)S(1)} %get-tuple-element.42.tile_ref, f32[1,1024]{1,0:T(1,128)S(1)} %get-tuple-element.43.top_ref, f32[1,1024]{1,0:T(1,128)S(1)} %get-tuple-element.48.level_ref, ...), custom_call_target="tpu_custom_call", output_to_operand_aliasing={{0}: (0, {})} | custom-call | tf_op jit(solution)/shard_map/pallas_call | solution.py:328
  59.1 2.0 %shard_map.71 = (f32[1,1024]{1,0:T(1,128)S(1)}, f32[1,4096]{1,0:T(1,128)S(1)}) custom-call(f32[1024,4096]{1,0:T(8,128)S(1)} %get-tuple-element.50.soft_ref, f32[1,1024]{1,0:T(1,128)S(1)} %get-tuple-element.51.refs_0_, f32[1,1024]{1,0:T(1,128)S(1)} %collective-permute-done.7.refs_1_, f32[1,1024]{1,0:T(1,128)S(1)} %collective-permute-done.8.refs_2_, ...), custom_call_target="tpu_custom_call" | custom-call | tf_op jit(solution)/shard_map/pallas_call | solution.py:328
  66.9 2.6 %collective-permute-start.13 = (f32[1,4096]{1,0:T(1,128)S(1)}, f32[1,4096]{1,0:T(1,128)S(1)}, u32[]{:S(2)}, u32[]{:S(2)}) collective-permute-start(f32[1,4096]{1,0:T(1,128)S(1)} %add_add_fusion.3.refs_0_), channel_id=1, source_target_pairs={{0,16},{4,20},{8,24},{12,28},{16,0},{20,4},{24,8},{28,12},{1,17},{... | collective-permute-start | bytes 49160 | tf_op jit(solution)/shard_map/ppermute | solution.py:353
  69.6 2.1 %collective-permute-done.13.refs_1_ = f32[1,4096]{1,0:T(1,128)S(1)} collective-permute-done((f32[1,4096]{1,0:T(1,128)S(1)}, f32[1,4096]{1,0:T(1,128)S(1)}, u32[]{:S(2)}, u32[]{:S(2)}) %collective-permute-start.13) | collective-permute-done | bytes 16416 | tf_op jit(solution)/shard_map/ppermute | solution.py:353
  71.6 1.9 %shard_map.72 = (f32[1,4096]{1,0:T(1,128)S(1)}, f32[1,1024]{1,0:T(1,128)S(1)}) custom-call(f32[1024,4096]{1,0:T(8,128)S(1)} %get-tuple-element.50.soft_ref, f32[1,1024]{1,0:T(1,128)S(1)} %get-tuple-element.52.inverse_ref, f32[1,4096]{1,0:T(1,128)S(1)} %bitcast.3, f32[1,4096]{1,0:T(1,128)S(1)} %add_add_fusion.3.refs_0_, ...), custom_call_target="tpu_custom_call" | custom-call | tf_op jit(solution)/shard_map/pallas_call | solution.py:328
  77.3 2.0 %shard_map.73 = (f32[1,1024]{1,0:T(1,128)S(1)}, f32[1,4096]{1,0:T(1,128)S(1)}) custom-call(f32[1024,4096]{1,0:T(8,128)S(1)} %get-tuple-element.50.soft_ref, f32[1,1024]{1,0:T(1,128)S(1)} %get-tuple-element.52.inverse_ref, f32[1,1024]{1,0:T(1,128)S(1)} %bitcast.4, f32[1,1024]{1,0:T(1,128)S(1)} %get-tuple-element.55.refs_0_, ...), custom_call_target="tpu_custom_call" | custom-call | tf_op jit(solution)/shard_map/pallas_call | solution.py:328
  79.3 2.6 %collective-permute-start.19 = (f32[1,4096]{1,0:T(1,128)S(1)}, f32[1,4096]{1,0:T(1,128)S(1)}, u32[]{:S(2)}, u32[]{:S(2)}) collective-permute-start(f32[1,4096]{1,0:T(1,128)S(1)} %get-tuple-element.56), channel_id=1, source_target_pairs={{0,12},{4,8},{8,4},{12,0},{16,28},{20,24},{24,20},{28,16},{1,13},{... | collective-permute-start | bytes 49160 | tf_op jit(solution)/shard_map/ppermute | solution.py:353
  84.0 1.6 %collective-permute-done.18 = f32[1,4096]{1,0:T(1,128)S(1)} collective-permute-done((f32[1,4096]{1,0:T(1,128)S(1)}, f32[1,4096]{1,0:T(1,128)S(1)}, u32[]{:S(2)}, u32[]{:S(2)}) %collective-permute-start.18) | collective-permute-done | bytes 16416 | tf_op jit(solution)/shard_map/ppermute | solution.py:353
  86.1 2.7 %collective-permute-start.20 = (f32[1,4096]{1,0:T(1,128)S(1)}, f32[1,4096]{1,0:T(1,128)S(1)}, u32[]{:S(2)}, u32[]{:S(2)}) collective-permute-start(f32[1,4096]{1,0:T(1,128)S(1)} %add_add_fusion.2.refs_0_), channel_id=1, source_target_pairs={{0,16},{4,20},{8,24},{12,28},{16,0},{20,4},{24,8},{28,12},{1,17},{... | collective-permute-start | bytes 49160 | tf_op jit(solution)/shard_map/ppermute | solution.py:353
  88.8 2.0 %collective-permute-done.20.refs_1_ = f32[1,4096]{1,0:T(1,128)S(1)} collective-permute-done((f32[1,4096]{1,0:T(1,128)S(1)}, f32[1,4096]{1,0:T(1,128)S(1)}, u32[]{:S(2)}, u32[]{:S(2)}) %collective-permute-start.20) | collective-permute-done | bytes 16416 | tf_op jit(solution)/shard_map/ppermute | solution.py:353
  90.8 1.7 %shard_map.74 = (f32[1,4096]{1,0:T(1,128)S(1)}, f32[1,1024]{1,0:T(1,128)S(1)}) custom-call(f32[1024,4096]{1,0:T(8,128)S(1)} %get-tuple-element.50.soft_ref, f32[1,4096]{1,0:T(1,128)S(1)} %add_add_fusion.2.refs_0_, f32[1,4096]{1,0:T(1,128)S(1)} %collective-permute-done.20.refs_1_), custom_call_target="tpu_custom_call" | custom-call | tf_op jit(solution)/shard_map/pallas_call | solution.py:328
  96.3 1.7 %shard_map.75 = (f32[1024,128]{1,0:T(8,128)S(1)}, f32[1024,128]{1,0:T(8,128)S(1)}, f32[1024,128]{1,0:T(8,128)S(1)}, f32[256,128]{1,0:T(8,128)S(1)}, f32[256,128]{1,0:T(8,128)S(1)}) custom-call(f32[1024,4096]{1,0:T(8,128)S(1)} %get-tuple-element.50.soft_ref, f32[1,1024]{1,0:T(1,128)S(1)} %get-tuple-element.52.inverse_ref, ...), custom_call_target="tpu_custom_call" | custom-call | tf_op jit(solution)/shard_map/pallas_call | solution.py:328
  98.1 1.6 %collective-permute-start.28 = (f32[256,128]{1,0:T(8,128)S(1)}, f32[256,128]{1,0:T(8,128)S(1)}, u32[]{:S(2)}, u32[]{:S(2)}) collective-permute-start(f32[256,128]{1,0:T(8,128)S(1)} %get-tuple-element.70), channel_id=1, source_target_pairs={{0,8},{8,16},{16,24},{24,28},{28,20},{20,12},{12,4},{4,0},{1,9},{9... | collective-permute-start | bytes 393224 | tf_op jit(solution)/shard_map/ppermute | solution.py:376
  100.1 6.8 %shard_map.76 = (f32[512,128]{1,0:T(8,128)S(1)}, f32[512,128]{1,0:T(8,128)S(1)}, f32[256,128]{1,0:T(8,128)S(1)}, f32[256,128]{1,0:T(8,128)S(1)}, f32[256,128]{1,...) custom-call(f32[1024,4096]{1,0:T(8,128)S(1)} %get-tuple-element.50.s, ...), custom_call_target="tpu_custom_call" | custom-call | tf_op jit(solution)/shard_map/pallas_call | solution.py:328
  114.7 1.6 %collective-permute-start.36 = (f32[256,128]{1,0:T(8,128)S(1)}, f32[256,128]{1,0:T(8,128)S(1)}, u32[]{:S(2)}, u32[]{:S(2)}) collective-permute-start(f32[256,128]{1,0:T(8,128)S(1)} %add.97), channel_id=1, source_target_pairs={{0,8},{8,16},{16,24},{24,28},{28,20},{20,12},{12,4},{4,0},{1,9},{9... | collective-permute-start | bytes 393224 | tf_op jit(solution)/shard_map/ppermute | solution.py:376
  117.5 2.3 %collective-permute-done.33 = f32[256,128]{1,0:T(8,128)S(1)} collective-permute-done((f32[256,128]{1,0:T(8,128)S(1)}, f32[256,128]{1,0:T(8,128)S(1)}, u32[]{:S(2)}, u32[]{:S(2)}) %collective-permute-start.33) | collective-permute-done | bytes 131104 | tf_op jit(solution)/shard_map/ppermute | solution.py:379
  120.4 1.6 %collective-permute-start.31 = (f32[256,128]{1,0:T(8,128)S(1)}, f32[256,128]{1,0:T(8,128)S(1)}, u32[]{:S(2)}, u32[]{:S(2)}) collective-permute-start(f32[256,128]{1,0:T(8,128)S(1)} %add.92), channel_id=1, source_target_pairs={{0,8},{8,16},{16,24},{24,28},{28,20},{20,12},{12,4},{4,0},{1,9},{9... | collective-permute-start | bytes 393224 | tf_op jit(solution)/shard_map/ppermute | solution.py:376
  122.8 1.6 %collective-permute-start.37 = (f32[256,128]{1,0:T(8,128)S(1)}, f32[256,128]{1,0:T(8,128)S(1)}, u32[]{:S(2)}, u32[]{:S(2)}) collective-permute-start(f32[256,128]{1,0:T(8,128)S(1)} %add.98), channel_id=1, source_target_pairs={{0,8},{8,16},{16,24},{24,28},{28,20},{20,12},{12,4},{4,0},{1,9},{9... | collective-permute-start | bytes 393224 | tf_op jit(solution)/shard_map/ppermute | solution.py:376
  125.1 1.7 %collective-permute-done.31 = f32[256,128]{1,0:T(8,128)S(1)} collective-permute-done((f32[256,128]{1,0:T(8,128)S(1)}, f32[256,128]{1,0:T(8,128)S(1)}, u32[]{:S(2)}, u32[]{:S(2)}) %collective-permute-start.31) | collective-permute-done | bytes 131104 | tf_op jit(solution)/shard_map/ppermute | solution.py:376
  126.8 1.6 %collective-permute-start.48 = (f32[256,128]{1,0:T(8,128)S(1)}, f32[256,128]{1,0:T(8,128)S(1)}, u32[]{:S(2)}, u32[]{:S(2)}) collective-permute-start(f32[256,128]{1,0:T(8,128)S(1)} %add_add_fusion.1.refs_3_), channel_id=1, source_target_pairs={{0,8},{8,16},{16,24},{24,28},{28,20},{20,12},{12,4},{4,0},{1,9},{9... | collective-permute-start | bytes 393224 | tf_op jit(solution)/shard_map/ppermute | solution.py:376
  142.0 2.7 %collective-permute-done.44.refs_7_ = f32[256,128]{1,0:T(8,128)S(1)} collective-permute-done((f32[256,128]{1,0:T(8,128)S(1)}, f32[256,128]{1,0:T(8,128)S(1)}, u32[]{:S(2)}, u32[]{:S(2)}) %collective-permute-start.44) | collective-permute-done | bytes 131104 | tf_op jit(solution)/shard_map/ppermute | solution.py:379
  144.7 2.0 %collective-permute-start.55 = (f32[256,128]{1,0:T(8,128)S(1)}, f32[256,128]{1,0:T(8,128)S(1)}, u32[]{:S(2)}, u32[]{:S(2)}) collective-permute-start(f32[256,128]{1,0:T(8,128)S(1)} %collective-permute-done.54.refs_16_), channel_id=1, source_target_pairs={{0,8},{8,16},{16,24},{24,28},{28,20},{20,12},{12,4},{4,0},{1,9},{9... | collective-permute-start | bytes 393224 | tf_op jit(solution)/shard_map/ppermute | solution.py:376
  148.8 1.7 %collective-permute-done.46.refs_9_ = f32[256,128]{1,0:T(8,128)S(1)} collective-permute-done((f32[256,128]{1,0:T(8,128)S(1)}, f32[256,128]{1,0:T(8,128)S(1)}, u32[]{:S(2)}, u32[]{:S(2)}) %collective-permute-start.46) | collective-permute-done | bytes 131104 | tf_op jit(solution)/shard_map/ppermute | solution.py:379
  153.2 1.6 %shard_map.77 = (f32[1024,128]{1,0:T(8,128)}, f32[4096,128]{1,0:T(8,128)}) custom-call(f32[256,128]{1,0:T(8,128)S(1)} %slice_add_fusion.refs_0_, f32[256,128]{1,0:T(8,128)S(1)} %collective-permute-done.26.refs_1_, f32[512,128]{1,0:T(8,128)S(1)} %collective-permute-done.27.refs_2_, f32[256,128]{1,0:T(8,128)S(1)} %add_add_fusion.1.refs_3_, ...), custom_call_target="tpu_custom_call" | custom-call | tf_op jit(solution)/shard_map/pallas_call | solution.py:467
  (113 shorter events, 53.4 us)
Async XLA Ops:
  98.1 9.4 %collective-permute-start.28 = (f32[256,128]{1,0:T(8,128)S(1)}, f32[256,128]{1,0:T(8,128)S(1)}, u32[]{:S(2)}, u32[]{:S(2)}) collective-permute-start(f32[256,128]{1,0:T(8,128)S(1)} %get-tuple-element.70), channel_id=1, source_target_pairs={{0,8},{8,16},{16,24},{24,28},{28,20},{20,12},{12,4},{4,0},{1,9},{9... | collective-permute-start | bytes 393224 | tf_op jit(solution)/shard_map/ppermute | solution.py:376
  99.7 11.0 %collective-permute-start.38 = (f32[256,128]{1,0:T(8,128)S(1)}, f32[256,128]{1,0:T(8,128)S(1)}, u32[]{:S(2)}, u32[]{:S(2)}) collective-permute-start(f32[256,128]{1,0:T(8,128)S(1)} %get-tuple-element.81), channel_id=1, source_target_pairs={{8,0},{16,8},{24,16},{28,24},{20,28},{12,20},{4,12},{0,4},{9,1},{1... | collective-permute-start | bytes 393224 | tf_op jit(solution)/shard_map/ppermute | solution.py:379
  106.9 5.0 %collective-permute-start.32 = (f32[256,128]{1,0:T(8,128)S(1)}, f32[256,128]{1,0:T(8,128)S(1)}, u32[]{:S(2)}, u32[]{:S(2)}) collective-permute-start(f32[256,128]{1,0:T(8,128)S(1)} %get-tuple-element.73), channel_id=1, source_target_pairs={{8,0},{16,8},{24,16},{28,24},{20,28},{12,20},{4,12},{0,4},{9,1},{1... | collective-permute-start | bytes 393224 | tf_op jit(solution)/shard_map/ppermute | solution.py:379
  107.5 5.5 %collective-permute-start.29 = (f32[256,128]{1,0:T(8,128)S(1)}, f32[256,128]{1,0:T(8,128)S(1)}, u32[]{:S(2)}, u32[]{:S(2)}) collective-permute-start(f32[256,128]{1,0:T(8,128)S(1)} %add.90), channel_id=1, source_target_pairs={{0,8},{8,16},{16,24},{24,28},{28,20},{20,12},{12,4},{4,0},{1,9},{9... | collective-permute-start | bytes 393224 | tf_op jit(solution)/shard_map/ppermute | solution.py:376
  109.1 5.6 %collective-permute-start.35 = (f32[256,128]{1,0:T(8,128)S(1)}, f32[256,128]{1,0:T(8,128)S(1)}, u32[]{:S(2)}, u32[]{:S(2)}) collective-permute-start(f32[256,128]{1,0:T(8,128)S(1)} %get-tuple-element.77), channel_id=1, source_target_pairs={{0,8},{8,16},{16,24},{24,28},{28,20},{20,12},{12,4},{4,0},{1,9},{9... | collective-permute-start | bytes 393224 | tf_op jit(solution)/shard_map/ppermute | solution.py:376
  110.6 11.4 %collective-permute-start.24 = (f32[512,128]{1,0:T(8,128)S(1)}, f32[512,128]{1,0:T(8,128)S(1)}, u32[]{:S(2)}, u32[]{:S(2)}) collective-permute-start(f32[512,128]{1,0:T(8,128)S(1)} %get-tuple-element.65), channel_id=1, source_target_pairs={{0,1},{1,0},{2,3},{3,2},{4,5},{5,4},{6,7},{7,6},{8,9},{9,8},{10,11... | collective-permute-start | bytes 786440 | tf_op jit(solution)/shard_map/ppermute | solution.py:353
  110.7 6.3 %collective-permute-start.39 = (f32[256,128]{1,0:T(8,128)S(1)}, f32[256,128]{1,0:T(8,128)S(1)}, u32[]{:S(2)}, u32[]{:S(2)}) collective-permute-start(f32[256,128]{1,0:T(8,128)S(1)} %add.100), channel_id=1, source_target_pairs={{8,0},{16,8},{24,16},{28,24},{20,28},{12,20},{4,12},{0,4},{9,1},{1... | collective-permute-start | bytes 393224 | tf_op jit(solution)/shard_map/ppermute | solution.py:379
  112.0 7.9 %collective-permute-start.33 = (f32[256,128]{1,0:T(8,128)S(1)}, f32[256,128]{1,0:T(8,128)S(1)}, u32[]{:S(2)}, u32[]{:S(2)}) collective-permute-start(f32[256,128]{1,0:T(8,128)S(1)} %add.94), channel_id=1, source_target_pairs={{8,0},{16,8},{24,16},{28,24},{20,28},{12,20},{4,12},{0,4},{9,1},{1... | collective-permute-start | bytes 393224 | tf_op jit(solution)/shard_map/ppermute | solution.py:379
  113.1 7.3 %collective-permute-start.30 = (f32[256,128]{1,0:T(8,128)S(1)}, f32[256,128]{1,0:T(8,128)S(1)}, u32[]{:S(2)}, u32[]{:S(2)}) collective-permute-start(f32[256,128]{1,0:T(8,128)S(1)} %add.91), channel_id=1, source_target_pairs={{0,8},{8,16},{16,24},{24,28},{28,20},{20,12},{12,4},{4,0},{1,9},{9... | collective-permute-start | bytes 393224 | tf_op jit(solution)/shard_map/ppermute | solution.py:376
  114.7 8.1 %collective-permute-start.36 = (f32[256,128]{1,0:T(8,128)S(1)}, f32[256,128]{1,0:T(8,128)S(1)}, u32[]{:S(2)}, u32[]{:S(2)}) collective-permute-start(f32[256,128]{1,0:T(8,128)S(1)} %add.97), channel_id=1, source_target_pairs={{0,8},{8,16},{16,24},{24,28},{28,20},{20,12},{12,4},{4,0},{1,9},{9... | collective-permute-start | bytes 393224 | tf_op jit(solution)/shard_map/ppermute | solution.py:376
  117.0 7.4 %collective-permute-start.40 = (f32[256,128]{1,0:T(8,128)S(1)}, f32[256,128]{1,0:T(8,128)S(1)}, u32[]{:S(2)}, u32[]{:S(2)}) collective-permute-start(f32[256,128]{1,0:T(8,128)S(1)} %add.101), channel_id=1, source_target_pairs={{8,0},{16,8},{24,16},{28,24},{20,28},{12,20},{4,12},{0,4},{9,1},{1... | collective-permute-start | bytes 393224 | tf_op jit(solution)/shard_map/ppermute | solution.py:379
  119.8 5.2 %collective-permute-start.34 = (f32[256,128]{1,0:T(8,128)S(1)}, f32[256,128]{1,0:T(8,128)S(1)}, u32[]{:S(2)}, u32[]{:S(2)}) collective-permute-start(f32[256,128]{1,0:T(8,128)S(1)} %add.95), channel_id=1, source_target_pairs={{8,0},{16,8},{24,16},{28,24},{20,28},{12,20},{4,12},{0,4},{9,1},{1... | collective-permute-start | bytes 393224 | tf_op jit(solution)/shard_map/ppermute | solution.py:379
  120.4 6.4 %collective-permute-start.31 = (f32[256,128]{1,0:T(8,128)S(1)}, f32[256,128]{1,0:T(8,128)S(1)}, u32[]{:S(2)}, u32[]{:S(2)}) collective-permute-start(f32[256,128]{1,0:T(8,128)S(1)} %add.92), channel_id=1, source_target_pairs={{0,8},{8,16},{16,24},{24,28},{28,20},{20,12},{12,4},{4,0},{1,9},{9... | collective-permute-start | bytes 393224 | tf_op jit(solution)/shard_map/ppermute | solution.py:376
  122.1 8.0 %collective-permute-start.25 = (f32[256,128]{1,0:T(8,128)S(1)}, f32[256,128]{1,0:T(8,128)S(1)}, u32[]{:S(2)}, u32[]{:S(2)}) collective-permute-start(f32[256,128]{1,0:T(8,128)S(1)} %slice.9), channel_id=1, source_target_pairs={{0,2},{1,3},{2,0},{3,1},{4,6},{5,7},{6,4},{7,5},{8,10},{9,11},{10,... | collective-permute-start | bytes 393224 | tf_op jit(solution)/shard_map/ppermute | solution.py:353
  122.8 6.8 %collective-permute-start.37 = (f32[256,128]{1,0:T(8,128)S(1)}, f32[256,128]{1,0:T(8,128)S(1)}, u32[]{:S(2)}, u32[]{:S(2)}) collective-permute-start(f32[256,128]{1,0:T(8,128)S(1)} %add.98), channel_id=1, source_target_pairs={{0,8},{8,16},{16,24},{24,28},{28,20},{20,12},{12,4},{4,0},{1,9},{9... | collective-permute-start | bytes 393224 | tf_op jit(solution)/shard_map/ppermute | solution.py:376
  124.4 5.1 %collective-permute-start.41 = (f32[256,128]{1,0:T(8,128)S(1)}, f32[256,128]{1,0:T(8,128)S(1)}, u32[]{:S(2)}, u32[]{:S(2)}) collective-permute-start(f32[256,128]{1,0:T(8,128)S(1)} %add.102), channel_id=1, source_target_pairs={{8,0},{16,8},{24,16},{28,24},{20,28},{12,20},{4,12},{0,4},{9,1},{1... | collective-permute-start | bytes 393224 | tf_op jit(solution)/shard_map/ppermute | solution.py:379
  126.8 6.7 %collective-permute-start.48 = (f32[256,128]{1,0:T(8,128)S(1)}, f32[256,128]{1,0:T(8,128)S(1)}, u32[]{:S(2)}, u32[]{:S(2)}) collective-permute-start(f32[256,128]{1,0:T(8,128)S(1)} %add_add_fusion.1.refs_3_), channel_id=1, source_target_pairs={{0,8},{8,16},{16,24},{24,28},{28,20},{20,12},{12,4},{4,0},{1,9},{9... | collective-permute-start | bytes 393224 | tf_op jit(solution)/shard_map/ppermute | solution.py:376
  129.6 6.1 %collective-permute-start.43 = (f32[256,128]{1,0:T(8,128)S(1)}, f32[256,128]{1,0:T(8,128)S(1)}, u32[]{:S(2)}, u32[]{:S(2)}) collective-permute-start(f32[256,128]{1,0:T(8,128)S(1)} %add_add_fusion.refs_4_), channel_id=1, source_target_pairs={{8,0},{16,8},{24,16},{28,24},{20,28},{12,20},{4,12},{0,4},{9,1},{1... | collective-permute-start | bytes 393224 | tf_op jit(solution)/shard_map/ppermute | solution.py:379
  130.1 6.0 %collective-permute-start.26 = (f32[256,128]{1,0:T(8,128)S(1)}, f32[256,128]{1,0:T(8,128)S(1)}, u32[]{:S(2)}, u32[]{:S(2)}) collective-permute-start(f32[256,128]{1,0:T(8,128)S(1)} %slice_add_fusion.refs_0_), channel_id=1, source_target_pairs={{0,2},{1,3},{2,0},{3,1},{4,6},{5,7},{6,4},{7,5},{8,10},{9,11},{10,... | collective-permute-start | bytes 393224 | tf_op jit(solution)/shard_map/ppermute | solution.py:353
  131.5 5.9 %collective-permute-start.42 = (f32[256,128]{1,0:T(8,128)S(1)}, f32[256,128]{1,0:T(8,128)S(1)}, u32[]{:S(2)}, u32[]{:S(2)}) collective-permute-start(f32[256,128]{1,0:T(8,128)S(1)} %add_add_fusion.1.refs_3_), channel_id=1, source_target_pairs={{8,0},{16,8},{24,16},{28,24},{20,28},{12,20},{4,12},{0,4},{9,1},{1... | collective-permute-start | bytes 393224 | tf_op jit(solution)/shard_map/ppermute | solution.py:379
  132.1 5.8 %collective-permute-start.53 = (f32[256,128]{1,0:T(8,128)S(1)}, f32[256,128]{1,0:T(8,128)S(1)}, u32[]{:S(2)}, u32[]{:S(2)}) collective-permute-start(f32[256,128]{1,0:T(8,128)S(1)} %add_add_fusion.refs_4_), channel_id=1, source_target_pairs={{0,8},{8,16},{16,24},{24,28},{28,20},{20,12},{12,4},{4,0},{1,9},{9... | collective-permute-start | bytes 393224 | tf_op jit(solution)/shard_map/ppermute | solution.py:376
  133.5 6.0 %collective-permute-start.49 = (f32[256,128]{1,0:T(8,128)S(1)}, f32[256,128]{1,0:T(8,128)S(1)}, u32[]{:S(2)}, u32[]{:S(2)}) collective-permute-start(f32[256,128]{1,0:T(8,128)S(1)} %collective-permute-done.48.refs_17_), channel_id=1, source_target_pairs={{0,8},{8,16},{16,24},{24,28},{28,20},{20,12},{12,4},{4,0},{1,9},{9... | collective-permute-start | bytes 393224 | tf_op jit(solution)/shard_map/ppermute | solution.py:376
  135.6 6.3 %collective-permute-start.45 = (f32[256,128]{1,0:T(8,128)S(1)}, f32[256,128]{1,0:T(8,128)S(1)}, u32[]{:S(2)}, u32[]{:S(2)}) collective-permute-start(f32[256,128]{1,0:T(8,128)S(1)} %collective-permute-done.43.refs_6_), channel_id=1, source_target_pairs={{8,0},{16,8},{24,16},{28,24},{20,28},{12,20},{4,12},{0,4},{9,1},{1... | collective-permute-start | bytes 393224 | tf_op jit(solution)/shard_map/ppermute | solution.py:379
  136.1 12.7 %collective-permute-start.27 = (f32[512,128]{1,0:T(8,128)S(1)}, f32[512,128]{1,0:T(8,128)S(1)}, u32[]{:S(2)}, u32[]{:S(2)}) collective-permute-start(f32[512,128]{1,0:T(8,128)S(1)} %pad_maximum_fusion), channel_id=1, source_target_pairs={{0,1},{1,0},{2,3},{3,2},{4,5},{5,4},{6,7},{7,6},{8,9},{9,8},{10,11... | collective-permute-start | bytes 786440 | tf_op jit(solution)/shard_map/ppermute | solution.py:353
  137.4 7.3 %collective-permute-start.44 = (f32[256,128]{1,0:T(8,128)S(1)}, f32[256,128]{1,0:T(8,128)S(1)}, u32[]{:S(2)}, u32[]{:S(2)}) collective-permute-start(f32[256,128]{1,0:T(8,128)S(1)} %collective-permute-done.42.refs_5_), channel_id=1, source_target_pairs={{8,0},{16,8},{24,16},{28,24},{20,28},{12,20},{4,12},{0,4},{9,1},{1... | collective-permute-start | bytes 393224 | tf_op jit(solution)/shard_map/ppermute | solution.py:379
  137.9 6.9 %collective-permute-start.54 = (f32[256,128]{1,0:T(8,128)S(1)}, f32[256,128]{1,0:T(8,128)S(1)}, u32[]{:S(2)}, u32[]{:S(2)}) collective-permute-start(f32[256,128]{1,0:T(8,128)S(1)} %collective-permute-done.53.refs_18_), channel_id=1, source_target_pairs={{0,8},{8,16},{16,24},{24,28},{28,20},{20,12},{12,4},{4,0},{1,9},{9... | collective-permute-start | bytes 393224 | tf_op jit(solution)/shard_map/ppermute | solution.py:376
  139.4 7.3 %collective-permute-start.50 = (f32[256,128]{1,0:T(8,128)S(1)}, f32[256,128]{1,0:T(8,128)S(1)}, u32[]{:S(2)}, u32[]{:S(2)}) collective-permute-start(f32[256,128]{1,0:T(8,128)S(1)} %collective-permute-done.49.refs_15_), channel_id=1, source_target_pairs={{0,8},{8,16},{16,24},{24,28},{28,20},{20,12},{12,4},{4,0},{1,9},{9... | collective-permute-start | bytes 393224 | tf_op jit(solution)/shard_map/ppermute | solution.py:376
  142.0 6.3 %collective-permute-start.47 = (f32[256,128]{1,0:T(8,128)S(1)}, f32[256,128]{1,0:T(8,128)S(1)}, u32[]{:S(2)}, u32[]{:S(2)}) collective-permute-start(f32[256,128]{1,0:T(8,128)S(1)} %collective-permute-done.45.refs_8_), channel_id=1, source_target_pairs={{8,0},{16,8},{24,16},{28,24},{20,28},{12,20},{4,12},{0,4},{9,1},{1... | collective-permute-start | bytes 393224 | tf_op jit(solution)/shard_map/ppermute | solution.py:379
  144.7 5.7 %collective-permute-start.46 = (f32[256,128]{1,0:T(8,128)S(1)}, f32[256,128]{1,0:T(8,128)S(1)}, u32[]{:S(2)}, u32[]{:S(2)}) collective-permute-start(f32[256,128]{1,0:T(8,128)S(1)} %collective-permute-done.44.refs_7_), channel_id=1, source_target_pairs={{8,0},{16,8},{24,16},{28,24},{20,28},{12,20},{4,12},{0,4},{9,1},{1... | collective-permute-start | bytes 393224 | tf_op jit(solution)/shard_map/ppermute | solution.py:379
  144.7 5.8 %collective-permute-start.55 = (f32[256,128]{1,0:T(8,128)S(1)}, f32[256,128]{1,0:T(8,128)S(1)}, u32[]{:S(2)}, u32[]{:S(2)}) collective-permute-start(f32[256,128]{1,0:T(8,128)S(1)} %collective-permute-done.54.refs_16_), channel_id=1, source_target_pairs={{0,8},{8,16},{16,24},{24,28},{28,20},{20,12},{12,4},{4,0},{1,9},{9... | collective-permute-start | bytes 393224 | tf_op jit(solution)/shard_map/ppermute | solution.py:376
  146.7 5.2 %collective-permute-start.51 = (f32[256,128]{1,0:T(8,128)S(1)}, f32[256,128]{1,0:T(8,128)S(1)}, u32[]{:S(2)}, u32[]{:S(2)}) collective-permute-start(f32[256,128]{1,0:T(8,128)S(1)} %collective-permute-done.50.refs_13_), channel_id=1, source_target_pairs={{0,8},{8,16},{16,24},{24,28},{28,20},{20,12},{12,4},{4,0},{1,9},{9... | collective-permute-start | bytes 393224 | tf_op jit(solution)/shard_map/ppermute | solution.py:376
  148.2 5.0 %collective-permute-start.52 = (f32[256,128]{1,0:T(8,128)S(1)}, f32[256,128]{1,0:T(8,128)S(1)}, u32[]{:S(2)}, u32[]{:S(2)}) collective-permute-start(f32[256,128]{1,0:T(8,128)S(1)} %collective-permute-done.47.refs_10_), channel_id=1, source_target_pairs={{8,0},{16,8},{24,16},{28,24},{20,28},{12,20},{4,12},{0,4},{9,1},{1... | collective-permute-start | bytes 393224 | tf_op jit(solution)/shard_map/ppermute | solution.py:379
  (26 other events, 134.3 us)

commit v3 on v2

--- a/solution.py
+++ b/solution.py
@@ -411,7 +411,11 @@
         return spread(x, "cols", 4, join)
 
     def over_rows(x, join=sum):
-        return spread(x, "rows", 4, join)
+        if lax.axis_size("rows") > 8:
+            return spread(x, "rows", 4, join)
+        n = lax.axis_size("rows")
+        copies = jnp.broadcast_to(x.reshape(1, -1, LANES), (n, columns // LANES, LANES))
+        return [join(list(lax.all_to_all(copies, "rows", 0, 0))).reshape(1, columns)]
 
     tile, top, local, crawl, bench, shift = pl.pallas_call(
         row_level_kernel,

time: 155 us -> 154 us (level)
  blocking collectives: 0 us -> 32.8 us
  starting transfers between devices: 58.3 us -> 36.9 us
  waiting for transfers between devices: 40.4 us -> 27.2 us
    all_to_all x0 -> x3, blocking collectives: none -> 32.8 us  [over_rows(): lax.all_to_all(copies, 'rows', 0, 0)]
    ppermute x28 -> x16, starting transfers between devices: 29.6 us -> 11.1 us  [exchange(): lax.ppermute(x, axis, [(i, i ^ k * stride) for i in range(n)])]
    ppermute x28 -> x16, waiting for transfers between devices: 23.2 us -> 8.42 us  [exchange(): lax.ppermute(x, axis, [(i, i ^ k * stride) for i in range(n)])]
    ppermute x14, starting transfers between devices: 22.5 us -> 13.6 us  [ahead(): return lax.ppermute(x, 'rows', up)]
    ppermute x14, starting transfers between devices: 6.07 us -> 12.2 us  [behind(): return lax.ppermute(x, 'rows', down)]
  transfers between devices with their start and end apart: 56 -> 44, of which waited for: 35 -> 22; matrix products, arithmetic and copies ran while one was open for 0% -> 0% of each run, Pallas kernels for 4% -> 4%
where the time goes in v3:
time: 154 us; the launch traced here: 153 us
  Pallas kernels  55 us (36%)
  starting transfers between devices  36.9 us (24%)
  blocking collectives  32.8 us (21%)
  waiting for transfers between devices  27.2 us (18%)
    pallas_call x8, Pallas kernels, call(): pl.pallas_call(kernel, in_specs=[pl.BlockSpec(memory_space=pltpu.VMEM)] *...  45 us
    all_to_all x3, blocking collectives, over_rows(): lax.all_to_all(copies, 'rows', 0, 0)  32.8 us
    ppermute x14, waiting for transfers between devices, behind(): return lax.ppermute(x, 'rows', down)  13.6 us
    ppermute x14, starting transfers between devices, ahead(): return lax.ppermute(x, 'rows', up)  13.6 us
    ppermute x14, starting transfers between devices, behind(): return lax.ppermute(x, 'rows', down)  12.2 us
    ppermute x16, starting transfers between devices, exchange(): lax.ppermute(x, axis, [(i, i ^ k * stride) for i in range(n)])  11.1 us
    ppermute x16, waiting for transfers between devices, exchange(): lax.ppermute(x, axis, [(i, i ^ k * stride) for i in range(n)])  8.42 us
    pallas_call x1, Pallas kernels, per_device(): pl.pallas_call(row_level_kernel, in_specs=[pl.BlockSpec(memory_space=pltp...  8.37 us
  transfers between devices with their start and end apart: 44, of which 22 were waited for; matrix products, arithmetic and copies ran while one was open for 0% of the time, Pallas kernels for 4%

profile of v3, /device:TPU:0, one launch (start us, length us, event | category | flops | bytes accessed | tf_op | source)
XLA Modules:
  0.0 153.4 jit_solution(1782843551937190435)
XLA Ops:
  0.6 8.4 %shard_map.68 = (f32[1024,4096]{1,0:T(8,128)S(1)}, f32[1,1024]{1,0:T(1,128)S(1)}, f32[1,1024]{1,0:T(1,128)S(1)}, bf16[1024,128]{1,0:T(8,128)(2,1)S(1)}, bf16[409...) custom-call(bf16[1024,128]{1,0:T(8,128)(2,1)} %crawl_hbm.1, bf16[4096,128]{1,0:T(8,128)(2,1)} %bench_hbm.1, f32[1,4096]{1,0:T(1,128)} %bitcast.31), custom_call_target="tpu_custom_call" | custom-call | tf_op jit(solution)/shard_map/pallas_call | solution.py:420
  9.0 2.4 %collective-permute-start.2 = (f32[1,1024]{1,0:T(1,128)S(1)}, f32[1,1024]{1,0:T(1,128)S(1)}, u32[]{:S(2)}, u32[]{:S(2)}) collective-permute-start(f32[1,1024]{1,0:T(1,128)S(1)} %get-tuple-element.44.refs_0_), channel_id=1, source_target_pairs={{0,3},{1,2},{2,1},{3,0},{4,7},{5,6},{6,5},{7,4},{8,11},{9,10},{10,... | collective-permute-start | bytes 12296 | tf_op jit(solution)/shard_map/ppermute | solution.py:353
  12.8 2.3 %collective-permute-done.1.refs_2_ = f32[1,1024]{1,0:T(1,128)S(1)} collective-permute-done((f32[1,1024]{1,0:T(1,128)S(1)}, f32[1,1024]{1,0:T(1,128)S(1)}, u32[]{:S(2)}, u32[]{:S(2)}) %collective-permute-start.1) | collective-permute-done | bytes 4128 | tf_op jit(solution)/shard_map/ppermute | solution.py:353
  15.1 19.2 %shard_map.69 = (f32[1,1024]{1,0:T(1,128)S(1)}, f32[1,4096]{1,0:T(1,128)S(1)}) custom-call(f32[1024,4096]{1,0:T(8,128)S(1)} %get-tuple-element.42.tile_ref, f32[1,1024]{1,0:T(1,128)S(1)} %get-tuple-element.43.top_ref, f32[1,1024]{1,0:T(1,128)S(1)} %get-tuple-element.44.refs_0_, f32[1,1024]{1,0:T(1,128)S(1)} %collective-permute-done.refs_1_, ...), custom_call_target="tpu_custom_call" | custom-call | tf_op jit(solution)/shard_map/pallas_call | solution.py:328
  34.3 13.0 %all_to_all.15 = f32[8,32,128]{2,1,0:T(8,128)S(1)} all-to-all(f32[8,32,128]{2,1,0:T(8,128)S(1)} %broadcast_in_dim.22), channel_id=1, replica_groups=mesh['rows'=8,'cols'=4] {'rows'}, dimensions={0} | all-to-all | bytes 262144 | tf_op jit(solution)/shard_map/all_to_all | solution.py:418
  47.5 9.5 %shard_map.70 = (f32[1024,4096]{1,0:T(8,128)S(1)}, f32[1,4096]{1,0:T(1,128)S(1)}, f32[1,1024]{1,0:T(1,128)S(1)}) custom-call(f32[1024,4096]{1,0:T(8,128)S(1)} %get-tuple-element.42.tile_ref, f32[1,1024]{1,0:T(1,128)S(1)} %get-tuple-element.43.top_ref, f32[1,1024]{1,0:T(1,128)S(1)} %get-tuple-element.48.level_ref, ...), custom_call_target="tpu_custom_call", output_to_operand_aliasing={{0}: (0, {})} | custom-call | tf_op jit(solution)/shard_map/pallas_call | solution.py:328
  60.8 2.0 %shard_map.71 = (f32[1,1024]{1,0:T(1,128)S(1)}, f32[1,4096]{1,0:T(1,128)S(1)}) custom-call(f32[1024,4096]{1,0:T(8,128)S(1)} %get-tuple-element.50.soft_ref, f32[1,1024]{1,0:T(1,128)S(1)} %get-tuple-element.51.refs_0_, f32[1,1024]{1,0:T(1,128)S(1)} %collective-permute-done.3.refs_1_, f32[1,1024]{1,0:T(1,128)S(1)} %collective-permute-done.4.refs_2_, ...), custom_call_target="tpu_custom_call" | custom-call | tf_op jit(solution)/shard_map/pallas_call | solution.py:328
  62.8 9.7 %all_to_all.16 = f32[8,32,128]{2,1,0:T(8,128)S(1)} all-to-all(f32[8,32,128]{2,1,0:T(8,128)S(1)} %broadcast_in_dim.24), channel_id=1, replica_groups=mesh['rows'=8,'cols'=4] {'rows'}, dimensions={0} | all-to-all | bytes 262144 | tf_op jit(solution)/shard_map/all_to_all | solution.py:418
  72.5 1.9 %shard_map.72 = (f32[1,4096]{1,0:T(1,128)S(1)}, f32[1,1024]{1,0:T(1,128)S(1)}) custom-call(f32[1024,4096]{1,0:T(8,128)S(1)} %get-tuple-element.50.soft_ref, f32[1,1024]{1,0:T(1,128)S(1)} %get-tuple-element.52.inverse_ref, f32[1,4096]{1,0:T(1,128)S(1)} %bitcast.18, f32[1,4096]{1,0:T(1,128)S(1)} %bitcast.16), custom_call_target="tpu_custom_call" | custom-call | tf_op jit(solution)/shard_map/pallas_call | solution.py:328
  78.2 2.0 %shard_map.73 = (f32[1,1024]{1,0:T(1,128)S(1)}, f32[1,4096]{1,0:T(1,128)S(1)}) custom-call(f32[1024,4096]{1,0:T(8,128)S(1)} %get-tuple-element.50.soft_ref, f32[1,1024]{1,0:T(1,128)S(1)} %get-tuple-element.52.inverse_ref, f32[1,1024]{1,0:T(1,128)S(1)} %bitcast.22, f32[1,1024]{1,0:T(1,128)S(1)} %get-tuple-element.55.refs_0_, ...), custom_call_target="tpu_custom_call" | custom-call | tf_op jit(solution)/shard_map/pallas_call | solution.py:328
  80.2 10.1 %all_to_all.17 = f32[8,32,128]{2,1,0:T(8,128)S(1)} all-to-all(f32[8,32,128]{2,1,0:T(8,128)S(1)} %broadcast_in_dim.26), channel_id=1, replica_groups=mesh['rows'=8,'cols'=4] {'rows'}, dimensions={0} | all-to-all | bytes 262144 | tf_op jit(solution)/shard_map/all_to_all | solution.py:418
  90.3 1.9 %shard_map.74 = (f32[1,4096]{1,0:T(1,128)S(1)}, f32[1,1024]{1,0:T(1,128)S(1)}) custom-call(f32[1024,4096]{1,0:T(8,128)S(1)} %get-tuple-element.50.soft_ref, f32[1,4096]{1,0:T(1,128)S(1)} %bitcast.17), custom_call_target="tpu_custom_call" | custom-call | tf_op jit(solution)/shard_map/pallas_call | solution.py:328
  96.0 1.7 %shard_map.75 = (f32[1024,128]{1,0:T(8,128)S(1)}, f32[1024,128]{1,0:T(8,128)S(1)}, f32[1024,128]{1,0:T(8,128)S(1)}, f32[256,128]{1,0:T(8,128)S(1)}, f32[256,128]{1,0:T(8,128)S(1)}) custom-call(f32[1024,4096]{1,0:T(8,128)S(1)} %get-tuple-element.50.soft_ref, f32[1,1024]{1,0:T(1,128)S(1)} %get-tuple-element.52.inverse_ref, ...), custom_call_target="tpu_custom_call" | custom-call | tf_op jit(solution)/shard_map/pallas_call | solution.py:328
  97.8 2.0 %collective-permute-start.26 = (f32[256,128]{1,0:T(8,128)S(1)}, f32[256,128]{1,0:T(8,128)S(1)}, u32[]{:S(2)}, u32[]{:S(2)}) collective-permute-start(f32[256,128]{1,0:T(8,128)S(1)} %get-tuple-element.81), channel_id=1, source_target_pairs={{8,0},{16,8},{24,16},{28,24},{20,28},{12,20},{4,12},{0,4},{9,1},{1... | collective-permute-start | bytes 393224 | tf_op jit(solution)/shard_map/ppermute | solution.py:379
  99.9 6.8 %shard_map.76 = (f32[512,128]{1,0:T(8,128)S(1)}, f32[512,128]{1,0:T(8,128)S(1)}, f32[256,128]{1,0:T(8,128)S(1)}, f32[256,128]{1,0:T(8,128)S(1)}, f32[256,128]{1,...) custom-call(f32[1024,4096]{1,0:T(8,128)S(1)} %get-tuple-element.50.s, ...), custom_call_target="tpu_custom_call" | custom-call | tf_op jit(solution)/shard_map/pallas_call | solution.py:328
  107.1 1.7 %collective-permute-start.17 = (f32[256,128]{1,0:T(8,128)S(1)}, f32[256,128]{1,0:T(8,128)S(1)}, u32[]{:S(2)}, u32[]{:S(2)}) collective-permute-start(f32[256,128]{1,0:T(8,128)S(1)} %add.306), channel_id=1, source_target_pairs={{0,8},{8,16},{16,24},{24,28},{28,20},{20,12},{12,4},{4,0},{1,9},{9... | collective-permute-start | bytes 393224 | tf_op jit(solution)/shard_map/ppermute | solution.py:376
  108.9 2.0 %collective-permute-start.27 = (f32[256,128]{1,0:T(8,128)S(1)}, f32[256,128]{1,0:T(8,128)S(1)}, u32[]{:S(2)}, u32[]{:S(2)}) collective-permute-start(f32[256,128]{1,0:T(8,128)S(1)} %add.316), channel_id=1, source_target_pairs={{8,0},{16,8},{24,16},{28,24},{20,28},{12,20},{4,12},{0,4},{9,1},{1... | collective-permute-start | bytes 393224 | tf_op jit(solution)/shard_map/ppermute | solution.py:379
  112.9 1.7 %collective-permute-start.18 = (f32[256,128]{1,0:T(8,128)S(1)}, f32[256,128]{1,0:T(8,128)S(1)}, u32[]{:S(2)}, u32[]{:S(2)}) collective-permute-start(f32[256,128]{1,0:T(8,128)S(1)} %add.307), channel_id=1, source_target_pairs={{0,8},{8,16},{16,24},{24,28},{28,20},{20,12},{12,4},{4,0},{1,9},{9... | collective-permute-start | bytes 393224 | tf_op jit(solution)/shard_map/ppermute | solution.py:376
  114.6 1.5 %collective-permute-start.24 = (f32[256,128]{1,0:T(8,128)S(1)}, f32[256,128]{1,0:T(8,128)S(1)}, u32[]{:S(2)}, u32[]{:S(2)}) collective-permute-start(f32[256,128]{1,0:T(8,128)S(1)} %add.313), channel_id=1, source_target_pairs={{0,8},{8,16},{16,24},{24,28},{28,20},{20,12},{12,4},{4,0},{1,9},{9... | collective-permute-start | bytes 393224 | tf_op jit(solution)/shard_map/ppermute | solution.py:376
  118.1 2.0 %collective-permute-start.22 = (f32[256,128]{1,0:T(8,128)S(1)}, f32[256,128]{1,0:T(8,128)S(1)}, u32[]{:S(2)}, u32[]{:S(2)}) collective-permute-start(f32[256,128]{1,0:T(8,128)S(1)} %add.311), channel_id=1, source_target_pairs={{8,0},{16,8},{24,16},{28,24},{20,28},{12,20},{4,12},{0,4},{9,1},{1... | collective-permute-start | bytes 393224 | tf_op jit(solution)/shard_map/ppermute | solution.py:379
  120.2 1.3 collective-permute-start.25
  121.6 1.3 collective-permute-start.13
  124.7 1.3 collective-permute-done.19
  126.4 2.4 %collective-permute-done.25 = f32[256,128]{1,0:T(8,128)S(1)} collective-permute-done((f32[256,128]{1,0:T(8,128)S(1)}, f32[256,128]{1,0:T(8,128)S(1)}, u32[]{:S(2)}, u32[]{:S(2)}) %collective-permute-start.25) | collective-permute-done | bytes 131104 | tf_op jit(solution)/shard_map/ppermute | solution.py:376
  129.9 1.8 %collective-permute-start.30 = (f32[256,128]{1,0:T(8,128)S(1)}, f32[256,128]{1,0:T(8,128)S(1)}, u32[]{:S(2)}, u32[]{:S(2)}) collective-permute-start(f32[256,128]{1,0:T(8,128)S(1)} %add_add_fusion.1.refs_3_), channel_id=1, source_target_pairs={{8,0},{16,8},{24,16},{28,24},{20,28},{12,20},{4,12},{0,4},{9,1},{1... | collective-permute-start | bytes 393224 | tf_op jit(solution)/shard_map/ppermute | solution.py:379
  131.9 2.0 %collective-permute-start.37 = (f32[256,128]{1,0:T(8,128)S(1)}, f32[256,128]{1,0:T(8,128)S(1)}, u32[]{:S(2)}, u32[]{:S(2)}) collective-permute-start(f32[256,128]{1,0:T(8,128)S(1)} %collective-permute-done.36.refs_17_), channel_id=1, source_target_pairs={{0,8},{8,16},{16,24},{24,28},{28,20},{20,12},{12,4},{4,0},{1,9},{9... | collective-permute-start | bytes 393224 | tf_op jit(solution)/shard_map/ppermute | solution.py:376
  136.8 1.6 %collective-permute-start.42 = (f32[256,128]{1,0:T(8,128)S(1)}, f32[256,128]{1,0:T(8,128)S(1)}, u32[]{:S(2)}, u32[]{:S(2)}) collective-permute-start(f32[256,128]{1,0:T(8,128)S(1)} %collective-permute-done.41.refs_18_), channel_id=1, source_target_pairs={{0,8},{8,16},{16,24},{24,28},{28,20},{20,12},{12,4},{4,0},{1,9},{9... | collective-permute-start | bytes 393224 | tf_op jit(solution)/shard_map/ppermute | solution.py:376
  139.1 2.1 %collective-permute-done.33.refs_8_ = f32[256,128]{1,0:T(8,128)S(1)} collective-permute-done((f32[256,128]{1,0:T(8,128)S(1)}, f32[256,128]{1,0:T(8,128)S(1)}, u32[]{:S(2)}, u32[]{:S(2)}) %collective-permute-start.33) | collective-permute-done | bytes 131104 | tf_op jit(solution)/shard_map/ppermute | solution.py:379
  141.2 2.6 %collective-permute-done.32.refs_7_ = f32[256,128]{1,0:T(8,128)S(1)} collective-permute-done((f32[256,128]{1,0:T(8,128)S(1)}, f32[256,128]{1,0:T(8,128)S(1)}, u32[]{:S(2)}, u32[]{:S(2)}) %collective-permute-start.32) | collective-permute-done | bytes 131104 | tf_op jit(solution)/shard_map/ppermute | solution.py:379
  143.8 2.0 %collective-permute-start.43 = (f32[256,128]{1,0:T(8,128)S(1)}, f32[256,128]{1,0:T(8,128)S(1)}, u32[]{:S(2)}, u32[]{:S(2)}) collective-permute-start(f32[256,128]{1,0:T(8,128)S(1)} %collective-permute-done.42.refs_16_), channel_id=1, source_target_pairs={{0,8},{8,16},{16,24},{24,28},{28,20},{20,12},{12,4},{4,0},{1,9},{9... | collective-permute-start | bytes 393224 | tf_op jit(solution)/shard_map/ppermute | solution.py:376
  147.9 2.3 %collective-permute-done.34.refs_9_ = f32[256,128]{1,0:T(8,128)S(1)} collective-permute-done((f32[256,128]{1,0:T(8,128)S(1)}, f32[256,128]{1,0:T(8,128)S(1)}, u32[]{:S(2)}, u32[]{:S(2)}) %collective-permute-start.34) | collective-permute-done | bytes 131104 | tf_op jit(solution)/shard_map/ppermute | solution.py:379
  151.8 1.6 %shard_map.77 = (f32[1024,128]{1,0:T(8,128)}, f32[4096,128]{1,0:T(8,128)}) custom-call(f32[256,128]{1,0:T(8,128)S(1)} %slice_add_fusion.refs_0_, f32[256,128]{1,0:T(8,128)S(1)} %collective-permute-done.14.refs_1_, f32[512,128]{1,0:T(8,128)S(1)} %collective-permute-done.15.refs_2_, f32[256,128]{1,0:T(8,128)S(1)} %add_add_fusion.1.refs_3_, ...), custom_call_target="tpu_custom_call" | custom-call | tf_op jit(solution)/shard_map/pallas_call | solution.py:471
  (96 shorter events, 28.3 us)
Async XLA Ops:
  97.8 9.3 %collective-permute-start.16 = (f32[256,128]{1,0:T(8,128)S(1)}, f32[256,128]{1,0:T(8,128)S(1)}, u32[]{:S(2)}, u32[]{:S(2)}) collective-permute-start(f32[256,128]{1,0:T(8,128)S(1)} %get-tuple-element.70), channel_id=1, source_target_pairs={{0,8},{8,16},{16,24},{24,28},{28,20},{20,12},{12,4},{4,0},{1,9},{9... | collective-permute-start | bytes 393224 | tf_op jit(solution)/shard_map/ppermute | solution.py:376
  97.8 11.1 %collective-permute-start.26 = (f32[256,128]{1,0:T(8,128)S(1)}, f32[256,128]{1,0:T(8,128)S(1)}, u32[]{:S(2)}, u32[]{:S(2)}) collective-permute-start(f32[256,128]{1,0:T(8,128)S(1)} %get-tuple-element.81), channel_id=1, source_target_pairs={{8,0},{16,8},{24,16},{28,24},{20,28},{12,20},{4,12},{0,4},{9,1},{1... | collective-permute-start | bytes 393224 | tf_op jit(solution)/shard_map/ppermute | solution.py:379
  106.7 5.0 %collective-permute-start.20 = (f32[256,128]{1,0:T(8,128)S(1)}, f32[256,128]{1,0:T(8,128)S(1)}, u32[]{:S(2)}, u32[]{:S(2)}) collective-permute-start(f32[256,128]{1,0:T(8,128)S(1)} %get-tuple-element.73), channel_id=1, source_target_pairs={{8,0},{16,8},{24,16},{28,24},{20,28},{12,20},{4,12},{0,4},{9,1},{1... | collective-permute-start | bytes 393224 | tf_op jit(solution)/shard_map/ppermute | solution.py:379
  107.1 5.7 %collective-permute-start.17 = (f32[256,128]{1,0:T(8,128)S(1)}, f32[256,128]{1,0:T(8,128)S(1)}, u32[]{:S(2)}, u32[]{:S(2)}) collective-permute-start(f32[256,128]{1,0:T(8,128)S(1)} %add.306), channel_id=1, source_target_pairs={{0,8},{8,16},{16,24},{24,28},{28,20},{20,12},{12,4},{4,0},{1,9},{9... | collective-permute-start | bytes 393224 | tf_op jit(solution)/shard_map/ppermute | solution.py:376
  108.8 5.7 %collective-permute-start.23 = (f32[256,128]{1,0:T(8,128)S(1)}, f32[256,128]{1,0:T(8,128)S(1)}, u32[]{:S(2)}, u32[]{:S(2)}) collective-permute-start(f32[256,128]{1,0:T(8,128)S(1)} %get-tuple-element.77), channel_id=1, source_target_pairs={{0,8},{8,16},{16,24},{24,28},{28,20},{20,12},{12,4},{4,0},{1,9},{9... | collective-permute-start | bytes 393224 | tf_op jit(solution)/shard_map/ppermute | solution.py:376
  108.9 12.7 %collective-permute-start.12 = (f32[512,128]{1,0:T(8,128)S(1)}, f32[512,128]{1,0:T(8,128)S(1)}, u32[]{:S(2)}, u32[]{:S(2)}) collective-permute-start(f32[512,128]{1,0:T(8,128)S(1)} %get-tuple-element.65), channel_id=1, source_target_pairs={{0,1},{1,0},{2,3},{3,2},{4,5},{5,4},{6,7},{7,6},{8,9},{9,8},{10,11... | collective-permute-start | bytes 786440 | tf_op jit(solution)/shard_map/ppermute | solution.py:353
  108.9 7.2 %collective-permute-start.27 = (f32[256,128]{1,0:T(8,128)S(1)}, f32[256,128]{1,0:T(8,128)S(1)}, u32[]{:S(2)}, u32[]{:S(2)}) collective-permute-start(f32[256,128]{1,0:T(8,128)S(1)} %add.316), channel_id=1, source_target_pairs={{8,0},{16,8},{24,16},{28,24},{20,28},{12,20},{4,12},{0,4},{9,1},{1... | collective-permute-start | bytes 393224 | tf_op jit(solution)/shard_map/ppermute | solution.py:379
  111.7 6.3 %collective-permute-start.21 = (f32[256,128]{1,0:T(8,128)S(1)}, f32[256,128]{1,0:T(8,128)S(1)}, u32[]{:S(2)}, u32[]{:S(2)}) collective-permute-start(f32[256,128]{1,0:T(8,128)S(1)} %add.310), channel_id=1, source_target_pairs={{8,0},{16,8},{24,16},{28,24},{20,28},{12,20},{4,12},{0,4},{9,1},{1... | collective-permute-start | bytes 393224 | tf_op jit(solution)/shard_map/ppermute | solution.py:379
  112.9 7.2 %collective-permute-start.18 = (f32[256,128]{1,0:T(8,128)S(1)}, f32[256,128]{1,0:T(8,128)S(1)}, u32[]{:S(2)}, u32[]{:S(2)}) collective-permute-start(f32[256,128]{1,0:T(8,128)S(1)} %add.307), channel_id=1, source_target_pairs={{0,8},{8,16},{16,24},{24,28},{28,20},{20,12},{12,4},{4,0},{1,9},{9... | collective-permute-start | bytes 393224 | tf_op jit(solution)/shard_map/ppermute | solution.py:376
  114.6 5.6 %collective-permute-start.24 = (f32[256,128]{1,0:T(8,128)S(1)}, f32[256,128]{1,0:T(8,128)S(1)}, u32[]{:S(2)}, u32[]{:S(2)}) collective-permute-start(f32[256,128]{1,0:T(8,128)S(1)} %add.313), channel_id=1, source_target_pairs={{0,8},{8,16},{16,24},{24,28},{28,20},{20,12},{12,4},{4,0},{1,9},{9... | collective-permute-start | bytes 393224 | tf_op jit(solution)/shard_map/ppermute | solution.py:376
  116.2 6.8 %collective-permute-start.28 = (f32[256,128]{1,0:T(8,128)S(1)}, f32[256,128]{1,0:T(8,128)S(1)}, u32[]{:S(2)}, u32[]{:S(2)}) collective-permute-start(f32[256,128]{1,0:T(8,128)S(1)} %add.317), channel_id=1, source_target_pairs={{8,0},{16,8},{24,16},{28,24},{20,28},{12,20},{4,12},{0,4},{9,1},{1... | collective-permute-start | bytes 393224 | tf_op jit(solution)/shard_map/ppermute | solution.py:379
  118.1 6.7 %collective-permute-start.22 = (f32[256,128]{1,0:T(8,128)S(1)}, f32[256,128]{1,0:T(8,128)S(1)}, u32[]{:S(2)}, u32[]{:S(2)}) collective-permute-start(f32[256,128]{1,0:T(8,128)S(1)} %add.311), channel_id=1, source_target_pairs={{8,0},{16,8},{24,16},{28,24},{20,28},{12,20},{4,12},{0,4},{9,1},{1... | collective-permute-start | bytes 393224 | tf_op jit(solution)/shard_map/ppermute | solution.py:379
  120.1 5.9 %collective-permute-start.19 = (f32[256,128]{1,0:T(8,128)S(1)}, f32[256,128]{1,0:T(8,128)S(1)}, u32[]{:S(2)}, u32[]{:S(2)}) collective-permute-start(f32[256,128]{1,0:T(8,128)S(1)} %add.308), channel_id=1, source_target_pairs={{0,8},{8,16},{16,24},{24,28},{28,20},{20,12},{12,4},{4,0},{1,9},{9... | collective-permute-start | bytes 393224 | tf_op jit(solution)/shard_map/ppermute | solution.py:376
  120.2 8.6 %collective-permute-start.25 = (f32[256,128]{1,0:T(8,128)S(1)}, f32[256,128]{1,0:T(8,128)S(1)}, u32[]{:S(2)}, u32[]{:S(2)}) collective-permute-start(f32[256,128]{1,0:T(8,128)S(1)} %add.314), channel_id=1, source_target_pairs={{0,8},{8,16},{16,24},{24,28},{28,20},{20,12},{12,4},{4,0},{1,9},{9... | collective-permute-start | bytes 393224 | tf_op jit(solution)/shard_map/ppermute | solution.py:376
  121.6 7.3 %collective-permute-start.13 = (f32[256,128]{1,0:T(8,128)S(1)}, f32[256,128]{1,0:T(8,128)S(1)}, u32[]{:S(2)}, u32[]{:S(2)}) collective-permute-start(f32[256,128]{1,0:T(8,128)S(1)} %slice.9), channel_id=1, source_target_pairs={{0,2},{1,3},{2,0},{3,1},{4,6},{5,7},{6,4},{7,5},{8,10},{9,11},{10,... | collective-permute-start | bytes 393224 | tf_op jit(solution)/shard_map/ppermute | solution.py:353
  123.0 5.9 %collective-permute-start.29 = (f32[256,128]{1,0:T(8,128)S(1)}, f32[256,128]{1,0:T(8,128)S(1)}, u32[]{:S(2)}, u32[]{:S(2)}) collective-permute-start(f32[256,128]{1,0:T(8,128)S(1)} %add.318), channel_id=1, source_target_pairs={{8,0},{16,8},{24,16},{28,24},{20,28},{12,20},{4,12},{0,4},{9,1},{1... | collective-permute-start | bytes 393224 | tf_op jit(solution)/shard_map/ppermute | solution.py:379
  126.1 5.8 %collective-permute-start.36 = (f32[256,128]{1,0:T(8,128)S(1)}, f32[256,128]{1,0:T(8,128)S(1)}, u32[]{:S(2)}, u32[]{:S(2)}) collective-permute-start(f32[256,128]{1,0:T(8,128)S(1)} %add_add_fusion.1.refs_3_), channel_id=1, source_target_pairs={{0,8},{8,16},{16,24},{24,28},{28,20},{20,12},{12,4},{4,0},{1,9},{9... | collective-permute-start | bytes 393224 | tf_op jit(solution)/shard_map/ppermute | solution.py:376
  128.9 6.1 %collective-permute-start.31 = (f32[256,128]{1,0:T(8,128)S(1)}, f32[256,128]{1,0:T(8,128)S(1)}, u32[]{:S(2)}, u32[]{:S(2)}) collective-permute-start(f32[256,128]{1,0:T(8,128)S(1)} %add_add_fusion.refs_4_), channel_id=1, source_target_pairs={{8,0},{16,8},{24,16},{28,24},{20,28},{12,20},{4,12},{0,4},{9,1},{1... | collective-permute-start | bytes 393224 | tf_op jit(solution)/shard_map/ppermute | solution.py:379
  129.0 5.9 %collective-permute-start.14 = (f32[256,128]{1,0:T(8,128)S(1)}, f32[256,128]{1,0:T(8,128)S(1)}, u32[]{:S(2)}, u32[]{:S(2)}) collective-permute-start(f32[256,128]{1,0:T(8,128)S(1)} %slice_add_fusion.refs_0_), channel_id=1, source_target_pairs={{0,2},{1,3},{2,0},{3,1},{4,6},{5,7},{6,4},{7,5},{8,10},{9,11},{10,... | collective-permute-start | bytes 393224 | tf_op jit(solution)/shard_map/ppermute | solution.py:353
  129.9 6.4 %collective-permute-start.30 = (f32[256,128]{1,0:T(8,128)S(1)}, f32[256,128]{1,0:T(8,128)S(1)}, u32[]{:S(2)}, u32[]{:S(2)}) collective-permute-start(f32[256,128]{1,0:T(8,128)S(1)} %add_add_fusion.1.refs_3_), channel_id=1, source_target_pairs={{8,0},{16,8},{24,16},{28,24},{20,28},{12,20},{4,12},{0,4},{9,1},{1... | collective-permute-start | bytes 393224 | tf_op jit(solution)/shard_map/ppermute | solution.py:379
  131.7 5.1 %collective-permute-start.41 = (f32[256,128]{1,0:T(8,128)S(1)}, f32[256,128]{1,0:T(8,128)S(1)}, u32[]{:S(2)}, u32[]{:S(2)}) collective-permute-start(f32[256,128]{1,0:T(8,128)S(1)} %add_add_fusion.refs_4_), channel_id=1, source_target_pairs={{0,8},{8,16},{16,24},{24,28},{28,20},{20,12},{12,4},{4,0},{1,9},{9... | collective-permute-start | bytes 393224 | tf_op jit(solution)/shard_map/ppermute | solution.py:376
  131.9 6.4 %collective-permute-start.37 = (f32[256,128]{1,0:T(8,128)S(1)}, f32[256,128]{1,0:T(8,128)S(1)}, u32[]{:S(2)}, u32[]{:S(2)}) collective-permute-start(f32[256,128]{1,0:T(8,128)S(1)} %collective-permute-done.36.refs_17_), channel_id=1, source_target_pairs={{0,8},{8,16},{16,24},{24,28},{28,20},{20,12},{12,4},{4,0},{1,9},{9... | collective-permute-start | bytes 393224 | tf_op jit(solution)/shard_map/ppermute | solution.py:376
  134.9 6.3 %collective-permute-start.33 = (f32[256,128]{1,0:T(8,128)S(1)}, f32[256,128]{1,0:T(8,128)S(1)}, u32[]{:S(2)}, u32[]{:S(2)}) collective-permute-start(f32[256,128]{1,0:T(8,128)S(1)} %collective-permute-done.31.refs_6_), channel_id=1, source_target_pairs={{8,0},{16,8},{24,16},{28,24},{20,28},{12,20},{4,12},{0,4},{9,1},{1... | collective-permute-start | bytes 393224 | tf_op jit(solution)/shard_map/ppermute | solution.py:379
  134.9 12.9 %collective-permute-start.15 = (f32[512,128]{1,0:T(8,128)S(1)}, f32[512,128]{1,0:T(8,128)S(1)}, u32[]{:S(2)}, u32[]{:S(2)}) collective-permute-start(f32[512,128]{1,0:T(8,128)S(1)} %pad_maximum_fusion), channel_id=1, source_target_pairs={{0,1},{1,0},{2,3},{3,2},{4,5},{5,4},{6,7},{7,6},{8,9},{9,8},{10,11... | collective-permute-start | bytes 786440 | tf_op jit(solution)/shard_map/ppermute | solution.py:353
  136.3 7.5 %collective-permute-start.32 = (f32[256,128]{1,0:T(8,128)S(1)}, f32[256,128]{1,0:T(8,128)S(1)}, u32[]{:S(2)}, u32[]{:S(2)}) collective-permute-start(f32[256,128]{1,0:T(8,128)S(1)} %collective-permute-done.30.refs_5_), channel_id=1, source_target_pairs={{8,0},{16,8},{24,16},{28,24},{20,28},{12,20},{4,12},{0,4},{9,1},{1... | collective-permute-start | bytes 393224 | tf_op jit(solution)/shard_map/ppermute | solution.py:379
  136.8 7.0 %collective-permute-start.42 = (f32[256,128]{1,0:T(8,128)S(1)}, f32[256,128]{1,0:T(8,128)S(1)}, u32[]{:S(2)}, u32[]{:S(2)}) collective-permute-start(f32[256,128]{1,0:T(8,128)S(1)} %collective-permute-done.41.refs_18_), channel_id=1, source_target_pairs={{0,8},{8,16},{16,24},{24,28},{28,20},{20,12},{12,4},{4,0},{1,9},{9... | collective-permute-start | bytes 393224 | tf_op jit(solution)/shard_map/ppermute | solution.py:376
  138.3 7.5 %collective-permute-start.38 = (f32[256,128]{1,0:T(8,128)S(1)}, f32[256,128]{1,0:T(8,128)S(1)}, u32[]{:S(2)}, u32[]{:S(2)}) collective-permute-start(f32[256,128]{1,0:T(8,128)S(1)} %collective-permute-done.37.refs_15_), channel_id=1, source_target_pairs={{0,8},{8,16},{16,24},{24,28},{28,20},{20,12},{12,4},{4,0},{1,9},{9... | collective-permute-start | bytes 393224 | tf_op jit(solution)/shard_map/ppermute | solution.py:376
  141.2 5.6 %collective-permute-start.35 = (f32[256,128]{1,0:T(8,128)S(1)}, f32[256,128]{1,0:T(8,128)S(1)}, u32[]{:S(2)}, u32[]{:S(2)}) collective-permute-start(f32[256,128]{1,0:T(8,128)S(1)} %collective-permute-done.33.refs_8_), channel_id=1, source_target_pairs={{8,0},{16,8},{24,16},{28,24},{20,28},{12,20},{4,12},{0,4},{9,1},{1... | collective-permute-start | bytes 393224 | tf_op jit(solution)/shard_map/ppermute | solution.py:379
  143.8 6.3 %collective-permute-start.34 = (f32[256,128]{1,0:T(8,128)S(1)}, f32[256,128]{1,0:T(8,128)S(1)}, u32[]{:S(2)}, u32[]{:S(2)}) collective-permute-start(f32[256,128]{1,0:T(8,128)S(1)} %collective-permute-done.32.refs_7_), channel_id=1, source_target_pairs={{8,0},{16,8},{24,16},{28,24},{20,28},{12,20},{4,12},{0,4},{9,1},{1... | collective-permute-start | bytes 393224 | tf_op jit(solution)/shard_map/ppermute | solution.py:379
  143.8 6.3 %collective-permute-start.43 = (f32[256,128]{1,0:T(8,128)S(1)}, f32[256,128]{1,0:T(8,128)S(1)}, u32[]{:S(2)}, u32[]{:S(2)}) collective-permute-start(f32[256,128]{1,0:T(8,128)S(1)} %collective-permute-done.42.refs_16_), channel_id=1, source_target_pairs={{0,8},{8,16},{16,24},{24,28},{28,20},{20,12},{12,4},{4,0},{1,9},{9... | collective-permute-start | bytes 393224 | tf_op jit(solution)/shard_map/ppermute | solution.py:376
  145.8 5.0 %collective-permute-start.39 = (f32[256,128]{1,0:T(8,128)S(1)}, f32[256,128]{1,0:T(8,128)S(1)}, u32[]{:S(2)}, u32[]{:S(2)}) collective-permute-start(f32[256,128]{1,0:T(8,128)S(1)} %collective-permute-done.38.refs_13_), channel_id=1, source_target_pairs={{0,8},{8,16},{16,24},{24,28},{28,20},{20,12},{12,4},{4,0},{1,9},{9... | collective-permute-start | bytes 393224 | tf_op jit(solution)/shard_map/ppermute | solution.py:376
  146.8 5.0 %collective-permute-start.40 = (f32[256,128]{1,0:T(8,128)S(1)}, f32[256,128]{1,0:T(8,128)S(1)}, u32[]{:S(2)}, u32[]{:S(2)}) collective-permute-start(f32[256,128]{1,0:T(8,128)S(1)} %collective-permute-done.35.refs_10_), channel_id=1, source_target_pairs={{8,0},{16,8},{24,16},{28,24},{20,28},{12,20},{4,12},{0,4},{9,1},{1... | collective-permute-start | bytes 393224 | tf_op jit(solution)/shard_map/ppermute | solution.py:379
  (14 other events, 81.5 us)

commit v4 on v3

--- a/solution.py
+++ b/solution.py
@@ -14,7 +14,7 @@
 LANES = 128
 WIDE = 512
 TALL = 256
-LIMIT = 20 * 2**20
+LIMIT = 8 * 2**20
 F32 = jnp.float32
 
 
@@ -50,7 +50,7 @@
     return row_form(partial_ref[...])
 
 
-def column_sums(tile_ref, weights_ref, out_ref):
+def column_sums(tile_ref, weights_ref, out_ref, scale_ref=None):
     starts = range(0, tile_ref.shape[1], LANES)
 
     def body(block, accs):
@@ -62,7 +62,8 @@
 
     accs = lax.fori_loop(0, tile_ref.shape[0] // 16, body, tuple(jnp.zeros((8, LANES), F32) for _ in starts))
     for acc, at in zip(accs, starts):
-        out_ref[:, at:at + LANES] = jnp.sum(acc, axis=0, keepdims=True)
+        total = jnp.sum(acc, axis=0, keepdims=True)
+        out_ref[:, at:at + LANES] = total if scale_ref is None else total * scale_ref[:, at:at + LANES]
 
 
 def exponent_block(crawl_ref, bench_ref, shift_ref, rows, columns):
@@ -155,34 +156,24 @@
 
 def soft_kernel(parts, tile_ref, top_ref, level_ref, *refs):
     part_refs = refs[:parts]
-    crawl_ref, bench_ref, shift_ref, soft_ref, mass_ref, sums_ref, partial, weights, scale = refs[parts:]
+    crawl_ref, bench_ref, shift_ref, soft_ref, left_ref, right_ref, mass_ref, sums_ref, partial, weights = refs[parts:]
     logs = log_sum([p[...] for p in part_refs])
-    mass_ref[...] = jnp.exp2(logs)
     lowest = jnp.min(logs)
-    height = 64
 
     @pl.when(lowest >= LOWEST)
     def _():
-        weights[...] = column_form(jnp.exp2(top_ref[...] - level_ref[...]))
-        scale[...] = jnp.exp2(-logs)
-
-        def body(block, _):
-            rows = pl.ds(pl.multiple_of(block * height, height), height)
-            weight = weights[rows, :]
-            acc = jnp.zeros((height, LANES), F32)
-            for at in range(0, tile_ref.shape[1], LANES):
-                value = tile_ref[rows, at:at + LANES] * weight * scale[:, at:at + LANES]
-                soft_ref[rows, at:at + LANES] = value
-                acc += value
-            partial[rows, :] = acc
-            return _
-
-        lax.fori_loop(0, tile_ref.shape[0] // height, body, 0)
+        left = jnp.exp2(top_ref[...] - level_ref[...])
+        left_ref[...] = left
+        right_ref[...] = jnp.exp2(-logs)
+        mass_ref[...] = jnp.ones_like(logs)
+        sums_ref[...] = row_sums(tile_ref, right_ref, partial) * left
 
     @pl.when(lowest < LOWEST)
     def _():
+        left_ref[...] = jnp.ones_like(left_ref)
+        mass_ref[...] = jnp.exp2(logs)
+        right_ref[...] = logs
         weights[...] = column_form(level_ref[...])
-        scale[...] = logs
         partial[...] = jnp.zeros_like(partial)
 
         def body(block, _):
@@ -192,7 +183,7 @@
             def column_block(column, _):
                 columns = pl.ds(pl.multiple_of(column * WIDE, WIDE), WIDE)
                 exponent = exponent_block(crawl_ref, bench_ref, shift_ref, rows, columns)
-                value = jnp.exp2(exponent - level - scale[:, columns])
+                value = jnp.exp2(exponent - level - right_ref[:, columns])
                 soft_ref[rows, columns] = value
                 partial[rows, :] += sum(value[:, lane:lane + LANES] for lane in range(0, WIDE, LANES))
                 return _
@@ -200,36 +191,36 @@
             return lax.fori_loop(0, tile_ref.shape[1] // WIDE, column_block, _)
 
         lax.fori_loop(0, tile_ref.shape[0] // TALL, body, 0)
-
-    sums_ref[...] = row_form(partial[...])
-
-
-def second_column_kernel(parts, soft_ref, *refs):
+        right_ref[...] = jnp.ones_like(right_ref)
+        sums_ref[...] = row_form(partial[...])
+
+
+def second_column_kernel(parts, soft_ref, left_ref, right_ref, *refs):
     part_refs, (inverse_ref, out_ref, weights) = refs[:parts], refs[parts:]
-    inverse = 1.0 / sum(p[...] for p in part_refs)
+    inverse = left_ref[...] / sum(p[...] for p in part_refs)
     inverse_ref[...] = inverse
     weights[...] = column_form(inverse)
-    column_sums(soft_ref, weights, out_ref)
-
-
-def second_row_kernel(parts, soft_ref, inverse_ref, cotangent_ref, *refs):
+    column_sums(soft_ref, weights, out_ref, right_ref)
+
+
+def second_row_kernel(parts, soft_ref, inverse_ref, right_ref, cotangent_ref, *refs):
     part_refs, (scaled_ref, out_ref, partial) = refs[:parts], refs[parts:]
-    scaled_ref[...] = cotangent_ref[...] / sum(p[...] for p in part_refs)
+    scaled_ref[...] = cotangent_ref[...] / sum(p[...] for p in part_refs) * right_ref[...]
     out_ref[...] = row_sums(soft_ref, scaled_ref, partial) * inverse_ref[...]
 
 
-def first_column_kernel(parts, soft_ref, inverse_ref, cotangent_ref, *refs):
+def first_column_kernel(parts, soft_ref, inverse_ref, right_ref, cotangent_ref, *refs):
     part_refs, (scaled_ref, out_ref, weights) = refs[:parts], refs[parts:]
     scaled = (cotangent_ref[...] - sum(p[...] for p in part_refs)) * inverse_ref[...]
     scaled_ref[...] = scaled
     weights[...] = column_form(-scaled)
-    column_sums(soft_ref, weights, out_ref)
-
-
-def first_row_kernel(parts, soft_ref, *refs):
+    column_sums(soft_ref, weights, out_ref, right_ref)
+
+
+def first_row_kernel(parts, soft_ref, left_ref, right_ref, *refs):
     part_refs, (back_ref, out_ref, partial) = refs[:parts], refs[parts:]
-    back_ref[...] = sum(p[...] for p in part_refs)
-    out_ref[...] = -row_sums(soft_ref, back_ref, partial)
+    back_ref[...] = sum(p[...] for p in part_refs) * right_ref[...]
+    out_ref[...] = -row_sums(soft_ref, back_ref, partial) * left_ref[...]
 
 
 def ring_order(n):
@@ -242,11 +233,41 @@
     return lax.select(place < n // 2, 2 * place, 2 * (n - 1 - place) + 1)
 
 
-def far_kernel(parts, n, soft_ref, inverse_ref, scaled2_ref, back_ref, mass_ref, scaled_ref, crawl_ref, *refs):
-    part_refs, (first, second, third, *piece_refs, flat) = refs[:parts], refs[parts:]
-    first[...] = column_form(-inverse_ref[...])
-    second[...] = column_form(-scaled_ref[...])
-    third[...] = column_form(-sum(p[...] for p in part_refs))
+def early_kernel(soft_ref, inverse_ref, scaled_ref, left_ref, scaled2_ref, right_ref, back_ref, mass_ref, *refs):
+    first_ref, early_ref, *row_refs = refs
+    height = 64
+    for row_ref, row in zip(row_refs, (inverse_ref, scaled_ref, left_ref)):
+        row_ref[...] = column_form(-row[...])
+
+    def body(block, _):
+        rows = pl.ds(pl.multiple_of(block * height, height), height)
+        a, b, c = (ref[rows, :] for ref in row_refs)
+        for at in range(0, soft_ref.shape[1], LANES):
+            span = slice(at, at + LANES)
+            factor = a * scaled2_ref[:, span] + b * right_ref[:, span] + c * back_ref[:, span]
+            early_ref[rows, span] = soft_ref[rows, span] * factor
+        return _
+
+    lax.fori_loop(0, soft_ref.shape[0] // height, body, 0)
+    mass = mass_ref[...]
+
+    @pl.when(jnp.max(jnp.abs(mass - 1.0)) > 0.0)
+    def _():
+        def scale(block, _):
+            rows = pl.ds(pl.multiple_of(block * 8, 8), 8)
+            first_ref[rows, :] = soft_ref[rows, :] * mass_ref[...]
+            return _
+
+        lax.fori_loop(0, soft_ref.shape[0] // 8, scale, 0)
+
+
+def score_grad(early, first, last):
+    return (early + first * last).astype(jnp.bfloat16)
+
+
+def far_kernel(parts, n, first_ref, early_ref, left_ref, crawl_ref, *refs):
+    part_refs, (last_ref, *piece_refs, flat) = refs[:parts], refs[parts:]
+    last_ref[...] = column_form(-left_ref[...] * sum(p[...] for p in part_refs))
     if not piece_refs:
         return
     width = flat.shape[1]
@@ -255,44 +276,42 @@
 
     def body(block, _):
         rows = pl.ds(pl.multiple_of(block * TALL, TALL), TALL)
-        a, b, c = first[rows, :], second[rows, :], third[rows, :]
+        last = last_ref[rows, :]
         pieces = []
         for lane in range(0, width, LANES):
             span = pl.ds(pl.multiple_of(start + lane, LANES), LANES)
-            factor = a * scaled2_ref[:, span] + b + (c * mass_ref[:, span] - back_ref[:, span])
-            pieces.append((soft_ref[rows, span] * factor).astype(jnp.bfloat16))
+            pieces.append(score_grad(early_ref[rows, span], first_ref[rows, span], last))
         grad = jnp.concatenate(pieces, axis=1)
         flat[...] += lax.dot_general(crawl_ref[rows, :], grad, (((0,), (0,)), ((), ())), preferred_element_type=F32)
         return _
 
-    lax.fori_loop(0, soft_ref.shape[0] // TALL, body, 0)
+    lax.fori_loop(0, first_ref.shape[0] // TALL, body, 0)
     half = width // 2
     for k, piece in enumerate(piece_refs):
         piece[...] = jnp.transpose(flat[:, k * half:(k + 1) * half])
 
 
-def gradient_kernel(n, places, soft_ref, first, second, third, scaled2_ref, back_ref, mass_ref, crawl_ref, bench_ref, *refs):
+def gradient_kernel(n, places, first_ref, early_ref, last_ref, crawl_ref, bench_ref, *refs):
     keep_ref, send_ref, *piece_refs, flat, whole, total = refs
     flat[...] = jnp.zeros_like(flat)
 
     def body(block, _):
         rows = pl.ds(pl.multiple_of(block * TALL, TALL), TALL)
-        a, b, c = first[rows, :], second[rows, :], third[rows, :]
+        last = last_ref[rows, :]
         x = crawl_ref[rows, :]
         acc = jnp.zeros((TALL, LANES), F32)
-        for at in range(0, soft_ref.shape[1], WIDE):
+        for at in range(0, first_ref.shape[1], WIDE):
             pieces = []
             for lane in range(at, at + WIDE, LANES):
                 span = slice(lane, lane + LANES)
-                factor = a * scaled2_ref[:, span] + b + (c * mass_ref[:, span] - back_ref[:, span])
-                pieces.append((soft_ref[rows, span] * factor).astype(jnp.bfloat16))
+                pieces.append(score_grad(early_ref[rows, span], first_ref[rows, span], last))
             grad = jnp.concatenate(pieces, axis=1)
             acc += jnp.dot(grad, bench_ref[at:at + WIDE, :], preferred_element_type=F32)
             flat[:, at:at + WIDE] += lax.dot_general(x, grad, (((0,), (0,)), ((), ())), preferred_element_type=F32)
         total[rows, :] = acc
         return _
 
-    lax.fori_loop(0, soft_ref.shape[0] // TALL, body, 0)
+    lax.fori_loop(0, first_ref.shape[0] // TALL, body, 0)
     me = lax.axis_index("cols")
     quarter = total.shape[0] // 4
     for k, (ref, low) in enumerate(((keep_ref, 0), (send_ref, 0), (keep_ref, quarter), (send_ref, quarter))):
@@ -411,9 +430,9 @@
         return spread(x, "cols", 4, join)
 
     def over_rows(x, join=sum):
-        if lax.axis_size("rows") > 8:
+        n = lax.axis_size("rows")
+        if n > 8:
             return spread(x, "rows", 4, join)
-        n = lax.axis_size("rows")
         copies = jnp.broadcast_to(x.reshape(1, -1, LANES), (n, columns // LANES, LANES))
         return [join(list(lax.all_to_all(copies, "rows", 0, 0))).reshape(1, columns)]
 
@@ -432,37 +451,42 @@
         functools.partial(column_level_kernel, len(parts)),
         [kept(tile), top, *parts, crawl, bench, shift], [row, column], [tall])
     parts = over_rows(local, log_sum)
-    soft, mass, local = call(
+    soft, left, right, mass, local = call(
         functools.partial(soft_kernel, len(parts)),
-        [kept(tile), top, level, *parts, crawl, bench, shift], [tile_shape, column, row],
-        [tall, tall, (1, columns)], aliases={0: 0})
+        [kept(tile), top, level, *parts, crawl, bench, shift], [tile_shape, row, column, column, row],
+        [tall, tall], aliases={0: 0})
+    soft = kept(soft)
     parts = over_cols(local)
-    inverse, local = call(functools.partial(second_column_kernel, len(parts)), [kept(soft), *parts], [row, column], [tall])
+    inverse, local = call(
+        functools.partial(second_column_kernel, len(parts)), [soft, left, right, *parts], [row, column], [tall])
     parts = over_rows(local)
     scaled2, local = call(
         functools.partial(second_row_kernel, len(parts)),
-        [kept(soft), inverse, col_cotangent, *parts], [column, row], [tall])
+        [soft, inverse, right, col_cotangent, *parts], [column, row], [tall])
     parts = over_cols(local)
     scaled, local = call(
         functools.partial(first_column_kernel, len(parts)),
-        [kept(soft), inverse, row_cotangent, *parts], [row, column], [tall])
+        [soft, inverse, right, row_cotangent, *parts], [row, column], [tall])
     parts = over_rows(local)
-    back, local = call(functools.partial(first_row_kernel, len(parts)), [kept(soft), *parts], [column, row], [tall])
+    back, local = call(
+        functools.partial(first_row_kernel, len(parts)), [soft, left, right, *parts], [column, row], [tall])
     parts = over_cols(local)
     n = lax.axis_size("rows")
     width = bench.shape[1]
     share = columns // n
     piece = shaped(share // 2, width)
     ahead = share % (2 * LANES) == 0
-    *factors, = call(
-        functools.partial(far_kernel, len(parts), n),
-        [kept(soft), inverse, scaled2, back, mass, scaled, crawl, *parts],
-        [shaped(*tall)] * 3 + [piece] * (2 * ahead), [(LANES, share)])
-    factors, far = factors[:3], factors[3:]
+    first, early = call(
+        early_kernel, [soft, inverse, scaled, left, scaled2, right, back, mass],
+        [tile_shape, tile_shape], [tall] * 3, aliases={0: 0})
+    first, early = kept(first), kept(early)
+    last, *far = call(
+        functools.partial(far_kernel, len(parts), n), [first, early, left, crawl, *parts],
+        [shaped(*tall)] + [piece] * (2 * ahead), [(LANES, share)])
     places = [at for at in range(n) if at != n // 2 or not ahead]
     keep, send, *pieces = call(
         functools.partial(gradient_kernel, n, places),
-        [kept(soft), *factors, scaled2, back, mass, crawl, bench],
+        [first, early, last, crawl, bench],
         [shaped(rows // 2, width)] * 2 + [piece] * (2 * len(places)), [(LANES, columns), (columns, LANES), tall])
     if ahead:
         pieces[n:n] = far

time: 154 us -> 158 us (1.026)
  Pallas kernels: 55 us -> 59.9 us
  starting transfers between devices: 36.9 us -> 34.9 us
    ppermute x14, waiting for transfers between devices: 5.13 us -> 16.7 us  [ahead(): return lax.ppermute(x, 'rows', up)]
    ppermute x14, waiting for transfers between devices: 13.6 us -> 4.38 us  [behind(): return lax.ppermute(x, 'rows', down)]
    pallas_call x8 -> x9, Pallas kernels: 45 us -> 49.9 us  [call(): pl.pallas_call(kernel, in_specs=[pl.BlockSpec(memory_space=pltpu.VMEM)] *...]
    ppermute x14, starting transfers between devices: 13.6 us -> 9.12 us  [ahead(): return lax.ppermute(x, 'rows', up)]
    ppermute x14, starting transfers between devices: 12.2 us -> 14.9 us  [behind(): return lax.ppermute(x, 'rows', down)]
  transfers between devices with their start and end apart: 44 -> 44, of which waited for: 22 -> 20; matrix products, arithmetic and copies ran while one was open for 0% -> 0% of each run, Pallas kernels for 4% -> 8%
where the time goes in v4:
time: 158 us
  Pallas kernels  59.9 us (38%)
  starting transfers between devices  34.9 us (22%)
  blocking collectives  32.9 us (21%)
  waiting for transfers between devices  28.6 us (18%)
    pallas_call x9, Pallas kernels, call(): pl.pallas_call(kernel, in_specs=[pl.BlockSpec(memory_space=pltpu.VMEM)] *...  49.9 us
    all_to_all x3, blocking collectives, over_rows(): lax.all_to_all(copies, 'rows', 0, 0)  32.9 us
    ppermute x14, waiting for transfers between devices, ahead(): return lax.ppermute(x, 'rows', up)  16.7 us
    ppermute x14, starting transfers between devices, behind(): return lax.ppermute(x, 'rows', down)  14.9 us
    ppermute x16, starting transfers between devices, exchange(): lax.ppermute(x, axis, [(i, i ^ k * stride) for i in range(n)])  10.9 us
    ppermute x14, starting transfers between devices, ahead(): return lax.ppermute(x, 'rows', up)  9.12 us
    pallas_call x1, Pallas kernels, per_device(): pl.pallas_call(row_level_kernel, in_specs=[pl.BlockSpec(memory_space=pltp...  8.39 us
    ppermute x16, waiting for transfers between devices, exchange(): lax.ppermute(x, axis, [(i, i ^ k * stride) for i in range(n)])  7.51 us
  transfers between devices with their start and end apart: 44, of which 20 were waited for; matrix products, arithmetic and copies ran while one was open for 0% of the time, Pallas kernels for 8%

profile of v4, /device:TPU:0, one launch (start us, length us, event | category | flops | bytes accessed | tf_op | source)
XLA Modules:
  0.0 157.8 jit_solution(5569947020871878380)
XLA Ops:
  0.6 8.4 %shard_map.68 = (f32[1024,4096]{1,0:T(8,128)S(1)}, f32[1,1024]{1,0:T(1,128)S(1)}, f32[1,1024]{1,0:T(1,128)S(1)}, bf16[1024,128]{1,0:T(8,128)(2,1)S(1)}, bf16[409...) custom-call(bf16[1024,128]{1,0:T(8,128)(2,1)} %crawl_hbm.1, bf16[4096,128]{1,0:T(8,128)(2,1)} %bench_hbm.1, f32[1,4096]{1,0:T(1,128)} %bitcast.31), custom_call_target="tpu_custom_call" | custom-call | tf_op jit(solution)/shard_map/pallas_call | solution.py:439
  9.5 2.6 %collective-permute-start.1 = (f32[1,1024]{1,0:T(1,128)S(1)}, f32[1,1024]{1,0:T(1,128)S(1)}, u32[]{:S(2)}, u32[]{:S(2)}) collective-permute-start(f32[1,1024]{1,0:T(1,128)S(1)} %get-tuple-element.46.refs_0_), channel_id=1, source_target_pairs={{0,2},{1,3},{2,0},{3,1},{4,6},{5,7},{6,4},{7,5},{8,10},{9,11},{10,... | collective-permute-start | bytes 12296 | tf_op jit(solution)/shard_map/ppermute | solution.py:372
  15.1 19.3 %shard_map.69 = (f32[1,1024]{1,0:T(1,128)S(1)}, f32[1,4096]{1,0:T(1,128)S(1)}) custom-call(f32[1024,4096]{1,0:T(8,128)S(1)} %get-tuple-element.44.tile_ref, f32[1,1024]{1,0:T(1,128)S(1)} %get-tuple-element.45.top_ref, f32[1,1024]{1,0:T(1,128)S(1)} %get-tuple-element.46.refs_0_, f32[1,1024]{1,0:T(1,128)S(1)} %collective-permute-done.refs_1_, ...), custom_call_target="tpu_custom_call" | custom-call | tf_op jit(solution)/shard_map/pallas_call | solution.py:347
  34.5 13.0 %all_to_all.15 = f32[8,32,128]{2,1,0:T(8,128)S(1)} all-to-all(f32[8,32,128]{2,1,0:T(8,128)S(1)} %broadcast_in_dim.22), channel_id=1, replica_groups=mesh['rows'=8,'cols'=4] {'rows'}, dimensions={0} | all-to-all | bytes 262144 | tf_op jit(solution)/shard_map/all_to_all | solution.py:437
  47.7 9.5 %shard_map.70 = (f32[1024,4096]{1,0:T(8,128)S(1)}, f32[1,1024]{1,0:T(1,128)S(1)}, f32[1,4096]{1,0:T(1,128)S(1)}, f32[1,4096]{1,0:T(1,128)S(1)}, f32[1,1024]{1,0:T(1,128)S(1)}) custom-call(f32[1024,4096]{1,0:T(8,128)S(1)} %get-tuple-element.44.tile_ref, f32[1,1024]{1,0:T(1,128)S(1)} %get-tuple-element.45.top_ref, ...), custom_call_target="tpu_custom_call", output_to_operand_aliasing={{0}: (0, {})} | custom-call | tf_op jit(solution)/shard_map/pallas_call | solution.py:347
  59.2 1.8 %collective-permute-done.4.refs_2_ = f32[1,1024]{1,0:T(1,128)S(1)} collective-permute-done((f32[1,1024]{1,0:T(1,128)S(1)}, f32[1,1024]{1,0:T(1,128)S(1)}, u32[]{:S(2)}, u32[]{:S(2)}) %collective-permute-start.4) | collective-permute-done | bytes 4128 | tf_op jit(solution)/shard_map/ppermute | solution.py:372
  61.0 2.0 %shard_map.71 = (f32[1,1024]{1,0:T(1,128)S(1)}, f32[1,4096]{1,0:T(1,128)S(1)}) custom-call(f32[1024,4096]{1,0:T(8,128)S(1)} %get-tuple-element.52.soft_ref, f32[1,1024]{1,0:T(1,128)S(1)} %get-tuple-element.53.left_ref, f32[1,4096]{1,0:T(1,128)S(1)} %get-tuple-element.54.right_ref, f32[1,1024]{1,0:T(1,128)S(1)} %get-tuple-element.55.refs_0_, ...), custom_call_target="tpu_custom_call" | custom-call | tf_op jit(solution)/shard_map/pallas_call | solution.py:347
  63.1 9.9 %all_to_all.16 = f32[8,32,128]{2,1,0:T(8,128)S(1)} all-to-all(f32[8,32,128]{2,1,0:T(8,128)S(1)} %broadcast_in_dim.24), channel_id=1, replica_groups=mesh['rows'=8,'cols'=4] {'rows'}, dimensions={0} | all-to-all | bytes 262144 | tf_op jit(solution)/shard_map/all_to_all | solution.py:437
  73.0 1.8 %shard_map.72 = (f32[1,4096]{1,0:T(1,128)S(1)}, f32[1,1024]{1,0:T(1,128)S(1)}) custom-call(f32[1024,4096]{1,0:T(8,128)S(1)} %get-tuple-element.52.soft_ref, f32[1,1024]{1,0:T(1,128)S(1)} %get-tuple-element.56.inverse_ref, f32[1,4096]{1,0:T(1,128)S(1)} %get-tuple-element.54.right_ref, f32[1,4096]{1,0:T(1,128)S(1)} %bitcast.21, f32[1,4096]{1,0:T(1,128)S(1)} %bitcast.17), custom_call_target="tpu_custom_call" | custom-call | tf_op jit(solution)/shard_map/pallas_call | solution.py:347
  76.7 1.8 %collective-permute-done.7.refs_2_ = f32[1,1024]{1,0:T(1,128)S(1)} collective-permute-done((f32[1,1024]{1,0:T(1,128)S(1)}, f32[1,1024]{1,0:T(1,128)S(1)}, u32[]{:S(2)}, u32[]{:S(2)}) %collective-permute-start.7) | collective-permute-done | bytes 4128 | tf_op jit(solution)/shard_map/ppermute | solution.py:372
  79.4 2.0 %shard_map.73 = (f32[1,1024]{1,0:T(1,128)S(1)}, f32[1,4096]{1,0:T(1,128)S(1)}) custom-call(f32[1024,4096]{1,0:T(8,128)S(1)} %get-tuple-element.52.soft_ref, f32[1,1024]{1,0:T(1,128)S(1)} %get-tuple-element.56.inverse_ref, f32[1,4096]{1,0:T(1,128)S(1)} %get-tuple-element.54.right_ref, f32[1,1024]{1,0:T(1,128)S(1)} %bitcast.22, ...), custom_call_target="tpu_custom_call" | custom-call | tf_op jit(solution)/shard_map/pallas_call | solution.py:347
  81.4 10.0 %all_to_all.17 = f32[8,32,128]{2,1,0:T(8,128)S(1)} all-to-all(f32[8,32,128]{2,1,0:T(8,128)S(1)} %broadcast_in_dim.26), channel_id=1, replica_groups=mesh['rows'=8,'cols'=4] {'rows'}, dimensions={0} | all-to-all | bytes 262144 | tf_op jit(solution)/shard_map/all_to_all | solution.py:437
  91.4 1.9 %shard_map.74 = (f32[1,4096]{1,0:T(1,128)S(1)}, f32[1,1024]{1,0:T(1,128)S(1)}) custom-call(f32[1024,4096]{1,0:T(8,128)S(1)} %get-tuple-element.52.soft_ref, f32[1,1024]{1,0:T(1,128)S(1)} %get-tuple-element.53.left_ref, f32[1,4096]{1,0:T(1,128)S(1)} %get-tuple-element.54.right_ref, f32[1,4096]{1,0:T(1,128)S(1)} %bitcast.16), custom_call_target="tpu_custom_call" | custom-call | tf_op jit(solution)/shard_map/pallas_call | solution.py:347
  95.5 6.4 %shard_map.75 = (f32[1024,4096]{1,0:T(8,128)S(1)}, f32[1024,4096]{1,0:T(8,128)S(1)}) custom-call(f32[1024,4096]{1,0:T(8,128)S(1)} %get-tuple-element.52.soft_ref, f32[1,1024]{1,0:T(1,128)S(1)} %get-tuple-element.56.inverse_ref, f32[1,1024]{1,0:T(1,128)S(1)} %get-tuple-element.59.scaled_ref, ...), custom_call_target="tpu_custom_call", output_to_operand_aliasing={{0}: (0, {})} | custom-call | tf_op jit(solution)/shard_map/pallas_call | solution.py:347
  101.9 1.6 shard_map.76
  104.0 1.6 %collective-permute-start.16 = (f32[256,128]{1,0:T(8,128)S(1)}, f32[256,128]{1,0:T(8,128)S(1)}, u32[]{:S(2)}, u32[]{:S(2)}) collective-permute-start(f32[256,128]{1,0:T(8,128)S(1)} %get-tuple-element.74), channel_id=1, source_target_pairs={{0,8},{8,16},{16,24},{24,28},{28,20},{20,12},{12,4},{4,0},{1,9},{9... | collective-permute-start | bytes 393224 | tf_op jit(solution)/shard_map/ppermute | solution.py:395
  105.6 5.5 %shard_map.77 = (f32[512,128]{1,0:T(8,128)S(1)}, f32[512,128]{1,0:T(8,128)S(1)}, f32[256,128]{1,0:T(8,128)S(1)}, f32[256,128]{1,0:T(8,128)S(1)}, f32[256,128]{1,...) custom-call(f32[1024,4096]{1,0:T(8,128)S(1)} %get-tuple-element.64.f, ...), custom_call_target="tpu_custom_call" | custom-call | tf_op jit(solution)/shard_map/pallas_call | solution.py:347
  111.2 2.0 %collective-permute-start.27 = (f32[256,128]{1,0:T(8,128)S(1)}, f32[256,128]{1,0:T(8,128)S(1)}, u32[]{:S(2)}, u32[]{:S(2)}) collective-permute-start(f32[256,128]{1,0:T(8,128)S(1)} %add.316), channel_id=1, source_target_pairs={{8,0},{16,8},{24,16},{28,24},{20,28},{12,20},{4,12},{0,4},{9,1},{1... | collective-permute-start | bytes 393224 | tf_op jit(solution)/shard_map/ppermute | solution.py:398
  113.6 1.7 %collective-permute-start.17 = (f32[256,128]{1,0:T(8,128)S(1)}, f32[256,128]{1,0:T(8,128)S(1)}, u32[]{:S(2)}, u32[]{:S(2)}) collective-permute-start(f32[256,128]{1,0:T(8,128)S(1)} %add.306), channel_id=1, source_target_pairs={{0,8},{8,16},{16,24},{24,28},{28,20},{20,12},{12,4},{4,0},{1,9},{9... | collective-permute-start | bytes 393224 | tf_op jit(solution)/shard_map/ppermute | solution.py:395
  117.5 1.7 %collective-permute-start.28 = (f32[256,128]{1,0:T(8,128)S(1)}, f32[256,128]{1,0:T(8,128)S(1)}, u32[]{:S(2)}, u32[]{:S(2)}) collective-permute-start(f32[256,128]{1,0:T(8,128)S(1)} %add.317), channel_id=1, source_target_pairs={{8,0},{16,8},{24,16},{28,24},{20,28},{12,20},{4,12},{0,4},{9,1},{1... | collective-permute-start | bytes 393224 | tf_op jit(solution)/shard_map/ppermute | solution.py:398
  119.5 1.7 %collective-permute-start.21 = (f32[256,128]{1,0:T(8,128)S(1)}, f32[256,128]{1,0:T(8,128)S(1)}, u32[]{:S(2)}, u32[]{:S(2)}) collective-permute-start(f32[256,128]{1,0:T(8,128)S(1)} %add.310), channel_id=1, source_target_pairs={{8,0},{16,8},{24,16},{28,24},{20,28},{12,20},{4,12},{0,4},{9,1},{1... | collective-permute-start | bytes 393224 | tf_op jit(solution)/shard_map/ppermute | solution.py:398
  122.8 1.7 %collective-permute-start.25 = (f32[256,128]{1,0:T(8,128)S(1)}, f32[256,128]{1,0:T(8,128)S(1)}, u32[]{:S(2)}, u32[]{:S(2)}) collective-permute-start(f32[256,128]{1,0:T(8,128)S(1)} %add.314), channel_id=1, source_target_pairs={{0,8},{8,16},{16,24},{24,28},{28,20},{20,12},{12,4},{4,0},{1,9},{9... | collective-permute-start | bytes 393224 | tf_op jit(solution)/shard_map/ppermute | solution.py:395
  127.8 2.6 %collective-permute-done.25 = f32[256,128]{1,0:T(8,128)S(1)} collective-permute-done((f32[256,128]{1,0:T(8,128)S(1)}, f32[256,128]{1,0:T(8,128)S(1)}, u32[]{:S(2)}, u32[]{:S(2)}) %collective-permute-start.25) | collective-permute-done | bytes 131104 | tf_op jit(solution)/shard_map/ppermute | solution.py:395
  130.9 2.3 %collective-permute-done.22 = f32[256,128]{1,0:T(8,128)S(1)} collective-permute-done((f32[256,128]{1,0:T(8,128)S(1)}, f32[256,128]{1,0:T(8,128)S(1)}, u32[]{:S(2)}, u32[]{:S(2)}) %collective-permute-start.22) | collective-permute-done | bytes 131104 | tf_op jit(solution)/shard_map/ppermute | solution.py:398
  134.4 1.6 %collective-permute-start.41 = (f32[256,128]{1,0:T(8,128)S(1)}, f32[256,128]{1,0:T(8,128)S(1)}, u32[]{:S(2)}, u32[]{:S(2)}) collective-permute-start(f32[256,128]{1,0:T(8,128)S(1)} %add_add_fusion.refs_4_), channel_id=1, source_target_pairs={{0,8},{8,16},{16,24},{24,28},{28,20},{20,12},{12,4},{4,0},{1,9},{9... | collective-permute-start | bytes 393224 | tf_op jit(solution)/shard_map/ppermute | solution.py:395
  139.4 1.7 %collective-permute-done.41.refs_18_ = f32[256,128]{1,0:T(8,128)S(1)} collective-permute-done((f32[256,128]{1,0:T(8,128)S(1)}, f32[256,128]{1,0:T(8,128)S(1)}, u32[]{:S(2)}, u32[]{:S(2)}) %collective-permute-start.41) | collective-permute-done | bytes 131104 | tf_op jit(solution)/shard_map/ppermute | solution.py:395
  141.2 1.9 %collective-permute-start.32 = (f32[256,128]{1,0:T(8,128)S(1)}, f32[256,128]{1,0:T(8,128)S(1)}, u32[]{:S(2)}, u32[]{:S(2)}) collective-permute-start(f32[256,128]{1,0:T(8,128)S(1)} %collective-permute-done.30.refs_5_), channel_id=1, source_target_pairs={{8,0},{16,8},{24,16},{28,24},{20,28},{12,20},{4,12},{0,4},{9,1},{1... | collective-permute-start | bytes 393224 | tf_op jit(solution)/shard_map/ppermute | solution.py:398
  143.5 2.1 %collective-permute-done.37.refs_15_ = f32[256,128]{1,0:T(8,128)S(1)} collective-permute-done((f32[256,128]{1,0:T(8,128)S(1)}, f32[256,128]{1,0:T(8,128)S(1)}, u32[]{:S(2)}, u32[]{:S(2)}) %collective-permute-start.37) | collective-permute-done | bytes 131104 | tf_op jit(solution)/shard_map/ppermute | solution.py:395
  145.6 2.6 %collective-permute-done.42.refs_16_ = f32[256,128]{1,0:T(8,128)S(1)} collective-permute-done((f32[256,128]{1,0:T(8,128)S(1)}, f32[256,128]{1,0:T(8,128)S(1)}, u32[]{:S(2)}, u32[]{:S(2)}) %collective-permute-start.42) | collective-permute-done | bytes 131104 | tf_op jit(solution)/shard_map/ppermute | solution.py:395
  148.2 2.0 %collective-permute-start.34 = (f32[256,128]{1,0:T(8,128)S(1)}, f32[256,128]{1,0:T(8,128)S(1)}, u32[]{:S(2)}, u32[]{:S(2)}) collective-permute-start(f32[256,128]{1,0:T(8,128)S(1)} %collective-permute-done.32.refs_7_), channel_id=1, source_target_pairs={{8,0},{16,8},{24,16},{28,24},{20,28},{12,20},{4,12},{0,4},{9,1},{1... | collective-permute-start | bytes 393224 | tf_op jit(solution)/shard_map/ppermute | solution.py:398
  152.3 2.3 %collective-permute-done.43.refs_14_ = f32[256,128]{1,0:T(8,128)S(1)} collective-permute-done((f32[256,128]{1,0:T(8,128)S(1)}, f32[256,128]{1,0:T(8,128)S(1)}, u32[]{:S(2)}, u32[]{:S(2)}) %collective-permute-start.43) | collective-permute-done | bytes 131104 | tf_op jit(solution)/shard_map/ppermute | solution.py:395
  156.2 1.6 %shard_map.78 = (f32[1024,128]{1,0:T(8,128)}, f32[4096,128]{1,0:T(8,128)}) custom-call(f32[256,128]{1,0:T(8,128)S(1)} %slice_add_fusion.refs_0_, f32[256,128]{1,0:T(8,128)S(1)} %collective-permute-done.14.refs_1_, f32[512,128]{1,0:T(8,128)S(1)} %collective-permute-done.15.refs_2_, f32[256,128]{1,0:T(8,128)S(1)} %add_add_fusion.1.refs_3_, ...), custom_call_target="tpu_custom_call" | custom-call | tf_op jit(solution)/shard_map/pallas_call | solution.py:495
  (97 shorter events, 28.4 us)
Async XLA Ops:
  93.3 8.6 %collective-permute-start.10 = (f32[1,1024]{1,0:T(1,128)S(1)}, f32[1,1024]{1,0:T(1,128)S(1)}, u32[]{:S(2)}, u32[]{:S(2)}) collective-permute-start(f32[1,1024]{1,0:T(1,128)S(1)} %get-tuple-element.66.refs_0_), channel_id=1, source_target_pairs={{0,2},{1,3},{2,0},{3,1},{4,6},{5,7},{6,4},{7,5},{8,10},{9,11},{10,... | collective-permute-start | bytes 12296 | tf_op jit(solution)/shard_map/ppermute | solution.py:372
  94.0 8.0 %collective-permute-start.11 = (f32[1,1024]{1,0:T(1,128)S(1)}, f32[1,1024]{1,0:T(1,128)S(1)}, u32[]{:S(2)}, u32[]{:S(2)}) collective-permute-start(f32[1,1024]{1,0:T(1,128)S(1)} %get-tuple-element.66.refs_0_), channel_id=1, source_target_pairs={{0,3},{1,2},{2,1},{3,0},{4,7},{5,6},{6,5},{7,4},{8,11},{9,10},{10,... | collective-permute-start | bytes 12296 | tf_op jit(solution)/shard_map/ppermute | solution.py:372
  94.0 8.0 %collective-permute-start.9 = (f32[1,1024]{1,0:T(1,128)S(1)}, f32[1,1024]{1,0:T(1,128)S(1)}, u32[]{:S(2)}, u32[]{:S(2)}) collective-permute-start(f32[1,1024]{1,0:T(1,128)S(1)} %get-tuple-element.66.refs_0_), channel_id=1, source_target_pairs={{0,1},{1,0},{2,3},{3,2},{4,5},{5,4},{6,7},{7,6},{8,9},{9,8},{10,11... | collective-permute-start | bytes 12296 | tf_op jit(solution)/shard_map/ppermute | solution.py:372
  103.5 7.6 %collective-permute-start.26 = (f32[256,128]{1,0:T(8,128)S(1)}, f32[256,128]{1,0:T(8,128)S(1)}, u32[]{:S(2)}, u32[]{:S(2)}) collective-permute-start(f32[256,128]{1,0:T(8,128)S(1)} %get-tuple-element.85), channel_id=1, source_target_pairs={{8,0},{16,8},{24,16},{28,24},{20,28},{12,20},{4,12},{0,4},{9,1},{1... | collective-permute-start | bytes 393224 | tf_op jit(solution)/shard_map/ppermute | solution.py:398
  104.0 9.7 %collective-permute-start.16 = (f32[256,128]{1,0:T(8,128)S(1)}, f32[256,128]{1,0:T(8,128)S(1)}, u32[]{:S(2)}, u32[]{:S(2)}) collective-permute-start(f32[256,128]{1,0:T(8,128)S(1)} %get-tuple-element.74), channel_id=1, source_target_pairs={{0,8},{8,16},{16,24},{24,28},{28,20},{20,12},{12,4},{4,0},{1,9},{9... | collective-permute-start | bytes 393224 | tf_op jit(solution)/shard_map/ppermute | solution.py:395
  111.2 6.3 %collective-permute-start.27 = (f32[256,128]{1,0:T(8,128)S(1)}, f32[256,128]{1,0:T(8,128)S(1)}, u32[]{:S(2)}, u32[]{:S(2)}) collective-permute-start(f32[256,128]{1,0:T(8,128)S(1)} %add.316), channel_id=1, source_target_pairs={{8,0},{16,8},{24,16},{28,24},{20,28},{12,20},{4,12},{0,4},{9,1},{1... | collective-permute-start | bytes 393224 | tf_op jit(solution)/shard_map/ppermute | solution.py:398
  113.2 6.2 %collective-permute-start.20 = (f32[256,128]{1,0:T(8,128)S(1)}, f32[256,128]{1,0:T(8,128)S(1)}, u32[]{:S(2)}, u32[]{:S(2)}) collective-permute-start(f32[256,128]{1,0:T(8,128)S(1)} %get-tuple-element.77), channel_id=1, source_target_pairs={{8,0},{16,8},{24,16},{28,24},{20,28},{12,20},{4,12},{0,4},{9,1},{1... | collective-permute-start | bytes 393224 | tf_op jit(solution)/shard_map/ppermute | solution.py:398
  113.6 12.7 %collective-permute-start.12 = (f32[512,128]{1,0:T(8,128)S(1)}, f32[512,128]{1,0:T(8,128)S(1)}, u32[]{:S(2)}, u32[]{:S(2)}) collective-permute-start(f32[512,128]{1,0:T(8,128)S(1)} %get-tuple-element.69), channel_id=1, source_target_pairs={{0,1},{1,0},{2,3},{3,2},{4,5},{5,4},{6,7},{7,6},{8,9},{9,8},{10,11... | collective-permute-start | bytes 786440 | tf_op jit(solution)/shard_map/ppermute | solution.py:372
  113.6 7.5 %collective-permute-start.17 = (f32[256,128]{1,0:T(8,128)S(1)}, f32[256,128]{1,0:T(8,128)S(1)}, u32[]{:S(2)}, u32[]{:S(2)}) collective-permute-start(f32[256,128]{1,0:T(8,128)S(1)} %add.306), channel_id=1, source_target_pairs={{0,8},{8,16},{16,24},{24,28},{28,20},{20,12},{12,4},{4,0},{1,9},{9... | collective-permute-start | bytes 393224 | tf_op jit(solution)/shard_map/ppermute | solution.py:395
  116.1 6.7 %collective-permute-start.24 = (f32[256,128]{1,0:T(8,128)S(1)}, f32[256,128]{1,0:T(8,128)S(1)}, u32[]{:S(2)}, u32[]{:S(2)}) collective-permute-start(f32[256,128]{1,0:T(8,128)S(1)} %add.313), channel_id=1, source_target_pairs={{0,8},{8,16},{16,24},{24,28},{28,20},{20,12},{12,4},{4,0},{1,9},{9... | collective-permute-start | bytes 393224 | tf_op jit(solution)/shard_map/ppermute | solution.py:395
  117.5 7.0 %collective-permute-start.28 = (f32[256,128]{1,0:T(8,128)S(1)}, f32[256,128]{1,0:T(8,128)S(1)}, u32[]{:S(2)}, u32[]{:S(2)}) collective-permute-start(f32[256,128]{1,0:T(8,128)S(1)} %add.317), channel_id=1, source_target_pairs={{8,0},{16,8},{24,16},{28,24},{20,28},{12,20},{4,12},{0,4},{9,1},{1... | collective-permute-start | bytes 393224 | tf_op jit(solution)/shard_map/ppermute | solution.py:398
  119.5 5.5 %collective-permute-start.21 = (f32[256,128]{1,0:T(8,128)S(1)}, f32[256,128]{1,0:T(8,128)S(1)}, u32[]{:S(2)}, u32[]{:S(2)}) collective-permute-start(f32[256,128]{1,0:T(8,128)S(1)} %add.310), channel_id=1, source_target_pairs={{8,0},{16,8},{24,16},{28,24},{20,28},{12,20},{4,12},{0,4},{9,1},{1... | collective-permute-start | bytes 393224 | tf_op jit(solution)/shard_map/ppermute | solution.py:398
  121.2 6.4 %collective-permute-start.18 = (f32[256,128]{1,0:T(8,128)S(1)}, f32[256,128]{1,0:T(8,128)S(1)}, u32[]{:S(2)}, u32[]{:S(2)}) collective-permute-start(f32[256,128]{1,0:T(8,128)S(1)} %add.307), channel_id=1, source_target_pairs={{0,8},{8,16},{16,24},{24,28},{28,20},{20,12},{12,4},{4,0},{1,9},{9... | collective-permute-start | bytes 393224 | tf_op jit(solution)/shard_map/ppermute | solution.py:395
  122.8 7.6 %collective-permute-start.25 = (f32[256,128]{1,0:T(8,128)S(1)}, f32[256,128]{1,0:T(8,128)S(1)}, u32[]{:S(2)}, u32[]{:S(2)}) collective-permute-start(f32[256,128]{1,0:T(8,128)S(1)} %add.314), channel_id=1, source_target_pairs={{0,8},{8,16},{16,24},{24,28},{28,20},{20,12},{12,4},{4,0},{1,9},{9... | collective-permute-start | bytes 393224 | tf_op jit(solution)/shard_map/ppermute | solution.py:395
  124.5 5.9 %collective-permute-start.29 = (f32[256,128]{1,0:T(8,128)S(1)}, f32[256,128]{1,0:T(8,128)S(1)}, u32[]{:S(2)}, u32[]{:S(2)}) collective-permute-start(f32[256,128]{1,0:T(8,128)S(1)} %add.318), channel_id=1, source_target_pairs={{8,0},{16,8},{24,16},{28,24},{20,28},{12,20},{4,12},{0,4},{9,1},{1... | collective-permute-start | bytes 393224 | tf_op jit(solution)/shard_map/ppermute | solution.py:398
  125.0 8.2 %collective-permute-start.22 = (f32[256,128]{1,0:T(8,128)S(1)}, f32[256,128]{1,0:T(8,128)S(1)}, u32[]{:S(2)}, u32[]{:S(2)}) collective-permute-start(f32[256,128]{1,0:T(8,128)S(1)} %add.311), channel_id=1, source_target_pairs={{8,0},{16,8},{24,16},{28,24},{20,28},{12,20},{4,12},{0,4},{9,1},{1... | collective-permute-start | bytes 393224 | tf_op jit(solution)/shard_map/ppermute | solution.py:398
  126.3 7.1 %collective-permute-start.13 = (f32[256,128]{1,0:T(8,128)S(1)}, f32[256,128]{1,0:T(8,128)S(1)}, u32[]{:S(2)}, u32[]{:S(2)}) collective-permute-start(f32[256,128]{1,0:T(8,128)S(1)} %slice.9), channel_id=1, source_target_pairs={{0,2},{1,3},{2,0},{3,1},{4,6},{5,7},{6,4},{7,5},{8,10},{9,11},{10,... | collective-permute-start | bytes 393224 | tf_op jit(solution)/shard_map/ppermute | solution.py:372
  127.6 5.6 %collective-permute-start.19 = (f32[256,128]{1,0:T(8,128)S(1)}, f32[256,128]{1,0:T(8,128)S(1)}, u32[]{:S(2)}, u32[]{:S(2)}) collective-permute-start(f32[256,128]{1,0:T(8,128)S(1)} %add.308), channel_id=1, source_target_pairs={{0,8},{8,16},{16,24},{24,28},{28,20},{20,12},{12,4},{4,0},{1,9},{9... | collective-permute-start | bytes 393224 | tf_op jit(solution)/shard_map/ppermute | solution.py:395
  130.5 6.0 %collective-permute-start.31 = (f32[256,128]{1,0:T(8,128)S(1)}, f32[256,128]{1,0:T(8,128)S(1)}, u32[]{:S(2)}, u32[]{:S(2)}) collective-permute-start(f32[256,128]{1,0:T(8,128)S(1)} %add_add_fusion.refs_4_), channel_id=1, source_target_pairs={{8,0},{16,8},{24,16},{28,24},{20,28},{12,20},{4,12},{0,4},{9,1},{1... | collective-permute-start | bytes 393224 | tf_op jit(solution)/shard_map/ppermute | solution.py:398
  133.2 6.0 %collective-permute-start.36 = (f32[256,128]{1,0:T(8,128)S(1)}, f32[256,128]{1,0:T(8,128)S(1)}, u32[]{:S(2)}, u32[]{:S(2)}) collective-permute-start(f32[256,128]{1,0:T(8,128)S(1)} %add_add_fusion.1.refs_3_), channel_id=1, source_target_pairs={{0,8},{8,16},{16,24},{24,28},{28,20},{20,12},{12,4},{4,0},{1,9},{9... | collective-permute-start | bytes 393224 | tf_op jit(solution)/shard_map/ppermute | solution.py:395
  133.5 5.8 %collective-permute-start.14 = (f32[256,128]{1,0:T(8,128)S(1)}, f32[256,128]{1,0:T(8,128)S(1)}, u32[]{:S(2)}, u32[]{:S(2)}) collective-permute-start(f32[256,128]{1,0:T(8,128)S(1)} %slice_add_fusion.refs_0_), channel_id=1, source_target_pairs={{0,2},{1,3},{2,0},{3,1},{4,6},{5,7},{6,4},{7,5},{8,10},{9,11},{10,... | collective-permute-start | bytes 393224 | tf_op jit(solution)/shard_map/ppermute | solution.py:372
  134.4 6.6 %collective-permute-start.41 = (f32[256,128]{1,0:T(8,128)S(1)}, f32[256,128]{1,0:T(8,128)S(1)}, u32[]{:S(2)}, u32[]{:S(2)}) collective-permute-start(f32[256,128]{1,0:T(8,128)S(1)} %add_add_fusion.refs_4_), channel_id=1, source_target_pairs={{0,8},{8,16},{16,24},{24,28},{28,20},{20,12},{12,4},{4,0},{1,9},{9... | collective-permute-start | bytes 393224 | tf_op jit(solution)/shard_map/ppermute | solution.py:395
  136.1 5.2 %collective-permute-start.30 = (f32[256,128]{1,0:T(8,128)S(1)}, f32[256,128]{1,0:T(8,128)S(1)}, u32[]{:S(2)}, u32[]{:S(2)}) collective-permute-start(f32[256,128]{1,0:T(8,128)S(1)} %add_add_fusion.1.refs_3_), channel_id=1, source_target_pairs={{8,0},{16,8},{24,16},{28,24},{20,28},{12,20},{4,12},{0,4},{9,1},{1... | collective-permute-start | bytes 393224 | tf_op jit(solution)/shard_map/ppermute | solution.py:398
  136.5 6.6 %collective-permute-start.33 = (f32[256,128]{1,0:T(8,128)S(1)}, f32[256,128]{1,0:T(8,128)S(1)}, u32[]{:S(2)}, u32[]{:S(2)}) collective-permute-start(f32[256,128]{1,0:T(8,128)S(1)} %collective-permute-done.31.refs_6_), channel_id=1, source_target_pairs={{8,0},{16,8},{24,16},{28,24},{20,28},{12,20},{4,12},{0,4},{9,1},{1... | collective-permute-start | bytes 393224 | tf_op jit(solution)/shard_map/ppermute | solution.py:398
  139.3 6.3 %collective-permute-start.37 = (f32[256,128]{1,0:T(8,128)S(1)}, f32[256,128]{1,0:T(8,128)S(1)}, u32[]{:S(2)}, u32[]{:S(2)}) collective-permute-start(f32[256,128]{1,0:T(8,128)S(1)} %collective-permute-done.36.refs_17_), channel_id=1, source_target_pairs={{0,8},{8,16},{16,24},{24,28},{28,20},{20,12},{12,4},{4,0},{1,9},{9... | collective-permute-start | bytes 393224 | tf_op jit(solution)/shard_map/ppermute | solution.py:395
  139.3 12.9 %collective-permute-start.15 = (f32[512,128]{1,0:T(8,128)S(1)}, f32[512,128]{1,0:T(8,128)S(1)}, u32[]{:S(2)}, u32[]{:S(2)}) collective-permute-start(f32[512,128]{1,0:T(8,128)S(1)} %pad_maximum_fusion), channel_id=1, source_target_pairs={{0,1},{1,0},{2,3},{3,2},{4,5},{5,4},{6,7},{7,6},{8,9},{9,8},{10,11... | collective-permute-start | bytes 786440 | tf_op jit(solution)/shard_map/ppermute | solution.py:372
  141.1 7.1 %collective-permute-start.42 = (f32[256,128]{1,0:T(8,128)S(1)}, f32[256,128]{1,0:T(8,128)S(1)}, u32[]{:S(2)}, u32[]{:S(2)}) collective-permute-start(f32[256,128]{1,0:T(8,128)S(1)} %collective-permute-done.41.refs_18_), channel_id=1, source_target_pairs={{0,8},{8,16},{16,24},{24,28},{28,20},{20,12},{12,4},{4,0},{1,9},{9... | collective-permute-start | bytes 393224 | tf_op jit(solution)/shard_map/ppermute | solution.py:395
  141.2 7.0 %collective-permute-start.32 = (f32[256,128]{1,0:T(8,128)S(1)}, f32[256,128]{1,0:T(8,128)S(1)}, u32[]{:S(2)}, u32[]{:S(2)}) collective-permute-start(f32[256,128]{1,0:T(8,128)S(1)} %collective-permute-done.30.refs_5_), channel_id=1, source_target_pairs={{8,0},{16,8},{24,16},{28,24},{20,28},{12,20},{4,12},{0,4},{9,1},{1... | collective-permute-start | bytes 393224 | tf_op jit(solution)/shard_map/ppermute | solution.py:398
  143.1 7.1 %collective-permute-start.35 = (f32[256,128]{1,0:T(8,128)S(1)}, f32[256,128]{1,0:T(8,128)S(1)}, u32[]{:S(2)}, u32[]{:S(2)}) collective-permute-start(f32[256,128]{1,0:T(8,128)S(1)} %collective-permute-done.33.refs_8_), channel_id=1, source_target_pairs={{8,0},{16,8},{24,16},{28,24},{20,28},{12,20},{4,12},{0,4},{9,1},{1... | collective-permute-start | bytes 393224 | tf_op jit(solution)/shard_map/ppermute | solution.py:398
  145.6 5.6 %collective-permute-start.38 = (f32[256,128]{1,0:T(8,128)S(1)}, f32[256,128]{1,0:T(8,128)S(1)}, u32[]{:S(2)}, u32[]{:S(2)}) collective-permute-start(f32[256,128]{1,0:T(8,128)S(1)} %collective-permute-done.37.refs_15_), channel_id=1, source_target_pairs={{0,8},{8,16},{16,24},{24,28},{28,20},{20,12},{12,4},{4,0},{1,9},{9... | collective-permute-start | bytes 393224 | tf_op jit(solution)/shard_map/ppermute | solution.py:395
  148.2 6.3 %collective-permute-start.43 = (f32[256,128]{1,0:T(8,128)S(1)}, f32[256,128]{1,0:T(8,128)S(1)}, u32[]{:S(2)}, u32[]{:S(2)}) collective-permute-start(f32[256,128]{1,0:T(8,128)S(1)} %collective-permute-done.42.refs_16_), channel_id=1, source_target_pairs={{0,8},{8,16},{16,24},{24,28},{28,20},{20,12},{12,4},{4,0},{1,9},{9... | collective-permute-start | bytes 393224 | tf_op jit(solution)/shard_map/ppermute | solution.py:395
  148.2 6.3 %collective-permute-start.34 = (f32[256,128]{1,0:T(8,128)S(1)}, f32[256,128]{1,0:T(8,128)S(1)}, u32[]{:S(2)}, u32[]{:S(2)}) collective-permute-start(f32[256,128]{1,0:T(8,128)S(1)} %collective-permute-done.32.refs_7_), channel_id=1, source_target_pairs={{8,0},{16,8},{24,16},{28,24},{20,28},{12,20},{4,12},{0,4},{9,1},{1... | collective-permute-start | bytes 393224 | tf_op jit(solution)/shard_map/ppermute | solution.py:398
  (14 other events, 86.3 us)

commit v5 on v4

--- a/solution.py
+++ b/solution.py
@@ -30,6 +30,10 @@
     return jnp.sum(jnp.transpose(partial), axis=0, keepdims=True)
 
 
+def transposed_product(a, b):
+    return lax.dot_general(a, b, (((0,), (0,)), ((), ())), preferred_element_type=F32)
+
+
 def log_sum(parts):
     top = functools.reduce(jnp.maximum, parts)
     return top + jnp.log2(sum(jnp.exp2(p - top) for p in parts))
@@ -73,7 +77,6 @@
 
 def row_level_kernel(crawl_hbm, bench_hbm, duals_hbm, tile_ref, top_ref, level_ref, crawl_ref, bench_ref, shift_ref,
                      top_scratch, sum_scratch, sems):
-    height = 64
     chunks = 4
     part = bench_ref.shape[0] // chunks
     copies = [pltpu.make_async_copy(crawl_hbm, crawl_ref, sems.at[chunks]),
@@ -87,36 +90,42 @@
         copy.wait()
     shift_ref[...] = shift_ref[...] * KAPPA
 
-    def fill(block, _, fetches=()):
+    highest = jnp.max(shift_ref[...])
+
+    def tops(block, _, fetches=()):
         rows = pl.ds(pl.multiple_of(block * TALL, TALL), TALL)
         top = jnp.full((TALL, LANES), -jnp.inf, F32)
         for at in range(0, tile_ref.shape[1], WIDE):
             for k, fetch in enumerate(fetches):
                 if at <= k * part < at + WIDE:
                     fetch.wait()
-            exponent = exponent_block(crawl_ref, bench_ref, shift_ref, rows, pl.ds(at, WIDE))
-            tile_ref[rows, at:at + WIDE] = exponent
+            scores = transposed_dot(crawl_ref[rows, :], bench_ref[at:at + WIDE, :])
             for lane in range(0, WIDE, LANES):
-                top = jnp.maximum(top, exponent[:, lane:lane + LANES])
-        top_scratch[rows, :] = top
+                top = jnp.maximum(top, scores[:, lane:lane + LANES])
+        top = jnp.max(top, axis=1, keepdims=True) * KAPPA + highest
+        top_scratch[rows, :] = jnp.broadcast_to(top, (TALL, LANES))
         return _
 
-    fill(0, 0, fetches)
-    lax.fori_loop(1, tile_ref.shape[0] // TALL, fill, 0)
-
-    def power(block, _):
-        rows = pl.ds(pl.multiple_of(block * height, height), height)
-        top = jnp.broadcast_to(jnp.max(top_scratch[rows, :], axis=1, keepdims=True), (height, LANES))
-        acc = jnp.zeros((height, LANES), F32)
-        for at in range(0, tile_ref.shape[1], LANES):
-            value = jnp.exp2(tile_ref[rows, at:at + LANES] - top)
-            tile_ref[rows, at:at + LANES] = value
-            acc += value
-        top_scratch[rows, :] = top
+    tops(0, 0, fetches)
+    lax.fori_loop(1, tile_ref.shape[0] // TALL, tops, 0)
+
+    def powers(block, _):
+        rows = pl.ds(pl.multiple_of(block * TALL, TALL), TALL)
+        top = top_scratch[rows, :]
+        acc = jnp.zeros((TALL, LANES), F32)
+        for at in range(0, tile_ref.shape[1], WIDE):
+            scores = transposed_dot(crawl_ref[rows, :], bench_ref[at:at + WIDE, :])
+            values = []
+            for lane in range(0, WIDE, LANES):
+                span = slice(at + lane, at + lane + LANES)
+                value = jnp.exp2(scores[:, lane:lane + LANES] * KAPPA + (shift_ref[:, span] - top))
+                tile_ref[rows, span] = value
+                values.append(value)
+            acc += sum(values)
         sum_scratch[rows, :] = acc
         return _
 
-    lax.fori_loop(0, tile_ref.shape[0] // height, power, 0)
+    lax.fori_loop(0, tile_ref.shape[0] // TALL, powers, 0)
     top = jnp.transpose(top_scratch[...])[0:1, :]
     top_ref[...] = top
     level_ref[...] = top + jnp.log2(row_form(sum_scratch[...]))
@@ -265,49 +274,57 @@
     return (early + first * last).astype(jnp.bfloat16)
 
 
-def far_kernel(parts, n, first_ref, early_ref, left_ref, crawl_ref, *refs):
+def far_kernel(parts, n, places, first_ref, early_ref, left_ref, crawl_ref, *refs):
     part_refs, (last_ref, *piece_refs, flat) = refs[:parts], refs[parts:]
     last_ref[...] = column_form(-left_ref[...] * sum(p[...] for p in part_refs))
-    if not piece_refs:
+    if not places:
         return
-    width = flat.shape[1]
-    start = ring_share(n, n // 2) * width
+    width = flat.shape[1] // len(places)
+    starts = [ring_share(n, at) * width for at in places]
     flat[...] = jnp.zeros_like(flat)
 
     def body(block, _):
         rows = pl.ds(pl.multiple_of(block * TALL, TALL), TALL)
         last = last_ref[rows, :]
-        pieces = []
-        for lane in range(0, width, LANES):
-            span = pl.ds(pl.multiple_of(start + lane, LANES), LANES)
-            pieces.append(score_grad(early_ref[rows, span], first_ref[rows, span], last))
-        grad = jnp.concatenate(pieces, axis=1)
-        flat[...] += lax.dot_general(crawl_ref[rows, :], grad, (((0,), (0,)), ((), ())), preferred_element_type=F32)
+        for k, start in enumerate(starts):
+            pieces = []
+            for lane in range(0, width, LANES):
+                span = pl.ds(pl.multiple_of(start + lane, LANES), LANES)
+                pieces.append(score_grad(early_ref[rows, span], first_ref[rows, span], last))
+            flat[:, k * width:(k + 1) * width] += transposed_product(crawl_ref[rows, :], jnp.concatenate(pieces, axis=1))
         return _
 
     lax.fori_loop(0, first_ref.shape[0] // TALL, body, 0)
-    half = width // 2
+    height = width // 2
     for k, piece in enumerate(piece_refs):
-        piece[...] = jnp.transpose(flat[:, k * half:(k + 1) * half])
+        piece[...] = jnp.transpose(flat[:, k * height:(k + 1) * height])
 
 
 def gradient_kernel(n, places, first_ref, early_ref, last_ref, crawl_ref, bench_ref, *refs):
+    in_order = len(places) < n
+    if in_order:
+        (near, far), refs = refs[:2], refs[2:]
+        refs[2][...], refs[3][...] = near[...], far[...]
+        refs = refs[:2] + refs[4:]
     keep_ref, send_ref, *piece_refs, flat, whole, total = refs
     flat[...] = jnp.zeros_like(flat)
+    columns = first_ref.shape[1]
+    width = columns // n if in_order else WIDE
+    starts = [ring_share(n, at) * width if in_order else at * width for at in range(columns // width)]
 
     def body(block, _):
         rows = pl.ds(pl.multiple_of(block * TALL, TALL), TALL)
         last = last_ref[rows, :]
-        x = crawl_ref[rows, :]
         acc = jnp.zeros((TALL, LANES), F32)
-        for at in range(0, first_ref.shape[1], WIDE):
+        for k, start in enumerate(starts):
             pieces = []
-            for lane in range(at, at + WIDE, LANES):
-                span = slice(lane, lane + LANES)
+            for lane in range(0, width, LANES):
+                span = pl.ds(pl.multiple_of(start + lane, LANES), LANES)
                 pieces.append(score_grad(early_ref[rows, span], first_ref[rows, span], last))
             grad = jnp.concatenate(pieces, axis=1)
-            acc += jnp.dot(grad, bench_ref[at:at + WIDE, :], preferred_element_type=F32)
-            flat[:, at:at + WIDE] += lax.dot_general(x, grad, (((0,), (0,)), ((), ())), preferred_element_type=F32)
+            acc += jnp.dot(grad, bench_ref[pl.ds(pl.multiple_of(start, width), width), :], preferred_element_type=F32)
+            if k in places or not in_order:
+                flat[:, k * width:(k + 1) * width] += transposed_product(crawl_ref[rows, :], grad)
         total[rows, :] = acc
         return _
 
@@ -317,11 +334,17 @@
     for k, (ref, low) in enumerate(((keep_ref, 0), (send_ref, 0), (keep_ref, quarter), (send_ref, quarter))):
         start = pl.multiple_of(lax.bitwise_xor(me, k) * quarter, quarter)
         ref[low:low + quarter, :] = total[pl.ds(start, quarter), :]
-    whole[...] = jnp.transpose(flat[...])
     height = piece_refs[0].shape[0]
+    if not in_order:
+        whole[...] = jnp.transpose(flat[...])
     for k, piece in enumerate(piece_refs):
-        start = ring_share(n, places[k // 2]) * 2 * height + k % 2 * height
-        piece[...] = whole[pl.ds(pl.multiple_of(start, height), height), :]
+        at = places[k // 2]
+        if in_order:
+            low = at * width + k % 2 * height
+            piece[...] = jnp.transpose(flat[:, low:low + height])
+        else:
+            start = ring_share(n, at) * 2 * height + k % 2 * height
+            piece[...] = whole[pl.ds(pl.multiple_of(start, height), height), :]
 
 
 def placing_kernel(n, *refs):
@@ -475,21 +498,24 @@
     width = bench.shape[1]
     share = columns // n
     piece = shaped(share // 2, width)
-    ahead = share % (2 * LANES) == 0
     first, early = call(
         early_kernel, [soft, inverse, scaled, left, scaled2, right, back, mass],
         [tile_shape, tile_shape], [tall] * 3, aliases={0: 0})
     first, early = kept(first), kept(early)
+    ahead = [n // 2 - 1, n // 2, n // 2 + 1] if n >= 4 and share % (2 * LANES) == 0 else []
     last, *far = call(
-        functools.partial(far_kernel, len(parts), n), [first, early, left, crawl, *parts],
-        [shaped(*tall)] + [piece] * (2 * ahead), [(LANES, share)])
-    places = [at for at in range(n) if at != n // 2 or not ahead]
+        functools.partial(far_kernel, len(parts), n, ahead), [first, early, left, crawl, *parts],
+        [shaped(*tall)] + [piece] * (2 * len(ahead)), [(LANES, share * max(1, len(ahead)))])
+    places = [at for at in range(n) if at not in ahead]
+    first_added = [far[0], far[5]] if ahead else []
     keep, send, *pieces = call(
         functools.partial(gradient_kernel, n, places),
-        [first, early, last, crawl, bench],
-        [shaped(rows // 2, width)] * 2 + [piece] * (2 * len(places)), [(LANES, columns), (columns, LANES), tall])
+        [first, early, last, crawl, bench, *first_added],
+        [shaped(rows // 2, width)] * 2 + [piece] * (len(first_added) + 2 * len(places)),
+        [(LANES, columns), (LANES, LANES) if ahead else (columns, LANES), tall])
     if ahead:
-        pieces[n:n] = far
+        far[0], far[5], *pieces = pieces
+        pieces[2 * ahead[0]:2 * ahead[0]] = far
     pieces = ring_all_reduce(pieces, n)
     quarters = quarter_all_reduce(keep, send)
     crawl_grad, bench_grad = pl.pallas_call(

time: 158 us -> 162 us (1.025)
  Pallas kernels: 59.9 us -> 63.5 us
    pallas_call x9, Pallas kernels: 49.9 us -> 53.2 us  [call(): pl.pallas_call(kernel, in_specs=[pl.BlockSpec(memory_space=pltpu.VMEM)] *...]
  transfers between devices with their start and end apart: 44 -> 44, of which waited for: 20 -> 19; matrix products, arithmetic and copies ran while one was open for 0% -> 0% of each run, Pallas kernels for 8% -> 9%
where the time goes in v5:
time: 162 us; the launch traced here: 161 us
  Pallas kernels  63.5 us (39%)
  starting transfers between devices  34.7 us (21%)
  blocking collectives  32.9 us (20%)
  waiting for transfers between devices  28.7 us (18%)
    pallas_call x9, Pallas kernels, call(): pl.pallas_call(kernel, in_specs=[pl.BlockSpec(memory_space=pltpu.VMEM)] *...  53.2 us
    all_to_all x3, blocking collectives, over_rows(): lax.all_to_all(copies, 'rows', 0, 0)  32.9 us
    ppermute x14, waiting for transfers between devices, ahead(): return lax.ppermute(x, 'rows', up)  16 us
    ppermute x14, starting transfers between devices, behind(): return lax.ppermute(x, 'rows', down)  14.9 us
    ppermute x16, starting transfers between devices, exchange(): lax.ppermute(x, axis, [(i, i ^ k * stride) for i in range(n)])  10.9 us
    ppermute x14, starting transfers between devices, ahead(): return lax.ppermute(x, 'rows', up)  8.93 us
    pallas_call x1, Pallas kernels, per_device(): pl.pallas_call(row_level_kernel, in_specs=[pl.BlockSpec(memory_space=pltp...  8.6 us
    ppermute x16, waiting for transfers between devices, exchange(): lax.ppermute(x, axis, [(i, i ^ k * stride) for i in range(n)])  7.51 us
  transfers between devices with their start and end apart: 44, of which 19 were waited for; matrix products, arithmetic and copies ran while one was open for 0% of the time, Pallas kernels for 9%

profile of v5, /device:TPU:0, one launch (start us, length us, event | category | flops | bytes accessed | tf_op | source)
XLA Modules:
  0.0 161.3 jit_solution(16880849368858437555)
XLA Ops:
  0.6 8.6 %shard_map.68 = (f32[1024,4096]{1,0:T(8,128)S(1)}, f32[1,1024]{1,0:T(1,128)S(1)}, f32[1,1024]{1,0:T(1,128)S(1)}, bf16[1024,128]{1,0:T(8,128)(2,1)S(1)}, bf16[409...) custom-call(bf16[1024,128]{1,0:T(8,128)(2,1)} %crawl_hbm.1, bf16[4096,128]{1,0:T(8,128)(2,1)} %bench_hbm.1, f32[1,4096]{1,0:T(1,128)} %bitcast.31), custom_call_target="tpu_custom_call" | custom-call | tf_op jit(solution)/shard_map/pallas_call | solution.py:462
  9.8 2.6 %collective-permute-start.1 = (f32[1,1024]{1,0:T(1,128)S(1)}, f32[1,1024]{1,0:T(1,128)S(1)}, u32[]{:S(2)}, u32[]{:S(2)}) collective-permute-start(f32[1,1024]{1,0:T(1,128)S(1)} %get-tuple-element.48.refs_0_), channel_id=1, source_target_pairs={{0,2},{1,3},{2,0},{3,1},{4,6},{5,7},{6,4},{7,5},{8,10},{9,11},{10,... | collective-permute-start | bytes 12296 | tf_op jit(solution)/shard_map/ppermute | solution.py:395
  15.4 19.3 %shard_map.69 = (f32[1,1024]{1,0:T(1,128)S(1)}, f32[1,4096]{1,0:T(1,128)S(1)}) custom-call(f32[1024,4096]{1,0:T(8,128)S(1)} %get-tuple-element.46.tile_ref, f32[1,1024]{1,0:T(1,128)S(1)} %get-tuple-element.47.top_ref, f32[1,1024]{1,0:T(1,128)S(1)} %get-tuple-element.48.refs_0_, f32[1,1024]{1,0:T(1,128)S(1)} %collective-permute-done.refs_1_, ...), custom_call_target="tpu_custom_call" | custom-call | tf_op jit(solution)/shard_map/pallas_call | solution.py:370
  34.7 13.0 %all_to_all.15 = f32[8,32,128]{2,1,0:T(8,128)S(1)} all-to-all(f32[8,32,128]{2,1,0:T(8,128)S(1)} %broadcast_in_dim.22), channel_id=1, replica_groups=mesh['rows'=8,'cols'=4] {'rows'}, dimensions={0} | all-to-all | bytes 262144 | tf_op jit(solution)/shard_map/all_to_all | solution.py:460
  48.0 9.5 %shard_map.70 = (f32[1024,4096]{1,0:T(8,128)S(1)}, f32[1,1024]{1,0:T(1,128)S(1)}, f32[1,4096]{1,0:T(1,128)S(1)}, f32[1,4096]{1,0:T(1,128)S(1)}, f32[1,1024]{1,0:T(1,128)S(1)}) custom-call(f32[1024,4096]{1,0:T(8,128)S(1)} %get-tuple-element.46.tile_ref, f32[1,1024]{1,0:T(1,128)S(1)} %get-tuple-element.47.top_ref, ...), custom_call_target="tpu_custom_call", output_to_operand_aliasing={{0}: (0, {})} | custom-call | tf_op jit(solution)/shard_map/pallas_call | solution.py:370
  59.4 1.8 %collective-permute-done.4.refs_2_ = f32[1,1024]{1,0:T(1,128)S(1)} collective-permute-done((f32[1,1024]{1,0:T(1,128)S(1)}, f32[1,1024]{1,0:T(1,128)S(1)}, u32[]{:S(2)}, u32[]{:S(2)}) %collective-permute-start.4) | collective-permute-done | bytes 4128 | tf_op jit(solution)/shard_map/ppermute | solution.py:395
  61.3 2.0 %shard_map.71 = (f32[1,1024]{1,0:T(1,128)S(1)}, f32[1,4096]{1,0:T(1,128)S(1)}) custom-call(f32[1024,4096]{1,0:T(8,128)S(1)} %get-tuple-element.54.soft_ref, f32[1,1024]{1,0:T(1,128)S(1)} %get-tuple-element.55.left_ref, f32[1,4096]{1,0:T(1,128)S(1)} %get-tuple-element.56.right_ref, f32[1,1024]{1,0:T(1,128)S(1)} %get-tuple-element.57.refs_0_, ...), custom_call_target="tpu_custom_call" | custom-call | tf_op jit(solution)/shard_map/pallas_call | solution.py:370
  63.3 9.9 %all_to_all.16 = f32[8,32,128]{2,1,0:T(8,128)S(1)} all-to-all(f32[8,32,128]{2,1,0:T(8,128)S(1)} %broadcast_in_dim.24), channel_id=1, replica_groups=mesh['rows'=8,'cols'=4] {'rows'}, dimensions={0} | all-to-all | bytes 262144 | tf_op jit(solution)/shard_map/all_to_all | solution.py:460
  73.3 1.8 %shard_map.72 = (f32[1,4096]{1,0:T(1,128)S(1)}, f32[1,1024]{1,0:T(1,128)S(1)}) custom-call(f32[1024,4096]{1,0:T(8,128)S(1)} %get-tuple-element.54.soft_ref, f32[1,1024]{1,0:T(1,128)S(1)} %get-tuple-element.58.inverse_ref, f32[1,4096]{1,0:T(1,128)S(1)} %get-tuple-element.56.right_ref, f32[1,4096]{1,0:T(1,128)S(1)} %bitcast.21, f32[1,4096]{1,0:T(1,128)S(1)} %bitcast.17), custom_call_target="tpu_custom_call" | custom-call | tf_op jit(solution)/shard_map/pallas_call | solution.py:370
  77.0 1.8 %collective-permute-done.7.refs_2_ = f32[1,1024]{1,0:T(1,128)S(1)} collective-permute-done((f32[1,1024]{1,0:T(1,128)S(1)}, f32[1,1024]{1,0:T(1,128)S(1)}, u32[]{:S(2)}, u32[]{:S(2)}) %collective-permute-start.7) | collective-permute-done | bytes 4128 | tf_op jit(solution)/shard_map/ppermute | solution.py:395
  79.6 2.0 %shard_map.73 = (f32[1,1024]{1,0:T(1,128)S(1)}, f32[1,4096]{1,0:T(1,128)S(1)}) custom-call(f32[1024,4096]{1,0:T(8,128)S(1)} %get-tuple-element.54.soft_ref, f32[1,1024]{1,0:T(1,128)S(1)} %get-tuple-element.58.inverse_ref, f32[1,4096]{1,0:T(1,128)S(1)} %get-tuple-element.56.right_ref, f32[1,1024]{1,0:T(1,128)S(1)} %bitcast.22, ...), custom_call_target="tpu_custom_call" | custom-call | tf_op jit(solution)/shard_map/pallas_call | solution.py:370
  81.7 10.0 %all_to_all.17 = f32[8,32,128]{2,1,0:T(8,128)S(1)} all-to-all(f32[8,32,128]{2,1,0:T(8,128)S(1)} %broadcast_in_dim.26), channel_id=1, replica_groups=mesh['rows'=8,'cols'=4] {'rows'}, dimensions={0} | all-to-all | bytes 262144 | tf_op jit(solution)/shard_map/all_to_all | solution.py:460
  91.7 1.9 %shard_map.74 = (f32[1,4096]{1,0:T(1,128)S(1)}, f32[1,1024]{1,0:T(1,128)S(1)}) custom-call(f32[1024,4096]{1,0:T(8,128)S(1)} %get-tuple-element.54.soft_ref, f32[1,1024]{1,0:T(1,128)S(1)} %get-tuple-element.55.left_ref, f32[1,4096]{1,0:T(1,128)S(1)} %get-tuple-element.56.right_ref, f32[1,4096]{1,0:T(1,128)S(1)} %bitcast.16), custom_call_target="tpu_custom_call" | custom-call | tf_op jit(solution)/shard_map/pallas_call | solution.py:370
  95.8 6.4 %shard_map.75 = (f32[1024,4096]{1,0:T(8,128)S(1)}, f32[1024,4096]{1,0:T(8,128)S(1)}) custom-call(f32[1024,4096]{1,0:T(8,128)S(1)} %get-tuple-element.54.soft_ref, f32[1,1024]{1,0:T(1,128)S(1)} %get-tuple-element.58.inverse_ref, f32[1,1024]{1,0:T(1,128)S(1)} %get-tuple-element.61.scaled_ref, ...), custom_call_target="tpu_custom_call", output_to_operand_aliasing={{0}: (0, {})} | custom-call | tf_op jit(solution)/shard_map/pallas_call | solution.py:370
  102.2 3.0 %shard_map.76 = (f32[1024,128]{1,0:T(8,128)S(1)}, f32[256,128]{1,0:T(8,128)S(1)}, f32[256,128]{1,0:T(8,128)S(1)}, f32[256,128]{1,0:T(8,128)S(1)}, f32[256,128]{1...) custom-call(f32[1024,4096]{1,0:T(8,128)S(1)} %get-tuple-element.66.first_ref, ...), custom_call_target="tpu_custom_call" | custom-call | tf_op jit(solution)/shard_map/pallas_call | solution.py:370
  107.3 7.4 %shard_map.77 = (f32[512,128]{1,0:T(8,128)S(1)}, f32[512,128]{1,0:T(8,128)S(1)}, f32[256,128]{1,0:T(8,128)S(1)}, f32[256,128]{1,0:T(8,128)S(1)}, f32[256,128]{1,...) custom-call(f32[1024,4096]{1,0:T(8,128)S(1)} %get-tuple-element.66.f, ...), custom_call_target="tpu_custom_call" | custom-call | tf_op jit(solution)/shard_map/pallas_call | solution.py:370
  114.7 2.0 %collective-permute-start.27 = (f32[256,128]{1,0:T(8,128)S(1)}, f32[256,128]{1,0:T(8,128)S(1)}, u32[]{:S(2)}, u32[]{:S(2)}) collective-permute-start(f32[256,128]{1,0:T(8,128)S(1)} %add.316), channel_id=1, source_target_pairs={{8,0},{16,8},{24,16},{28,24},{20,28},{12,20},{4,12},{0,4},{9,1},{1... | collective-permute-start | bytes 393224 | tf_op jit(solution)/shard_map/ppermute | solution.py:421
  117.2 1.7 %collective-permute-start.17 = (f32[256,128]{1,0:T(8,128)S(1)}, f32[256,128]{1,0:T(8,128)S(1)}, u32[]{:S(2)}, u32[]{:S(2)}) collective-permute-start(f32[256,128]{1,0:T(8,128)S(1)} %add.306), channel_id=1, source_target_pairs={{0,8},{8,16},{16,24},{24,28},{28,20},{20,12},{12,4},{4,0},{1,9},{9... | collective-permute-start | bytes 393224 | tf_op jit(solution)/shard_map/ppermute | solution.py:418
  119.0 2.0 %collective-permute-done.27 = f32[256,128]{1,0:T(8,128)S(1)} collective-permute-done((f32[256,128]{1,0:T(8,128)S(1)}, f32[256,128]{1,0:T(8,128)S(1)}, u32[]{:S(2)}, u32[]{:S(2)}) %collective-permute-start.27) | collective-permute-done | bytes 131104 | tf_op jit(solution)/shard_map/ppermute | solution.py:421
  121.1 1.7 %collective-permute-start.28 = (f32[256,128]{1,0:T(8,128)S(1)}, f32[256,128]{1,0:T(8,128)S(1)}, u32[]{:S(2)}, u32[]{:S(2)}) collective-permute-start(f32[256,128]{1,0:T(8,128)S(1)} %add.317), channel_id=1, source_target_pairs={{8,0},{16,8},{24,16},{28,24},{20,28},{12,20},{4,12},{0,4},{9,1},{1... | collective-permute-start | bytes 393224 | tf_op jit(solution)/shard_map/ppermute | solution.py:421
  123.0 1.7 %collective-permute-start.21 = (f32[256,128]{1,0:T(8,128)S(1)}, f32[256,128]{1,0:T(8,128)S(1)}, u32[]{:S(2)}, u32[]{:S(2)}) collective-permute-start(f32[256,128]{1,0:T(8,128)S(1)} %add.310), channel_id=1, source_target_pairs={{8,0},{16,8},{24,16},{28,24},{20,28},{12,20},{4,12},{0,4},{9,1},{1... | collective-permute-start | bytes 393224 | tf_op jit(solution)/shard_map/ppermute | solution.py:421
  126.3 1.7 %collective-permute-start.25 = (f32[256,128]{1,0:T(8,128)S(1)}, f32[256,128]{1,0:T(8,128)S(1)}, u32[]{:S(2)}, u32[]{:S(2)}) collective-permute-start(f32[256,128]{1,0:T(8,128)S(1)} %add.314), channel_id=1, source_target_pairs={{0,8},{8,16},{16,24},{24,28},{28,20},{20,12},{12,4},{4,0},{1,9},{9... | collective-permute-start | bytes 393224 | tf_op jit(solution)/shard_map/ppermute | solution.py:418
  131.4 2.6 %collective-permute-done.25 = f32[256,128]{1,0:T(8,128)S(1)} collective-permute-done((f32[256,128]{1,0:T(8,128)S(1)}, f32[256,128]{1,0:T(8,128)S(1)}, u32[]{:S(2)}, u32[]{:S(2)}) %collective-permute-start.25) | collective-permute-done | bytes 131104 | tf_op jit(solution)/shard_map/ppermute | solution.py:418
  134.4 2.3 %collective-permute-done.22 = f32[256,128]{1,0:T(8,128)S(1)} collective-permute-done((f32[256,128]{1,0:T(8,128)S(1)}, f32[256,128]{1,0:T(8,128)S(1)}, u32[]{:S(2)}, u32[]{:S(2)}) %collective-permute-start.22) | collective-permute-done | bytes 131104 | tf_op jit(solution)/shard_map/ppermute | solution.py:421
  138.0 1.6 %collective-permute-start.41 = (f32[256,128]{1,0:T(8,128)S(1)}, f32[256,128]{1,0:T(8,128)S(1)}, u32[]{:S(2)}, u32[]{:S(2)}) collective-permute-start(f32[256,128]{1,0:T(8,128)S(1)} %add_add_fusion.refs_4_), channel_id=1, source_target_pairs={{0,8},{8,16},{16,24},{24,28},{28,20},{20,12},{12,4},{4,0},{1,9},{9... | collective-permute-start | bytes 393224 | tf_op jit(solution)/shard_map/ppermute | solution.py:418
  142.9 1.7 %collective-permute-done.41.refs_18_ = f32[256,128]{1,0:T(8,128)S(1)} collective-permute-done((f32[256,128]{1,0:T(8,128)S(1)}, f32[256,128]{1,0:T(8,128)S(1)}, u32[]{:S(2)}, u32[]{:S(2)}) %collective-permute-start.41) | collective-permute-done | bytes 131104 | tf_op jit(solution)/shard_map/ppermute | solution.py:418
  144.7 1.9 %collective-permute-start.32 = (f32[256,128]{1,0:T(8,128)S(1)}, f32[256,128]{1,0:T(8,128)S(1)}, u32[]{:S(2)}, u32[]{:S(2)}) collective-permute-start(f32[256,128]{1,0:T(8,128)S(1)} %collective-permute-done.30.refs_5_), channel_id=1, source_target_pairs={{8,0},{16,8},{24,16},{28,24},{20,28},{12,20},{4,12},{0,4},{9,1},{1... | collective-permute-start | bytes 393224 | tf_op jit(solution)/shard_map/ppermute | solution.py:421
  147.0 2.1 %collective-permute-done.37.refs_15_ = f32[256,128]{1,0:T(8,128)S(1)} collective-permute-done((f32[256,128]{1,0:T(8,128)S(1)}, f32[256,128]{1,0:T(8,128)S(1)}, u32[]{:S(2)}, u32[]{:S(2)}) %collective-permute-start.37) | collective-permute-done | bytes 131104 | tf_op jit(solution)/shard_map/ppermute | solution.py:418
  149.1 2.6 %collective-permute-done.42.refs_16_ = f32[256,128]{1,0:T(8,128)S(1)} collective-permute-done((f32[256,128]{1,0:T(8,128)S(1)}, f32[256,128]{1,0:T(8,128)S(1)}, u32[]{:S(2)}, u32[]{:S(2)}) %collective-permute-start.42) | collective-permute-done | bytes 131104 | tf_op jit(solution)/shard_map/ppermute | solution.py:418
  151.7 2.0 %collective-permute-start.34 = (f32[256,128]{1,0:T(8,128)S(1)}, f32[256,128]{1,0:T(8,128)S(1)}, u32[]{:S(2)}, u32[]{:S(2)}) collective-permute-start(f32[256,128]{1,0:T(8,128)S(1)} %collective-permute-done.32.refs_7_), channel_id=1, source_target_pairs={{8,0},{16,8},{24,16},{28,24},{20,28},{12,20},{4,12},{0,4},{9,1},{1... | collective-permute-start | bytes 393224 | tf_op jit(solution)/shard_map/ppermute | solution.py:421
  155.8 2.3 %collective-permute-done.43.refs_14_ = f32[256,128]{1,0:T(8,128)S(1)} collective-permute-done((f32[256,128]{1,0:T(8,128)S(1)}, f32[256,128]{1,0:T(8,128)S(1)}, u32[]{:S(2)}, u32[]{:S(2)}) %collective-permute-start.43) | collective-permute-done | bytes 131104 | tf_op jit(solution)/shard_map/ppermute | solution.py:418
  159.7 1.6 %shard_map.78 = (f32[1024,128]{1,0:T(8,128)}, f32[4096,128]{1,0:T(8,128)}) custom-call(f32[256,128]{1,0:T(8,128)S(1)} %slice_add_fusion.refs_0_, f32[256,128]{1,0:T(8,128)S(1)} %collective-permute-done.14.refs_1_, f32[512,128]{1,0:T(8,128)S(1)} %collective-permute-done.15.refs_2_, f32[256,128]{1,0:T(8,128)S(1)} %add_add_fusion.1.refs_3_, ...), custom_call_target="tpu_custom_call" | custom-call | tf_op jit(solution)/shard_map/pallas_call | solution.py:521
  (97 shorter events, 27.9 us)
Async XLA Ops:
  93.5 8.6 %collective-permute-start.10 = (f32[1,1024]{1,0:T(1,128)S(1)}, f32[1,1024]{1,0:T(1,128)S(1)}, u32[]{:S(2)}, u32[]{:S(2)}) collective-permute-start(f32[1,1024]{1,0:T(1,128)S(1)} %get-tuple-element.68.refs_0_), channel_id=1, source_target_pairs={{0,2},{1,3},{2,0},{3,1},{4,6},{5,7},{6,4},{7,5},{8,10},{9,11},{10,... | collective-permute-start | bytes 12296 | tf_op jit(solution)/shard_map/ppermute | solution.py:395
  94.2 8.0 %collective-permute-start.11 = (f32[1,1024]{1,0:T(1,128)S(1)}, f32[1,1024]{1,0:T(1,128)S(1)}, u32[]{:S(2)}, u32[]{:S(2)}) collective-permute-start(f32[1,1024]{1,0:T(1,128)S(1)} %get-tuple-element.68.refs_0_), channel_id=1, source_target_pairs={{0,3},{1,2},{2,1},{3,0},{4,7},{5,6},{6,5},{7,4},{8,11},{9,10},{10,... | collective-permute-start | bytes 12296 | tf_op jit(solution)/shard_map/ppermute | solution.py:395
  94.2 8.0 %collective-permute-start.9 = (f32[1,1024]{1,0:T(1,128)S(1)}, f32[1,1024]{1,0:T(1,128)S(1)}, u32[]{:S(2)}, u32[]{:S(2)}) collective-permute-start(f32[1,1024]{1,0:T(1,128)S(1)} %get-tuple-element.68.refs_0_), channel_id=1, source_target_pairs={{0,1},{1,0},{2,3},{3,2},{4,5},{5,4},{6,7},{7,6},{8,9},{9,8},{10,11... | collective-permute-start | bytes 12296 | tf_op jit(solution)/shard_map/ppermute | solution.py:395
  105.2 9.5 %collective-permute-start.26 = (f32[256,128]{1,0:T(8,128)S(1)}, f32[256,128]{1,0:T(8,128)S(1)}, u32[]{:S(2)}, u32[]{:S(2)}) collective-permute-start(f32[256,128]{1,0:T(8,128)S(1)} %get-tuple-element.89), channel_id=1, source_target_pairs={{8,0},{16,8},{24,16},{28,24},{20,28},{12,20},{4,12},{0,4},{9,1},{1... | collective-permute-start | bytes 393224 | tf_op jit(solution)/shard_map/ppermute | solution.py:421
  105.6 13.3 %collective-permute-start.23 = (f32[256,128]{1,0:T(8,128)S(1)}, f32[256,128]{1,0:T(8,128)S(1)}, u32[]{:S(2)}, u32[]{:S(2)}) collective-permute-start(f32[256,128]{1,0:T(8,128)S(1)} %get-tuple-element.85), channel_id=1, source_target_pairs={{0,8},{8,16},{16,24},{24,28},{28,20},{20,12},{12,4},{4,0},{1,9},{9... | collective-permute-start | bytes 393224 | tf_op jit(solution)/shard_map/ppermute | solution.py:418
  107.2 9.9 %collective-permute-start.16 = (f32[256,128]{1,0:T(8,128)S(1)}, f32[256,128]{1,0:T(8,128)S(1)}, u32[]{:S(2)}, u32[]{:S(2)}) collective-permute-start(f32[256,128]{1,0:T(8,128)S(1)} %get-tuple-element.78), channel_id=1, source_target_pairs={{0,8},{8,16},{16,24},{24,28},{28,20},{20,12},{12,4},{4,0},{1,9},{9... | collective-permute-start | bytes 393224 | tf_op jit(solution)/shard_map/ppermute | solution.py:418
  114.7 6.3 %collective-permute-start.27 = (f32[256,128]{1,0:T(8,128)S(1)}, f32[256,128]{1,0:T(8,128)S(1)}, u32[]{:S(2)}, u32[]{:S(2)}) collective-permute-start(f32[256,128]{1,0:T(8,128)S(1)} %add.316), channel_id=1, source_target_pairs={{8,0},{16,8},{24,16},{28,24},{20,28},{12,20},{4,12},{0,4},{9,1},{1... | collective-permute-start | bytes 393224 | tf_op jit(solution)/shard_map/ppermute | solution.py:421
  116.8 6.2 %collective-permute-start.20 = (f32[256,128]{1,0:T(8,128)S(1)}, f32[256,128]{1,0:T(8,128)S(1)}, u32[]{:S(2)}, u32[]{:S(2)}) collective-permute-start(f32[256,128]{1,0:T(8,128)S(1)} %get-tuple-element.81), channel_id=1, source_target_pairs={{8,0},{16,8},{24,16},{28,24},{20,28},{12,20},{4,12},{0,4},{9,1},{1... | collective-permute-start | bytes 393224 | tf_op jit(solution)/shard_map/ppermute | solution.py:421
  117.1 12.7 %collective-permute-start.12 = (f32[512,128]{1,0:T(8,128)S(1)}, f32[512,128]{1,0:T(8,128)S(1)}, u32[]{:S(2)}, u32[]{:S(2)}) collective-permute-start(f32[512,128]{1,0:T(8,128)S(1)} %get-tuple-element.73), channel_id=1, source_target_pairs={{0,1},{1,0},{2,3},{3,2},{4,5},{5,4},{6,7},{7,6},{8,9},{9,8},{10,11... | collective-permute-start | bytes 786440 | tf_op jit(solution)/shard_map/ppermute | solution.py:395
  117.2 7.5 %collective-permute-start.17 = (f32[256,128]{1,0:T(8,128)S(1)}, f32[256,128]{1,0:T(8,128)S(1)}, u32[]{:S(2)}, u32[]{:S(2)}) collective-permute-start(f32[256,128]{1,0:T(8,128)S(1)} %add.306), channel_id=1, source_target_pairs={{0,8},{8,16},{16,24},{24,28},{28,20},{20,12},{12,4},{4,0},{1,9},{9... | collective-permute-start | bytes 393224 | tf_op jit(solution)/shard_map/ppermute | solution.py:418
  118.9 7.4 %collective-permute-start.24 = (f32[256,128]{1,0:T(8,128)S(1)}, f32[256,128]{1,0:T(8,128)S(1)}, u32[]{:S(2)}, u32[]{:S(2)}) collective-permute-start(f32[256,128]{1,0:T(8,128)S(1)} %add.313), channel_id=1, source_target_pairs={{0,8},{8,16},{16,24},{24,28},{28,20},{20,12},{12,4},{4,0},{1,9},{9... | collective-permute-start | bytes 393224 | tf_op jit(solution)/shard_map/ppermute | solution.py:418
  121.1 7.0 %collective-permute-start.28 = (f32[256,128]{1,0:T(8,128)S(1)}, f32[256,128]{1,0:T(8,128)S(1)}, u32[]{:S(2)}, u32[]{:S(2)}) collective-permute-start(f32[256,128]{1,0:T(8,128)S(1)} %add.317), channel_id=1, source_target_pairs={{8,0},{16,8},{24,16},{28,24},{20,28},{12,20},{4,12},{0,4},{9,1},{1... | collective-permute-start | bytes 393224 | tf_op jit(solution)/shard_map/ppermute | solution.py:421
  123.0 5.5 %collective-permute-start.21 = (f32[256,128]{1,0:T(8,128)S(1)}, f32[256,128]{1,0:T(8,128)S(1)}, u32[]{:S(2)}, u32[]{:S(2)}) collective-permute-start(f32[256,128]{1,0:T(8,128)S(1)} %add.310), channel_id=1, source_target_pairs={{8,0},{16,8},{24,16},{28,24},{20,28},{12,20},{4,12},{0,4},{9,1},{1... | collective-permute-start | bytes 393224 | tf_op jit(solution)/shard_map/ppermute | solution.py:421
  124.7 6.4 %collective-permute-start.18 = (f32[256,128]{1,0:T(8,128)S(1)}, f32[256,128]{1,0:T(8,128)S(1)}, u32[]{:S(2)}, u32[]{:S(2)}) collective-permute-start(f32[256,128]{1,0:T(8,128)S(1)} %add.307), channel_id=1, source_target_pairs={{0,8},{8,16},{16,24},{24,28},{28,20},{20,12},{12,4},{4,0},{1,9},{9... | collective-permute-start | bytes 393224 | tf_op jit(solution)/shard_map/ppermute | solution.py:418
  126.3 7.6 %collective-permute-start.25 = (f32[256,128]{1,0:T(8,128)S(1)}, f32[256,128]{1,0:T(8,128)S(1)}, u32[]{:S(2)}, u32[]{:S(2)}) collective-permute-start(f32[256,128]{1,0:T(8,128)S(1)} %add.314), channel_id=1, source_target_pairs={{0,8},{8,16},{16,24},{24,28},{28,20},{20,12},{12,4},{4,0},{1,9},{9... | collective-permute-start | bytes 393224 | tf_op jit(solution)/shard_map/ppermute | solution.py:418
  128.1 5.9 %collective-permute-start.29 = (f32[256,128]{1,0:T(8,128)S(1)}, f32[256,128]{1,0:T(8,128)S(1)}, u32[]{:S(2)}, u32[]{:S(2)}) collective-permute-start(f32[256,128]{1,0:T(8,128)S(1)} %add.318), channel_id=1, source_target_pairs={{8,0},{16,8},{24,16},{28,24},{20,28},{12,20},{4,12},{0,4},{9,1},{1... | collective-permute-start | bytes 393224 | tf_op jit(solution)/shard_map/ppermute | solution.py:421
  128.5 8.2 %collective-permute-start.22 = (f32[256,128]{1,0:T(8,128)S(1)}, f32[256,128]{1,0:T(8,128)S(1)}, u32[]{:S(2)}, u32[]{:S(2)}) collective-permute-start(f32[256,128]{1,0:T(8,128)S(1)} %add.311), channel_id=1, source_target_pairs={{8,0},{16,8},{24,16},{28,24},{20,28},{12,20},{4,12},{0,4},{9,1},{1... | collective-permute-start | bytes 393224 | tf_op jit(solution)/shard_map/ppermute | solution.py:421
  129.9 7.1 %collective-permute-start.13 = (f32[256,128]{1,0:T(8,128)S(1)}, f32[256,128]{1,0:T(8,128)S(1)}, u32[]{:S(2)}, u32[]{:S(2)}) collective-permute-start(f32[256,128]{1,0:T(8,128)S(1)} %slice.9), channel_id=1, source_target_pairs={{0,2},{1,3},{2,0},{3,1},{4,6},{5,7},{6,4},{7,5},{8,10},{9,11},{10,... | collective-permute-start | bytes 393224 | tf_op jit(solution)/shard_map/ppermute | solution.py:395
  131.2 5.6 %collective-permute-start.19 = (f32[256,128]{1,0:T(8,128)S(1)}, f32[256,128]{1,0:T(8,128)S(1)}, u32[]{:S(2)}, u32[]{:S(2)}) collective-permute-start(f32[256,128]{1,0:T(8,128)S(1)} %add.308), channel_id=1, source_target_pairs={{0,8},{8,16},{16,24},{24,28},{28,20},{20,12},{12,4},{4,0},{1,9},{9... | collective-permute-start | bytes 393224 | tf_op jit(solution)/shard_map/ppermute | solution.py:418
  134.0 6.0 %collective-permute-start.31 = (f32[256,128]{1,0:T(8,128)S(1)}, f32[256,128]{1,0:T(8,128)S(1)}, u32[]{:S(2)}, u32[]{:S(2)}) collective-permute-start(f32[256,128]{1,0:T(8,128)S(1)} %add_add_fusion.refs_4_), channel_id=1, source_target_pairs={{8,0},{16,8},{24,16},{28,24},{20,28},{12,20},{4,12},{0,4},{9,1},{1... | collective-permute-start | bytes 393224 | tf_op jit(solution)/shard_map/ppermute | solution.py:421
  136.8 6.0 %collective-permute-start.36 = (f32[256,128]{1,0:T(8,128)S(1)}, f32[256,128]{1,0:T(8,128)S(1)}, u32[]{:S(2)}, u32[]{:S(2)}) collective-permute-start(f32[256,128]{1,0:T(8,128)S(1)} %add_add_fusion.1.refs_3_), channel_id=1, source_target_pairs={{0,8},{8,16},{16,24},{24,28},{28,20},{20,12},{12,4},{4,0},{1,9},{9... | collective-permute-start | bytes 393224 | tf_op jit(solution)/shard_map/ppermute | solution.py:418
  137.0 5.8 %collective-permute-start.14 = (f32[256,128]{1,0:T(8,128)S(1)}, f32[256,128]{1,0:T(8,128)S(1)}, u32[]{:S(2)}, u32[]{:S(2)}) collective-permute-start(f32[256,128]{1,0:T(8,128)S(1)} %slice_add_fusion.refs_0_), channel_id=1, source_target_pairs={{0,2},{1,3},{2,0},{3,1},{4,6},{5,7},{6,4},{7,5},{8,10},{9,11},{10,... | collective-permute-start | bytes 393224 | tf_op jit(solution)/shard_map/ppermute | solution.py:395
  138.0 6.6 %collective-permute-start.41 = (f32[256,128]{1,0:T(8,128)S(1)}, f32[256,128]{1,0:T(8,128)S(1)}, u32[]{:S(2)}, u32[]{:S(2)}) collective-permute-start(f32[256,128]{1,0:T(8,128)S(1)} %add_add_fusion.refs_4_), channel_id=1, source_target_pairs={{0,8},{8,16},{16,24},{24,28},{28,20},{20,12},{12,4},{4,0},{1,9},{9... | collective-permute-start | bytes 393224 | tf_op jit(solution)/shard_map/ppermute | solution.py:418
  140.0 6.6 %collective-permute-start.33 = (f32[256,128]{1,0:T(8,128)S(1)}, f32[256,128]{1,0:T(8,128)S(1)}, u32[]{:S(2)}, u32[]{:S(2)}) collective-permute-start(f32[256,128]{1,0:T(8,128)S(1)} %collective-permute-done.31.refs_6_), channel_id=1, source_target_pairs={{8,0},{16,8},{24,16},{28,24},{20,28},{12,20},{4,12},{0,4},{9,1},{1... | collective-permute-start | bytes 393224 | tf_op jit(solution)/shard_map/ppermute | solution.py:421
  142.8 6.3 %collective-permute-start.37 = (f32[256,128]{1,0:T(8,128)S(1)}, f32[256,128]{1,0:T(8,128)S(1)}, u32[]{:S(2)}, u32[]{:S(2)}) collective-permute-start(f32[256,128]{1,0:T(8,128)S(1)} %collective-permute-done.36.refs_17_), channel_id=1, source_target_pairs={{0,8},{8,16},{16,24},{24,28},{28,20},{20,12},{12,4},{4,0},{1,9},{9... | collective-permute-start | bytes 393224 | tf_op jit(solution)/shard_map/ppermute | solution.py:418
  142.8 12.9 %collective-permute-start.15 = (f32[512,128]{1,0:T(8,128)S(1)}, f32[512,128]{1,0:T(8,128)S(1)}, u32[]{:S(2)}, u32[]{:S(2)}) collective-permute-start(f32[512,128]{1,0:T(8,128)S(1)} %pad_maximum_fusion), channel_id=1, source_target_pairs={{0,1},{1,0},{2,3},{3,2},{4,5},{5,4},{6,7},{7,6},{8,9},{9,8},{10,11... | collective-permute-start | bytes 786440 | tf_op jit(solution)/shard_map/ppermute | solution.py:395
  144.6 7.1 %collective-permute-start.42 = (f32[256,128]{1,0:T(8,128)S(1)}, f32[256,128]{1,0:T(8,128)S(1)}, u32[]{:S(2)}, u32[]{:S(2)}) collective-permute-start(f32[256,128]{1,0:T(8,128)S(1)} %collective-permute-done.41.refs_18_), channel_id=1, source_target_pairs={{0,8},{8,16},{16,24},{24,28},{28,20},{20,12},{12,4},{4,0},{1,9},{9... | collective-permute-start | bytes 393224 | tf_op jit(solution)/shard_map/ppermute | solution.py:418
  144.7 7.0 %collective-permute-start.32 = (f32[256,128]{1,0:T(8,128)S(1)}, f32[256,128]{1,0:T(8,128)S(1)}, u32[]{:S(2)}, u32[]{:S(2)}) collective-permute-start(f32[256,128]{1,0:T(8,128)S(1)} %collective-permute-done.30.refs_5_), channel_id=1, source_target_pairs={{8,0},{16,8},{24,16},{28,24},{20,28},{12,20},{4,12},{0,4},{9,1},{1... | collective-permute-start | bytes 393224 | tf_op jit(solution)/shard_map/ppermute | solution.py:421
  146.6 7.1 %collective-permute-start.35 = (f32[256,128]{1,0:T(8,128)S(1)}, f32[256,128]{1,0:T(8,128)S(1)}, u32[]{:S(2)}, u32[]{:S(2)}) collective-permute-start(f32[256,128]{1,0:T(8,128)S(1)} %collective-permute-done.33.refs_8_), channel_id=1, source_target_pairs={{8,0},{16,8},{24,16},{28,24},{20,28},{12,20},{4,12},{0,4},{9,1},{1... | collective-permute-start | bytes 393224 | tf_op jit(solution)/shard_map/ppermute | solution.py:421
  149.1 5.6 %collective-permute-start.38 = (f32[256,128]{1,0:T(8,128)S(1)}, f32[256,128]{1,0:T(8,128)S(1)}, u32[]{:S(2)}, u32[]{:S(2)}) collective-permute-start(f32[256,128]{1,0:T(8,128)S(1)} %collective-permute-done.37.refs_15_), channel_id=1, source_target_pairs={{0,8},{8,16},{16,24},{24,28},{28,20},{20,12},{12,4},{4,0},{1,9},{9... | collective-permute-start | bytes 393224 | tf_op jit(solution)/shard_map/ppermute | solution.py:418
  151.7 6.3 %collective-permute-start.43 = (f32[256,128]{1,0:T(8,128)S(1)}, f32[256,128]{1,0:T(8,128)S(1)}, u32[]{:S(2)}, u32[]{:S(2)}) collective-permute-start(f32[256,128]{1,0:T(8,128)S(1)} %collective-permute-done.42.refs_16_), channel_id=1, source_target_pairs={{0,8},{8,16},{16,24},{24,28},{28,20},{20,12},{12,4},{4,0},{1,9},{9... | collective-permute-start | bytes 393224 | tf_op jit(solution)/shard_map/ppermute | solution.py:418
  151.7 6.3 %collective-permute-start.34 = (f32[256,128]{1,0:T(8,128)S(1)}, f32[256,128]{1,0:T(8,128)S(1)}, u32[]{:S(2)}, u32[]{:S(2)}) collective-permute-start(f32[256,128]{1,0:T(8,128)S(1)} %collective-permute-done.32.refs_7_), channel_id=1, source_target_pairs={{8,0},{16,8},{24,16},{28,24},{20,28},{12,20},{4,12},{0,4},{9,1},{1... | collective-permute-start | bytes 393224 | tf_op jit(solution)/shard_map/ppermute | solution.py:421
  (14 other events, 86.4 us)

commit v6 on v4

--- a/solution.py
+++ b/solution.py
@@ -10,7 +10,7 @@
 
 EPSILON = 0.05
 KAPPA = math.log2(math.e) / EPSILON
-LOWEST = -90.0
+LOWEST = -64.0
 LANES = 128
 WIDE = 512
 TALL = 256
@@ -233,22 +233,37 @@
     return lax.select(place < n // 2, 2 * place, 2 * (n - 1 - place) + 1)
 
 
+def thirds(x):
+    parts = []
+    for _ in range(3):
+        parts.append(x.astype(jnp.bfloat16).astype(F32))
+        x = x - parts[-1]
+    return parts
+
+
 def early_kernel(soft_ref, inverse_ref, scaled_ref, left_ref, scaled2_ref, right_ref, back_ref, mass_ref, *refs):
-    first_ref, early_ref, *row_refs = refs
-    height = 64
-    for row_ref, row in zip(row_refs, (inverse_ref, scaled_ref, left_ref)):
-        row_ref[...] = column_form(-row[...])
+    first_ref, early_ref, row_parts, column_parts = refs
+    row_parts[...] = jnp.zeros_like(row_parts)
+    column_parts[...] = jnp.zeros_like(column_parts)
+    at = 0
+    for row, column in ((inverse_ref, scaled2_ref), (scaled_ref, right_ref), (left_ref, back_ref)):
+        r, c = thirds(-row[...]), thirds(column[...])
+        for i, j in ((0, 0), (0, 1), (1, 0), (1, 1), (0, 2), (2, 0)):
+            row_parts[at:at + 1, :] = r[i]
+            column_parts[at:at + 1, :] = c[j]
+            at += 1
 
     def body(block, _):
-        rows = pl.ds(pl.multiple_of(block * height, height), height)
-        a, b, c = (ref[rows, :] for ref in row_refs)
-        for at in range(0, soft_ref.shape[1], LANES):
-            span = slice(at, at + LANES)
-            factor = a * scaled2_ref[:, span] + b * right_ref[:, span] + c * back_ref[:, span]
+        rows = pl.ds(pl.multiple_of(block * TALL, TALL), TALL)
+        r = row_parts[:, rows].astype(jnp.bfloat16)
+        for at in range(0, soft_ref.shape[1], WIDE):
+            span = slice(at, at + WIDE)
+            factor = lax.dot_general(
+                r, column_parts[:, span].astype(jnp.bfloat16), (((0,), (0,)), ((), ())), preferred_element_type=F32)
             early_ref[rows, span] = soft_ref[rows, span] * factor
         return _
 
-    lax.fori_loop(0, soft_ref.shape[0] // height, body, 0)
+    lax.fori_loop(0, soft_ref.shape[0] // TALL, body, 0)
     mass = mass_ref[...]
 
     @pl.when(jnp.max(jnp.abs(mass - 1.0)) > 0.0)
@@ -478,7 +493,7 @@
     ahead = share % (2 * LANES) == 0
     first, early = call(
         early_kernel, [soft, inverse, scaled, left, scaled2, right, back, mass],
-        [tile_shape, tile_shape], [tall] * 3, aliases={0: 0})
+        [tile_shape, tile_shape], [(32, rows), (32, columns)], aliases={0: 0})
     first, early = kept(first), kept(early)
     last, *far = call(
         functools.partial(far_kernel, len(parts), n), [first, early, left, crawl, *parts],

time: 158 us -> 157 us (level)
  transfers between devices with their start and end apart: 44 -> 44, of which waited for: 20 -> 20; matrix products, arithmetic and copies ran while one was open for 0% -> 0% of each run, Pallas kernels for 8% -> 7%
where the time goes in v6:
time: 157 us
  Pallas kernels  59.2 us (38%)
  starting transfers between devices  34.9 us (22%)
  blocking collectives  32.9 us (21%)
  waiting for transfers between devices  28.6 us (18%)
    pallas_call x9, Pallas kernels, call(): pl.pallas_call(kernel, in_specs=[pl.BlockSpec(memory_space=pltpu.VMEM)] *...  49.1 us
    all_to_all x3, blocking collectives, over_rows(): lax.all_to_all(copies, 'rows', 0, 0)  32.9 us
    ppermute x14, waiting for transfers between devices, ahead(): return lax.ppermute(x, 'rows', up)  16.7 us
    ppermute x14, starting transfers between devices, behind(): return lax.ppermute(x, 'rows', down)  14.9 us
    ppermute x16, starting transfers between devices, exchange(): lax.ppermute(x, axis, [(i, i ^ k * stride) for i in range(n)])  10.9 us
    ppermute x14, starting transfers between devices, ahead(): return lax.ppermute(x, 'rows', up)  9.12 us
    pallas_call x1, Pallas kernels, per_device(): pl.pallas_call(row_level_kernel, in_specs=[pl.BlockSpec(memory_space=pltp...  8.39 us
    ppermute x16, waiting for transfers between devices, exchange(): lax.ppermute(x, axis, [(i, i ^ k * stride) for i in range(n)])  7.51 us
  transfers between devices with their start and end apart: 44, of which 20 were waited for; matrix products, arithmetic and copies ran while one was open for 0% of the time, Pallas kernels for 7%

profile of v6, /device:TPU:0, one launch (start us, length us, event | category | flops | bytes accessed | tf_op | source)
XLA Modules:
  0.0 157.1 jit_solution(10293706495121714918)
XLA Ops:
  0.6 8.4 %shard_map.68 = (f32[1024,4096]{1,0:T(8,128)S(1)}, f32[1,1024]{1,0:T(1,128)S(1)}, f32[1,1024]{1,0:T(1,128)S(1)}, bf16[1024,128]{1,0:T(8,128)(2,1)S(1)}, bf16[409...) custom-call(bf16[1024,128]{1,0:T(8,128)(2,1)} %crawl_hbm.1, bf16[4096,128]{1,0:T(8,128)(2,1)} %bench_hbm.1, f32[1,4096]{1,0:T(1,128)} %bitcast.31), custom_call_target="tpu_custom_call" | custom-call | tf_op jit(solution)/shard_map/pallas_call | solution.py:454
  9.5 2.6 %collective-permute-start.1 = (f32[1,1024]{1,0:T(1,128)S(1)}, f32[1,1024]{1,0:T(1,128)S(1)}, u32[]{:S(2)}, u32[]{:S(2)}) collective-permute-start(f32[1,1024]{1,0:T(1,128)S(1)} %get-tuple-element.46.refs_0_), channel_id=1, source_target_pairs={{0,2},{1,3},{2,0},{3,1},{4,6},{5,7},{6,4},{7,5},{8,10},{9,11},{10,... | collective-permute-start | bytes 12296 | tf_op jit(solution)/shard_map/ppermute | solution.py:387
  15.1 19.3 %shard_map.69 = (f32[1,1024]{1,0:T(1,128)S(1)}, f32[1,4096]{1,0:T(1,128)S(1)}) custom-call(f32[1024,4096]{1,0:T(8,128)S(1)} %get-tuple-element.44.tile_ref, f32[1,1024]{1,0:T(1,128)S(1)} %get-tuple-element.45.top_ref, f32[1,1024]{1,0:T(1,128)S(1)} %get-tuple-element.46.refs_0_, f32[1,1024]{1,0:T(1,128)S(1)} %collective-permute-done.refs_1_, ...), custom_call_target="tpu_custom_call" | custom-call | tf_op jit(solution)/shard_map/pallas_call | solution.py:362
  34.5 13.0 %all_to_all.15 = f32[8,32,128]{2,1,0:T(8,128)S(1)} all-to-all(f32[8,32,128]{2,1,0:T(8,128)S(1)} %broadcast_in_dim.22), channel_id=1, replica_groups=mesh['rows'=8,'cols'=4] {'rows'}, dimensions={0} | all-to-all | bytes 262144 | tf_op jit(solution)/shard_map/all_to_all | solution.py:452
  47.7 9.5 %shard_map.70 = (f32[1024,4096]{1,0:T(8,128)S(1)}, f32[1,1024]{1,0:T(1,128)S(1)}, f32[1,4096]{1,0:T(1,128)S(1)}, f32[1,4096]{1,0:T(1,128)S(1)}, f32[1,1024]{1,0:T(1,128)S(1)}) custom-call(f32[1024,4096]{1,0:T(8,128)S(1)} %get-tuple-element.44.tile_ref, f32[1,1024]{1,0:T(1,128)S(1)} %get-tuple-element.45.top_ref, ...), custom_call_target="tpu_custom_call", output_to_operand_aliasing={{0}: (0, {})} | custom-call | tf_op jit(solution)/shard_map/pallas_call | solution.py:362
  59.2 1.8 %collective-permute-done.4.refs_2_ = f32[1,1024]{1,0:T(1,128)S(1)} collective-permute-done((f32[1,1024]{1,0:T(1,128)S(1)}, f32[1,1024]{1,0:T(1,128)S(1)}, u32[]{:S(2)}, u32[]{:S(2)}) %collective-permute-start.4) | collective-permute-done | bytes 4128 | tf_op jit(solution)/shard_map/ppermute | solution.py:387
  61.0 2.0 %shard_map.71 = (f32[1,1024]{1,0:T(1,128)S(1)}, f32[1,4096]{1,0:T(1,128)S(1)}) custom-call(f32[1024,4096]{1,0:T(8,128)S(1)} %get-tuple-element.52.soft_ref, f32[1,1024]{1,0:T(1,128)S(1)} %get-tuple-element.53.left_ref, f32[1,4096]{1,0:T(1,128)S(1)} %get-tuple-element.54.right_ref, f32[1,1024]{1,0:T(1,128)S(1)} %get-tuple-element.55.refs_0_, ...), custom_call_target="tpu_custom_call" | custom-call | tf_op jit(solution)/shard_map/pallas_call | solution.py:362
  63.1 9.9 %all_to_all.16 = f32[8,32,128]{2,1,0:T(8,128)S(1)} all-to-all(f32[8,32,128]{2,1,0:T(8,128)S(1)} %broadcast_in_dim.24), channel_id=1, replica_groups=mesh['rows'=8,'cols'=4] {'rows'}, dimensions={0} | all-to-all | bytes 262144 | tf_op jit(solution)/shard_map/all_to_all | solution.py:452
  73.0 1.8 %shard_map.72 = (f32[1,4096]{1,0:T(1,128)S(1)}, f32[1,1024]{1,0:T(1,128)S(1)}) custom-call(f32[1024,4096]{1,0:T(8,128)S(1)} %get-tuple-element.52.soft_ref, f32[1,1024]{1,0:T(1,128)S(1)} %get-tuple-element.56.inverse_ref, f32[1,4096]{1,0:T(1,128)S(1)} %get-tuple-element.54.right_ref, f32[1,4096]{1,0:T(1,128)S(1)} %bitcast.21, f32[1,4096]{1,0:T(1,128)S(1)} %bitcast.17), custom_call_target="tpu_custom_call" | custom-call | tf_op jit(solution)/shard_map/pallas_call | solution.py:362
  76.7 1.8 %collective-permute-done.7.refs_2_ = f32[1,1024]{1,0:T(1,128)S(1)} collective-permute-done((f32[1,1024]{1,0:T(1,128)S(1)}, f32[1,1024]{1,0:T(1,128)S(1)}, u32[]{:S(2)}, u32[]{:S(2)}) %collective-permute-start.7) | collective-permute-done | bytes 4128 | tf_op jit(solution)/shard_map/ppermute | solution.py:387
  79.4 2.0 %shard_map.73 = (f32[1,1024]{1,0:T(1,128)S(1)}, f32[1,4096]{1,0:T(1,128)S(1)}) custom-call(f32[1024,4096]{1,0:T(8,128)S(1)} %get-tuple-element.52.soft_ref, f32[1,1024]{1,0:T(1,128)S(1)} %get-tuple-element.56.inverse_ref, f32[1,4096]{1,0:T(1,128)S(1)} %get-tuple-element.54.right_ref, f32[1,1024]{1,0:T(1,128)S(1)} %bitcast.22, ...), custom_call_target="tpu_custom_call" | custom-call | tf_op jit(solution)/shard_map/pallas_call | solution.py:362
  81.4 10.0 %all_to_all.17 = f32[8,32,128]{2,1,0:T(8,128)S(1)} all-to-all(f32[8,32,128]{2,1,0:T(8,128)S(1)} %broadcast_in_dim.26), channel_id=1, replica_groups=mesh['rows'=8,'cols'=4] {'rows'}, dimensions={0} | all-to-all | bytes 262144 | tf_op jit(solution)/shard_map/all_to_all | solution.py:452
  91.4 1.9 %shard_map.74 = (f32[1,4096]{1,0:T(1,128)S(1)}, f32[1,1024]{1,0:T(1,128)S(1)}) custom-call(f32[1024,4096]{1,0:T(8,128)S(1)} %get-tuple-element.52.soft_ref, f32[1,1024]{1,0:T(1,128)S(1)} %get-tuple-element.53.left_ref, f32[1,4096]{1,0:T(1,128)S(1)} %get-tuple-element.54.right_ref, f32[1,4096]{1,0:T(1,128)S(1)} %bitcast.16), custom_call_target="tpu_custom_call" | custom-call | tf_op jit(solution)/shard_map/pallas_call | solution.py:362
  95.5 5.7 %shard_map.75 = (f32[1024,4096]{1,0:T(8,128)S(1)}, f32[1024,4096]{1,0:T(8,128)S(1)}) custom-call(f32[1024,4096]{1,0:T(8,128)S(1)} %get-tuple-element.52.soft_ref, f32[1,1024]{1,0:T(1,128)S(1)} %get-tuple-element.56.inverse_ref, f32[1,1024]{1,0:T(1,128)S(1)} %get-tuple-element.59.scaled_ref, ...), custom_call_target="tpu_custom_call", output_to_operand_aliasing={{0}: (0, {})} | custom-call | tf_op jit(solution)/shard_map/pallas_call | solution.py:362
  101.2 1.6 shard_map.76
  103.3 1.6 %collective-permute-start.16 = (f32[256,128]{1,0:T(8,128)S(1)}, f32[256,128]{1,0:T(8,128)S(1)}, u32[]{:S(2)}, u32[]{:S(2)}) collective-permute-start(f32[256,128]{1,0:T(8,128)S(1)} %get-tuple-element.74), channel_id=1, source_target_pairs={{0,8},{8,16},{16,24},{24,28},{28,20},{20,12},{12,4},{4,0},{1,9},{9... | collective-permute-start | bytes 393224 | tf_op jit(solution)/shard_map/ppermute | solution.py:410
  104.9 5.5 %shard_map.77 = (f32[512,128]{1,0:T(8,128)S(1)}, f32[512,128]{1,0:T(8,128)S(1)}, f32[256,128]{1,0:T(8,128)S(1)}, f32[256,128]{1,0:T(8,128)S(1)}, f32[256,128]{1,...) custom-call(f32[1024,4096]{1,0:T(8,128)S(1)} %get-tuple-element.64.f, ...), custom_call_target="tpu_custom_call" | custom-call | tf_op jit(solution)/shard_map/pallas_call | solution.py:362
  110.5 2.0 %collective-permute-start.27 = (f32[256,128]{1,0:T(8,128)S(1)}, f32[256,128]{1,0:T(8,128)S(1)}, u32[]{:S(2)}, u32[]{:S(2)}) collective-permute-start(f32[256,128]{1,0:T(8,128)S(1)} %add.316), channel_id=1, source_target_pairs={{8,0},{16,8},{24,16},{28,24},{20,28},{12,20},{4,12},{0,4},{9,1},{1... | collective-permute-start | bytes 393224 | tf_op jit(solution)/shard_map/ppermute | solution.py:413
  112.9 1.7 %collective-permute-start.17 = (f32[256,128]{1,0:T(8,128)S(1)}, f32[256,128]{1,0:T(8,128)S(1)}, u32[]{:S(2)}, u32[]{:S(2)}) collective-permute-start(f32[256,128]{1,0:T(8,128)S(1)} %add.306), channel_id=1, source_target_pairs={{0,8},{8,16},{16,24},{24,28},{28,20},{20,12},{12,4},{4,0},{1,9},{9... | collective-permute-start | bytes 393224 | tf_op jit(solution)/shard_map/ppermute | solution.py:410
  116.8 1.7 %collective-permute-start.28 = (f32[256,128]{1,0:T(8,128)S(1)}, f32[256,128]{1,0:T(8,128)S(1)}, u32[]{:S(2)}, u32[]{:S(2)}) collective-permute-start(f32[256,128]{1,0:T(8,128)S(1)} %add.317), channel_id=1, source_target_pairs={{8,0},{16,8},{24,16},{28,24},{20,28},{12,20},{4,12},{0,4},{9,1},{1... | collective-permute-start | bytes 393224 | tf_op jit(solution)/shard_map/ppermute | solution.py:413
  118.7 1.7 %collective-permute-start.21 = (f32[256,128]{1,0:T(8,128)S(1)}, f32[256,128]{1,0:T(8,128)S(1)}, u32[]{:S(2)}, u32[]{:S(2)}) collective-permute-start(f32[256,128]{1,0:T(8,128)S(1)} %add.310), channel_id=1, source_target_pairs={{8,0},{16,8},{24,16},{28,24},{20,28},{12,20},{4,12},{0,4},{9,1},{1... | collective-permute-start | bytes 393224 | tf_op jit(solution)/shard_map/ppermute | solution.py:413
  122.1 1.7 %collective-permute-start.25 = (f32[256,128]{1,0:T(8,128)S(1)}, f32[256,128]{1,0:T(8,128)S(1)}, u32[]{:S(2)}, u32[]{:S(2)}) collective-permute-start(f32[256,128]{1,0:T(8,128)S(1)} %add.314), channel_id=1, source_target_pairs={{0,8},{8,16},{16,24},{24,28},{28,20},{20,12},{12,4},{4,0},{1,9},{9... | collective-permute-start | bytes 393224 | tf_op jit(solution)/shard_map/ppermute | solution.py:410
  127.1 2.6 %collective-permute-done.25 = f32[256,128]{1,0:T(8,128)S(1)} collective-permute-done((f32[256,128]{1,0:T(8,128)S(1)}, f32[256,128]{1,0:T(8,128)S(1)}, u32[]{:S(2)}, u32[]{:S(2)}) %collective-permute-start.25) | collective-permute-done | bytes 131104 | tf_op jit(solution)/shard_map/ppermute | solution.py:410
  130.2 2.3 %collective-permute-done.22 = f32[256,128]{1,0:T(8,128)S(1)} collective-permute-done((f32[256,128]{1,0:T(8,128)S(1)}, f32[256,128]{1,0:T(8,128)S(1)}, u32[]{:S(2)}, u32[]{:S(2)}) %collective-permute-start.22) | collective-permute-done | bytes 131104 | tf_op jit(solution)/shard_map/ppermute | solution.py:413
  133.7 1.6 %collective-permute-start.41 = (f32[256,128]{1,0:T(8,128)S(1)}, f32[256,128]{1,0:T(8,128)S(1)}, u32[]{:S(2)}, u32[]{:S(2)}) collective-permute-start(f32[256,128]{1,0:T(8,128)S(1)} %add_add_fusion.refs_4_), channel_id=1, source_target_pairs={{0,8},{8,16},{16,24},{24,28},{28,20},{20,12},{12,4},{4,0},{1,9},{9... | collective-permute-start | bytes 393224 | tf_op jit(solution)/shard_map/ppermute | solution.py:410
  138.7 1.7 %collective-permute-done.41.refs_18_ = f32[256,128]{1,0:T(8,128)S(1)} collective-permute-done((f32[256,128]{1,0:T(8,128)S(1)}, f32[256,128]{1,0:T(8,128)S(1)}, u32[]{:S(2)}, u32[]{:S(2)}) %collective-permute-start.41) | collective-permute-done | bytes 131104 | tf_op jit(solution)/shard_map/ppermute | solution.py:410
  140.5 1.9 %collective-permute-start.32 = (f32[256,128]{1,0:T(8,128)S(1)}, f32[256,128]{1,0:T(8,128)S(1)}, u32[]{:S(2)}, u32[]{:S(2)}) collective-permute-start(f32[256,128]{1,0:T(8,128)S(1)} %collective-permute-done.30.refs_5_), channel_id=1, source_target_pairs={{8,0},{16,8},{24,16},{28,24},{20,28},{12,20},{4,12},{0,4},{9,1},{1... | collective-permute-start | bytes 393224 | tf_op jit(solution)/shard_map/ppermute | solution.py:413
  142.8 2.1 %collective-permute-done.37.refs_15_ = f32[256,128]{1,0:T(8,128)S(1)} collective-permute-done((f32[256,128]{1,0:T(8,128)S(1)}, f32[256,128]{1,0:T(8,128)S(1)}, u32[]{:S(2)}, u32[]{:S(2)}) %collective-permute-start.37) | collective-permute-done | bytes 131104 | tf_op jit(solution)/shard_map/ppermute | solution.py:410
  144.9 2.6 %collective-permute-done.42.refs_16_ = f32[256,128]{1,0:T(8,128)S(1)} collective-permute-done((f32[256,128]{1,0:T(8,128)S(1)}, f32[256,128]{1,0:T(8,128)S(1)}, u32[]{:S(2)}, u32[]{:S(2)}) %collective-permute-start.42) | collective-permute-done | bytes 131104 | tf_op jit(solution)/shard_map/ppermute | solution.py:410
  147.5 2.0 %collective-permute-start.34 = (f32[256,128]{1,0:T(8,128)S(1)}, f32[256,128]{1,0:T(8,128)S(1)}, u32[]{:S(2)}, u32[]{:S(2)}) collective-permute-start(f32[256,128]{1,0:T(8,128)S(1)} %collective-permute-done.32.refs_7_), channel_id=1, source_target_pairs={{8,0},{16,8},{24,16},{28,24},{20,28},{12,20},{4,12},{0,4},{9,1},{1... | collective-permute-start | bytes 393224 | tf_op jit(solution)/shard_map/ppermute | solution.py:413
  151.5 2.3 %collective-permute-done.43.refs_14_ = f32[256,128]{1,0:T(8,128)S(1)} collective-permute-done((f32[256,128]{1,0:T(8,128)S(1)}, f32[256,128]{1,0:T(8,128)S(1)}, u32[]{:S(2)}, u32[]{:S(2)}) %collective-permute-start.43) | collective-permute-done | bytes 131104 | tf_op jit(solution)/shard_map/ppermute | solution.py:410
  155.4 1.6 %shard_map.78 = (f32[1024,128]{1,0:T(8,128)}, f32[4096,128]{1,0:T(8,128)}) custom-call(f32[256,128]{1,0:T(8,128)S(1)} %slice_add_fusion.refs_0_, f32[256,128]{1,0:T(8,128)S(1)} %collective-permute-done.14.refs_1_, f32[512,128]{1,0:T(8,128)S(1)} %collective-permute-done.15.refs_2_, f32[256,128]{1,0:T(8,128)S(1)} %add_add_fusion.1.refs_3_, ...), custom_call_target="tpu_custom_call" | custom-call | tf_op jit(solution)/shard_map/pallas_call | solution.py:510
  (97 shorter events, 28.4 us)
Async XLA Ops:
  93.3 7.9 %collective-permute-start.10 = (f32[1,1024]{1,0:T(1,128)S(1)}, f32[1,1024]{1,0:T(1,128)S(1)}, u32[]{:S(2)}, u32[]{:S(2)}) collective-permute-start(f32[1,1024]{1,0:T(1,128)S(1)} %get-tuple-element.66.refs_0_), channel_id=1, source_target_pairs={{0,2},{1,3},{2,0},{3,1},{4,6},{5,7},{6,4},{7,5},{8,10},{9,11},{10,... | collective-permute-start | bytes 12296 | tf_op jit(solution)/shard_map/ppermute | solution.py:387
  94.0 7.3 %collective-permute-start.11 = (f32[1,1024]{1,0:T(1,128)S(1)}, f32[1,1024]{1,0:T(1,128)S(1)}, u32[]{:S(2)}, u32[]{:S(2)}) collective-permute-start(f32[1,1024]{1,0:T(1,128)S(1)} %get-tuple-element.66.refs_0_), channel_id=1, source_target_pairs={{0,3},{1,2},{2,1},{3,0},{4,7},{5,6},{6,5},{7,4},{8,11},{9,10},{10,... | collective-permute-start | bytes 12296 | tf_op jit(solution)/shard_map/ppermute | solution.py:387
  94.0 7.3 %collective-permute-start.9 = (f32[1,1024]{1,0:T(1,128)S(1)}, f32[1,1024]{1,0:T(1,128)S(1)}, u32[]{:S(2)}, u32[]{:S(2)}) collective-permute-start(f32[1,1024]{1,0:T(1,128)S(1)} %get-tuple-element.66.refs_0_), channel_id=1, source_target_pairs={{0,1},{1,0},{2,3},{3,2},{4,5},{5,4},{6,7},{7,6},{8,9},{9,8},{10,11... | collective-permute-start | bytes 12296 | tf_op jit(solution)/shard_map/ppermute | solution.py:387
  102.8 7.6 %collective-permute-start.26 = (f32[256,128]{1,0:T(8,128)S(1)}, f32[256,128]{1,0:T(8,128)S(1)}, u32[]{:S(2)}, u32[]{:S(2)}) collective-permute-start(f32[256,128]{1,0:T(8,128)S(1)} %get-tuple-element.85), channel_id=1, source_target_pairs={{8,0},{16,8},{24,16},{28,24},{20,28},{12,20},{4,12},{0,4},{9,1},{1... | collective-permute-start | bytes 393224 | tf_op jit(solution)/shard_map/ppermute | solution.py:413
  103.3 9.7 %collective-permute-start.16 = (f32[256,128]{1,0:T(8,128)S(1)}, f32[256,128]{1,0:T(8,128)S(1)}, u32[]{:S(2)}, u32[]{:S(2)}) collective-permute-start(f32[256,128]{1,0:T(8,128)S(1)} %get-tuple-element.74), channel_id=1, source_target_pairs={{0,8},{8,16},{16,24},{24,28},{28,20},{20,12},{12,4},{4,0},{1,9},{9... | collective-permute-start | bytes 393224 | tf_op jit(solution)/shard_map/ppermute | solution.py:410
  110.5 6.3 %collective-permute-start.27 = (f32[256,128]{1,0:T(8,128)S(1)}, f32[256,128]{1,0:T(8,128)S(1)}, u32[]{:S(2)}, u32[]{:S(2)}) collective-permute-start(f32[256,128]{1,0:T(8,128)S(1)} %add.316), channel_id=1, source_target_pairs={{8,0},{16,8},{24,16},{28,24},{20,28},{12,20},{4,12},{0,4},{9,1},{1... | collective-permute-start | bytes 393224 | tf_op jit(solution)/shard_map/ppermute | solution.py:413
  112.5 6.2 %collective-permute-start.20 = (f32[256,128]{1,0:T(8,128)S(1)}, f32[256,128]{1,0:T(8,128)S(1)}, u32[]{:S(2)}, u32[]{:S(2)}) collective-permute-start(f32[256,128]{1,0:T(8,128)S(1)} %get-tuple-element.77), channel_id=1, source_target_pairs={{8,0},{16,8},{24,16},{28,24},{20,28},{12,20},{4,12},{0,4},{9,1},{1... | collective-permute-start | bytes 393224 | tf_op jit(solution)/shard_map/ppermute | solution.py:413
  112.9 12.7 %collective-permute-start.12 = (f32[512,128]{1,0:T(8,128)S(1)}, f32[512,128]{1,0:T(8,128)S(1)}, u32[]{:S(2)}, u32[]{:S(2)}) collective-permute-start(f32[512,128]{1,0:T(8,128)S(1)} %get-tuple-element.69), channel_id=1, source_target_pairs={{0,1},{1,0},{2,3},{3,2},{4,5},{5,4},{6,7},{7,6},{8,9},{9,8},{10,11... | collective-permute-start | bytes 786440 | tf_op jit(solution)/shard_map/ppermute | solution.py:387
  112.9 7.5 %collective-permute-start.17 = (f32[256,128]{1,0:T(8,128)S(1)}, f32[256,128]{1,0:T(8,128)S(1)}, u32[]{:S(2)}, u32[]{:S(2)}) collective-permute-start(f32[256,128]{1,0:T(8,128)S(1)} %add.306), channel_id=1, source_target_pairs={{0,8},{8,16},{16,24},{24,28},{28,20},{20,12},{12,4},{4,0},{1,9},{9... | collective-permute-start | bytes 393224 | tf_op jit(solution)/shard_map/ppermute | solution.py:410
  115.4 6.7 %collective-permute-start.24 = (f32[256,128]{1,0:T(8,128)S(1)}, f32[256,128]{1,0:T(8,128)S(1)}, u32[]{:S(2)}, u32[]{:S(2)}) collective-permute-start(f32[256,128]{1,0:T(8,128)S(1)} %add.313), channel_id=1, source_target_pairs={{0,8},{8,16},{16,24},{24,28},{28,20},{20,12},{12,4},{4,0},{1,9},{9... | collective-permute-start | bytes 393224 | tf_op jit(solution)/shard_map/ppermute | solution.py:410
  116.8 7.0 %collective-permute-start.28 = (f32[256,128]{1,0:T(8,128)S(1)}, f32[256,128]{1,0:T(8,128)S(1)}, u32[]{:S(2)}, u32[]{:S(2)}) collective-permute-start(f32[256,128]{1,0:T(8,128)S(1)} %add.317), channel_id=1, source_target_pairs={{8,0},{16,8},{24,16},{28,24},{20,28},{12,20},{4,12},{0,4},{9,1},{1... | collective-permute-start | bytes 393224 | tf_op jit(solution)/shard_map/ppermute | solution.py:413
  118.7 5.5 %collective-permute-start.21 = (f32[256,128]{1,0:T(8,128)S(1)}, f32[256,128]{1,0:T(8,128)S(1)}, u32[]{:S(2)}, u32[]{:S(2)}) collective-permute-start(f32[256,128]{1,0:T(8,128)S(1)} %add.310), channel_id=1, source_target_pairs={{8,0},{16,8},{24,16},{28,24},{20,28},{12,20},{4,12},{0,4},{9,1},{1... | collective-permute-start | bytes 393224 | tf_op jit(solution)/shard_map/ppermute | solution.py:413
  120.5 6.4 %collective-permute-start.18 = (f32[256,128]{1,0:T(8,128)S(1)}, f32[256,128]{1,0:T(8,128)S(1)}, u32[]{:S(2)}, u32[]{:S(2)}) collective-permute-start(f32[256,128]{1,0:T(8,128)S(1)} %add.307), channel_id=1, source_target_pairs={{0,8},{8,16},{16,24},{24,28},{28,20},{20,12},{12,4},{4,0},{1,9},{9... | collective-permute-start | bytes 393224 | tf_op jit(solution)/shard_map/ppermute | solution.py:410
  122.1 7.6 %collective-permute-start.25 = (f32[256,128]{1,0:T(8,128)S(1)}, f32[256,128]{1,0:T(8,128)S(1)}, u32[]{:S(2)}, u32[]{:S(2)}) collective-permute-start(f32[256,128]{1,0:T(8,128)S(1)} %add.314), channel_id=1, source_target_pairs={{0,8},{8,16},{16,24},{24,28},{28,20},{20,12},{12,4},{4,0},{1,9},{9... | collective-permute-start | bytes 393224 | tf_op jit(solution)/shard_map/ppermute | solution.py:410
  123.8 5.9 %collective-permute-start.29 = (f32[256,128]{1,0:T(8,128)S(1)}, f32[256,128]{1,0:T(8,128)S(1)}, u32[]{:S(2)}, u32[]{:S(2)}) collective-permute-start(f32[256,128]{1,0:T(8,128)S(1)} %add.318), channel_id=1, source_target_pairs={{8,0},{16,8},{24,16},{28,24},{20,28},{12,20},{4,12},{0,4},{9,1},{1... | collective-permute-start | bytes 393224 | tf_op jit(solution)/shard_map/ppermute | solution.py:413
  124.3 8.2 %collective-permute-start.22 = (f32[256,128]{1,0:T(8,128)S(1)}, f32[256,128]{1,0:T(8,128)S(1)}, u32[]{:S(2)}, u32[]{:S(2)}) collective-permute-start(f32[256,128]{1,0:T(8,128)S(1)} %add.311), channel_id=1, source_target_pairs={{8,0},{16,8},{24,16},{28,24},{20,28},{12,20},{4,12},{0,4},{9,1},{1... | collective-permute-start | bytes 393224 | tf_op jit(solution)/shard_map/ppermute | solution.py:413
  125.6 7.1 %collective-permute-start.13 = (f32[256,128]{1,0:T(8,128)S(1)}, f32[256,128]{1,0:T(8,128)S(1)}, u32[]{:S(2)}, u32[]{:S(2)}) collective-permute-start(f32[256,128]{1,0:T(8,128)S(1)} %slice.9), channel_id=1, source_target_pairs={{0,2},{1,3},{2,0},{3,1},{4,6},{5,7},{6,4},{7,5},{8,10},{9,11},{10,... | collective-permute-start | bytes 393224 | tf_op jit(solution)/shard_map/ppermute | solution.py:387
  126.9 5.6 %collective-permute-start.19 = (f32[256,128]{1,0:T(8,128)S(1)}, f32[256,128]{1,0:T(8,128)S(1)}, u32[]{:S(2)}, u32[]{:S(2)}) collective-permute-start(f32[256,128]{1,0:T(8,128)S(1)} %add.308), channel_id=1, source_target_pairs={{0,8},{8,16},{16,24},{24,28},{28,20},{20,12},{12,4},{4,0},{1,9},{9... | collective-permute-start | bytes 393224 | tf_op jit(solution)/shard_map/ppermute | solution.py:410
  129.8 6.0 %collective-permute-start.31 = (f32[256,128]{1,0:T(8,128)S(1)}, f32[256,128]{1,0:T(8,128)S(1)}, u32[]{:S(2)}, u32[]{:S(2)}) collective-permute-start(f32[256,128]{1,0:T(8,128)S(1)} %add_add_fusion.refs_4_), channel_id=1, source_target_pairs={{8,0},{16,8},{24,16},{28,24},{20,28},{12,20},{4,12},{0,4},{9,1},{1... | collective-permute-start | bytes 393224 | tf_op jit(solution)/shard_map/ppermute | solution.py:413
  132.5 6.0 %collective-permute-start.36 = (f32[256,128]{1,0:T(8,128)S(1)}, f32[256,128]{1,0:T(8,128)S(1)}, u32[]{:S(2)}, u32[]{:S(2)}) collective-permute-start(f32[256,128]{1,0:T(8,128)S(1)} %add_add_fusion.1.refs_3_), channel_id=1, source_target_pairs={{0,8},{8,16},{16,24},{24,28},{28,20},{20,12},{12,4},{4,0},{1,9},{9... | collective-permute-start | bytes 393224 | tf_op jit(solution)/shard_map/ppermute | solution.py:410
  132.8 5.8 %collective-permute-start.14 = (f32[256,128]{1,0:T(8,128)S(1)}, f32[256,128]{1,0:T(8,128)S(1)}, u32[]{:S(2)}, u32[]{:S(2)}) collective-permute-start(f32[256,128]{1,0:T(8,128)S(1)} %slice_add_fusion.refs_0_), channel_id=1, source_target_pairs={{0,2},{1,3},{2,0},{3,1},{4,6},{5,7},{6,4},{7,5},{8,10},{9,11},{10,... | collective-permute-start | bytes 393224 | tf_op jit(solution)/shard_map/ppermute | solution.py:387
  133.7 6.6 %collective-permute-start.41 = (f32[256,128]{1,0:T(8,128)S(1)}, f32[256,128]{1,0:T(8,128)S(1)}, u32[]{:S(2)}, u32[]{:S(2)}) collective-permute-start(f32[256,128]{1,0:T(8,128)S(1)} %add_add_fusion.refs_4_), channel_id=1, source_target_pairs={{0,8},{8,16},{16,24},{24,28},{28,20},{20,12},{12,4},{4,0},{1,9},{9... | collective-permute-start | bytes 393224 | tf_op jit(solution)/shard_map/ppermute | solution.py:410
  135.3 5.2 %collective-permute-start.30 = (f32[256,128]{1,0:T(8,128)S(1)}, f32[256,128]{1,0:T(8,128)S(1)}, u32[]{:S(2)}, u32[]{:S(2)}) collective-permute-start(f32[256,128]{1,0:T(8,128)S(1)} %add_add_fusion.1.refs_3_), channel_id=1, source_target_pairs={{8,0},{16,8},{24,16},{28,24},{20,28},{12,20},{4,12},{0,4},{9,1},{1... | collective-permute-start | bytes 393224 | tf_op jit(solution)/shard_map/ppermute | solution.py:413
  135.7 6.6 %collective-permute-start.33 = (f32[256,128]{1,0:T(8,128)S(1)}, f32[256,128]{1,0:T(8,128)S(1)}, u32[]{:S(2)}, u32[]{:S(2)}) collective-permute-start(f32[256,128]{1,0:T(8,128)S(1)} %collective-permute-done.31.refs_6_), channel_id=1, source_target_pairs={{8,0},{16,8},{24,16},{28,24},{20,28},{12,20},{4,12},{0,4},{9,1},{1... | collective-permute-start | bytes 393224 | tf_op jit(solution)/shard_map/ppermute | solution.py:413
  138.6 6.3 %collective-permute-start.37 = (f32[256,128]{1,0:T(8,128)S(1)}, f32[256,128]{1,0:T(8,128)S(1)}, u32[]{:S(2)}, u32[]{:S(2)}) collective-permute-start(f32[256,128]{1,0:T(8,128)S(1)} %collective-permute-done.36.refs_17_), channel_id=1, source_target_pairs={{0,8},{8,16},{16,24},{24,28},{28,20},{20,12},{12,4},{4,0},{1,9},{9... | collective-permute-start | bytes 393224 | tf_op jit(solution)/shard_map/ppermute | solution.py:410
  138.6 12.9 %collective-permute-start.15 = (f32[512,128]{1,0:T(8,128)S(1)}, f32[512,128]{1,0:T(8,128)S(1)}, u32[]{:S(2)}, u32[]{:S(2)}) collective-permute-start(f32[512,128]{1,0:T(8,128)S(1)} %pad_maximum_fusion), channel_id=1, source_target_pairs={{0,1},{1,0},{2,3},{3,2},{4,5},{5,4},{6,7},{7,6},{8,9},{9,8},{10,11... | collective-permute-start | bytes 786440 | tf_op jit(solution)/shard_map/ppermute | solution.py:387
  140.4 7.1 %collective-permute-start.42 = (f32[256,128]{1,0:T(8,128)S(1)}, f32[256,128]{1,0:T(8,128)S(1)}, u32[]{:S(2)}, u32[]{:S(2)}) collective-permute-start(f32[256,128]{1,0:T(8,128)S(1)} %collective-permute-done.41.refs_18_), channel_id=1, source_target_pairs={{0,8},{8,16},{16,24},{24,28},{28,20},{20,12},{12,4},{4,0},{1,9},{9... | collective-permute-start | bytes 393224 | tf_op jit(solution)/shard_map/ppermute | solution.py:410
  140.5 7.0 %collective-permute-start.32 = (f32[256,128]{1,0:T(8,128)S(1)}, f32[256,128]{1,0:T(8,128)S(1)}, u32[]{:S(2)}, u32[]{:S(2)}) collective-permute-start(f32[256,128]{1,0:T(8,128)S(1)} %collective-permute-done.30.refs_5_), channel_id=1, source_target_pairs={{8,0},{16,8},{24,16},{28,24},{20,28},{12,20},{4,12},{0,4},{9,1},{1... | collective-permute-start | bytes 393224 | tf_op jit(solution)/shard_map/ppermute | solution.py:413
  142.4 7.1 %collective-permute-start.35 = (f32[256,128]{1,0:T(8,128)S(1)}, f32[256,128]{1,0:T(8,128)S(1)}, u32[]{:S(2)}, u32[]{:S(2)}) collective-permute-start(f32[256,128]{1,0:T(8,128)S(1)} %collective-permute-done.33.refs_8_), channel_id=1, source_target_pairs={{8,0},{16,8},{24,16},{28,24},{20,28},{12,20},{4,12},{0,4},{9,1},{1... | collective-permute-start | bytes 393224 | tf_op jit(solution)/shard_map/ppermute | solution.py:413
  144.9 5.6 %collective-permute-start.38 = (f32[256,128]{1,0:T(8,128)S(1)}, f32[256,128]{1,0:T(8,128)S(1)}, u32[]{:S(2)}, u32[]{:S(2)}) collective-permute-start(f32[256,128]{1,0:T(8,128)S(1)} %collective-permute-done.37.refs_15_), channel_id=1, source_target_pairs={{0,8},{8,16},{16,24},{24,28},{28,20},{20,12},{12,4},{4,0},{1,9},{9... | collective-permute-start | bytes 393224 | tf_op jit(solution)/shard_map/ppermute | solution.py:410
  147.5 6.3 %collective-permute-start.43 = (f32[256,128]{1,0:T(8,128)S(1)}, f32[256,128]{1,0:T(8,128)S(1)}, u32[]{:S(2)}, u32[]{:S(2)}) collective-permute-start(f32[256,128]{1,0:T(8,128)S(1)} %collective-permute-done.42.refs_16_), channel_id=1, source_target_pairs={{0,8},{8,16},{16,24},{24,28},{28,20},{20,12},{12,4},{4,0},{1,9},{9... | collective-permute-start | bytes 393224 | tf_op jit(solution)/shard_map/ppermute | solution.py:410
  147.5 6.3 %collective-permute-start.34 = (f32[256,128]{1,0:T(8,128)S(1)}, f32[256,128]{1,0:T(8,128)S(1)}, u32[]{:S(2)}, u32[]{:S(2)}) collective-permute-start(f32[256,128]{1,0:T(8,128)S(1)} %collective-permute-done.32.refs_7_), channel_id=1, source_target_pairs={{8,0},{16,8},{24,16},{28,24},{20,28},{12,20},{4,12},{0,4},{9,1},{1... | collective-permute-start | bytes 393224 | tf_op jit(solution)/shard_map/ppermute | solution.py:413
  (14 other events, 86.3 us)

commit v7 on v6

--- a/solution.py
+++ b/solution.py
@@ -13,7 +13,7 @@
 LOWEST = -64.0
 LANES = 128
 WIDE = 512
-TALL = 256
+TALL = 512
 LIMIT = 8 * 2**20
 F32 = jnp.float32
 

time: 157 us -> 148 us (0.943)
  Pallas kernels: 59.2 us -> 49.4 us
    pallas_call x9, Pallas kernels: 49.1 us -> 39.8 us  [call(): pl.pallas_call(kernel, in_specs=[pl.BlockSpec(memory_space=pltpu.VMEM)] *...]
  transfers between devices with their start and end apart: 44 -> 44, of which waited for: 20 -> 21; matrix products, arithmetic and copies ran while one was open for 0% -> 0% of each run, Pallas kernels for 7% -> 7%
where the time goes in v7:
time: 148 us
  Pallas kernels  49.4 us (33%)
  starting transfers between devices  35 us (24%)
  blocking collectives  32.9 us (22%)
  waiting for transfers between devices  28.6 us (19%)
    pallas_call x9, Pallas kernels, call(): pl.pallas_call(kernel, in_specs=[pl.BlockSpec(memory_space=pltpu.VMEM)] *...  39.8 us
    all_to_all x3, blocking collectives, over_rows(): lax.all_to_all(copies, 'rows', 0, 0)  32.9 us
    ppermute x14, waiting for transfers between devices, ahead(): return lax.ppermute(x, 'rows', up)  16.7 us
    ppermute x14, starting transfers between devices, behind(): return lax.ppermute(x, 'rows', down)  14.9 us
    ppermute x16, starting transfers between devices, exchange(): lax.ppermute(x, axis, [(i, i ^ k * stride) for i in range(n)])  10.9 us
    ppermute x14, starting transfers between devices, ahead(): return lax.ppermute(x, 'rows', up)  9.19 us
    pallas_call x1, Pallas kernels, per_device(): pl.pallas_call(row_level_kernel, in_specs=[pl.BlockSpec(memory_space=pltp...  7.95 us
    ppermute x16, waiting for transfers between devices, exchange(): lax.ppermute(x, axis, [(i, i ^ k * stride) for i in range(n)])  7.52 us
  transfers between devices with their start and end apart: 44, of which 21 were waited for; matrix products, arithmetic and copies ran while one was open for 0% of the time, Pallas kernels for 7%

profile of v7, /device:TPU:0, one launch (start us, length us, event | category | flops | bytes accessed | tf_op | source)
XLA Modules:
  0.0 147.5 jit_solution(11805646497403049935)
XLA Ops:
  0.6 7.9 %shard_map.68 = (f32[1024,4096]{1,0:T(8,128)S(1)}, f32[1,1024]{1,0:T(1,128)S(1)}, f32[1,1024]{1,0:T(1,128)S(1)}, bf16[1024,128]{1,0:T(8,128)(2,1)S(1)}, bf16[409...) custom-call(bf16[1024,128]{1,0:T(8,128)(2,1)} %crawl_hbm.1, bf16[4096,128]{1,0:T(8,128)(2,1)} %bench_hbm.1, f32[1,4096]{1,0:T(1,128)} %bitcast.31), custom_call_target="tpu_custom_call" | custom-call | tf_op jit(solution)/shard_map/pallas_call | solution.py:454
  9.1 2.6 %collective-permute-start.1 = (f32[1,1024]{1,0:T(1,128)S(1)}, f32[1,1024]{1,0:T(1,128)S(1)}, u32[]{:S(2)}, u32[]{:S(2)}) collective-permute-start(f32[1,1024]{1,0:T(1,128)S(1)} %get-tuple-element.46.refs_0_), channel_id=1, source_target_pairs={{0,2},{1,3},{2,0},{3,1},{4,6},{5,7},{6,4},{7,5},{8,10},{9,11},{10,... | collective-permute-start | bytes 12296 | tf_op jit(solution)/shard_map/ppermute | solution.py:387
  14.7 13.8 %shard_map.69 = (f32[1,1024]{1,0:T(1,128)S(1)}, f32[1,4096]{1,0:T(1,128)S(1)}) custom-call(f32[1024,4096]{1,0:T(8,128)S(1)} %get-tuple-element.44.tile_ref, f32[1,1024]{1,0:T(1,128)S(1)} %get-tuple-element.45.top_ref, f32[1,1024]{1,0:T(1,128)S(1)} %get-tuple-element.46.refs_0_, f32[1,1024]{1,0:T(1,128)S(1)} %collective-permute-done.refs_1_, ...), custom_call_target="tpu_custom_call" | custom-call | tf_op jit(solution)/shard_map/pallas_call | solution.py:362
  28.5 13.0 %all_to_all.15 = f32[8,32,128]{2,1,0:T(8,128)S(1)} all-to-all(f32[8,32,128]{2,1,0:T(8,128)S(1)} %broadcast_in_dim.22), channel_id=1, replica_groups=mesh['rows'=8,'cols'=4] {'rows'}, dimensions={0} | all-to-all | bytes 262144 | tf_op jit(solution)/shard_map/all_to_all | solution.py:452
  41.8 6.8 %shard_map.70 = (f32[1024,4096]{1,0:T(8,128)S(1)}, f32[1,1024]{1,0:T(1,128)S(1)}, f32[1,4096]{1,0:T(1,128)S(1)}, f32[1,4096]{1,0:T(1,128)S(1)}, f32[1,1024]{1,0:T(1,128)S(1)}) custom-call(f32[1024,4096]{1,0:T(8,128)S(1)} %get-tuple-element.44.tile_ref, f32[1,1024]{1,0:T(1,128)S(1)} %get-tuple-element.45.top_ref, ...), custom_call_target="tpu_custom_call", output_to_operand_aliasing={{0}: (0, {})} | custom-call | tf_op jit(solution)/shard_map/pallas_call | solution.py:362
  50.5 1.8 %collective-permute-done.4.refs_2_ = f32[1,1024]{1,0:T(1,128)S(1)} collective-permute-done((f32[1,1024]{1,0:T(1,128)S(1)}, f32[1,1024]{1,0:T(1,128)S(1)}, u32[]{:S(2)}, u32[]{:S(2)}) %collective-permute-start.4) | collective-permute-done | bytes 4128 | tf_op jit(solution)/shard_map/ppermute | solution.py:387
  52.4 2.0 %shard_map.71 = (f32[1,1024]{1,0:T(1,128)S(1)}, f32[1,4096]{1,0:T(1,128)S(1)}) custom-call(f32[1024,4096]{1,0:T(8,128)S(1)} %get-tuple-element.52.soft_ref, f32[1,1024]{1,0:T(1,128)S(1)} %get-tuple-element.53.left_ref, f32[1,4096]{1,0:T(1,128)S(1)} %get-tuple-element.54.right_ref, f32[1,1024]{1,0:T(1,128)S(1)} %get-tuple-element.55.refs_0_, ...), custom_call_target="tpu_custom_call" | custom-call | tf_op jit(solution)/shard_map/pallas_call | solution.py:362
  54.4 9.9 %all_to_all.16 = f32[8,32,128]{2,1,0:T(8,128)S(1)} all-to-all(f32[8,32,128]{2,1,0:T(8,128)S(1)} %broadcast_in_dim.24), channel_id=1, replica_groups=mesh['rows'=8,'cols'=4] {'rows'}, dimensions={0} | all-to-all | bytes 262144 | tf_op jit(solution)/shard_map/all_to_all | solution.py:452
  64.4 1.8 %shard_map.72 = (f32[1,4096]{1,0:T(1,128)S(1)}, f32[1,1024]{1,0:T(1,128)S(1)}) custom-call(f32[1024,4096]{1,0:T(8,128)S(1)} %get-tuple-element.52.soft_ref, f32[1,1024]{1,0:T(1,128)S(1)} %get-tuple-element.56.inverse_ref, f32[1,4096]{1,0:T(1,128)S(1)} %get-tuple-element.54.right_ref, f32[1,4096]{1,0:T(1,128)S(1)} %bitcast.21, f32[1,4096]{1,0:T(1,128)S(1)} %bitcast.17), custom_call_target="tpu_custom_call" | custom-call | tf_op jit(solution)/shard_map/pallas_call | solution.py:362
  68.1 1.8 %collective-permute-done.7.refs_2_ = f32[1,1024]{1,0:T(1,128)S(1)} collective-permute-done((f32[1,1024]{1,0:T(1,128)S(1)}, f32[1,1024]{1,0:T(1,128)S(1)}, u32[]{:S(2)}, u32[]{:S(2)}) %collective-permute-start.7) | collective-permute-done | bytes 4128 | tf_op jit(solution)/shard_map/ppermute | solution.py:387
  70.8 2.0 %shard_map.73 = (f32[1,1024]{1,0:T(1,128)S(1)}, f32[1,4096]{1,0:T(1,128)S(1)}) custom-call(f32[1024,4096]{1,0:T(8,128)S(1)} %get-tuple-element.52.soft_ref, f32[1,1024]{1,0:T(1,128)S(1)} %get-tuple-element.56.inverse_ref, f32[1,4096]{1,0:T(1,128)S(1)} %get-tuple-element.54.right_ref, f32[1,1024]{1,0:T(1,128)S(1)} %bitcast.22, ...), custom_call_target="tpu_custom_call" | custom-call | tf_op jit(solution)/shard_map/pallas_call | solution.py:362
  72.8 10.0 %all_to_all.17 = f32[8,32,128]{2,1,0:T(8,128)S(1)} all-to-all(f32[8,32,128]{2,1,0:T(8,128)S(1)} %broadcast_in_dim.26), channel_id=1, replica_groups=mesh['rows'=8,'cols'=4] {'rows'}, dimensions={0} | all-to-all | bytes 262144 | tf_op jit(solution)/shard_map/all_to_all | solution.py:452
  82.8 1.9 %shard_map.74 = (f32[1,4096]{1,0:T(1,128)S(1)}, f32[1,1024]{1,0:T(1,128)S(1)}) custom-call(f32[1024,4096]{1,0:T(8,128)S(1)} %get-tuple-element.52.soft_ref, f32[1,1024]{1,0:T(1,128)S(1)} %get-tuple-element.53.left_ref, f32[1,4096]{1,0:T(1,128)S(1)} %get-tuple-element.54.right_ref, f32[1,4096]{1,0:T(1,128)S(1)} %bitcast.16), custom_call_target="tpu_custom_call" | custom-call | tf_op jit(solution)/shard_map/pallas_call | solution.py:362
  86.9 5.3 %shard_map.75 = (f32[1024,4096]{1,0:T(8,128)S(1)}, f32[1024,4096]{1,0:T(8,128)S(1)}) custom-call(f32[1024,4096]{1,0:T(8,128)S(1)} %get-tuple-element.52.soft_ref, f32[1,1024]{1,0:T(1,128)S(1)} %get-tuple-element.56.inverse_ref, f32[1,1024]{1,0:T(1,128)S(1)} %get-tuple-element.59.scaled_ref, ...), custom_call_target="tpu_custom_call", output_to_operand_aliasing={{0}: (0, {})} | custom-call | tf_op jit(solution)/shard_map/pallas_call | solution.py:362
  93.9 1.6 %collective-permute-start.16 = (f32[256,128]{1,0:T(8,128)S(1)}, f32[256,128]{1,0:T(8,128)S(1)}, u32[]{:S(2)}, u32[]{:S(2)}) collective-permute-start(f32[256,128]{1,0:T(8,128)S(1)} %get-tuple-element.74), channel_id=1, source_target_pairs={{0,8},{8,16},{16,24},{24,28},{28,20},{20,12},{12,4},{4,0},{1,9},{9... | collective-permute-start | bytes 393224 | tf_op jit(solution)/shard_map/ppermute | solution.py:410
  95.6 5.0 %shard_map.77 = (f32[512,128]{1,0:T(8,128)S(1)}, f32[512,128]{1,0:T(8,128)S(1)}, f32[256,128]{1,0:T(8,128)S(1)}, f32[256,128]{1,0:T(8,128)S(1)}, f32[256,128]{1,...) custom-call(f32[1024,4096]{1,0:T(8,128)S(1)} %get-tuple-element.64.f, ...), custom_call_target="tpu_custom_call" | custom-call | tf_op jit(solution)/shard_map/pallas_call | solution.py:362
  100.7 2.0 %collective-permute-start.27 = (f32[256,128]{1,0:T(8,128)S(1)}, f32[256,128]{1,0:T(8,128)S(1)}, u32[]{:S(2)}, u32[]{:S(2)}) collective-permute-start(f32[256,128]{1,0:T(8,128)S(1)} %add.316), channel_id=1, source_target_pairs={{8,0},{16,8},{24,16},{28,24},{20,28},{12,20},{4,12},{0,4},{9,1},{1... | collective-permute-start | bytes 393224 | tf_op jit(solution)/shard_map/ppermute | solution.py:413
  103.2 1.7 %collective-permute-start.17 = (f32[256,128]{1,0:T(8,128)S(1)}, f32[256,128]{1,0:T(8,128)S(1)}, u32[]{:S(2)}, u32[]{:S(2)}) collective-permute-start(f32[256,128]{1,0:T(8,128)S(1)} %add.306), channel_id=1, source_target_pairs={{0,8},{8,16},{16,24},{24,28},{28,20},{20,12},{12,4},{4,0},{1,9},{9... | collective-permute-start | bytes 393224 | tf_op jit(solution)/shard_map/ppermute | solution.py:410
  107.1 1.7 %collective-permute-start.28 = (f32[256,128]{1,0:T(8,128)S(1)}, f32[256,128]{1,0:T(8,128)S(1)}, u32[]{:S(2)}, u32[]{:S(2)}) collective-permute-start(f32[256,128]{1,0:T(8,128)S(1)} %add.317), channel_id=1, source_target_pairs={{8,0},{16,8},{24,16},{28,24},{20,28},{12,20},{4,12},{0,4},{9,1},{1... | collective-permute-start | bytes 393224 | tf_op jit(solution)/shard_map/ppermute | solution.py:413
  109.0 1.7 %collective-permute-start.21 = (f32[256,128]{1,0:T(8,128)S(1)}, f32[256,128]{1,0:T(8,128)S(1)}, u32[]{:S(2)}, u32[]{:S(2)}) collective-permute-start(f32[256,128]{1,0:T(8,128)S(1)} %add.310), channel_id=1, source_target_pairs={{8,0},{16,8},{24,16},{28,24},{20,28},{12,20},{4,12},{0,4},{9,1},{1... | collective-permute-start | bytes 393224 | tf_op jit(solution)/shard_map/ppermute | solution.py:413
  112.4 1.7 %collective-permute-start.25 = (f32[256,128]{1,0:T(8,128)S(1)}, f32[256,128]{1,0:T(8,128)S(1)}, u32[]{:S(2)}, u32[]{:S(2)}) collective-permute-start(f32[256,128]{1,0:T(8,128)S(1)} %add.314), channel_id=1, source_target_pairs={{0,8},{8,16},{16,24},{24,28},{28,20},{20,12},{12,4},{4,0},{1,9},{9... | collective-permute-start | bytes 393224 | tf_op jit(solution)/shard_map/ppermute | solution.py:410
  117.4 2.5 %collective-permute-done.25 = f32[256,128]{1,0:T(8,128)S(1)} collective-permute-done((f32[256,128]{1,0:T(8,128)S(1)}, f32[256,128]{1,0:T(8,128)S(1)}, u32[]{:S(2)}, u32[]{:S(2)}) %collective-permute-start.25) | collective-permute-done | bytes 131104 | tf_op jit(solution)/shard_map/ppermute | solution.py:410
  120.5 2.3 %collective-permute-done.22 = f32[256,128]{1,0:T(8,128)S(1)} collective-permute-done((f32[256,128]{1,0:T(8,128)S(1)}, f32[256,128]{1,0:T(8,128)S(1)}, u32[]{:S(2)}, u32[]{:S(2)}) %collective-permute-start.22) | collective-permute-done | bytes 131104 | tf_op jit(solution)/shard_map/ppermute | solution.py:413
  124.0 1.6 %collective-permute-start.41 = (f32[256,128]{1,0:T(8,128)S(1)}, f32[256,128]{1,0:T(8,128)S(1)}, u32[]{:S(2)}, u32[]{:S(2)}) collective-permute-start(f32[256,128]{1,0:T(8,128)S(1)} %add_add_fusion.refs_4_), channel_id=1, source_target_pairs={{0,8},{8,16},{16,24},{24,28},{28,20},{20,12},{12,4},{4,0},{1,9},{9... | collective-permute-start | bytes 393224 | tf_op jit(solution)/shard_map/ppermute | solution.py:410
  126.0 1.6 %collective-permute-start.33 = (f32[256,128]{1,0:T(8,128)S(1)}, f32[256,128]{1,0:T(8,128)S(1)}, u32[]{:S(2)}, u32[]{:S(2)}) collective-permute-start(f32[256,128]{1,0:T(8,128)S(1)} %collective-permute-done.31.refs_6_), channel_id=1, source_target_pairs={{8,0},{16,8},{24,16},{28,24},{20,28},{12,20},{4,12},{0,4},{9,1},{1... | collective-permute-start | bytes 393224 | tf_op jit(solution)/shard_map/ppermute | solution.py:413
  129.0 1.7 %collective-permute-done.41.refs_18_ = f32[256,128]{1,0:T(8,128)S(1)} collective-permute-done((f32[256,128]{1,0:T(8,128)S(1)}, f32[256,128]{1,0:T(8,128)S(1)}, u32[]{:S(2)}, u32[]{:S(2)}) %collective-permute-start.41) | collective-permute-done | bytes 131104 | tf_op jit(solution)/shard_map/ppermute | solution.py:410
  130.8 1.9 %collective-permute-start.32 = (f32[256,128]{1,0:T(8,128)S(1)}, f32[256,128]{1,0:T(8,128)S(1)}, u32[]{:S(2)}, u32[]{:S(2)}) collective-permute-start(f32[256,128]{1,0:T(8,128)S(1)} %collective-permute-done.30.refs_5_), channel_id=1, source_target_pairs={{8,0},{16,8},{24,16},{28,24},{20,28},{12,20},{4,12},{0,4},{9,1},{1... | collective-permute-start | bytes 393224 | tf_op jit(solution)/shard_map/ppermute | solution.py:413
  133.1 2.1 %collective-permute-done.37.refs_15_ = f32[256,128]{1,0:T(8,128)S(1)} collective-permute-done((f32[256,128]{1,0:T(8,128)S(1)}, f32[256,128]{1,0:T(8,128)S(1)}, u32[]{:S(2)}, u32[]{:S(2)}) %collective-permute-start.37) | collective-permute-done | bytes 131104 | tf_op jit(solution)/shard_map/ppermute | solution.py:410
  135.1 2.6 %collective-permute-done.42.refs_16_ = f32[256,128]{1,0:T(8,128)S(1)} collective-permute-done((f32[256,128]{1,0:T(8,128)S(1)}, f32[256,128]{1,0:T(8,128)S(1)}, u32[]{:S(2)}, u32[]{:S(2)}) %collective-permute-start.42) | collective-permute-done | bytes 131104 | tf_op jit(solution)/shard_map/ppermute | solution.py:410
  137.8 2.0 %collective-permute-start.34 = (f32[256,128]{1,0:T(8,128)S(1)}, f32[256,128]{1,0:T(8,128)S(1)}, u32[]{:S(2)}, u32[]{:S(2)}) collective-permute-start(f32[256,128]{1,0:T(8,128)S(1)} %collective-permute-done.32.refs_7_), channel_id=1, source_target_pairs={{8,0},{16,8},{24,16},{28,24},{20,28},{12,20},{4,12},{0,4},{9,1},{1... | collective-permute-start | bytes 393224 | tf_op jit(solution)/shard_map/ppermute | solution.py:413
  141.8 2.3 %collective-permute-done.43.refs_14_ = f32[256,128]{1,0:T(8,128)S(1)} collective-permute-done((f32[256,128]{1,0:T(8,128)S(1)}, f32[256,128]{1,0:T(8,128)S(1)}, u32[]{:S(2)}, u32[]{:S(2)}) %collective-permute-start.43) | collective-permute-done | bytes 131104 | tf_op jit(solution)/shard_map/ppermute | solution.py:410
  145.7 1.6 %shard_map.78 = (f32[1024,128]{1,0:T(8,128)}, f32[4096,128]{1,0:T(8,128)}) custom-call(f32[256,128]{1,0:T(8,128)S(1)} %slice_add_fusion.refs_0_, f32[256,128]{1,0:T(8,128)S(1)} %collective-permute-done.14.refs_1_, f32[512,128]{1,0:T(8,128)S(1)} %collective-permute-done.15.refs_2_, f32[256,128]{1,0:T(8,128)S(1)} %add_add_fusion.1.refs_3_, ...), custom_call_target="tpu_custom_call" | custom-call | tf_op jit(solution)/shard_map/pallas_call | solution.py:510
  (97 shorter events, 28.1 us)
Async XLA Ops:
  84.7 7.5 %collective-permute-start.10 = (f32[1,1024]{1,0:T(1,128)S(1)}, f32[1,1024]{1,0:T(1,128)S(1)}, u32[]{:S(2)}, u32[]{:S(2)}) collective-permute-start(f32[1,1024]{1,0:T(1,128)S(1)} %get-tuple-element.66.refs_0_), channel_id=1, source_target_pairs={{0,2},{1,3},{2,0},{3,1},{4,6},{5,7},{6,4},{7,5},{8,10},{9,11},{10,... | collective-permute-start | bytes 12296 | tf_op jit(solution)/shard_map/ppermute | solution.py:387
  85.3 6.9 %collective-permute-start.11 = (f32[1,1024]{1,0:T(1,128)S(1)}, f32[1,1024]{1,0:T(1,128)S(1)}, u32[]{:S(2)}, u32[]{:S(2)}) collective-permute-start(f32[1,1024]{1,0:T(1,128)S(1)} %get-tuple-element.66.refs_0_), channel_id=1, source_target_pairs={{0,3},{1,2},{2,1},{3,0},{4,7},{5,6},{6,5},{7,4},{8,11},{9,10},{10,... | collective-permute-start | bytes 12296 | tf_op jit(solution)/shard_map/ppermute | solution.py:387
  85.3 6.9 %collective-permute-start.9 = (f32[1,1024]{1,0:T(1,128)S(1)}, f32[1,1024]{1,0:T(1,128)S(1)}, u32[]{:S(2)}, u32[]{:S(2)}) collective-permute-start(f32[1,1024]{1,0:T(1,128)S(1)} %get-tuple-element.66.refs_0_), channel_id=1, source_target_pairs={{0,1},{1,0},{2,3},{3,2},{4,5},{5,4},{6,7},{7,6},{8,9},{9,8},{10,11... | collective-permute-start | bytes 12296 | tf_op jit(solution)/shard_map/ppermute | solution.py:387
  93.5 7.2 %collective-permute-start.26 = (f32[256,128]{1,0:T(8,128)S(1)}, f32[256,128]{1,0:T(8,128)S(1)}, u32[]{:S(2)}, u32[]{:S(2)}) collective-permute-start(f32[256,128]{1,0:T(8,128)S(1)} %get-tuple-element.85), channel_id=1, source_target_pairs={{8,0},{16,8},{24,16},{28,24},{20,28},{12,20},{4,12},{0,4},{9,1},{1... | collective-permute-start | bytes 393224 | tf_op jit(solution)/shard_map/ppermute | solution.py:413
  93.9 9.2 %collective-permute-start.16 = (f32[256,128]{1,0:T(8,128)S(1)}, f32[256,128]{1,0:T(8,128)S(1)}, u32[]{:S(2)}, u32[]{:S(2)}) collective-permute-start(f32[256,128]{1,0:T(8,128)S(1)} %get-tuple-element.74), channel_id=1, source_target_pairs={{0,8},{8,16},{16,24},{24,28},{28,20},{20,12},{12,4},{4,0},{1,9},{9... | collective-permute-start | bytes 393224 | tf_op jit(solution)/shard_map/ppermute | solution.py:410
  100.7 6.3 %collective-permute-start.27 = (f32[256,128]{1,0:T(8,128)S(1)}, f32[256,128]{1,0:T(8,128)S(1)}, u32[]{:S(2)}, u32[]{:S(2)}) collective-permute-start(f32[256,128]{1,0:T(8,128)S(1)} %add.316), channel_id=1, source_target_pairs={{8,0},{16,8},{24,16},{28,24},{20,28},{12,20},{4,12},{0,4},{9,1},{1... | collective-permute-start | bytes 393224 | tf_op jit(solution)/shard_map/ppermute | solution.py:413
  102.8 6.2 %collective-permute-start.20 = (f32[256,128]{1,0:T(8,128)S(1)}, f32[256,128]{1,0:T(8,128)S(1)}, u32[]{:S(2)}, u32[]{:S(2)}) collective-permute-start(f32[256,128]{1,0:T(8,128)S(1)} %get-tuple-element.77), channel_id=1, source_target_pairs={{8,0},{16,8},{24,16},{28,24},{20,28},{12,20},{4,12},{0,4},{9,1},{1... | collective-permute-start | bytes 393224 | tf_op jit(solution)/shard_map/ppermute | solution.py:413
  103.2 12.7 %collective-permute-start.12 = (f32[512,128]{1,0:T(8,128)S(1)}, f32[512,128]{1,0:T(8,128)S(1)}, u32[]{:S(2)}, u32[]{:S(2)}) collective-permute-start(f32[512,128]{1,0:T(8,128)S(1)} %get-tuple-element.69), channel_id=1, source_target_pairs={{0,1},{1,0},{2,3},{3,2},{4,5},{5,4},{6,7},{7,6},{8,9},{9,8},{10,11... | collective-permute-start | bytes 786440 | tf_op jit(solution)/shard_map/ppermute | solution.py:387
  103.2 7.5 %collective-permute-start.17 = (f32[256,128]{1,0:T(8,128)S(1)}, f32[256,128]{1,0:T(8,128)S(1)}, u32[]{:S(2)}, u32[]{:S(2)}) collective-permute-start(f32[256,128]{1,0:T(8,128)S(1)} %add.306), channel_id=1, source_target_pairs={{0,8},{8,16},{16,24},{24,28},{28,20},{20,12},{12,4},{4,0},{1,9},{9... | collective-permute-start | bytes 393224 | tf_op jit(solution)/shard_map/ppermute | solution.py:410
  105.7 6.7 %collective-permute-start.24 = (f32[256,128]{1,0:T(8,128)S(1)}, f32[256,128]{1,0:T(8,128)S(1)}, u32[]{:S(2)}, u32[]{:S(2)}) collective-permute-start(f32[256,128]{1,0:T(8,128)S(1)} %add.313), channel_id=1, source_target_pairs={{0,8},{8,16},{16,24},{24,28},{28,20},{20,12},{12,4},{4,0},{1,9},{9... | collective-permute-start | bytes 393224 | tf_op jit(solution)/shard_map/ppermute | solution.py:410
  107.1 7.0 %collective-permute-start.28 = (f32[256,128]{1,0:T(8,128)S(1)}, f32[256,128]{1,0:T(8,128)S(1)}, u32[]{:S(2)}, u32[]{:S(2)}) collective-permute-start(f32[256,128]{1,0:T(8,128)S(1)} %add.317), channel_id=1, source_target_pairs={{8,0},{16,8},{24,16},{28,24},{20,28},{12,20},{4,12},{0,4},{9,1},{1... | collective-permute-start | bytes 393224 | tf_op jit(solution)/shard_map/ppermute | solution.py:413
  109.0 5.5 %collective-permute-start.21 = (f32[256,128]{1,0:T(8,128)S(1)}, f32[256,128]{1,0:T(8,128)S(1)}, u32[]{:S(2)}, u32[]{:S(2)}) collective-permute-start(f32[256,128]{1,0:T(8,128)S(1)} %add.310), channel_id=1, source_target_pairs={{8,0},{16,8},{24,16},{28,24},{20,28},{12,20},{4,12},{0,4},{9,1},{1... | collective-permute-start | bytes 393224 | tf_op jit(solution)/shard_map/ppermute | solution.py:413
  110.7 6.4 %collective-permute-start.18 = (f32[256,128]{1,0:T(8,128)S(1)}, f32[256,128]{1,0:T(8,128)S(1)}, u32[]{:S(2)}, u32[]{:S(2)}) collective-permute-start(f32[256,128]{1,0:T(8,128)S(1)} %add.307), channel_id=1, source_target_pairs={{0,8},{8,16},{16,24},{24,28},{28,20},{20,12},{12,4},{4,0},{1,9},{9... | collective-permute-start | bytes 393224 | tf_op jit(solution)/shard_map/ppermute | solution.py:410
  112.4 7.6 %collective-permute-start.25 = (f32[256,128]{1,0:T(8,128)S(1)}, f32[256,128]{1,0:T(8,128)S(1)}, u32[]{:S(2)}, u32[]{:S(2)}) collective-permute-start(f32[256,128]{1,0:T(8,128)S(1)} %add.314), channel_id=1, source_target_pairs={{0,8},{8,16},{16,24},{24,28},{28,20},{20,12},{12,4},{4,0},{1,9},{9... | collective-permute-start | bytes 393224 | tf_op jit(solution)/shard_map/ppermute | solution.py:410
  114.1 5.9 %collective-permute-start.29 = (f32[256,128]{1,0:T(8,128)S(1)}, f32[256,128]{1,0:T(8,128)S(1)}, u32[]{:S(2)}, u32[]{:S(2)}) collective-permute-start(f32[256,128]{1,0:T(8,128)S(1)} %add.318), channel_id=1, source_target_pairs={{8,0},{16,8},{24,16},{28,24},{20,28},{12,20},{4,12},{0,4},{9,1},{1... | collective-permute-start | bytes 393224 | tf_op jit(solution)/shard_map/ppermute | solution.py:413
  114.5 8.2 %collective-permute-start.22 = (f32[256,128]{1,0:T(8,128)S(1)}, f32[256,128]{1,0:T(8,128)S(1)}, u32[]{:S(2)}, u32[]{:S(2)}) collective-permute-start(f32[256,128]{1,0:T(8,128)S(1)} %add.311), channel_id=1, source_target_pairs={{8,0},{16,8},{24,16},{28,24},{20,28},{12,20},{4,12},{0,4},{9,1},{1... | collective-permute-start | bytes 393224 | tf_op jit(solution)/shard_map/ppermute | solution.py:413
  115.9 7.1 %collective-permute-start.13 = (f32[256,128]{1,0:T(8,128)S(1)}, f32[256,128]{1,0:T(8,128)S(1)}, u32[]{:S(2)}, u32[]{:S(2)}) collective-permute-start(f32[256,128]{1,0:T(8,128)S(1)} %slice.9), channel_id=1, source_target_pairs={{0,2},{1,3},{2,0},{3,1},{4,6},{5,7},{6,4},{7,5},{8,10},{9,11},{10,... | collective-permute-start | bytes 393224 | tf_op jit(solution)/shard_map/ppermute | solution.py:387
  117.1 5.6 %collective-permute-start.19 = (f32[256,128]{1,0:T(8,128)S(1)}, f32[256,128]{1,0:T(8,128)S(1)}, u32[]{:S(2)}, u32[]{:S(2)}) collective-permute-start(f32[256,128]{1,0:T(8,128)S(1)} %add.308), channel_id=1, source_target_pairs={{0,8},{8,16},{16,24},{24,28},{28,20},{20,12},{12,4},{4,0},{1,9},{9... | collective-permute-start | bytes 393224 | tf_op jit(solution)/shard_map/ppermute | solution.py:410
  120.0 6.0 %collective-permute-start.31 = (f32[256,128]{1,0:T(8,128)S(1)}, f32[256,128]{1,0:T(8,128)S(1)}, u32[]{:S(2)}, u32[]{:S(2)}) collective-permute-start(f32[256,128]{1,0:T(8,128)S(1)} %add_add_fusion.refs_4_), channel_id=1, source_target_pairs={{8,0},{16,8},{24,16},{28,24},{20,28},{12,20},{4,12},{0,4},{9,1},{1... | collective-permute-start | bytes 393224 | tf_op jit(solution)/shard_map/ppermute | solution.py:413
  122.8 6.1 %collective-permute-start.36 = (f32[256,128]{1,0:T(8,128)S(1)}, f32[256,128]{1,0:T(8,128)S(1)}, u32[]{:S(2)}, u32[]{:S(2)}) collective-permute-start(f32[256,128]{1,0:T(8,128)S(1)} %add_add_fusion.1.refs_3_), channel_id=1, source_target_pairs={{0,8},{8,16},{16,24},{24,28},{28,20},{20,12},{12,4},{4,0},{1,9},{9... | collective-permute-start | bytes 393224 | tf_op jit(solution)/shard_map/ppermute | solution.py:410
  123.0 5.8 %collective-permute-start.14 = (f32[256,128]{1,0:T(8,128)S(1)}, f32[256,128]{1,0:T(8,128)S(1)}, u32[]{:S(2)}, u32[]{:S(2)}) collective-permute-start(f32[256,128]{1,0:T(8,128)S(1)} %slice_add_fusion.refs_0_), channel_id=1, source_target_pairs={{0,2},{1,3},{2,0},{3,1},{4,6},{5,7},{6,4},{7,5},{8,10},{9,11},{10,... | collective-permute-start | bytes 393224 | tf_op jit(solution)/shard_map/ppermute | solution.py:387
  124.0 6.7 %collective-permute-start.41 = (f32[256,128]{1,0:T(8,128)S(1)}, f32[256,128]{1,0:T(8,128)S(1)}, u32[]{:S(2)}, u32[]{:S(2)}) collective-permute-start(f32[256,128]{1,0:T(8,128)S(1)} %add_add_fusion.refs_4_), channel_id=1, source_target_pairs={{0,8},{8,16},{16,24},{24,28},{28,20},{20,12},{12,4},{4,0},{1,9},{9... | collective-permute-start | bytes 393224 | tf_op jit(solution)/shard_map/ppermute | solution.py:410
  125.6 5.2 %collective-permute-start.30 = (f32[256,128]{1,0:T(8,128)S(1)}, f32[256,128]{1,0:T(8,128)S(1)}, u32[]{:S(2)}, u32[]{:S(2)}) collective-permute-start(f32[256,128]{1,0:T(8,128)S(1)} %add_add_fusion.1.refs_3_), channel_id=1, source_target_pairs={{8,0},{16,8},{24,16},{28,24},{20,28},{12,20},{4,12},{0,4},{9,1},{1... | collective-permute-start | bytes 393224 | tf_op jit(solution)/shard_map/ppermute | solution.py:413
  126.0 6.7 %collective-permute-start.33 = (f32[256,128]{1,0:T(8,128)S(1)}, f32[256,128]{1,0:T(8,128)S(1)}, u32[]{:S(2)}, u32[]{:S(2)}) collective-permute-start(f32[256,128]{1,0:T(8,128)S(1)} %collective-permute-done.31.refs_6_), channel_id=1, source_target_pairs={{8,0},{16,8},{24,16},{28,24},{20,28},{12,20},{4,12},{0,4},{9,1},{1... | collective-permute-start | bytes 393224 | tf_op jit(solution)/shard_map/ppermute | solution.py:413
  128.9 6.3 %collective-permute-start.37 = (f32[256,128]{1,0:T(8,128)S(1)}, f32[256,128]{1,0:T(8,128)S(1)}, u32[]{:S(2)}, u32[]{:S(2)}) collective-permute-start(f32[256,128]{1,0:T(8,128)S(1)} %collective-permute-done.36.refs_17_), channel_id=1, source_target_pairs={{0,8},{8,16},{16,24},{24,28},{28,20},{20,12},{12,4},{4,0},{1,9},{9... | collective-permute-start | bytes 393224 | tf_op jit(solution)/shard_map/ppermute | solution.py:410
  128.9 12.9 %collective-permute-start.15 = (f32[512,128]{1,0:T(8,128)S(1)}, f32[512,128]{1,0:T(8,128)S(1)}, u32[]{:S(2)}, u32[]{:S(2)}) collective-permute-start(f32[512,128]{1,0:T(8,128)S(1)} %pad_maximum_fusion), channel_id=1, source_target_pairs={{0,1},{1,0},{2,3},{3,2},{4,5},{5,4},{6,7},{7,6},{8,9},{9,8},{10,11... | collective-permute-start | bytes 786440 | tf_op jit(solution)/shard_map/ppermute | solution.py:387
  130.6 7.1 %collective-permute-start.42 = (f32[256,128]{1,0:T(8,128)S(1)}, f32[256,128]{1,0:T(8,128)S(1)}, u32[]{:S(2)}, u32[]{:S(2)}) collective-permute-start(f32[256,128]{1,0:T(8,128)S(1)} %collective-permute-done.41.refs_18_), channel_id=1, source_target_pairs={{0,8},{8,16},{16,24},{24,28},{28,20},{20,12},{12,4},{4,0},{1,9},{9... | collective-permute-start | bytes 393224 | tf_op jit(solution)/shard_map/ppermute | solution.py:410
  130.8 7.0 %collective-permute-start.32 = (f32[256,128]{1,0:T(8,128)S(1)}, f32[256,128]{1,0:T(8,128)S(1)}, u32[]{:S(2)}, u32[]{:S(2)}) collective-permute-start(f32[256,128]{1,0:T(8,128)S(1)} %collective-permute-done.30.refs_5_), channel_id=1, source_target_pairs={{8,0},{16,8},{24,16},{28,24},{20,28},{12,20},{4,12},{0,4},{9,1},{1... | collective-permute-start | bytes 393224 | tf_op jit(solution)/shard_map/ppermute | solution.py:413
  132.6 7.1 %collective-permute-start.35 = (f32[256,128]{1,0:T(8,128)S(1)}, f32[256,128]{1,0:T(8,128)S(1)}, u32[]{:S(2)}, u32[]{:S(2)}) collective-permute-start(f32[256,128]{1,0:T(8,128)S(1)} %collective-permute-done.33.refs_8_), channel_id=1, source_target_pairs={{8,0},{16,8},{24,16},{28,24},{20,28},{12,20},{4,12},{0,4},{9,1},{1... | collective-permute-start | bytes 393224 | tf_op jit(solution)/shard_map/ppermute | solution.py:413
  135.1 5.6 %collective-permute-start.38 = (f32[256,128]{1,0:T(8,128)S(1)}, f32[256,128]{1,0:T(8,128)S(1)}, u32[]{:S(2)}, u32[]{:S(2)}) collective-permute-start(f32[256,128]{1,0:T(8,128)S(1)} %collective-permute-done.37.refs_15_), channel_id=1, source_target_pairs={{0,8},{8,16},{16,24},{24,28},{28,20},{20,12},{12,4},{4,0},{1,9},{9... | collective-permute-start | bytes 393224 | tf_op jit(solution)/shard_map/ppermute | solution.py:410
  137.8 6.3 %collective-permute-start.43 = (f32[256,128]{1,0:T(8,128)S(1)}, f32[256,128]{1,0:T(8,128)S(1)}, u32[]{:S(2)}, u32[]{:S(2)}) collective-permute-start(f32[256,128]{1,0:T(8,128)S(1)} %collective-permute-done.42.refs_16_), channel_id=1, source_target_pairs={{0,8},{8,16},{16,24},{24,28},{28,20},{20,12},{12,4},{4,0},{1,9},{9... | collective-permute-start | bytes 393224 | tf_op jit(solution)/shard_map/ppermute | solution.py:410
  137.8 6.3 %collective-permute-start.34 = (f32[256,128]{1,0:T(8,128)S(1)}, f32[256,128]{1,0:T(8,128)S(1)}, u32[]{:S(2)}, u32[]{:S(2)}) collective-permute-start(f32[256,128]{1,0:T(8,128)S(1)} %collective-permute-done.32.refs_7_), channel_id=1, source_target_pairs={{8,0},{16,8},{24,16},{28,24},{20,28},{12,20},{4,12},{0,4},{9,1},{1... | collective-permute-start | bytes 393224 | tf_op jit(solution)/shard_map/ppermute | solution.py:413
  (14 other events, 83.7 us)

commit v8 on v7

--- a/solution.py
+++ b/solution.py
@@ -13,7 +13,7 @@
 LOWEST = -64.0
 LANES = 128
 WIDE = 512
-TALL = 512
+TALL = 1024
 LIMIT = 8 * 2**20
 F32 = jnp.float32
 

time: 148 us -> 140 us (0.946)
  Pallas kernels: 49.4 us -> 41.6 us
    pallas_call x9, Pallas kernels: 39.8 us -> 32 us  [call(): pl.pallas_call(kernel, in_specs=[pl.BlockSpec(memory_space=pltpu.VMEM)] *...]
  transfers between devices with their start and end apart: 44 -> 44, of which waited for: 21 -> 20; matrix products, arithmetic and copies ran while one was open for 0% -> 0% of each run, Pallas kernels for 7% -> 6%
where the time goes in v8:
time: 140 us
  Pallas kernels  41.6 us (30%)
  starting transfers between devices  35 us (25%)
  blocking collectives  32.9 us (24%)
  waiting for transfers between devices  28.6 us (20%)
    all_to_all x3, blocking collectives, over_rows(): lax.all_to_all(copies, 'rows', 0, 0)  32.9 us
    pallas_call x9, Pallas kernels, call(): pl.pallas_call(kernel, in_specs=[pl.BlockSpec(memory_space=pltpu.VMEM)] *...  32 us
    ppermute x14, waiting for transfers between devices, ahead(): return lax.ppermute(x, 'rows', up)  16.7 us
    ppermute x14, starting transfers between devices, behind(): return lax.ppermute(x, 'rows', down)  14.9 us
    ppermute x16, starting transfers between devices, exchange(): lax.ppermute(x, axis, [(i, i ^ k * stride) for i in range(n)])  10.9 us
    ppermute x14, starting transfers between devices, ahead(): return lax.ppermute(x, 'rows', up)  9.15 us
    pallas_call x1, Pallas kernels, per_device(): pl.pallas_call(row_level_kernel, in_specs=[pl.BlockSpec(memory_space=pltp...  7.97 us
    ppermute x16, waiting for transfers between devices, exchange(): lax.ppermute(x, axis, [(i, i ^ k * stride) for i in range(n)])  7.51 us
  transfers between devices with their start and end apart: 44, of which 20 were waited for; matrix products, arithmetic and copies ran while one was open for 0% of the time, Pallas kernels for 6%

profile of v8, /device:TPU:0, one launch (start us, length us, event | category | flops | bytes accessed | tf_op | source)
XLA Modules:
  0.0 139.6 jit_solution(8146485741573106623)
XLA Ops:
  0.6 8.0 %shard_map.68 = (f32[1024,4096]{1,0:T(8,128)S(1)}, f32[1,1024]{1,0:T(1,128)S(1)}, f32[1,1024]{1,0:T(1,128)S(1)}, bf16[1024,128]{1,0:T(8,128)(2,1)S(1)}, bf16[409...) custom-call(bf16[1024,128]{1,0:T(8,128)(2,1)} %crawl_hbm.1, bf16[4096,128]{1,0:T(8,128)(2,1)} %bench_hbm.1, f32[1,4096]{1,0:T(1,128)} %bitcast.31), custom_call_target="tpu_custom_call" | custom-call | tf_op jit(solution)/shard_map/pallas_call | solution.py:454
  9.1 2.6 %collective-permute-start.1 = (f32[1,1024]{1,0:T(1,128)S(1)}, f32[1,1024]{1,0:T(1,128)S(1)}, u32[]{:S(2)}, u32[]{:S(2)}) collective-permute-start(f32[1,1024]{1,0:T(1,128)S(1)} %get-tuple-element.46.refs_0_), channel_id=1, source_target_pairs={{0,2},{1,3},{2,0},{3,1},{4,6},{5,7},{6,4},{7,5},{8,10},{9,11},{10,... | collective-permute-start | bytes 12296 | tf_op jit(solution)/shard_map/ppermute | solution.py:387
  14.7 9.0 %shard_map.69 = (f32[1,1024]{1,0:T(1,128)S(1)}, f32[1,4096]{1,0:T(1,128)S(1)}) custom-call(f32[1024,4096]{1,0:T(8,128)S(1)} %get-tuple-element.44.tile_ref, f32[1,1024]{1,0:T(1,128)S(1)} %get-tuple-element.45.top_ref, f32[1,1024]{1,0:T(1,128)S(1)} %get-tuple-element.46.refs_0_, f32[1,1024]{1,0:T(1,128)S(1)} %collective-permute-done.refs_1_, ...), custom_call_target="tpu_custom_call" | custom-call | tf_op jit(solution)/shard_map/pallas_call | solution.py:362
  23.8 13.0 %all_to_all.15 = f32[8,32,128]{2,1,0:T(8,128)S(1)} all-to-all(f32[8,32,128]{2,1,0:T(8,128)S(1)} %broadcast_in_dim.22), channel_id=1, replica_groups=mesh['rows'=8,'cols'=4] {'rows'}, dimensions={0} | all-to-all | bytes 262144 | tf_op jit(solution)/shard_map/all_to_all | solution.py:452
  37.0 5.4 %shard_map.70 = (f32[1024,4096]{1,0:T(8,128)S(1)}, f32[1,1024]{1,0:T(1,128)S(1)}, f32[1,4096]{1,0:T(1,128)S(1)}, f32[1,4096]{1,0:T(1,128)S(1)}, f32[1,1024]{1,0:T(1,128)S(1)}) custom-call(f32[1024,4096]{1,0:T(8,128)S(1)} %get-tuple-element.44.tile_ref, f32[1,1024]{1,0:T(1,128)S(1)} %get-tuple-element.45.top_ref, ...), custom_call_target="tpu_custom_call", output_to_operand_aliasing={{0}: (0, {})} | custom-call | tf_op jit(solution)/shard_map/pallas_call | solution.py:362
  44.3 1.8 %collective-permute-done.4.refs_2_ = f32[1,1024]{1,0:T(1,128)S(1)} collective-permute-done((f32[1,1024]{1,0:T(1,128)S(1)}, f32[1,1024]{1,0:T(1,128)S(1)}, u32[]{:S(2)}, u32[]{:S(2)}) %collective-permute-start.4) | collective-permute-done | bytes 4128 | tf_op jit(solution)/shard_map/ppermute | solution.py:387
  46.2 2.0 %shard_map.71 = (f32[1,1024]{1,0:T(1,128)S(1)}, f32[1,4096]{1,0:T(1,128)S(1)}) custom-call(f32[1024,4096]{1,0:T(8,128)S(1)} %get-tuple-element.52.soft_ref, f32[1,1024]{1,0:T(1,128)S(1)} %get-tuple-element.53.left_ref, f32[1,4096]{1,0:T(1,128)S(1)} %get-tuple-element.54.right_ref, f32[1,1024]{1,0:T(1,128)S(1)} %get-tuple-element.55.refs_0_, ...), custom_call_target="tpu_custom_call" | custom-call | tf_op jit(solution)/shard_map/pallas_call | solution.py:362
  48.2 10.0 %all_to_all.16 = f32[8,32,128]{2,1,0:T(8,128)S(1)} all-to-all(f32[8,32,128]{2,1,0:T(8,128)S(1)} %broadcast_in_dim.24), channel_id=1, replica_groups=mesh['rows'=8,'cols'=4] {'rows'}, dimensions={0} | all-to-all | bytes 262144 | tf_op jit(solution)/shard_map/all_to_all | solution.py:452
  58.2 1.8 %shard_map.72 = (f32[1,4096]{1,0:T(1,128)S(1)}, f32[1,1024]{1,0:T(1,128)S(1)}) custom-call(f32[1024,4096]{1,0:T(8,128)S(1)} %get-tuple-element.52.soft_ref, f32[1,1024]{1,0:T(1,128)S(1)} %get-tuple-element.56.inverse_ref, f32[1,4096]{1,0:T(1,128)S(1)} %get-tuple-element.54.right_ref, f32[1,4096]{1,0:T(1,128)S(1)} %bitcast.21, f32[1,4096]{1,0:T(1,128)S(1)} %bitcast.17), custom_call_target="tpu_custom_call" | custom-call | tf_op jit(solution)/shard_map/pallas_call | solution.py:362
  61.9 1.8 %collective-permute-done.7.refs_2_ = f32[1,1024]{1,0:T(1,128)S(1)} collective-permute-done((f32[1,1024]{1,0:T(1,128)S(1)}, f32[1,1024]{1,0:T(1,128)S(1)}, u32[]{:S(2)}, u32[]{:S(2)}) %collective-permute-start.7) | collective-permute-done | bytes 4128 | tf_op jit(solution)/shard_map/ppermute | solution.py:387
  64.6 2.0 %shard_map.73 = (f32[1,1024]{1,0:T(1,128)S(1)}, f32[1,4096]{1,0:T(1,128)S(1)}) custom-call(f32[1024,4096]{1,0:T(8,128)S(1)} %get-tuple-element.52.soft_ref, f32[1,1024]{1,0:T(1,128)S(1)} %get-tuple-element.56.inverse_ref, f32[1,4096]{1,0:T(1,128)S(1)} %get-tuple-element.54.right_ref, f32[1,1024]{1,0:T(1,128)S(1)} %bitcast.22, ...), custom_call_target="tpu_custom_call" | custom-call | tf_op jit(solution)/shard_map/pallas_call | solution.py:362
  66.6 10.0 %all_to_all.17 = f32[8,32,128]{2,1,0:T(8,128)S(1)} all-to-all(f32[8,32,128]{2,1,0:T(8,128)S(1)} %broadcast_in_dim.26), channel_id=1, replica_groups=mesh['rows'=8,'cols'=4] {'rows'}, dimensions={0} | all-to-all | bytes 262144 | tf_op jit(solution)/shard_map/all_to_all | solution.py:452
  76.6 1.9 %shard_map.74 = (f32[1,4096]{1,0:T(1,128)S(1)}, f32[1,1024]{1,0:T(1,128)S(1)}) custom-call(f32[1024,4096]{1,0:T(8,128)S(1)} %get-tuple-element.52.soft_ref, f32[1,1024]{1,0:T(1,128)S(1)} %get-tuple-element.53.left_ref, f32[1,4096]{1,0:T(1,128)S(1)} %get-tuple-element.54.right_ref, f32[1,4096]{1,0:T(1,128)S(1)} %bitcast.16), custom_call_target="tpu_custom_call" | custom-call | tf_op jit(solution)/shard_map/pallas_call | solution.py:362
  80.7 4.8 %shard_map.75 = (f32[1024,4096]{1,0:T(8,128)S(1)}, f32[1024,4096]{1,0:T(8,128)S(1)}) custom-call(f32[1024,4096]{1,0:T(8,128)S(1)} %get-tuple-element.52.soft_ref, f32[1,1024]{1,0:T(1,128)S(1)} %get-tuple-element.56.inverse_ref, f32[1,1024]{1,0:T(1,128)S(1)} %get-tuple-element.59.scaled_ref, ...), custom_call_target="tpu_custom_call", output_to_operand_aliasing={{0}: (0, {})} | custom-call | tf_op jit(solution)/shard_map/pallas_call | solution.py:362
  86.9 1.6 %collective-permute-start.16 = (f32[256,128]{1,0:T(8,128)S(1)}, f32[256,128]{1,0:T(8,128)S(1)}, u32[]{:S(2)}, u32[]{:S(2)}) collective-permute-start(f32[256,128]{1,0:T(8,128)S(1)} %get-tuple-element.74), channel_id=1, source_target_pairs={{0,8},{8,16},{16,24},{24,28},{28,20},{20,12},{12,4},{4,0},{1,9},{9... | collective-permute-start | bytes 393224 | tf_op jit(solution)/shard_map/ppermute | solution.py:410
  88.6 4.2 %shard_map.77 = (f32[512,128]{1,0:T(8,128)S(1)}, f32[512,128]{1,0:T(8,128)S(1)}, f32[256,128]{1,0:T(8,128)S(1)}, f32[256,128]{1,0:T(8,128)S(1)}, f32[256,128]{1,...) custom-call(f32[1024,4096]{1,0:T(8,128)S(1)} %get-tuple-element.64.f, ...), custom_call_target="tpu_custom_call" | custom-call | tf_op jit(solution)/shard_map/pallas_call | solution.py:362
  92.9 2.0 %collective-permute-start.27 = (f32[256,128]{1,0:T(8,128)S(1)}, f32[256,128]{1,0:T(8,128)S(1)}, u32[]{:S(2)}, u32[]{:S(2)}) collective-permute-start(f32[256,128]{1,0:T(8,128)S(1)} %add.316), channel_id=1, source_target_pairs={{8,0},{16,8},{24,16},{28,24},{20,28},{12,20},{4,12},{0,4},{9,1},{1... | collective-permute-start | bytes 393224 | tf_op jit(solution)/shard_map/ppermute | solution.py:413
  95.3 1.7 %collective-permute-start.17 = (f32[256,128]{1,0:T(8,128)S(1)}, f32[256,128]{1,0:T(8,128)S(1)}, u32[]{:S(2)}, u32[]{:S(2)}) collective-permute-start(f32[256,128]{1,0:T(8,128)S(1)} %add.306), channel_id=1, source_target_pairs={{0,8},{8,16},{16,24},{24,28},{28,20},{20,12},{12,4},{4,0},{1,9},{9... | collective-permute-start | bytes 393224 | tf_op jit(solution)/shard_map/ppermute | solution.py:410
  99.2 1.7 %collective-permute-start.28 = (f32[256,128]{1,0:T(8,128)S(1)}, f32[256,128]{1,0:T(8,128)S(1)}, u32[]{:S(2)}, u32[]{:S(2)}) collective-permute-start(f32[256,128]{1,0:T(8,128)S(1)} %add.317), channel_id=1, source_target_pairs={{8,0},{16,8},{24,16},{28,24},{20,28},{12,20},{4,12},{0,4},{9,1},{1... | collective-permute-start | bytes 393224 | tf_op jit(solution)/shard_map/ppermute | solution.py:413
  101.1 1.7 %collective-permute-start.21 = (f32[256,128]{1,0:T(8,128)S(1)}, f32[256,128]{1,0:T(8,128)S(1)}, u32[]{:S(2)}, u32[]{:S(2)}) collective-permute-start(f32[256,128]{1,0:T(8,128)S(1)} %add.310), channel_id=1, source_target_pairs={{8,0},{16,8},{24,16},{28,24},{20,28},{12,20},{4,12},{0,4},{9,1},{1... | collective-permute-start | bytes 393224 | tf_op jit(solution)/shard_map/ppermute | solution.py:413
  104.5 1.7 %collective-permute-start.25 = (f32[256,128]{1,0:T(8,128)S(1)}, f32[256,128]{1,0:T(8,128)S(1)}, u32[]{:S(2)}, u32[]{:S(2)}) collective-permute-start(f32[256,128]{1,0:T(8,128)S(1)} %add.314), channel_id=1, source_target_pairs={{0,8},{8,16},{16,24},{24,28},{28,20},{20,12},{12,4},{4,0},{1,9},{9... | collective-permute-start | bytes 393224 | tf_op jit(solution)/shard_map/ppermute | solution.py:410
  109.5 2.5 %collective-permute-done.25 = f32[256,128]{1,0:T(8,128)S(1)} collective-permute-done((f32[256,128]{1,0:T(8,128)S(1)}, f32[256,128]{1,0:T(8,128)S(1)}, u32[]{:S(2)}, u32[]{:S(2)}) %collective-permute-start.25) | collective-permute-done | bytes 131104 | tf_op jit(solution)/shard_map/ppermute | solution.py:410
  112.6 2.3 %collective-permute-done.22 = f32[256,128]{1,0:T(8,128)S(1)} collective-permute-done((f32[256,128]{1,0:T(8,128)S(1)}, f32[256,128]{1,0:T(8,128)S(1)}, u32[]{:S(2)}, u32[]{:S(2)}) %collective-permute-start.22) | collective-permute-done | bytes 131104 | tf_op jit(solution)/shard_map/ppermute | solution.py:413
  116.1 1.6 %collective-permute-start.41 = (f32[256,128]{1,0:T(8,128)S(1)}, f32[256,128]{1,0:T(8,128)S(1)}, u32[]{:S(2)}, u32[]{:S(2)}) collective-permute-start(f32[256,128]{1,0:T(8,128)S(1)} %add_add_fusion.refs_4_), channel_id=1, source_target_pairs={{0,8},{8,16},{16,24},{24,28},{28,20},{20,12},{12,4},{4,0},{1,9},{9... | collective-permute-start | bytes 393224 | tf_op jit(solution)/shard_map/ppermute | solution.py:410
  118.1 1.6 %collective-permute-start.33 = (f32[256,128]{1,0:T(8,128)S(1)}, f32[256,128]{1,0:T(8,128)S(1)}, u32[]{:S(2)}, u32[]{:S(2)}) collective-permute-start(f32[256,128]{1,0:T(8,128)S(1)} %collective-permute-done.31.refs_6_), channel_id=1, source_target_pairs={{8,0},{16,8},{24,16},{28,24},{20,28},{12,20},{4,12},{0,4},{9,1},{1... | collective-permute-start | bytes 393224 | tf_op jit(solution)/shard_map/ppermute | solution.py:413
  121.1 1.7 %collective-permute-done.41.refs_18_ = f32[256,128]{1,0:T(8,128)S(1)} collective-permute-done((f32[256,128]{1,0:T(8,128)S(1)}, f32[256,128]{1,0:T(8,128)S(1)}, u32[]{:S(2)}, u32[]{:S(2)}) %collective-permute-start.41) | collective-permute-done | bytes 131104 | tf_op jit(solution)/shard_map/ppermute | solution.py:410
  122.9 1.9 %collective-permute-start.32 = (f32[256,128]{1,0:T(8,128)S(1)}, f32[256,128]{1,0:T(8,128)S(1)}, u32[]{:S(2)}, u32[]{:S(2)}) collective-permute-start(f32[256,128]{1,0:T(8,128)S(1)} %collective-permute-done.30.refs_5_), channel_id=1, source_target_pairs={{8,0},{16,8},{24,16},{28,24},{20,28},{12,20},{4,12},{0,4},{9,1},{1... | collective-permute-start | bytes 393224 | tf_op jit(solution)/shard_map/ppermute | solution.py:413
  125.2 2.1 %collective-permute-done.37.refs_15_ = f32[256,128]{1,0:T(8,128)S(1)} collective-permute-done((f32[256,128]{1,0:T(8,128)S(1)}, f32[256,128]{1,0:T(8,128)S(1)}, u32[]{:S(2)}, u32[]{:S(2)}) %collective-permute-start.37) | collective-permute-done | bytes 131104 | tf_op jit(solution)/shard_map/ppermute | solution.py:410
  127.3 2.6 %collective-permute-done.42.refs_16_ = f32[256,128]{1,0:T(8,128)S(1)} collective-permute-done((f32[256,128]{1,0:T(8,128)S(1)}, f32[256,128]{1,0:T(8,128)S(1)}, u32[]{:S(2)}, u32[]{:S(2)}) %collective-permute-start.42) | collective-permute-done | bytes 131104 | tf_op jit(solution)/shard_map/ppermute | solution.py:410
  129.9 2.0 %collective-permute-start.34 = (f32[256,128]{1,0:T(8,128)S(1)}, f32[256,128]{1,0:T(8,128)S(1)}, u32[]{:S(2)}, u32[]{:S(2)}) collective-permute-start(f32[256,128]{1,0:T(8,128)S(1)} %collective-permute-done.32.refs_7_), channel_id=1, source_target_pairs={{8,0},{16,8},{24,16},{28,24},{20,28},{12,20},{4,12},{0,4},{9,1},{1... | collective-permute-start | bytes 393224 | tf_op jit(solution)/shard_map/ppermute | solution.py:413
  133.9 2.3 %collective-permute-done.43.refs_14_ = f32[256,128]{1,0:T(8,128)S(1)} collective-permute-done((f32[256,128]{1,0:T(8,128)S(1)}, f32[256,128]{1,0:T(8,128)S(1)}, u32[]{:S(2)}, u32[]{:S(2)}) %collective-permute-start.43) | collective-permute-done | bytes 131104 | tf_op jit(solution)/shard_map/ppermute | solution.py:410
  137.8 1.6 %shard_map.78 = (f32[1024,128]{1,0:T(8,128)}, f32[4096,128]{1,0:T(8,128)}) custom-call(f32[256,128]{1,0:T(8,128)S(1)} %slice_add_fusion.refs_0_, f32[256,128]{1,0:T(8,128)S(1)} %collective-permute-done.14.refs_1_, f32[512,128]{1,0:T(8,128)S(1)} %collective-permute-done.15.refs_2_, f32[256,128]{1,0:T(8,128)S(1)} %add_add_fusion.1.refs_3_, ...), custom_call_target="tpu_custom_call" | custom-call | tf_op jit(solution)/shard_map/pallas_call | solution.py:510
  (97 shorter events, 27.8 us)
Async XLA Ops:
  78.5 7.1 %collective-permute-start.10 = (f32[1,1024]{1,0:T(1,128)S(1)}, f32[1,1024]{1,0:T(1,128)S(1)}, u32[]{:S(2)}, u32[]{:S(2)}) collective-permute-start(f32[1,1024]{1,0:T(1,128)S(1)} %get-tuple-element.66.refs_0_), channel_id=1, source_target_pairs={{0,2},{1,3},{2,0},{3,1},{4,6},{5,7},{6,4},{7,5},{8,10},{9,11},{10,... | collective-permute-start | bytes 12296 | tf_op jit(solution)/shard_map/ppermute | solution.py:387
  79.1 6.4 %collective-permute-start.11 = (f32[1,1024]{1,0:T(1,128)S(1)}, f32[1,1024]{1,0:T(1,128)S(1)}, u32[]{:S(2)}, u32[]{:S(2)}) collective-permute-start(f32[1,1024]{1,0:T(1,128)S(1)} %get-tuple-element.66.refs_0_), channel_id=1, source_target_pairs={{0,3},{1,2},{2,1},{3,0},{4,7},{5,6},{6,5},{7,4},{8,11},{9,10},{10,... | collective-permute-start | bytes 12296 | tf_op jit(solution)/shard_map/ppermute | solution.py:387
  79.1 6.4 %collective-permute-start.9 = (f32[1,1024]{1,0:T(1,128)S(1)}, f32[1,1024]{1,0:T(1,128)S(1)}, u32[]{:S(2)}, u32[]{:S(2)}) collective-permute-start(f32[1,1024]{1,0:T(1,128)S(1)} %get-tuple-element.66.refs_0_), channel_id=1, source_target_pairs={{0,1},{1,0},{2,3},{3,2},{4,5},{5,4},{6,7},{7,6},{8,9},{9,8},{10,11... | collective-permute-start | bytes 12296 | tf_op jit(solution)/shard_map/ppermute | solution.py:387
  86.5 6.4 %collective-permute-start.26 = (f32[256,128]{1,0:T(8,128)S(1)}, f32[256,128]{1,0:T(8,128)S(1)}, u32[]{:S(2)}, u32[]{:S(2)}) collective-permute-start(f32[256,128]{1,0:T(8,128)S(1)} %get-tuple-element.85), channel_id=1, source_target_pairs={{8,0},{16,8},{24,16},{28,24},{20,28},{12,20},{4,12},{0,4},{9,1},{1... | collective-permute-start | bytes 393224 | tf_op jit(solution)/shard_map/ppermute | solution.py:413
  86.9 8.4 %collective-permute-start.16 = (f32[256,128]{1,0:T(8,128)S(1)}, f32[256,128]{1,0:T(8,128)S(1)}, u32[]{:S(2)}, u32[]{:S(2)}) collective-permute-start(f32[256,128]{1,0:T(8,128)S(1)} %get-tuple-element.74), channel_id=1, source_target_pairs={{0,8},{8,16},{16,24},{24,28},{28,20},{20,12},{12,4},{4,0},{1,9},{9... | collective-permute-start | bytes 393224 | tf_op jit(solution)/shard_map/ppermute | solution.py:410
  92.9 6.3 %collective-permute-start.27 = (f32[256,128]{1,0:T(8,128)S(1)}, f32[256,128]{1,0:T(8,128)S(1)}, u32[]{:S(2)}, u32[]{:S(2)}) collective-permute-start(f32[256,128]{1,0:T(8,128)S(1)} %add.316), channel_id=1, source_target_pairs={{8,0},{16,8},{24,16},{28,24},{20,28},{12,20},{4,12},{0,4},{9,1},{1... | collective-permute-start | bytes 393224 | tf_op jit(solution)/shard_map/ppermute | solution.py:413
  94.9 6.2 %collective-permute-start.20 = (f32[256,128]{1,0:T(8,128)S(1)}, f32[256,128]{1,0:T(8,128)S(1)}, u32[]{:S(2)}, u32[]{:S(2)}) collective-permute-start(f32[256,128]{1,0:T(8,128)S(1)} %get-tuple-element.77), channel_id=1, source_target_pairs={{8,0},{16,8},{24,16},{28,24},{20,28},{12,20},{4,12},{0,4},{9,1},{1... | collective-permute-start | bytes 393224 | tf_op jit(solution)/shard_map/ppermute | solution.py:413
  95.3 12.7 %collective-permute-start.12 = (f32[512,128]{1,0:T(8,128)S(1)}, f32[512,128]{1,0:T(8,128)S(1)}, u32[]{:S(2)}, u32[]{:S(2)}) collective-permute-start(f32[512,128]{1,0:T(8,128)S(1)} %get-tuple-element.69), channel_id=1, source_target_pairs={{0,1},{1,0},{2,3},{3,2},{4,5},{5,4},{6,7},{7,6},{8,9},{9,8},{10,11... | collective-permute-start | bytes 786440 | tf_op jit(solution)/shard_map/ppermute | solution.py:387
  95.3 7.5 %collective-permute-start.17 = (f32[256,128]{1,0:T(8,128)S(1)}, f32[256,128]{1,0:T(8,128)S(1)}, u32[]{:S(2)}, u32[]{:S(2)}) collective-permute-start(f32[256,128]{1,0:T(8,128)S(1)} %add.306), channel_id=1, source_target_pairs={{0,8},{8,16},{16,24},{24,28},{28,20},{20,12},{12,4},{4,0},{1,9},{9... | collective-permute-start | bytes 393224 | tf_op jit(solution)/shard_map/ppermute | solution.py:410
  97.8 6.7 %collective-permute-start.24 = (f32[256,128]{1,0:T(8,128)S(1)}, f32[256,128]{1,0:T(8,128)S(1)}, u32[]{:S(2)}, u32[]{:S(2)}) collective-permute-start(f32[256,128]{1,0:T(8,128)S(1)} %add.313), channel_id=1, source_target_pairs={{0,8},{8,16},{16,24},{24,28},{28,20},{20,12},{12,4},{4,0},{1,9},{9... | collective-permute-start | bytes 393224 | tf_op jit(solution)/shard_map/ppermute | solution.py:410
  99.2 7.0 %collective-permute-start.28 = (f32[256,128]{1,0:T(8,128)S(1)}, f32[256,128]{1,0:T(8,128)S(1)}, u32[]{:S(2)}, u32[]{:S(2)}) collective-permute-start(f32[256,128]{1,0:T(8,128)S(1)} %add.317), channel_id=1, source_target_pairs={{8,0},{16,8},{24,16},{28,24},{20,28},{12,20},{4,12},{0,4},{9,1},{1... | collective-permute-start | bytes 393224 | tf_op jit(solution)/shard_map/ppermute | solution.py:413
  101.1 5.5 %collective-permute-start.21 = (f32[256,128]{1,0:T(8,128)S(1)}, f32[256,128]{1,0:T(8,128)S(1)}, u32[]{:S(2)}, u32[]{:S(2)}) collective-permute-start(f32[256,128]{1,0:T(8,128)S(1)} %add.310), channel_id=1, source_target_pairs={{8,0},{16,8},{24,16},{28,24},{20,28},{12,20},{4,12},{0,4},{9,1},{1... | collective-permute-start | bytes 393224 | tf_op jit(solution)/shard_map/ppermute | solution.py:413
  102.9 6.4 %collective-permute-start.18 = (f32[256,128]{1,0:T(8,128)S(1)}, f32[256,128]{1,0:T(8,128)S(1)}, u32[]{:S(2)}, u32[]{:S(2)}) collective-permute-start(f32[256,128]{1,0:T(8,128)S(1)} %add.307), channel_id=1, source_target_pairs={{0,8},{8,16},{16,24},{24,28},{28,20},{20,12},{12,4},{4,0},{1,9},{9... | collective-permute-start | bytes 393224 | tf_op jit(solution)/shard_map/ppermute | solution.py:410
  104.5 7.6 %collective-permute-start.25 = (f32[256,128]{1,0:T(8,128)S(1)}, f32[256,128]{1,0:T(8,128)S(1)}, u32[]{:S(2)}, u32[]{:S(2)}) collective-permute-start(f32[256,128]{1,0:T(8,128)S(1)} %add.314), channel_id=1, source_target_pairs={{0,8},{8,16},{16,24},{24,28},{28,20},{20,12},{12,4},{4,0},{1,9},{9... | collective-permute-start | bytes 393224 | tf_op jit(solution)/shard_map/ppermute | solution.py:410
  106.2 5.9 %collective-permute-start.29 = (f32[256,128]{1,0:T(8,128)S(1)}, f32[256,128]{1,0:T(8,128)S(1)}, u32[]{:S(2)}, u32[]{:S(2)}) collective-permute-start(f32[256,128]{1,0:T(8,128)S(1)} %add.318), channel_id=1, source_target_pairs={{8,0},{16,8},{24,16},{28,24},{20,28},{12,20},{4,12},{0,4},{9,1},{1... | collective-permute-start | bytes 393224 | tf_op jit(solution)/shard_map/ppermute | solution.py:413
  106.7 8.2 %collective-permute-start.22 = (f32[256,128]{1,0:T(8,128)S(1)}, f32[256,128]{1,0:T(8,128)S(1)}, u32[]{:S(2)}, u32[]{:S(2)}) collective-permute-start(f32[256,128]{1,0:T(8,128)S(1)} %add.311), channel_id=1, source_target_pairs={{8,0},{16,8},{24,16},{28,24},{20,28},{12,20},{4,12},{0,4},{9,1},{1... | collective-permute-start | bytes 393224 | tf_op jit(solution)/shard_map/ppermute | solution.py:413
  108.0 7.1 %collective-permute-start.13 = (f32[256,128]{1,0:T(8,128)S(1)}, f32[256,128]{1,0:T(8,128)S(1)}, u32[]{:S(2)}, u32[]{:S(2)}) collective-permute-start(f32[256,128]{1,0:T(8,128)S(1)} %slice.9), channel_id=1, source_target_pairs={{0,2},{1,3},{2,0},{3,1},{4,6},{5,7},{6,4},{7,5},{8,10},{9,11},{10,... | collective-permute-start | bytes 393224 | tf_op jit(solution)/shard_map/ppermute | solution.py:387
  109.3 5.6 %collective-permute-start.19 = (f32[256,128]{1,0:T(8,128)S(1)}, f32[256,128]{1,0:T(8,128)S(1)}, u32[]{:S(2)}, u32[]{:S(2)}) collective-permute-start(f32[256,128]{1,0:T(8,128)S(1)} %add.308), channel_id=1, source_target_pairs={{0,8},{8,16},{16,24},{24,28},{28,20},{20,12},{12,4},{4,0},{1,9},{9... | collective-permute-start | bytes 393224 | tf_op jit(solution)/shard_map/ppermute | solution.py:410
  112.1 6.0 %collective-permute-start.31 = (f32[256,128]{1,0:T(8,128)S(1)}, f32[256,128]{1,0:T(8,128)S(1)}, u32[]{:S(2)}, u32[]{:S(2)}) collective-permute-start(f32[256,128]{1,0:T(8,128)S(1)} %add_add_fusion.refs_4_), channel_id=1, source_target_pairs={{8,0},{16,8},{24,16},{28,24},{20,28},{12,20},{4,12},{0,4},{9,1},{1... | collective-permute-start | bytes 393224 | tf_op jit(solution)/shard_map/ppermute | solution.py:413
  114.9 6.0 %collective-permute-start.36 = (f32[256,128]{1,0:T(8,128)S(1)}, f32[256,128]{1,0:T(8,128)S(1)}, u32[]{:S(2)}, u32[]{:S(2)}) collective-permute-start(f32[256,128]{1,0:T(8,128)S(1)} %add_add_fusion.1.refs_3_), channel_id=1, source_target_pairs={{0,8},{8,16},{16,24},{24,28},{28,20},{20,12},{12,4},{4,0},{1,9},{9... | collective-permute-start | bytes 393224 | tf_op jit(solution)/shard_map/ppermute | solution.py:410
  115.2 5.8 %collective-permute-start.14 = (f32[256,128]{1,0:T(8,128)S(1)}, f32[256,128]{1,0:T(8,128)S(1)}, u32[]{:S(2)}, u32[]{:S(2)}) collective-permute-start(f32[256,128]{1,0:T(8,128)S(1)} %slice_add_fusion.refs_0_), channel_id=1, source_target_pairs={{0,2},{1,3},{2,0},{3,1},{4,6},{5,7},{6,4},{7,5},{8,10},{9,11},{10,... | collective-permute-start | bytes 393224 | tf_op jit(solution)/shard_map/ppermute | solution.py:387
  116.1 6.6 %collective-permute-start.41 = (f32[256,128]{1,0:T(8,128)S(1)}, f32[256,128]{1,0:T(8,128)S(1)}, u32[]{:S(2)}, u32[]{:S(2)}) collective-permute-start(f32[256,128]{1,0:T(8,128)S(1)} %add_add_fusion.refs_4_), channel_id=1, source_target_pairs={{0,8},{8,16},{16,24},{24,28},{28,20},{20,12},{12,4},{4,0},{1,9},{9... | collective-permute-start | bytes 393224 | tf_op jit(solution)/shard_map/ppermute | solution.py:410
  117.7 5.2 %collective-permute-start.30 = (f32[256,128]{1,0:T(8,128)S(1)}, f32[256,128]{1,0:T(8,128)S(1)}, u32[]{:S(2)}, u32[]{:S(2)}) collective-permute-start(f32[256,128]{1,0:T(8,128)S(1)} %add_add_fusion.1.refs_3_), channel_id=1, source_target_pairs={{8,0},{16,8},{24,16},{28,24},{20,28},{12,20},{4,12},{0,4},{9,1},{1... | collective-permute-start | bytes 393224 | tf_op jit(solution)/shard_map/ppermute | solution.py:413
  118.1 6.6 %collective-permute-start.33 = (f32[256,128]{1,0:T(8,128)S(1)}, f32[256,128]{1,0:T(8,128)S(1)}, u32[]{:S(2)}, u32[]{:S(2)}) collective-permute-start(f32[256,128]{1,0:T(8,128)S(1)} %collective-permute-done.31.refs_6_), channel_id=1, source_target_pairs={{8,0},{16,8},{24,16},{28,24},{20,28},{12,20},{4,12},{0,4},{9,1},{1... | collective-permute-start | bytes 393224 | tf_op jit(solution)/shard_map/ppermute | solution.py:413
  121.0 6.3 %collective-permute-start.37 = (f32[256,128]{1,0:T(8,128)S(1)}, f32[256,128]{1,0:T(8,128)S(1)}, u32[]{:S(2)}, u32[]{:S(2)}) collective-permute-start(f32[256,128]{1,0:T(8,128)S(1)} %collective-permute-done.36.refs_17_), channel_id=1, source_target_pairs={{0,8},{8,16},{16,24},{24,28},{28,20},{20,12},{12,4},{4,0},{1,9},{9... | collective-permute-start | bytes 393224 | tf_op jit(solution)/shard_map/ppermute | solution.py:410
  121.0 12.9 %collective-permute-start.15 = (f32[512,128]{1,0:T(8,128)S(1)}, f32[512,128]{1,0:T(8,128)S(1)}, u32[]{:S(2)}, u32[]{:S(2)}) collective-permute-start(f32[512,128]{1,0:T(8,128)S(1)} %pad_maximum_fusion), channel_id=1, source_target_pairs={{0,1},{1,0},{2,3},{3,2},{4,5},{5,4},{6,7},{7,6},{8,9},{9,8},{10,11... | collective-permute-start | bytes 786440 | tf_op jit(solution)/shard_map/ppermute | solution.py:387
  122.7 7.1 %collective-permute-start.42 = (f32[256,128]{1,0:T(8,128)S(1)}, f32[256,128]{1,0:T(8,128)S(1)}, u32[]{:S(2)}, u32[]{:S(2)}) collective-permute-start(f32[256,128]{1,0:T(8,128)S(1)} %collective-permute-done.41.refs_18_), channel_id=1, source_target_pairs={{0,8},{8,16},{16,24},{24,28},{28,20},{20,12},{12,4},{4,0},{1,9},{9... | collective-permute-start | bytes 393224 | tf_op jit(solution)/shard_map/ppermute | solution.py:410
  122.9 7.0 %collective-permute-start.32 = (f32[256,128]{1,0:T(8,128)S(1)}, f32[256,128]{1,0:T(8,128)S(1)}, u32[]{:S(2)}, u32[]{:S(2)}) collective-permute-start(f32[256,128]{1,0:T(8,128)S(1)} %collective-permute-done.30.refs_5_), channel_id=1, source_target_pairs={{8,0},{16,8},{24,16},{28,24},{20,28},{12,20},{4,12},{0,4},{9,1},{1... | collective-permute-start | bytes 393224 | tf_op jit(solution)/shard_map/ppermute | solution.py:413
  124.8 7.1 %collective-permute-start.35 = (f32[256,128]{1,0:T(8,128)S(1)}, f32[256,128]{1,0:T(8,128)S(1)}, u32[]{:S(2)}, u32[]{:S(2)}) collective-permute-start(f32[256,128]{1,0:T(8,128)S(1)} %collective-permute-done.33.refs_8_), channel_id=1, source_target_pairs={{8,0},{16,8},{24,16},{28,24},{20,28},{12,20},{4,12},{0,4},{9,1},{1... | collective-permute-start | bytes 393224 | tf_op jit(solution)/shard_map/ppermute | solution.py:413
  127.3 5.6 %collective-permute-start.38 = (f32[256,128]{1,0:T(8,128)S(1)}, f32[256,128]{1,0:T(8,128)S(1)}, u32[]{:S(2)}, u32[]{:S(2)}) collective-permute-start(f32[256,128]{1,0:T(8,128)S(1)} %collective-permute-done.37.refs_15_), channel_id=1, source_target_pairs={{0,8},{8,16},{16,24},{24,28},{28,20},{20,12},{12,4},{4,0},{1,9},{9... | collective-permute-start | bytes 393224 | tf_op jit(solution)/shard_map/ppermute | solution.py:410
  129.9 6.3 %collective-permute-start.43 = (f32[256,128]{1,0:T(8,128)S(1)}, f32[256,128]{1,0:T(8,128)S(1)}, u32[]{:S(2)}, u32[]{:S(2)}) collective-permute-start(f32[256,128]{1,0:T(8,128)S(1)} %collective-permute-done.42.refs_16_), channel_id=1, source_target_pairs={{0,8},{8,16},{16,24},{24,28},{28,20},{20,12},{12,4},{4,0},{1,9},{9... | collective-permute-start | bytes 393224 | tf_op jit(solution)/shard_map/ppermute | solution.py:410
  129.9 6.3 %collective-permute-start.34 = (f32[256,128]{1,0:T(8,128)S(1)}, f32[256,128]{1,0:T(8,128)S(1)}, u32[]{:S(2)}, u32[]{:S(2)}) collective-permute-start(f32[256,128]{1,0:T(8,128)S(1)} %collective-permute-done.32.refs_7_), channel_id=1, source_target_pairs={{8,0},{16,8},{24,16},{28,24},{20,28},{12,20},{4,12},{0,4},{9,1},{1... | collective-permute-start | bytes 393224 | tf_op jit(solution)/shard_map/ppermute | solution.py:413
  (14 other events, 82.2 us)

commit v9 on v8

--- a/solution.py
+++ b/solution.py
@@ -12,7 +12,7 @@
 KAPPA = math.log2(math.e) / EPSILON
 LOWEST = -64.0
 LANES = 128
-WIDE = 512
+WIDE = 1024
 TALL = 1024
 LIMIT = 8 * 2**20
 F32 = jnp.float32

time: 140 us -> 139 us (level)
  transfers between devices with their start and end apart: 44 -> 44, of which waited for: 20 -> 20; matrix products, arithmetic and copies ran while one was open for 0% -> 0% of each run, Pallas kernels for 6% -> 7%
where the time goes in v9:
time: 139 us
  Pallas kernels  40.5 us (29%)
  starting transfers between devices  34.9 us (25%)
  blocking collectives  32.9 us (24%)
  waiting for transfers between devices  28.6 us (21%)
    all_to_all x3, blocking collectives, over_rows(): lax.all_to_all(copies, 'rows', 0, 0)  32.9 us
    pallas_call x9, Pallas kernels, call(): pl.pallas_call(kernel, in_specs=[pl.BlockSpec(memory_space=pltpu.VMEM)] *...  30.8 us
    ppermute x14, waiting for transfers between devices, ahead(): return lax.ppermute(x, 'rows', up)  16.7 us
    ppermute x14, starting transfers between devices, behind(): return lax.ppermute(x, 'rows', down)  14.9 us
    ppermute x16, starting transfers between devices, exchange(): lax.ppermute(x, axis, [(i, i ^ k * stride) for i in range(n)])  10.9 us
    ppermute x14, starting transfers between devices, ahead(): return lax.ppermute(x, 'rows', up)  9.07 us
    pallas_call x1, Pallas kernels, per_device(): pl.pallas_call(row_level_kernel, in_specs=[pl.BlockSpec(memory_space=pltp...  8 us
    ppermute x16, waiting for transfers between devices, exchange(): lax.ppermute(x, axis, [(i, i ^ k * stride) for i in range(n)])  7.51 us
  transfers between devices with their start and end apart: 44, of which 20 were waited for; matrix products, arithmetic and copies ran while one was open for 0% of the time, Pallas kernels for 7%

profile of v9, /device:TPU:0, one launch (start us, length us, event | category | flops | bytes accessed | tf_op | source)
XLA Modules:
  0.0 138.6 jit_solution(6078971885293207096)
XLA Ops:
  0.6 8.0 %shard_map.68 = (f32[1024,4096]{1,0:T(8,128)S(1)}, f32[1,1024]{1,0:T(1,128)S(1)}, f32[1,1024]{1,0:T(1,128)S(1)}, bf16[1024,128]{1,0:T(8,128)(2,1)S(1)}, bf16[409...) custom-call(bf16[1024,128]{1,0:T(8,128)(2,1)} %crawl_hbm.1, bf16[4096,128]{1,0:T(8,128)(2,1)} %bench_hbm.1, f32[1,4096]{1,0:T(1,128)} %bitcast.31), custom_call_target="tpu_custom_call" | custom-call | tf_op jit(solution)/shard_map/pallas_call | solution.py:454
  9.2 2.6 %collective-permute-start.1 = (f32[1,1024]{1,0:T(1,128)S(1)}, f32[1,1024]{1,0:T(1,128)S(1)}, u32[]{:S(2)}, u32[]{:S(2)}) collective-permute-start(f32[1,1024]{1,0:T(1,128)S(1)} %get-tuple-element.46.refs_0_), channel_id=1, source_target_pairs={{0,2},{1,3},{2,0},{3,1},{4,6},{5,7},{6,4},{7,5},{8,10},{9,11},{10,... | collective-permute-start | bytes 12296 | tf_op jit(solution)/shard_map/ppermute | solution.py:387
  14.8 8.4 %shard_map.69 = (f32[1,1024]{1,0:T(1,128)S(1)}, f32[1,4096]{1,0:T(1,128)S(1)}) custom-call(f32[1024,4096]{1,0:T(8,128)S(1)} %get-tuple-element.44.tile_ref, f32[1,1024]{1,0:T(1,128)S(1)} %get-tuple-element.45.top_ref, f32[1,1024]{1,0:T(1,128)S(1)} %get-tuple-element.46.refs_0_, f32[1,1024]{1,0:T(1,128)S(1)} %collective-permute-done.refs_1_, ...), custom_call_target="tpu_custom_call" | custom-call | tf_op jit(solution)/shard_map/pallas_call | solution.py:362
  23.1 13.0 %all_to_all.15 = f32[8,32,128]{2,1,0:T(8,128)S(1)} all-to-all(f32[8,32,128]{2,1,0:T(8,128)S(1)} %broadcast_in_dim.22), channel_id=1, replica_groups=mesh['rows'=8,'cols'=4] {'rows'}, dimensions={0} | all-to-all | bytes 262144 | tf_op jit(solution)/shard_map/all_to_all | solution.py:452
  36.4 4.7 %shard_map.70 = (f32[1024,4096]{1,0:T(8,128)S(1)}, f32[1,1024]{1,0:T(1,128)S(1)}, f32[1,4096]{1,0:T(1,128)S(1)}, f32[1,4096]{1,0:T(1,128)S(1)}, f32[1,1024]{1,0:T(1,128)S(1)}) custom-call(f32[1024,4096]{1,0:T(8,128)S(1)} %get-tuple-element.44.tile_ref, f32[1,1024]{1,0:T(1,128)S(1)} %get-tuple-element.45.top_ref, ...), custom_call_target="tpu_custom_call", output_to_operand_aliasing={{0}: (0, {})} | custom-call | tf_op jit(solution)/shard_map/pallas_call | solution.py:362
  43.0 1.8 %collective-permute-done.4.refs_2_ = f32[1,1024]{1,0:T(1,128)S(1)} collective-permute-done((f32[1,1024]{1,0:T(1,128)S(1)}, f32[1,1024]{1,0:T(1,128)S(1)}, u32[]{:S(2)}, u32[]{:S(2)}) %collective-permute-start.4) | collective-permute-done | bytes 4128 | tf_op jit(solution)/shard_map/ppermute | solution.py:387
  44.9 2.0 %shard_map.71 = (f32[1,1024]{1,0:T(1,128)S(1)}, f32[1,4096]{1,0:T(1,128)S(1)}) custom-call(f32[1024,4096]{1,0:T(8,128)S(1)} %get-tuple-element.52.soft_ref, f32[1,1024]{1,0:T(1,128)S(1)} %get-tuple-element.53.left_ref, f32[1,4096]{1,0:T(1,128)S(1)} %get-tuple-element.54.right_ref, f32[1,1024]{1,0:T(1,128)S(1)} %get-tuple-element.55.refs_0_, ...), custom_call_target="tpu_custom_call" | custom-call | tf_op jit(solution)/shard_map/pallas_call | solution.py:362
  46.9 9.9 %all_to_all.16 = f32[8,32,128]{2,1,0:T(8,128)S(1)} all-to-all(f32[8,32,128]{2,1,0:T(8,128)S(1)} %broadcast_in_dim.24), channel_id=1, replica_groups=mesh['rows'=8,'cols'=4] {'rows'}, dimensions={0} | all-to-all | bytes 262144 | tf_op jit(solution)/shard_map/all_to_all | solution.py:452
  56.8 1.8 %shard_map.72 = (f32[1,4096]{1,0:T(1,128)S(1)}, f32[1,1024]{1,0:T(1,128)S(1)}) custom-call(f32[1024,4096]{1,0:T(8,128)S(1)} %get-tuple-element.52.soft_ref, f32[1,1024]{1,0:T(1,128)S(1)} %get-tuple-element.56.inverse_ref, f32[1,4096]{1,0:T(1,128)S(1)} %get-tuple-element.54.right_ref, f32[1,4096]{1,0:T(1,128)S(1)} %bitcast.21, f32[1,4096]{1,0:T(1,128)S(1)} %bitcast.17), custom_call_target="tpu_custom_call" | custom-call | tf_op jit(solution)/shard_map/pallas_call | solution.py:362
  60.5 1.8 %collective-permute-done.7.refs_2_ = f32[1,1024]{1,0:T(1,128)S(1)} collective-permute-done((f32[1,1024]{1,0:T(1,128)S(1)}, f32[1,1024]{1,0:T(1,128)S(1)}, u32[]{:S(2)}, u32[]{:S(2)}) %collective-permute-start.7) | collective-permute-done | bytes 4128 | tf_op jit(solution)/shard_map/ppermute | solution.py:387
  63.2 2.0 %shard_map.73 = (f32[1,1024]{1,0:T(1,128)S(1)}, f32[1,4096]{1,0:T(1,128)S(1)}) custom-call(f32[1024,4096]{1,0:T(8,128)S(1)} %get-tuple-element.52.soft_ref, f32[1,1024]{1,0:T(1,128)S(1)} %get-tuple-element.56.inverse_ref, f32[1,4096]{1,0:T(1,128)S(1)} %get-tuple-element.54.right_ref, f32[1,1024]{1,0:T(1,128)S(1)} %bitcast.22, ...), custom_call_target="tpu_custom_call" | custom-call | tf_op jit(solution)/shard_map/pallas_call | solution.py:362
  65.2 10.0 %all_to_all.17 = f32[8,32,128]{2,1,0:T(8,128)S(1)} all-to-all(f32[8,32,128]{2,1,0:T(8,128)S(1)} %broadcast_in_dim.26), channel_id=1, replica_groups=mesh['rows'=8,'cols'=4] {'rows'}, dimensions={0} | all-to-all | bytes 262144 | tf_op jit(solution)/shard_map/all_to_all | solution.py:452
  75.2 1.9 %shard_map.74 = (f32[1,4096]{1,0:T(1,128)S(1)}, f32[1,1024]{1,0:T(1,128)S(1)}) custom-call(f32[1024,4096]{1,0:T(8,128)S(1)} %get-tuple-element.52.soft_ref, f32[1,1024]{1,0:T(1,128)S(1)} %get-tuple-element.53.left_ref, f32[1,4096]{1,0:T(1,128)S(1)} %get-tuple-element.54.right_ref, f32[1,4096]{1,0:T(1,128)S(1)} %bitcast.16), custom_call_target="tpu_custom_call" | custom-call | tf_op jit(solution)/shard_map/pallas_call | solution.py:362
  79.3 5.0 %shard_map.75 = (f32[1024,4096]{1,0:T(8,128)S(1)}, f32[1024,4096]{1,0:T(8,128)S(1)}) custom-call(f32[1024,4096]{1,0:T(8,128)S(1)} %get-tuple-element.52.soft_ref, f32[1,1024]{1,0:T(1,128)S(1)} %get-tuple-element.56.inverse_ref, f32[1,1024]{1,0:T(1,128)S(1)} %get-tuple-element.59.scaled_ref, ...), custom_call_target="tpu_custom_call", output_to_operand_aliasing={{0}: (0, {})} | custom-call | tf_op jit(solution)/shard_map/pallas_call | solution.py:362
  85.8 1.6 %collective-permute-start.16 = (f32[256,128]{1,0:T(8,128)S(1)}, f32[256,128]{1,0:T(8,128)S(1)}, u32[]{:S(2)}, u32[]{:S(2)}) collective-permute-start(f32[256,128]{1,0:T(8,128)S(1)} %get-tuple-element.74), channel_id=1, source_target_pairs={{0,8},{8,16},{16,24},{24,28},{28,20},{20,12},{12,4},{4,0},{1,9},{9... | collective-permute-start | bytes 393224 | tf_op jit(solution)/shard_map/ppermute | solution.py:410
  87.4 4.3 %shard_map.77 = (f32[512,128]{1,0:T(8,128)S(1)}, f32[512,128]{1,0:T(8,128)S(1)}, f32[256,128]{1,0:T(8,128)S(1)}, f32[256,128]{1,0:T(8,128)S(1)}, f32[256,128]{1,...) custom-call(f32[1024,4096]{1,0:T(8,128)S(1)} %get-tuple-element.64.f, ...), custom_call_target="tpu_custom_call" | custom-call | tf_op jit(solution)/shard_map/pallas_call | solution.py:362
  91.8 2.0 %collective-permute-start.27 = (f32[256,128]{1,0:T(8,128)S(1)}, f32[256,128]{1,0:T(8,128)S(1)}, u32[]{:S(2)}, u32[]{:S(2)}) collective-permute-start(f32[256,128]{1,0:T(8,128)S(1)} %add.316), channel_id=1, source_target_pairs={{8,0},{16,8},{24,16},{28,24},{20,28},{12,20},{4,12},{0,4},{9,1},{1... | collective-permute-start | bytes 393224 | tf_op jit(solution)/shard_map/ppermute | solution.py:413
  94.2 1.7 %collective-permute-start.17 = (f32[256,128]{1,0:T(8,128)S(1)}, f32[256,128]{1,0:T(8,128)S(1)}, u32[]{:S(2)}, u32[]{:S(2)}) collective-permute-start(f32[256,128]{1,0:T(8,128)S(1)} %add.306), channel_id=1, source_target_pairs={{0,8},{8,16},{16,24},{24,28},{28,20},{20,12},{12,4},{4,0},{1,9},{9... | collective-permute-start | bytes 393224 | tf_op jit(solution)/shard_map/ppermute | solution.py:410
  98.1 1.7 %collective-permute-start.28 = (f32[256,128]{1,0:T(8,128)S(1)}, f32[256,128]{1,0:T(8,128)S(1)}, u32[]{:S(2)}, u32[]{:S(2)}) collective-permute-start(f32[256,128]{1,0:T(8,128)S(1)} %add.317), channel_id=1, source_target_pairs={{8,0},{16,8},{24,16},{28,24},{20,28},{12,20},{4,12},{0,4},{9,1},{1... | collective-permute-start | bytes 393224 | tf_op jit(solution)/shard_map/ppermute | solution.py:413
  100.1 1.7 %collective-permute-start.21 = (f32[256,128]{1,0:T(8,128)S(1)}, f32[256,128]{1,0:T(8,128)S(1)}, u32[]{:S(2)}, u32[]{:S(2)}) collective-permute-start(f32[256,128]{1,0:T(8,128)S(1)} %add.310), channel_id=1, source_target_pairs={{8,0},{16,8},{24,16},{28,24},{20,28},{12,20},{4,12},{0,4},{9,1},{1... | collective-permute-start | bytes 393224 | tf_op jit(solution)/shard_map/ppermute | solution.py:413
  103.4 1.7 %collective-permute-start.25 = (f32[256,128]{1,0:T(8,128)S(1)}, f32[256,128]{1,0:T(8,128)S(1)}, u32[]{:S(2)}, u32[]{:S(2)}) collective-permute-start(f32[256,128]{1,0:T(8,128)S(1)} %add.314), channel_id=1, source_target_pairs={{0,8},{8,16},{16,24},{24,28},{28,20},{20,12},{12,4},{4,0},{1,9},{9... | collective-permute-start | bytes 393224 | tf_op jit(solution)/shard_map/ppermute | solution.py:410
  108.4 2.6 %collective-permute-done.25 = f32[256,128]{1,0:T(8,128)S(1)} collective-permute-done((f32[256,128]{1,0:T(8,128)S(1)}, f32[256,128]{1,0:T(8,128)S(1)}, u32[]{:S(2)}, u32[]{:S(2)}) %collective-permute-start.25) | collective-permute-done | bytes 131104 | tf_op jit(solution)/shard_map/ppermute | solution.py:410
  111.5 2.3 %collective-permute-done.22 = f32[256,128]{1,0:T(8,128)S(1)} collective-permute-done((f32[256,128]{1,0:T(8,128)S(1)}, f32[256,128]{1,0:T(8,128)S(1)}, u32[]{:S(2)}, u32[]{:S(2)}) %collective-permute-start.22) | collective-permute-done | bytes 131104 | tf_op jit(solution)/shard_map/ppermute | solution.py:413
  115.0 1.6 %collective-permute-start.41 = (f32[256,128]{1,0:T(8,128)S(1)}, f32[256,128]{1,0:T(8,128)S(1)}, u32[]{:S(2)}, u32[]{:S(2)}) collective-permute-start(f32[256,128]{1,0:T(8,128)S(1)} %add_add_fusion.refs_4_), channel_id=1, source_target_pairs={{0,8},{8,16},{16,24},{24,28},{28,20},{20,12},{12,4},{4,0},{1,9},{9... | collective-permute-start | bytes 393224 | tf_op jit(solution)/shard_map/ppermute | solution.py:410
  117.1 1.6 %collective-permute-start.33 = (f32[256,128]{1,0:T(8,128)S(1)}, f32[256,128]{1,0:T(8,128)S(1)}, u32[]{:S(2)}, u32[]{:S(2)}) collective-permute-start(f32[256,128]{1,0:T(8,128)S(1)} %collective-permute-done.31.refs_6_), channel_id=1, source_target_pairs={{8,0},{16,8},{24,16},{28,24},{20,28},{12,20},{4,12},{0,4},{9,1},{1... | collective-permute-start | bytes 393224 | tf_op jit(solution)/shard_map/ppermute | solution.py:413
  120.0 1.7 %collective-permute-done.41.refs_18_ = f32[256,128]{1,0:T(8,128)S(1)} collective-permute-done((f32[256,128]{1,0:T(8,128)S(1)}, f32[256,128]{1,0:T(8,128)S(1)}, u32[]{:S(2)}, u32[]{:S(2)}) %collective-permute-start.41) | collective-permute-done | bytes 131104 | tf_op jit(solution)/shard_map/ppermute | solution.py:410
  121.8 1.9 %collective-permute-start.32 = (f32[256,128]{1,0:T(8,128)S(1)}, f32[256,128]{1,0:T(8,128)S(1)}, u32[]{:S(2)}, u32[]{:S(2)}) collective-permute-start(f32[256,128]{1,0:T(8,128)S(1)} %collective-permute-done.30.refs_5_), channel_id=1, source_target_pairs={{8,0},{16,8},{24,16},{28,24},{20,28},{12,20},{4,12},{0,4},{9,1},{1... | collective-permute-start | bytes 393224 | tf_op jit(solution)/shard_map/ppermute | solution.py:413
  124.1 2.1 %collective-permute-done.37.refs_15_ = f32[256,128]{1,0:T(8,128)S(1)} collective-permute-done((f32[256,128]{1,0:T(8,128)S(1)}, f32[256,128]{1,0:T(8,128)S(1)}, u32[]{:S(2)}, u32[]{:S(2)}) %collective-permute-start.37) | collective-permute-done | bytes 131104 | tf_op jit(solution)/shard_map/ppermute | solution.py:410
  126.2 2.6 %collective-permute-done.42.refs_16_ = f32[256,128]{1,0:T(8,128)S(1)} collective-permute-done((f32[256,128]{1,0:T(8,128)S(1)}, f32[256,128]{1,0:T(8,128)S(1)}, u32[]{:S(2)}, u32[]{:S(2)}) %collective-permute-start.42) | collective-permute-done | bytes 131104 | tf_op jit(solution)/shard_map/ppermute | solution.py:410
  128.8 2.0 %collective-permute-start.34 = (f32[256,128]{1,0:T(8,128)S(1)}, f32[256,128]{1,0:T(8,128)S(1)}, u32[]{:S(2)}, u32[]{:S(2)}) collective-permute-start(f32[256,128]{1,0:T(8,128)S(1)} %collective-permute-done.32.refs_7_), channel_id=1, source_target_pairs={{8,0},{16,8},{24,16},{28,24},{20,28},{12,20},{4,12},{0,4},{9,1},{1... | collective-permute-start | bytes 393224 | tf_op jit(solution)/shard_map/ppermute | solution.py:413
  132.8 2.3 %collective-permute-done.43.refs_14_ = f32[256,128]{1,0:T(8,128)S(1)} collective-permute-done((f32[256,128]{1,0:T(8,128)S(1)}, f32[256,128]{1,0:T(8,128)S(1)}, u32[]{:S(2)}, u32[]{:S(2)}) %collective-permute-start.43) | collective-permute-done | bytes 131104 | tf_op jit(solution)/shard_map/ppermute | solution.py:410
  136.7 1.6 %shard_map.78 = (f32[1024,128]{1,0:T(8,128)}, f32[4096,128]{1,0:T(8,128)}) custom-call(f32[256,128]{1,0:T(8,128)S(1)} %slice_add_fusion.refs_0_, f32[256,128]{1,0:T(8,128)S(1)} %collective-permute-done.14.refs_1_, f32[512,128]{1,0:T(8,128)S(1)} %collective-permute-done.15.refs_2_, f32[256,128]{1,0:T(8,128)S(1)} %add_add_fusion.1.refs_3_, ...), custom_call_target="tpu_custom_call" | custom-call | tf_op jit(solution)/shard_map/pallas_call | solution.py:510
  (97 shorter events, 27.7 us)
Async XLA Ops:
  77.1 7.2 %collective-permute-start.10 = (f32[1,1024]{1,0:T(1,128)S(1)}, f32[1,1024]{1,0:T(1,128)S(1)}, u32[]{:S(2)}, u32[]{:S(2)}) collective-permute-start(f32[1,1024]{1,0:T(1,128)S(1)} %get-tuple-element.66.refs_0_), channel_id=1, source_target_pairs={{0,2},{1,3},{2,0},{3,1},{4,6},{5,7},{6,4},{7,5},{8,10},{9,11},{10,... | collective-permute-start | bytes 12296 | tf_op jit(solution)/shard_map/ppermute | solution.py:387
  77.8 6.6 %collective-permute-start.11 = (f32[1,1024]{1,0:T(1,128)S(1)}, f32[1,1024]{1,0:T(1,128)S(1)}, u32[]{:S(2)}, u32[]{:S(2)}) collective-permute-start(f32[1,1024]{1,0:T(1,128)S(1)} %get-tuple-element.66.refs_0_), channel_id=1, source_target_pairs={{0,3},{1,2},{2,1},{3,0},{4,7},{5,6},{6,5},{7,4},{8,11},{9,10},{10,... | collective-permute-start | bytes 12296 | tf_op jit(solution)/shard_map/ppermute | solution.py:387
  77.8 6.6 %collective-permute-start.9 = (f32[1,1024]{1,0:T(1,128)S(1)}, f32[1,1024]{1,0:T(1,128)S(1)}, u32[]{:S(2)}, u32[]{:S(2)}) collective-permute-start(f32[1,1024]{1,0:T(1,128)S(1)} %get-tuple-element.66.refs_0_), channel_id=1, source_target_pairs={{0,1},{1,0},{2,3},{3,2},{4,5},{5,4},{6,7},{7,6},{8,9},{9,8},{10,11... | collective-permute-start | bytes 12296 | tf_op jit(solution)/shard_map/ppermute | solution.py:387
  85.3 6.4 %collective-permute-start.26 = (f32[256,128]{1,0:T(8,128)S(1)}, f32[256,128]{1,0:T(8,128)S(1)}, u32[]{:S(2)}, u32[]{:S(2)}) collective-permute-start(f32[256,128]{1,0:T(8,128)S(1)} %get-tuple-element.85), channel_id=1, source_target_pairs={{8,0},{16,8},{24,16},{28,24},{20,28},{12,20},{4,12},{0,4},{9,1},{1... | collective-permute-start | bytes 393224 | tf_op jit(solution)/shard_map/ppermute | solution.py:413
  85.8 8.5 %collective-permute-start.16 = (f32[256,128]{1,0:T(8,128)S(1)}, f32[256,128]{1,0:T(8,128)S(1)}, u32[]{:S(2)}, u32[]{:S(2)}) collective-permute-start(f32[256,128]{1,0:T(8,128)S(1)} %get-tuple-element.74), channel_id=1, source_target_pairs={{0,8},{8,16},{16,24},{24,28},{28,20},{20,12},{12,4},{4,0},{1,9},{9... | collective-permute-start | bytes 393224 | tf_op jit(solution)/shard_map/ppermute | solution.py:410
  91.8 6.3 %collective-permute-start.27 = (f32[256,128]{1,0:T(8,128)S(1)}, f32[256,128]{1,0:T(8,128)S(1)}, u32[]{:S(2)}, u32[]{:S(2)}) collective-permute-start(f32[256,128]{1,0:T(8,128)S(1)} %add.316), channel_id=1, source_target_pairs={{8,0},{16,8},{24,16},{28,24},{20,28},{12,20},{4,12},{0,4},{9,1},{1... | collective-permute-start | bytes 393224 | tf_op jit(solution)/shard_map/ppermute | solution.py:413
  93.8 6.2 %collective-permute-start.20 = (f32[256,128]{1,0:T(8,128)S(1)}, f32[256,128]{1,0:T(8,128)S(1)}, u32[]{:S(2)}, u32[]{:S(2)}) collective-permute-start(f32[256,128]{1,0:T(8,128)S(1)} %get-tuple-element.77), channel_id=1, source_target_pairs={{8,0},{16,8},{24,16},{28,24},{20,28},{12,20},{4,12},{0,4},{9,1},{1... | collective-permute-start | bytes 393224 | tf_op jit(solution)/shard_map/ppermute | solution.py:413
  94.2 12.7 %collective-permute-start.12 = (f32[512,128]{1,0:T(8,128)S(1)}, f32[512,128]{1,0:T(8,128)S(1)}, u32[]{:S(2)}, u32[]{:S(2)}) collective-permute-start(f32[512,128]{1,0:T(8,128)S(1)} %get-tuple-element.69), channel_id=1, source_target_pairs={{0,1},{1,0},{2,3},{3,2},{4,5},{5,4},{6,7},{7,6},{8,9},{9,8},{10,11... | collective-permute-start | bytes 786440 | tf_op jit(solution)/shard_map/ppermute | solution.py:387
  94.2 7.5 %collective-permute-start.17 = (f32[256,128]{1,0:T(8,128)S(1)}, f32[256,128]{1,0:T(8,128)S(1)}, u32[]{:S(2)}, u32[]{:S(2)}) collective-permute-start(f32[256,128]{1,0:T(8,128)S(1)} %add.306), channel_id=1, source_target_pairs={{0,8},{8,16},{16,24},{24,28},{28,20},{20,12},{12,4},{4,0},{1,9},{9... | collective-permute-start | bytes 393224 | tf_op jit(solution)/shard_map/ppermute | solution.py:410
  96.7 6.7 %collective-permute-start.24 = (f32[256,128]{1,0:T(8,128)S(1)}, f32[256,128]{1,0:T(8,128)S(1)}, u32[]{:S(2)}, u32[]{:S(2)}) collective-permute-start(f32[256,128]{1,0:T(8,128)S(1)} %add.313), channel_id=1, source_target_pairs={{0,8},{8,16},{16,24},{24,28},{28,20},{20,12},{12,4},{4,0},{1,9},{9... | collective-permute-start | bytes 393224 | tf_op jit(solution)/shard_map/ppermute | solution.py:410
  98.1 7.0 %collective-permute-start.28 = (f32[256,128]{1,0:T(8,128)S(1)}, f32[256,128]{1,0:T(8,128)S(1)}, u32[]{:S(2)}, u32[]{:S(2)}) collective-permute-start(f32[256,128]{1,0:T(8,128)S(1)} %add.317), channel_id=1, source_target_pairs={{8,0},{16,8},{24,16},{28,24},{20,28},{12,20},{4,12},{0,4},{9,1},{1... | collective-permute-start | bytes 393224 | tf_op jit(solution)/shard_map/ppermute | solution.py:413
  100.1 5.5 %collective-permute-start.21 = (f32[256,128]{1,0:T(8,128)S(1)}, f32[256,128]{1,0:T(8,128)S(1)}, u32[]{:S(2)}, u32[]{:S(2)}) collective-permute-start(f32[256,128]{1,0:T(8,128)S(1)} %add.310), channel_id=1, source_target_pairs={{8,0},{16,8},{24,16},{28,24},{20,28},{12,20},{4,12},{0,4},{9,1},{1... | collective-permute-start | bytes 393224 | tf_op jit(solution)/shard_map/ppermute | solution.py:413
  101.8 6.4 %collective-permute-start.18 = (f32[256,128]{1,0:T(8,128)S(1)}, f32[256,128]{1,0:T(8,128)S(1)}, u32[]{:S(2)}, u32[]{:S(2)}) collective-permute-start(f32[256,128]{1,0:T(8,128)S(1)} %add.307), channel_id=1, source_target_pairs={{0,8},{8,16},{16,24},{24,28},{28,20},{20,12},{12,4},{4,0},{1,9},{9... | collective-permute-start | bytes 393224 | tf_op jit(solution)/shard_map/ppermute | solution.py:410
  103.4 7.6 %collective-permute-start.25 = (f32[256,128]{1,0:T(8,128)S(1)}, f32[256,128]{1,0:T(8,128)S(1)}, u32[]{:S(2)}, u32[]{:S(2)}) collective-permute-start(f32[256,128]{1,0:T(8,128)S(1)} %add.314), channel_id=1, source_target_pairs={{0,8},{8,16},{16,24},{24,28},{28,20},{20,12},{12,4},{4,0},{1,9},{9... | collective-permute-start | bytes 393224 | tf_op jit(solution)/shard_map/ppermute | solution.py:410
  105.1 5.9 %collective-permute-start.29 = (f32[256,128]{1,0:T(8,128)S(1)}, f32[256,128]{1,0:T(8,128)S(1)}, u32[]{:S(2)}, u32[]{:S(2)}) collective-permute-start(f32[256,128]{1,0:T(8,128)S(1)} %add.318), channel_id=1, source_target_pairs={{8,0},{16,8},{24,16},{28,24},{20,28},{12,20},{4,12},{0,4},{9,1},{1... | collective-permute-start | bytes 393224 | tf_op jit(solution)/shard_map/ppermute | solution.py:413
  105.6 8.2 %collective-permute-start.22 = (f32[256,128]{1,0:T(8,128)S(1)}, f32[256,128]{1,0:T(8,128)S(1)}, u32[]{:S(2)}, u32[]{:S(2)}) collective-permute-start(f32[256,128]{1,0:T(8,128)S(1)} %add.311), channel_id=1, source_target_pairs={{8,0},{16,8},{24,16},{28,24},{20,28},{12,20},{4,12},{0,4},{9,1},{1... | collective-permute-start | bytes 393224 | tf_op jit(solution)/shard_map/ppermute | solution.py:413
  106.9 7.1 %collective-permute-start.13 = (f32[256,128]{1,0:T(8,128)S(1)}, f32[256,128]{1,0:T(8,128)S(1)}, u32[]{:S(2)}, u32[]{:S(2)}) collective-permute-start(f32[256,128]{1,0:T(8,128)S(1)} %slice.9), channel_id=1, source_target_pairs={{0,2},{1,3},{2,0},{3,1},{4,6},{5,7},{6,4},{7,5},{8,10},{9,11},{10,... | collective-permute-start | bytes 393224 | tf_op jit(solution)/shard_map/ppermute | solution.py:387
  108.2 5.6 %collective-permute-start.19 = (f32[256,128]{1,0:T(8,128)S(1)}, f32[256,128]{1,0:T(8,128)S(1)}, u32[]{:S(2)}, u32[]{:S(2)}) collective-permute-start(f32[256,128]{1,0:T(8,128)S(1)} %add.308), channel_id=1, source_target_pairs={{0,8},{8,16},{16,24},{24,28},{28,20},{20,12},{12,4},{4,0},{1,9},{9... | collective-permute-start | bytes 393224 | tf_op jit(solution)/shard_map/ppermute | solution.py:410
  111.1 6.0 %collective-permute-start.31 = (f32[256,128]{1,0:T(8,128)S(1)}, f32[256,128]{1,0:T(8,128)S(1)}, u32[]{:S(2)}, u32[]{:S(2)}) collective-permute-start(f32[256,128]{1,0:T(8,128)S(1)} %add_add_fusion.refs_4_), channel_id=1, source_target_pairs={{8,0},{16,8},{24,16},{28,24},{20,28},{12,20},{4,12},{0,4},{9,1},{1... | collective-permute-start | bytes 393224 | tf_op jit(solution)/shard_map/ppermute | solution.py:413
  113.8 6.0 %collective-permute-start.36 = (f32[256,128]{1,0:T(8,128)S(1)}, f32[256,128]{1,0:T(8,128)S(1)}, u32[]{:S(2)}, u32[]{:S(2)}) collective-permute-start(f32[256,128]{1,0:T(8,128)S(1)} %add_add_fusion.1.refs_3_), channel_id=1, source_target_pairs={{0,8},{8,16},{16,24},{24,28},{28,20},{20,12},{12,4},{4,0},{1,9},{9... | collective-permute-start | bytes 393224 | tf_op jit(solution)/shard_map/ppermute | solution.py:410
  114.1 5.8 %collective-permute-start.14 = (f32[256,128]{1,0:T(8,128)S(1)}, f32[256,128]{1,0:T(8,128)S(1)}, u32[]{:S(2)}, u32[]{:S(2)}) collective-permute-start(f32[256,128]{1,0:T(8,128)S(1)} %slice_add_fusion.refs_0_), channel_id=1, source_target_pairs={{0,2},{1,3},{2,0},{3,1},{4,6},{5,7},{6,4},{7,5},{8,10},{9,11},{10,... | collective-permute-start | bytes 393224 | tf_op jit(solution)/shard_map/ppermute | solution.py:387
  115.0 6.6 %collective-permute-start.41 = (f32[256,128]{1,0:T(8,128)S(1)}, f32[256,128]{1,0:T(8,128)S(1)}, u32[]{:S(2)}, u32[]{:S(2)}) collective-permute-start(f32[256,128]{1,0:T(8,128)S(1)} %add_add_fusion.refs_4_), channel_id=1, source_target_pairs={{0,8},{8,16},{16,24},{24,28},{28,20},{20,12},{12,4},{4,0},{1,9},{9... | collective-permute-start | bytes 393224 | tf_op jit(solution)/shard_map/ppermute | solution.py:410
  116.7 5.2 %collective-permute-start.30 = (f32[256,128]{1,0:T(8,128)S(1)}, f32[256,128]{1,0:T(8,128)S(1)}, u32[]{:S(2)}, u32[]{:S(2)}) collective-permute-start(f32[256,128]{1,0:T(8,128)S(1)} %add_add_fusion.1.refs_3_), channel_id=1, source_target_pairs={{8,0},{16,8},{24,16},{28,24},{20,28},{12,20},{4,12},{0,4},{9,1},{1... | collective-permute-start | bytes 393224 | tf_op jit(solution)/shard_map/ppermute | solution.py:413
  117.1 6.6 %collective-permute-start.33 = (f32[256,128]{1,0:T(8,128)S(1)}, f32[256,128]{1,0:T(8,128)S(1)}, u32[]{:S(2)}, u32[]{:S(2)}) collective-permute-start(f32[256,128]{1,0:T(8,128)S(1)} %collective-permute-done.31.refs_6_), channel_id=1, source_target_pairs={{8,0},{16,8},{24,16},{28,24},{20,28},{12,20},{4,12},{0,4},{9,1},{1... | collective-permute-start | bytes 393224 | tf_op jit(solution)/shard_map/ppermute | solution.py:413
  119.9 6.3 %collective-permute-start.37 = (f32[256,128]{1,0:T(8,128)S(1)}, f32[256,128]{1,0:T(8,128)S(1)}, u32[]{:S(2)}, u32[]{:S(2)}) collective-permute-start(f32[256,128]{1,0:T(8,128)S(1)} %collective-permute-done.36.refs_17_), channel_id=1, source_target_pairs={{0,8},{8,16},{16,24},{24,28},{28,20},{20,12},{12,4},{4,0},{1,9},{9... | collective-permute-start | bytes 393224 | tf_op jit(solution)/shard_map/ppermute | solution.py:410
  119.9 12.9 %collective-permute-start.15 = (f32[512,128]{1,0:T(8,128)S(1)}, f32[512,128]{1,0:T(8,128)S(1)}, u32[]{:S(2)}, u32[]{:S(2)}) collective-permute-start(f32[512,128]{1,0:T(8,128)S(1)} %pad_maximum_fusion), channel_id=1, source_target_pairs={{0,1},{1,0},{2,3},{3,2},{4,5},{5,4},{6,7},{7,6},{8,9},{9,8},{10,11... | collective-permute-start | bytes 786440 | tf_op jit(solution)/shard_map/ppermute | solution.py:387
  121.7 7.1 %collective-permute-start.42 = (f32[256,128]{1,0:T(8,128)S(1)}, f32[256,128]{1,0:T(8,128)S(1)}, u32[]{:S(2)}, u32[]{:S(2)}) collective-permute-start(f32[256,128]{1,0:T(8,128)S(1)} %collective-permute-done.41.refs_18_), channel_id=1, source_target_pairs={{0,8},{8,16},{16,24},{24,28},{28,20},{20,12},{12,4},{4,0},{1,9},{9... | collective-permute-start | bytes 393224 | tf_op jit(solution)/shard_map/ppermute | solution.py:410
  121.8 7.0 %collective-permute-start.32 = (f32[256,128]{1,0:T(8,128)S(1)}, f32[256,128]{1,0:T(8,128)S(1)}, u32[]{:S(2)}, u32[]{:S(2)}) collective-permute-start(f32[256,128]{1,0:T(8,128)S(1)} %collective-permute-done.30.refs_5_), channel_id=1, source_target_pairs={{8,0},{16,8},{24,16},{28,24},{20,28},{12,20},{4,12},{0,4},{9,1},{1... | collective-permute-start | bytes 393224 | tf_op jit(solution)/shard_map/ppermute | solution.py:413
  123.7 7.1 %collective-permute-start.35 = (f32[256,128]{1,0:T(8,128)S(1)}, f32[256,128]{1,0:T(8,128)S(1)}, u32[]{:S(2)}, u32[]{:S(2)}) collective-permute-start(f32[256,128]{1,0:T(8,128)S(1)} %collective-permute-done.33.refs_8_), channel_id=1, source_target_pairs={{8,0},{16,8},{24,16},{28,24},{20,28},{12,20},{4,12},{0,4},{9,1},{1... | collective-permute-start | bytes 393224 | tf_op jit(solution)/shard_map/ppermute | solution.py:413
  126.2 5.6 %collective-permute-start.38 = (f32[256,128]{1,0:T(8,128)S(1)}, f32[256,128]{1,0:T(8,128)S(1)}, u32[]{:S(2)}, u32[]{:S(2)}) collective-permute-start(f32[256,128]{1,0:T(8,128)S(1)} %collective-permute-done.37.refs_15_), channel_id=1, source_target_pairs={{0,8},{8,16},{16,24},{24,28},{28,20},{20,12},{12,4},{4,0},{1,9},{9... | collective-permute-start | bytes 393224 | tf_op jit(solution)/shard_map/ppermute | solution.py:410
  128.8 6.3 %collective-permute-start.43 = (f32[256,128]{1,0:T(8,128)S(1)}, f32[256,128]{1,0:T(8,128)S(1)}, u32[]{:S(2)}, u32[]{:S(2)}) collective-permute-start(f32[256,128]{1,0:T(8,128)S(1)} %collective-permute-done.42.refs_16_), channel_id=1, source_target_pairs={{0,8},{8,16},{16,24},{24,28},{28,20},{20,12},{12,4},{4,0},{1,9},{9... | collective-permute-start | bytes 393224 | tf_op jit(solution)/shard_map/ppermute | solution.py:410
  128.8 6.3 %collective-permute-start.34 = (f32[256,128]{1,0:T(8,128)S(1)}, f32[256,128]{1,0:T(8,128)S(1)}, u32[]{:S(2)}, u32[]{:S(2)}) collective-permute-start(f32[256,128]{1,0:T(8,128)S(1)} %collective-permute-done.32.refs_7_), channel_id=1, source_target_pairs={{8,0},{16,8},{24,16},{28,24},{20,28},{12,20},{4,12},{0,4},{9,1},{1... | collective-permute-start | bytes 393224 | tf_op jit(solution)/shard_map/ppermute | solution.py:413
  (14 other events, 81.5 us)

commit v10 on v8

--- a/solution.py
+++ b/solution.py
@@ -36,7 +36,7 @@
 
 
 def row_sums(tile_ref, weights_ref, partial_ref):
-    height = 64
+    height = 128
 
     def body(block, _):
         rows = pl.ds(pl.multiple_of(block * height, height), height)
@@ -73,7 +73,7 @@
 
 def row_level_kernel(crawl_hbm, bench_hbm, duals_hbm, tile_ref, top_ref, level_ref, crawl_ref, bench_ref, shift_ref,
                      top_scratch, sum_scratch, sems):
-    height = 64
+    height = 128
     chunks = 4
     part = bench_ref.shape[0] // chunks
     copies = [pltpu.make_async_copy(crawl_hbm, crawl_ref, sems.at[chunks]),

time: 140 us -> 139 us (level)
  transfers between devices with their start and end apart: 44 -> 44, of which waited for: 20 -> 20; matrix products, arithmetic and copies ran while one was open for 0% -> 0% of each run, Pallas kernels for 6% -> 7%
where the time goes in v10:
time: 139 us
  Pallas kernels  40.5 us (29%)
  starting transfers between devices  35 us (25%)
  blocking collectives  32.9 us (24%)
  waiting for transfers between devices  28.6 us (21%)
    all_to_all x3, blocking collectives, over_rows(): lax.all_to_all(copies, 'rows', 0, 0)  32.9 us
    pallas_call x9, Pallas kernels, call(): pl.pallas_call(kernel, in_specs=[pl.BlockSpec(memory_space=pltpu.VMEM)] *...  31.5 us
    ppermute x14, waiting for transfers between devices, ahead(): return lax.ppermute(x, 'rows', up)  16.7 us
    ppermute x14, starting transfers between devices, behind(): return lax.ppermute(x, 'rows', down)  14.9 us
    ppermute x16, starting transfers between devices, exchange(): lax.ppermute(x, axis, [(i, i ^ k * stride) for i in range(n)])  10.9 us
    ppermute x14, starting transfers between devices, ahead(): return lax.ppermute(x, 'rows', up)  9.15 us
    ppermute x16, waiting for transfers between devices, exchange(): lax.ppermute(x, axis, [(i, i ^ k * stride) for i in range(n)])  7.51 us
    pallas_call x1, Pallas kernels, per_device(): pl.pallas_call(row_level_kernel, in_specs=[pl.BlockSpec(memory_space=pltp...  7.35 us
  transfers between devices with their start and end apart: 44, of which 20 were waited for; matrix products, arithmetic and copies ran while one was open for 0% of the time, Pallas kernels for 7%

profile of v10, /device:TPU:0, one launch (start us, length us, event | category | flops | bytes accessed | tf_op | source)
XLA Modules:
  0.0 138.5 jit_solution(1482105444526001087)
XLA Ops:
  0.6 7.4 %shard_map.68 = (f32[1024,4096]{1,0:T(8,128)S(1)}, f32[1,1024]{1,0:T(1,128)S(1)}, f32[1,1024]{1,0:T(1,128)S(1)}, bf16[1024,128]{1,0:T(8,128)(2,1)S(1)}, bf16[409...) custom-call(bf16[1024,128]{1,0:T(8,128)(2,1)} %crawl_hbm.1, bf16[4096,128]{1,0:T(8,128)(2,1)} %bench_hbm.1, f32[1,4096]{1,0:T(1,128)} %bitcast.31), custom_call_target="tpu_custom_call" | custom-call | tf_op jit(solution)/shard_map/pallas_call | solution.py:454
  8.5 2.6 %collective-permute-start.1 = (f32[1,1024]{1,0:T(1,128)S(1)}, f32[1,1024]{1,0:T(1,128)S(1)}, u32[]{:S(2)}, u32[]{:S(2)}) collective-permute-start(f32[1,1024]{1,0:T(1,128)S(1)} %get-tuple-element.46.refs_0_), channel_id=1, source_target_pairs={{0,2},{1,3},{2,0},{3,1},{4,6},{5,7},{6,4},{7,5},{8,10},{9,11},{10,... | collective-permute-start | bytes 12296 | tf_op jit(solution)/shard_map/ppermute | solution.py:387
  14.1 9.0 %shard_map.69 = (f32[1,1024]{1,0:T(1,128)S(1)}, f32[1,4096]{1,0:T(1,128)S(1)}) custom-call(f32[1024,4096]{1,0:T(8,128)S(1)} %get-tuple-element.44.tile_ref, f32[1,1024]{1,0:T(1,128)S(1)} %get-tuple-element.45.top_ref, f32[1,1024]{1,0:T(1,128)S(1)} %get-tuple-element.46.refs_0_, f32[1,1024]{1,0:T(1,128)S(1)} %collective-permute-done.refs_1_, ...), custom_call_target="tpu_custom_call" | custom-call | tf_op jit(solution)/shard_map/pallas_call | solution.py:362
  23.1 13.0 %all_to_all.15 = f32[8,32,128]{2,1,0:T(8,128)S(1)} all-to-all(f32[8,32,128]{2,1,0:T(8,128)S(1)} %broadcast_in_dim.22), channel_id=1, replica_groups=mesh['rows'=8,'cols'=4] {'rows'}, dimensions={0} | all-to-all | bytes 262144 | tf_op jit(solution)/shard_map/all_to_all | solution.py:452
  36.4 5.4 %shard_map.70 = (f32[1024,4096]{1,0:T(8,128)S(1)}, f32[1,1024]{1,0:T(1,128)S(1)}, f32[1,4096]{1,0:T(1,128)S(1)}, f32[1,4096]{1,0:T(1,128)S(1)}, f32[1,1024]{1,0:T(1,128)S(1)}) custom-call(f32[1024,4096]{1,0:T(8,128)S(1)} %get-tuple-element.44.tile_ref, f32[1,1024]{1,0:T(1,128)S(1)} %get-tuple-element.45.top_ref, ...), custom_call_target="tpu_custom_call", output_to_operand_aliasing={{0}: (0, {})} | custom-call | tf_op jit(solution)/shard_map/pallas_call | solution.py:362
  43.7 1.8 %collective-permute-done.4.refs_2_ = f32[1,1024]{1,0:T(1,128)S(1)} collective-permute-done((f32[1,1024]{1,0:T(1,128)S(1)}, f32[1,1024]{1,0:T(1,128)S(1)}, u32[]{:S(2)}, u32[]{:S(2)}) %collective-permute-start.4) | collective-permute-done | bytes 4128 | tf_op jit(solution)/shard_map/ppermute | solution.py:387
  45.6 2.0 %shard_map.71 = (f32[1,1024]{1,0:T(1,128)S(1)}, f32[1,4096]{1,0:T(1,128)S(1)}) custom-call(f32[1024,4096]{1,0:T(8,128)S(1)} %get-tuple-element.52.soft_ref, f32[1,1024]{1,0:T(1,128)S(1)} %get-tuple-element.53.left_ref, f32[1,4096]{1,0:T(1,128)S(1)} %get-tuple-element.54.right_ref, f32[1,1024]{1,0:T(1,128)S(1)} %get-tuple-element.55.refs_0_, ...), custom_call_target="tpu_custom_call" | custom-call | tf_op jit(solution)/shard_map/pallas_call | solution.py:362
  47.6 10.0 %all_to_all.16 = f32[8,32,128]{2,1,0:T(8,128)S(1)} all-to-all(f32[8,32,128]{2,1,0:T(8,128)S(1)} %broadcast_in_dim.24), channel_id=1, replica_groups=mesh['rows'=8,'cols'=4] {'rows'}, dimensions={0} | all-to-all | bytes 262144 | tf_op jit(solution)/shard_map/all_to_all | solution.py:452
  61.0 1.8 %collective-permute-done.7.refs_2_ = f32[1,1024]{1,0:T(1,128)S(1)} collective-permute-done((f32[1,1024]{1,0:T(1,128)S(1)}, f32[1,1024]{1,0:T(1,128)S(1)}, u32[]{:S(2)}, u32[]{:S(2)}) %collective-permute-start.7) | collective-permute-done | bytes 4128 | tf_op jit(solution)/shard_map/ppermute | solution.py:387
  63.7 2.0 %shard_map.73 = (f32[1,1024]{1,0:T(1,128)S(1)}, f32[1,4096]{1,0:T(1,128)S(1)}) custom-call(f32[1024,4096]{1,0:T(8,128)S(1)} %get-tuple-element.52.soft_ref, f32[1,1024]{1,0:T(1,128)S(1)} %get-tuple-element.56.inverse_ref, f32[1,4096]{1,0:T(1,128)S(1)} %get-tuple-element.54.right_ref, f32[1,1024]{1,0:T(1,128)S(1)} %bitcast.22, ...), custom_call_target="tpu_custom_call" | custom-call | tf_op jit(solution)/shard_map/pallas_call | solution.py:362
  65.7 10.0 %all_to_all.17 = f32[8,32,128]{2,1,0:T(8,128)S(1)} all-to-all(f32[8,32,128]{2,1,0:T(8,128)S(1)} %broadcast_in_dim.26), channel_id=1, replica_groups=mesh['rows'=8,'cols'=4] {'rows'}, dimensions={0} | all-to-all | bytes 262144 | tf_op jit(solution)/shard_map/all_to_all | solution.py:452
  75.7 1.6 %shard_map.74 = (f32[1,4096]{1,0:T(1,128)S(1)}, f32[1,1024]{1,0:T(1,128)S(1)}) custom-call(f32[1024,4096]{1,0:T(8,128)S(1)} %get-tuple-element.52.soft_ref, f32[1,1024]{1,0:T(1,128)S(1)} %get-tuple-element.53.left_ref, f32[1,4096]{1,0:T(1,128)S(1)} %get-tuple-element.54.right_ref, f32[1,4096]{1,0:T(1,128)S(1)} %bitcast.16), custom_call_target="tpu_custom_call" | custom-call | tf_op jit(solution)/shard_map/pallas_call | solution.py:362
  78.0 1.6 %collective-permute-start.9 = (f32[1,1024]{1,0:T(1,128)S(1)}, f32[1,1024]{1,0:T(1,128)S(1)}, u32[]{:S(2)}, u32[]{:S(2)}) collective-permute-start(f32[1,1024]{1,0:T(1,128)S(1)} %get-tuple-element.66.refs_0_), channel_id=1, source_target_pairs={{0,1},{1,0},{2,3},{3,2},{4,5},{5,4},{6,7},{7,6},{8,9},{9,8},{10,11... | collective-permute-start | bytes 12296 | tf_op jit(solution)/shard_map/ppermute | solution.py:387
  79.6 4.8 %shard_map.75 = (f32[1024,4096]{1,0:T(8,128)S(1)}, f32[1024,4096]{1,0:T(8,128)S(1)}) custom-call(f32[1024,4096]{1,0:T(8,128)S(1)} %get-tuple-element.52.soft_ref, f32[1,1024]{1,0:T(1,128)S(1)} %get-tuple-element.56.inverse_ref, f32[1,1024]{1,0:T(1,128)S(1)} %get-tuple-element.59.scaled_ref, ...), custom_call_target="tpu_custom_call", output_to_operand_aliasing={{0}: (0, {})} | custom-call | tf_op jit(solution)/shard_map/pallas_call | solution.py:362
  85.8 1.6 %collective-permute-start.16 = (f32[256,128]{1,0:T(8,128)S(1)}, f32[256,128]{1,0:T(8,128)S(1)}, u32[]{:S(2)}, u32[]{:S(2)}) collective-permute-start(f32[256,128]{1,0:T(8,128)S(1)} %get-tuple-element.74), channel_id=1, source_target_pairs={{0,8},{8,16},{16,24},{24,28},{28,20},{20,12},{12,4},{4,0},{1,9},{9... | collective-permute-start | bytes 393224 | tf_op jit(solution)/shard_map/ppermute | solution.py:410
  87.4 4.2 %shard_map.77 = (f32[512,128]{1,0:T(8,128)S(1)}, f32[512,128]{1,0:T(8,128)S(1)}, f32[256,128]{1,0:T(8,128)S(1)}, f32[256,128]{1,0:T(8,128)S(1)}, f32[256,128]{1,...) custom-call(f32[1024,4096]{1,0:T(8,128)S(1)} %get-tuple-element.64.f, ...), custom_call_target="tpu_custom_call" | custom-call | tf_op jit(solution)/shard_map/pallas_call | solution.py:362
  91.7 2.0 %collective-permute-start.27 = (f32[256,128]{1,0:T(8,128)S(1)}, f32[256,128]{1,0:T(8,128)S(1)}, u32[]{:S(2)}, u32[]{:S(2)}) collective-permute-start(f32[256,128]{1,0:T(8,128)S(1)} %add.316), channel_id=1, source_target_pairs={{8,0},{16,8},{24,16},{28,24},{20,28},{12,20},{4,12},{0,4},{9,1},{1... | collective-permute-start | bytes 393224 | tf_op jit(solution)/shard_map/ppermute | solution.py:413
  94.2 1.7 %collective-permute-start.17 = (f32[256,128]{1,0:T(8,128)S(1)}, f32[256,128]{1,0:T(8,128)S(1)}, u32[]{:S(2)}, u32[]{:S(2)}) collective-permute-start(f32[256,128]{1,0:T(8,128)S(1)} %add.306), channel_id=1, source_target_pairs={{0,8},{8,16},{16,24},{24,28},{28,20},{20,12},{12,4},{4,0},{1,9},{9... | collective-permute-start | bytes 393224 | tf_op jit(solution)/shard_map/ppermute | solution.py:410
  98.1 1.7 %collective-permute-start.28 = (f32[256,128]{1,0:T(8,128)S(1)}, f32[256,128]{1,0:T(8,128)S(1)}, u32[]{:S(2)}, u32[]{:S(2)}) collective-permute-start(f32[256,128]{1,0:T(8,128)S(1)} %add.317), channel_id=1, source_target_pairs={{8,0},{16,8},{24,16},{28,24},{20,28},{12,20},{4,12},{0,4},{9,1},{1... | collective-permute-start | bytes 393224 | tf_op jit(solution)/shard_map/ppermute | solution.py:413
  100.0 1.7 %collective-permute-start.21 = (f32[256,128]{1,0:T(8,128)S(1)}, f32[256,128]{1,0:T(8,128)S(1)}, u32[]{:S(2)}, u32[]{:S(2)}) collective-permute-start(f32[256,128]{1,0:T(8,128)S(1)} %add.310), channel_id=1, source_target_pairs={{8,0},{16,8},{24,16},{28,24},{20,28},{12,20},{4,12},{0,4},{9,1},{1... | collective-permute-start | bytes 393224 | tf_op jit(solution)/shard_map/ppermute | solution.py:413
  103.4 1.7 %collective-permute-start.25 = (f32[256,128]{1,0:T(8,128)S(1)}, f32[256,128]{1,0:T(8,128)S(1)}, u32[]{:S(2)}, u32[]{:S(2)}) collective-permute-start(f32[256,128]{1,0:T(8,128)S(1)} %add.314), channel_id=1, source_target_pairs={{0,8},{8,16},{16,24},{24,28},{28,20},{20,12},{12,4},{4,0},{1,9},{9... | collective-permute-start | bytes 393224 | tf_op jit(solution)/shard_map/ppermute | solution.py:410
  108.4 2.5 %collective-permute-done.25 = f32[256,128]{1,0:T(8,128)S(1)} collective-permute-done((f32[256,128]{1,0:T(8,128)S(1)}, f32[256,128]{1,0:T(8,128)S(1)}, u32[]{:S(2)}, u32[]{:S(2)}) %collective-permute-start.25) | collective-permute-done | bytes 131104 | tf_op jit(solution)/shard_map/ppermute | solution.py:410
  111.5 2.3 %collective-permute-done.22 = f32[256,128]{1,0:T(8,128)S(1)} collective-permute-done((f32[256,128]{1,0:T(8,128)S(1)}, f32[256,128]{1,0:T(8,128)S(1)}, u32[]{:S(2)}, u32[]{:S(2)}) %collective-permute-start.22) | collective-permute-done | bytes 131104 | tf_op jit(solution)/shard_map/ppermute | solution.py:413
  115.0 1.6 %collective-permute-start.41 = (f32[256,128]{1,0:T(8,128)S(1)}, f32[256,128]{1,0:T(8,128)S(1)}, u32[]{:S(2)}, u32[]{:S(2)}) collective-permute-start(f32[256,128]{1,0:T(8,128)S(1)} %add_add_fusion.refs_4_), channel_id=1, source_target_pairs={{0,8},{8,16},{16,24},{24,28},{28,20},{20,12},{12,4},{4,0},{1,9},{9... | collective-permute-start | bytes 393224 | tf_op jit(solution)/shard_map/ppermute | solution.py:410
  117.0 1.6 %collective-permute-start.33 = (f32[256,128]{1,0:T(8,128)S(1)}, f32[256,128]{1,0:T(8,128)S(1)}, u32[]{:S(2)}, u32[]{:S(2)}) collective-permute-start(f32[256,128]{1,0:T(8,128)S(1)} %collective-permute-done.31.refs_6_), channel_id=1, source_target_pairs={{8,0},{16,8},{24,16},{28,24},{20,28},{12,20},{4,12},{0,4},{9,1},{1... | collective-permute-start | bytes 393224 | tf_op jit(solution)/shard_map/ppermute | solution.py:413
  120.0 1.7 %collective-permute-done.41.refs_18_ = f32[256,128]{1,0:T(8,128)S(1)} collective-permute-done((f32[256,128]{1,0:T(8,128)S(1)}, f32[256,128]{1,0:T(8,128)S(1)}, u32[]{:S(2)}, u32[]{:S(2)}) %collective-permute-start.41) | collective-permute-done | bytes 131104 | tf_op jit(solution)/shard_map/ppermute | solution.py:410
  121.8 1.9 %collective-permute-start.32 = (f32[256,128]{1,0:T(8,128)S(1)}, f32[256,128]{1,0:T(8,128)S(1)}, u32[]{:S(2)}, u32[]{:S(2)}) collective-permute-start(f32[256,128]{1,0:T(8,128)S(1)} %collective-permute-done.30.refs_5_), channel_id=1, source_target_pairs={{8,0},{16,8},{24,16},{28,24},{20,28},{12,20},{4,12},{0,4},{9,1},{1... | collective-permute-start | bytes 393224 | tf_op jit(solution)/shard_map/ppermute | solution.py:413
  124.1 2.1 %collective-permute-done.37.refs_15_ = f32[256,128]{1,0:T(8,128)S(1)} collective-permute-done((f32[256,128]{1,0:T(8,128)S(1)}, f32[256,128]{1,0:T(8,128)S(1)}, u32[]{:S(2)}, u32[]{:S(2)}) %collective-permute-start.37) | collective-permute-done | bytes 131104 | tf_op jit(solution)/shard_map/ppermute | solution.py:410
  126.1 2.6 %collective-permute-done.42.refs_16_ = f32[256,128]{1,0:T(8,128)S(1)} collective-permute-done((f32[256,128]{1,0:T(8,128)S(1)}, f32[256,128]{1,0:T(8,128)S(1)}, u32[]{:S(2)}, u32[]{:S(2)}) %collective-permute-start.42) | collective-permute-done | bytes 131104 | tf_op jit(solution)/shard_map/ppermute | solution.py:410
  128.8 2.0 %collective-permute-start.34 = (f32[256,128]{1,0:T(8,128)S(1)}, f32[256,128]{1,0:T(8,128)S(1)}, u32[]{:S(2)}, u32[]{:S(2)}) collective-permute-start(f32[256,128]{1,0:T(8,128)S(1)} %collective-permute-done.32.refs_7_), channel_id=1, source_target_pairs={{8,0},{16,8},{24,16},{28,24},{20,28},{12,20},{4,12},{0,4},{9,1},{1... | collective-permute-start | bytes 393224 | tf_op jit(solution)/shard_map/ppermute | solution.py:413
  132.8 2.3 %collective-permute-done.43.refs_14_ = f32[256,128]{1,0:T(8,128)S(1)} collective-permute-done((f32[256,128]{1,0:T(8,128)S(1)}, f32[256,128]{1,0:T(8,128)S(1)}, u32[]{:S(2)}, u32[]{:S(2)}) %collective-permute-start.43) | collective-permute-done | bytes 131104 | tf_op jit(solution)/shard_map/ppermute | solution.py:410
  136.7 1.6 %shard_map.78 = (f32[1024,128]{1,0:T(8,128)}, f32[4096,128]{1,0:T(8,128)}) custom-call(f32[256,128]{1,0:T(8,128)S(1)} %slice_add_fusion.refs_0_, f32[256,128]{1,0:T(8,128)S(1)} %collective-permute-done.14.refs_1_, f32[512,128]{1,0:T(8,128)S(1)} %collective-permute-done.15.refs_2_, f32[256,128]{1,0:T(8,128)S(1)} %add_add_fusion.1.refs_3_, ...), custom_call_target="tpu_custom_call" | custom-call | tf_op jit(solution)/shard_map/pallas_call | solution.py:510
  (97 shorter events, 27.8 us)
Async XLA Ops:
  77.3 7.1 %collective-permute-start.10 = (f32[1,1024]{1,0:T(1,128)S(1)}, f32[1,1024]{1,0:T(1,128)S(1)}, u32[]{:S(2)}, u32[]{:S(2)}) collective-permute-start(f32[1,1024]{1,0:T(1,128)S(1)} %get-tuple-element.66.refs_0_), channel_id=1, source_target_pairs={{0,2},{1,3},{2,0},{3,1},{4,6},{5,7},{6,4},{7,5},{8,10},{9,11},{10,... | collective-permute-start | bytes 12296 | tf_op jit(solution)/shard_map/ppermute | solution.py:387
  78.0 6.4 %collective-permute-start.11 = (f32[1,1024]{1,0:T(1,128)S(1)}, f32[1,1024]{1,0:T(1,128)S(1)}, u32[]{:S(2)}, u32[]{:S(2)}) collective-permute-start(f32[1,1024]{1,0:T(1,128)S(1)} %get-tuple-element.66.refs_0_), channel_id=1, source_target_pairs={{0,3},{1,2},{2,1},{3,0},{4,7},{5,6},{6,5},{7,4},{8,11},{9,10},{10,... | collective-permute-start | bytes 12296 | tf_op jit(solution)/shard_map/ppermute | solution.py:387
  78.0 6.4 %collective-permute-start.9 = (f32[1,1024]{1,0:T(1,128)S(1)}, f32[1,1024]{1,0:T(1,128)S(1)}, u32[]{:S(2)}, u32[]{:S(2)}) collective-permute-start(f32[1,1024]{1,0:T(1,128)S(1)} %get-tuple-element.66.refs_0_), channel_id=1, source_target_pairs={{0,1},{1,0},{2,3},{3,2},{4,5},{5,4},{6,7},{7,6},{8,9},{9,8},{10,11... | collective-permute-start | bytes 12296 | tf_op jit(solution)/shard_map/ppermute | solution.py:387
  85.4 6.4 %collective-permute-start.26 = (f32[256,128]{1,0:T(8,128)S(1)}, f32[256,128]{1,0:T(8,128)S(1)}, u32[]{:S(2)}, u32[]{:S(2)}) collective-permute-start(f32[256,128]{1,0:T(8,128)S(1)} %get-tuple-element.85), channel_id=1, source_target_pairs={{8,0},{16,8},{24,16},{28,24},{20,28},{12,20},{4,12},{0,4},{9,1},{1... | collective-permute-start | bytes 393224 | tf_op jit(solution)/shard_map/ppermute | solution.py:413
  85.8 8.4 %collective-permute-start.16 = (f32[256,128]{1,0:T(8,128)S(1)}, f32[256,128]{1,0:T(8,128)S(1)}, u32[]{:S(2)}, u32[]{:S(2)}) collective-permute-start(f32[256,128]{1,0:T(8,128)S(1)} %get-tuple-element.74), channel_id=1, source_target_pairs={{0,8},{8,16},{16,24},{24,28},{28,20},{20,12},{12,4},{4,0},{1,9},{9... | collective-permute-start | bytes 393224 | tf_op jit(solution)/shard_map/ppermute | solution.py:410
  91.7 6.3 %collective-permute-start.27 = (f32[256,128]{1,0:T(8,128)S(1)}, f32[256,128]{1,0:T(8,128)S(1)}, u32[]{:S(2)}, u32[]{:S(2)}) collective-permute-start(f32[256,128]{1,0:T(8,128)S(1)} %add.316), channel_id=1, source_target_pairs={{8,0},{16,8},{24,16},{28,24},{20,28},{12,20},{4,12},{0,4},{9,1},{1... | collective-permute-start | bytes 393224 | tf_op jit(solution)/shard_map/ppermute | solution.py:413
  93.8 6.2 %collective-permute-start.20 = (f32[256,128]{1,0:T(8,128)S(1)}, f32[256,128]{1,0:T(8,128)S(1)}, u32[]{:S(2)}, u32[]{:S(2)}) collective-permute-start(f32[256,128]{1,0:T(8,128)S(1)} %get-tuple-element.77), channel_id=1, source_target_pairs={{8,0},{16,8},{24,16},{28,24},{20,28},{12,20},{4,12},{0,4},{9,1},{1... | collective-permute-start | bytes 393224 | tf_op jit(solution)/shard_map/ppermute | solution.py:413
  94.2 12.7 %collective-permute-start.12 = (f32[512,128]{1,0:T(8,128)S(1)}, f32[512,128]{1,0:T(8,128)S(1)}, u32[]{:S(2)}, u32[]{:S(2)}) collective-permute-start(f32[512,128]{1,0:T(8,128)S(1)} %get-tuple-element.69), channel_id=1, source_target_pairs={{0,1},{1,0},{2,3},{3,2},{4,5},{5,4},{6,7},{7,6},{8,9},{9,8},{10,11... | collective-permute-start | bytes 786440 | tf_op jit(solution)/shard_map/ppermute | solution.py:387
  94.2 7.5 %collective-permute-start.17 = (f32[256,128]{1,0:T(8,128)S(1)}, f32[256,128]{1,0:T(8,128)S(1)}, u32[]{:S(2)}, u32[]{:S(2)}) collective-permute-start(f32[256,128]{1,0:T(8,128)S(1)} %add.306), channel_id=1, source_target_pairs={{0,8},{8,16},{16,24},{24,28},{28,20},{20,12},{12,4},{4,0},{1,9},{9... | collective-permute-start | bytes 393224 | tf_op jit(solution)/shard_map/ppermute | solution.py:410
  96.7 6.7 %collective-permute-start.24 = (f32[256,128]{1,0:T(8,128)S(1)}, f32[256,128]{1,0:T(8,128)S(1)}, u32[]{:S(2)}, u32[]{:S(2)}) collective-permute-start(f32[256,128]{1,0:T(8,128)S(1)} %add.313), channel_id=1, source_target_pairs={{0,8},{8,16},{16,24},{24,28},{28,20},{20,12},{12,4},{4,0},{1,9},{9... | collective-permute-start | bytes 393224 | tf_op jit(solution)/shard_map/ppermute | solution.py:410
  98.1 7.0 %collective-permute-start.28 = (f32[256,128]{1,0:T(8,128)S(1)}, f32[256,128]{1,0:T(8,128)S(1)}, u32[]{:S(2)}, u32[]{:S(2)}) collective-permute-start(f32[256,128]{1,0:T(8,128)S(1)} %add.317), channel_id=1, source_target_pairs={{8,0},{16,8},{24,16},{28,24},{20,28},{12,20},{4,12},{0,4},{9,1},{1... | collective-permute-start | bytes 393224 | tf_op jit(solution)/shard_map/ppermute | solution.py:413
  100.0 5.5 %collective-permute-start.21 = (f32[256,128]{1,0:T(8,128)S(1)}, f32[256,128]{1,0:T(8,128)S(1)}, u32[]{:S(2)}, u32[]{:S(2)}) collective-permute-start(f32[256,128]{1,0:T(8,128)S(1)} %add.310), channel_id=1, source_target_pairs={{8,0},{16,8},{24,16},{28,24},{20,28},{12,20},{4,12},{0,4},{9,1},{1... | collective-permute-start | bytes 393224 | tf_op jit(solution)/shard_map/ppermute | solution.py:413
  101.7 6.4 %collective-permute-start.18 = (f32[256,128]{1,0:T(8,128)S(1)}, f32[256,128]{1,0:T(8,128)S(1)}, u32[]{:S(2)}, u32[]{:S(2)}) collective-permute-start(f32[256,128]{1,0:T(8,128)S(1)} %add.307), channel_id=1, source_target_pairs={{0,8},{8,16},{16,24},{24,28},{28,20},{20,12},{12,4},{4,0},{1,9},{9... | collective-permute-start | bytes 393224 | tf_op jit(solution)/shard_map/ppermute | solution.py:410
  103.4 7.6 %collective-permute-start.25 = (f32[256,128]{1,0:T(8,128)S(1)}, f32[256,128]{1,0:T(8,128)S(1)}, u32[]{:S(2)}, u32[]{:S(2)}) collective-permute-start(f32[256,128]{1,0:T(8,128)S(1)} %add.314), channel_id=1, source_target_pairs={{0,8},{8,16},{16,24},{24,28},{28,20},{20,12},{12,4},{4,0},{1,9},{9... | collective-permute-start | bytes 393224 | tf_op jit(solution)/shard_map/ppermute | solution.py:410
  105.1 5.9 %collective-permute-start.29 = (f32[256,128]{1,0:T(8,128)S(1)}, f32[256,128]{1,0:T(8,128)S(1)}, u32[]{:S(2)}, u32[]{:S(2)}) collective-permute-start(f32[256,128]{1,0:T(8,128)S(1)} %add.318), channel_id=1, source_target_pairs={{8,0},{16,8},{24,16},{28,24},{20,28},{12,20},{4,12},{0,4},{9,1},{1... | collective-permute-start | bytes 393224 | tf_op jit(solution)/shard_map/ppermute | solution.py:413
  105.6 8.2 %collective-permute-start.22 = (f32[256,128]{1,0:T(8,128)S(1)}, f32[256,128]{1,0:T(8,128)S(1)}, u32[]{:S(2)}, u32[]{:S(2)}) collective-permute-start(f32[256,128]{1,0:T(8,128)S(1)} %add.311), channel_id=1, source_target_pairs={{8,0},{16,8},{24,16},{28,24},{20,28},{12,20},{4,12},{0,4},{9,1},{1... | collective-permute-start | bytes 393224 | tf_op jit(solution)/shard_map/ppermute | solution.py:413
  106.9 7.1 %collective-permute-start.13 = (f32[256,128]{1,0:T(8,128)S(1)}, f32[256,128]{1,0:T(8,128)S(1)}, u32[]{:S(2)}, u32[]{:S(2)}) collective-permute-start(f32[256,128]{1,0:T(8,128)S(1)} %slice.9), channel_id=1, source_target_pairs={{0,2},{1,3},{2,0},{3,1},{4,6},{5,7},{6,4},{7,5},{8,10},{9,11},{10,... | collective-permute-start | bytes 393224 | tf_op jit(solution)/shard_map/ppermute | solution.py:387
  108.2 5.6 %collective-permute-start.19 = (f32[256,128]{1,0:T(8,128)S(1)}, f32[256,128]{1,0:T(8,128)S(1)}, u32[]{:S(2)}, u32[]{:S(2)}) collective-permute-start(f32[256,128]{1,0:T(8,128)S(1)} %add.308), channel_id=1, source_target_pairs={{0,8},{8,16},{16,24},{24,28},{28,20},{20,12},{12,4},{4,0},{1,9},{9... | collective-permute-start | bytes 393224 | tf_op jit(solution)/shard_map/ppermute | solution.py:410
  111.0 6.0 %collective-permute-start.31 = (f32[256,128]{1,0:T(8,128)S(1)}, f32[256,128]{1,0:T(8,128)S(1)}, u32[]{:S(2)}, u32[]{:S(2)}) collective-permute-start(f32[256,128]{1,0:T(8,128)S(1)} %add_add_fusion.refs_4_), channel_id=1, source_target_pairs={{8,0},{16,8},{24,16},{28,24},{20,28},{12,20},{4,12},{0,4},{9,1},{1... | collective-permute-start | bytes 393224 | tf_op jit(solution)/shard_map/ppermute | solution.py:413
  113.8 6.0 %collective-permute-start.36 = (f32[256,128]{1,0:T(8,128)S(1)}, f32[256,128]{1,0:T(8,128)S(1)}, u32[]{:S(2)}, u32[]{:S(2)}) collective-permute-start(f32[256,128]{1,0:T(8,128)S(1)} %add_add_fusion.1.refs_3_), channel_id=1, source_target_pairs={{0,8},{8,16},{16,24},{24,28},{28,20},{20,12},{12,4},{4,0},{1,9},{9... | collective-permute-start | bytes 393224 | tf_op jit(solution)/shard_map/ppermute | solution.py:410
  114.0 5.8 %collective-permute-start.14 = (f32[256,128]{1,0:T(8,128)S(1)}, f32[256,128]{1,0:T(8,128)S(1)}, u32[]{:S(2)}, u32[]{:S(2)}) collective-permute-start(f32[256,128]{1,0:T(8,128)S(1)} %slice_add_fusion.refs_0_), channel_id=1, source_target_pairs={{0,2},{1,3},{2,0},{3,1},{4,6},{5,7},{6,4},{7,5},{8,10},{9,11},{10,... | collective-permute-start | bytes 393224 | tf_op jit(solution)/shard_map/ppermute | solution.py:387
  115.0 6.6 %collective-permute-start.41 = (f32[256,128]{1,0:T(8,128)S(1)}, f32[256,128]{1,0:T(8,128)S(1)}, u32[]{:S(2)}, u32[]{:S(2)}) collective-permute-start(f32[256,128]{1,0:T(8,128)S(1)} %add_add_fusion.refs_4_), channel_id=1, source_target_pairs={{0,8},{8,16},{16,24},{24,28},{28,20},{20,12},{12,4},{4,0},{1,9},{9... | collective-permute-start | bytes 393224 | tf_op jit(solution)/shard_map/ppermute | solution.py:410
  116.6 5.2 %collective-permute-start.30 = (f32[256,128]{1,0:T(8,128)S(1)}, f32[256,128]{1,0:T(8,128)S(1)}, u32[]{:S(2)}, u32[]{:S(2)}) collective-permute-start(f32[256,128]{1,0:T(8,128)S(1)} %add_add_fusion.1.refs_3_), channel_id=1, source_target_pairs={{8,0},{16,8},{24,16},{28,24},{20,28},{12,20},{4,12},{0,4},{9,1},{1... | collective-permute-start | bytes 393224 | tf_op jit(solution)/shard_map/ppermute | solution.py:413
  117.0 6.6 %collective-permute-start.33 = (f32[256,128]{1,0:T(8,128)S(1)}, f32[256,128]{1,0:T(8,128)S(1)}, u32[]{:S(2)}, u32[]{:S(2)}) collective-permute-start(f32[256,128]{1,0:T(8,128)S(1)} %collective-permute-done.31.refs_6_), channel_id=1, source_target_pairs={{8,0},{16,8},{24,16},{28,24},{20,28},{12,20},{4,12},{0,4},{9,1},{1... | collective-permute-start | bytes 393224 | tf_op jit(solution)/shard_map/ppermute | solution.py:413
  119.9 6.3 %collective-permute-start.37 = (f32[256,128]{1,0:T(8,128)S(1)}, f32[256,128]{1,0:T(8,128)S(1)}, u32[]{:S(2)}, u32[]{:S(2)}) collective-permute-start(f32[256,128]{1,0:T(8,128)S(1)} %collective-permute-done.36.refs_17_), channel_id=1, source_target_pairs={{0,8},{8,16},{16,24},{24,28},{28,20},{20,12},{12,4},{4,0},{1,9},{9... | collective-permute-start | bytes 393224 | tf_op jit(solution)/shard_map/ppermute | solution.py:410
  119.9 12.9 %collective-permute-start.15 = (f32[512,128]{1,0:T(8,128)S(1)}, f32[512,128]{1,0:T(8,128)S(1)}, u32[]{:S(2)}, u32[]{:S(2)}) collective-permute-start(f32[512,128]{1,0:T(8,128)S(1)} %pad_maximum_fusion), channel_id=1, source_target_pairs={{0,1},{1,0},{2,3},{3,2},{4,5},{5,4},{6,7},{7,6},{8,9},{9,8},{10,11... | collective-permute-start | bytes 786440 | tf_op jit(solution)/shard_map/ppermute | solution.py:387
  121.6 7.1 %collective-permute-start.42 = (f32[256,128]{1,0:T(8,128)S(1)}, f32[256,128]{1,0:T(8,128)S(1)}, u32[]{:S(2)}, u32[]{:S(2)}) collective-permute-start(f32[256,128]{1,0:T(8,128)S(1)} %collective-permute-done.41.refs_18_), channel_id=1, source_target_pairs={{0,8},{8,16},{16,24},{24,28},{28,20},{20,12},{12,4},{4,0},{1,9},{9... | collective-permute-start | bytes 393224 | tf_op jit(solution)/shard_map/ppermute | solution.py:410
  121.8 7.0 %collective-permute-start.32 = (f32[256,128]{1,0:T(8,128)S(1)}, f32[256,128]{1,0:T(8,128)S(1)}, u32[]{:S(2)}, u32[]{:S(2)}) collective-permute-start(f32[256,128]{1,0:T(8,128)S(1)} %collective-permute-done.30.refs_5_), channel_id=1, source_target_pairs={{8,0},{16,8},{24,16},{28,24},{20,28},{12,20},{4,12},{0,4},{9,1},{1... | collective-permute-start | bytes 393224 | tf_op jit(solution)/shard_map/ppermute | solution.py:413
  123.7 7.1 %collective-permute-start.35 = (f32[256,128]{1,0:T(8,128)S(1)}, f32[256,128]{1,0:T(8,128)S(1)}, u32[]{:S(2)}, u32[]{:S(2)}) collective-permute-start(f32[256,128]{1,0:T(8,128)S(1)} %collective-permute-done.33.refs_8_), channel_id=1, source_target_pairs={{8,0},{16,8},{24,16},{28,24},{20,28},{12,20},{4,12},{0,4},{9,1},{1... | collective-permute-start | bytes 393224 | tf_op jit(solution)/shard_map/ppermute | solution.py:413
  126.1 5.6 %collective-permute-start.38 = (f32[256,128]{1,0:T(8,128)S(1)}, f32[256,128]{1,0:T(8,128)S(1)}, u32[]{:S(2)}, u32[]{:S(2)}) collective-permute-start(f32[256,128]{1,0:T(8,128)S(1)} %collective-permute-done.37.refs_15_), channel_id=1, source_target_pairs={{0,8},{8,16},{16,24},{24,28},{28,20},{20,12},{12,4},{4,0},{1,9},{9... | collective-permute-start | bytes 393224 | tf_op jit(solution)/shard_map/ppermute | solution.py:410
  128.8 6.3 %collective-permute-start.43 = (f32[256,128]{1,0:T(8,128)S(1)}, f32[256,128]{1,0:T(8,128)S(1)}, u32[]{:S(2)}, u32[]{:S(2)}) collective-permute-start(f32[256,128]{1,0:T(8,128)S(1)} %collective-permute-done.42.refs_16_), channel_id=1, source_target_pairs={{0,8},{8,16},{16,24},{24,28},{28,20},{20,12},{12,4},{4,0},{1,9},{9... | collective-permute-start | bytes 393224 | tf_op jit(solution)/shard_map/ppermute | solution.py:410
  128.8 6.3 %collective-permute-start.34 = (f32[256,128]{1,0:T(8,128)S(1)}, f32[256,128]{1,0:T(8,128)S(1)}, u32[]{:S(2)}, u32[]{:S(2)}) collective-permute-start(f32[256,128]{1,0:T(8,128)S(1)} %collective-permute-done.32.refs_7_), channel_id=1, source_target_pairs={{8,0},{16,8},{24,16},{28,24},{20,28},{12,20},{4,12},{0,4},{9,1},{1... | collective-permute-start | bytes 393224 | tf_op jit(solution)/shard_map/ppermute | solution.py:413
  (14 other events, 82.0 us)
